TPU v7x, 32 devices: a whole 2x2x4 slice. The times are simulated.
32 devices in a mesh: dp: 16 (over z, y, x), tensor: 2 (over core).
Axes of the slice: x: 2, y: 2, z: 4, core: 2. Of those that a mesh axis runs over, the one named last changes fastest.
Arguments:
- layer_input: bfloat16 [16384, 768], P('dp'), may hold values from -6 to 6
- cotangent: bfloat16 [16384, 768], P('dp'), may hold values from -6 to 6
- segment_ids: int32 [16384], P('dp'), may hold values from -1 to 1, as said below
- attend_weight: float32 [768, 2304], P('dp', 'tensor'), may hold values from -0.21875 to 0.21875
- output_weight: float32 [768, 768], P('dp', 'tensor'), may hold values from -1.25 to 1.25
- widen_weight: float32 [768, 3072], P('dp', 'tensor'), may hold values from -0.21875 to 0.21875
- narrow_weight: float32 [768, 3072], P('dp', 'tensor'), may hold values from -0.109375 to 0.109375
- attend_moment: float32 [768, 2304], P('dp', 'tensor')
- output_moment: float32 [768, 768], P('dp', 'tensor')
- widen_moment: float32 [768, 3072], P('dp', 'tensor')
- narrow_moment: float32 [768, 3072], P('dp', 'tensor')
- vector_params: float32 [13, 768], replicated
- vector_first: float32 [13, 768], replicated
- vector_second: float32 [13, 768], replicated, as said below
Outputs:
- block_output: bfloat16 [16384, 768], P('dp', 'tensor')
- input_grad: float32 [16384, 768], P('dp')
- attend_grad: float32 [768, 2304], P('dp', 'tensor')
- output_grad: float32 [768, 768], P('dp', 'tensor')
- widen_grad: float32 [768, 3072], P('dp', 'tensor')
- narrow_grad: float32 [768, 3072], P('dp', 'tensor')
- momentum_attend: float32 [768, 2304], P('dp', 'tensor')
- momentum_output: float32 [768, 768], P('dp', 'tensor')
- momentum_widen: float32 [768, 3072], P('dp', 'tensor')
- momentum_narrow: float32 [768, 3072], P('dp', 'tensor')
- updated_attend: float32 [768, 2304], P('dp', 'tensor')
- updated_output: float32 [768, 768], P('dp', 'tensor')
- updated_widen: float32 [768, 3072], P('dp', 'tensor')
- updated_narrow: float32 [768, 3072], P('dp', 'tensor')
- vector_grad: float32 [13, 768], replicated
- first_moment: float32 [13, 768], replicated
- second_moment: float32 [13, 768], replicated
- updated_vectors: float32 [13, 768], replicated
Inputs may be any that keep to these rules, and one draw needn't show every extreme that they name: `segment_ids`: in each group of 1024 slots the ids are 0 and possibly then 1 over a live prefix of one or more blocks of 512 slots (the last possibly partly filled), followed by -1; id 0 covers 512 // 2 slots or more; in every draw some group is one sequence of all 1024 slots. `vector_second`: entries are positive.
All inputs are finite; a program needn't handle non-finite values.
Results may differ from a plain program's by a relative error of at most 0.009.
The roundings to bfloat16 on the way count: a program that leaves them out, or rounds other values in their place, can miss the bound.
Values may be sent and summed in bfloat16 or wider, within the bound.
No kernel may reach another device: no remote copies, remote signals or barrier semaphores. Data moves between devices by JAX's collectives and lax.ppermute only.
A program may use at most 192 MiB of HBM per device.

v0:
```python
import math

import jax
import jax.numpy as jnp
from jax import lax
from jax.sharding import PartitionSpec as P

D = 768
HEAD_DIM = 64
FF = 3072
ROTARY = 16
BLOCK = 512
NS_STEPS = 5
STEP = 10


HIGHEST = lax.Precision.HIGHEST
NORM_EPS = 1e-05
POLY_ONE = 3.4445
POLY_TWO = -4.775
POLY_THREE = 2.0315
SCALE_EPS = 1e-07
MUON_BETA = 0.9
MUON_RATE = 0.03
MUON_DECAY = 0.1
BETA_ONE = 0.9
BETA_TWO = 0.95
ADAM_RATE = 0.1
ADAM_EPS = 1e-08


def as_sent(value):
    return jax.tree.map(lambda a: a.astype(jnp.bfloat16) if a.dtype == jnp.float32 else a, value)


def spread(value, axis, source):
    kept = jnp.where(lax.axis_index(axis) == source, value, 0).astype(value.dtype)
    return lax.psum(kept, axis)


def norm_stats(values):
    row_mean = jnp.mean(values, axis=-1, keepdims=True)
    centered = values - row_mean
    row_var = jnp.mean(centered * centered, axis=-1, keepdims=True)
    inverse = lax.rsqrt(row_var + NORM_EPS)
    return (centered * inverse, inverse)


def norm_backward(incoming, normed, inverse, gain):
    scaled = incoming * gain
    return inverse * (
        scaled
        - jnp.mean(scaled, axis=-1, keepdims=True)
        - normed * jnp.mean(scaled * normed, axis=-1, keepdims=True)
    )


def rotate(values, cosines, sines):
    first_half = values[..., : ROTARY // 2]
    second_half = values[..., ROTARY // 2 : ROTARY]
    remainder = values[..., ROTARY:]
    return jnp.concatenate(
        [
            first_half * cosines - second_half * sines,
            second_half * cosines + first_half * sines,
            remainder,
        ],
        axis=-1,
    )


def rotate_back(values, cosines, sines):
    first_half = values[..., : ROTARY // 2]
    second_half = values[..., ROTARY // 2 : ROTARY]
    remainder = values[..., ROTARY:]
    return jnp.concatenate(
        [
            first_half * cosines + second_half * sines,
            second_half * cosines - first_half * sines,
            remainder,
        ],
        axis=-1,
    )


def rotary_tables(segments):
    token_index = jnp.arange(segments.shape[0], dtype=jnp.int32)
    leading = jnp.sum((segments == 0).astype(jnp.int32))
    position = (token_index - jnp.where(segments == 1, leading, 0)).astype(jnp.float32)
    exponent = jnp.arange(ROTARY // 2, dtype=jnp.int32).astype(jnp.float32) * (2.0 / ROTARY)
    frequency = jnp.exp(-math.log(10000.0) * exponent)
    angles = position[:, None] * frequency[None, :]
    return (jnp.cos(angles)[:, None, :], jnp.sin(angles)[:, None, :])


def gram_sum(matrices):
    square = jnp.einsum(
        "mdk,mek->mde", matrices, matrices, precision=HIGHEST, preferred_element_type=jnp.float32
    )
    gram_share = lax.psum_scatter(square, "tensor", scatter_dimension=1, tiled=True)
    return lax.all_gather(gram_share, "tensor", axis=1, tiled=True)


def newton(matrices):
    square = gram_sum(matrices)
    trace_sum = jnp.sum(jnp.diagonal(square, axis1=1, axis2=2), axis=1)
    factor = 1.0 / (jnp.sqrt(trace_sum) + SCALE_EPS)
    current = matrices * factor[:, None, None]
    square = square * (factor * factor)[:, None, None]
    for iteration in range(NS_STEPS):
        if iteration > 0:
            square = gram_sum(current)
        polynomial = POLY_TWO * square + POLY_THREE * jnp.einsum(
            "mde,mef->mdf", square, square, precision=HIGHEST
        )
        current = POLY_ONE * current + jnp.einsum(
            "mde,mek->mdk", polynomial, current, precision=HIGHEST
        )
    return current


def shards(
    layer_input,
    cotangent,
    segment_ids,
    attend_weight,
    output_weight,
    widen_weight,
    narrow_weight,
    attend_moment,
    output_moment,
    widen_moment,
    narrow_moment,
    vector_params,
    vector_first,
    vector_second,
):
    tensor_size = lax.axis_size("tensor")
    tensor_rank = lax.axis_index("tensor")
    data_size = lax.axis_size("dp")
    data_rank = lax.axis_index("dp")
    masters = (attend_weight, output_weight, widen_weight, narrow_weight)
    attend_low, output_low, widen_low, narrow_low = (
        lax.all_gather(attend_weight.astype(jnp.bfloat16), "dp", axis=0, tiled=True),
        lax.all_gather(output_weight.astype(jnp.bfloat16), "dp", axis=0, tiled=True),
        lax.all_gather(widen_weight.astype(jnp.bfloat16), "dp", axis=0, tiled=True),
        lax.all_gather(narrow_weight.astype(jnp.bfloat16), "dp", axis=0, tiled=True),
    )
    length = layer_input.shape[0]
    triple_cols = attend_low.shape[1]
    local_heads = triple_cols // (3 * HEAD_DIM)
    widen_cols = widen_low.shape[1]
    widen_rows = FF // D
    feature_share = D // tensor_size
    blocks = length // BLOCK
    float_input = layer_input.astype(jnp.float32)
    first_gain = vector_params[0]
    second_gain = vector_params[2]
    attend_bias = lax.dynamic_slice_in_dim(
        vector_params[4:7].reshape(-1), tensor_rank * triple_cols, triple_cols
    )
    widen_bias = lax.dynamic_slice_in_dim(
        vector_params[8 : 8 + widen_rows].reshape(-1), tensor_rank * widen_cols, widen_cols
    )
    normed, inverse = norm_stats(float_input)
    first_norm = (normed * first_gain + vector_params[1]).astype(jnp.bfloat16)
    second_norm = (normed * second_gain + vector_params[3]).astype(jnp.bfloat16)
    triple = jnp.dot(first_norm, attend_low, preferred_element_type=jnp.float32) + attend_bias
    triple = triple.reshape(length, local_heads, 3, HEAD_DIM)
    cosines, sines = rotary_tables(segment_ids)
    queries = rotate(triple[:, :, 0], cosines, sines).astype(jnp.bfloat16)
    key_heads = rotate(triple[:, :, 1], cosines, sines).astype(jnp.bfloat16)
    values = triple[:, :, 2].astype(jnp.bfloat16)
    token_index = jnp.arange(length, dtype=jnp.int32)

    def block_scores(first_row):
        row_index = first_row + jnp.arange(BLOCK, dtype=jnp.int32)
        block_queries = lax.dynamic_slice_in_dim(queries, first_row, BLOCK, 0)
        block_segments = lax.dynamic_slice_in_dim(segment_ids, first_row, BLOCK, 0)
        scores = jnp.einsum(
            "qhd,khd->hqk", block_queries, key_heads, preferred_element_type=jnp.float32
        ) / math.sqrt(HEAD_DIM)
        allowed = (token_index[None, :] <= row_index[:, None]) & (
            segment_ids[None, :] == block_segments[:, None]
        )
        return jnp.where(allowed[None], scores, -jnp.inf)

    def attend_block(block_index):
        scores = block_scores(block_index * BLOCK)
        row_top = jnp.max(scores, axis=-1, keepdims=True)
        exponent = jnp.exp(scores - row_top)
        row_total = jnp.sum(exponent, axis=-1, keepdims=True)
        softmax_low = (exponent / row_total).astype(jnp.bfloat16)
        mixture = jnp.einsum(
            "hqk,khd->qhd", softmax_low, values, preferred_element_type=jnp.float32
        )
        return (mixture.astype(jnp.bfloat16), row_top + jnp.log(row_total))

    def attend_any(block_index):
        return attend_block(block_index)

    mixed_blocks, logsum = lax.map(attend_any, jnp.arange(blocks, dtype=jnp.int32))
    mixture = mixed_blocks.reshape(length, local_heads * HEAD_DIM)
    attended = jnp.einsum("sk,dk->sd", mixture, output_low, preferred_element_type=jnp.float32)
    widened = jnp.dot(second_norm, widen_low, preferred_element_type=jnp.float32) + widen_bias
    activated = jax.nn.gelu(widened, approximate=False).astype(jnp.bfloat16)
    narrowed = jnp.einsum("sf,df->sd", activated, narrow_low, preferred_element_type=jnp.float32)
    branch = lax.psum_scatter(attended + narrowed, "tensor", scatter_dimension=1, tiled=True)
    live_rows = (segment_ids >= 0).astype(jnp.float32)[:, None]
    column_start = tensor_rank * feature_share

    def own_columns(array):
        return lax.dynamic_slice_in_dim(array, column_start, feature_share, array.ndim - 1)

    block_output = (
        live_rows
        * (
            own_columns(float_input)
            + branch
            + own_columns(vector_params[7])
            + own_columns(vector_params[8 + widen_rows])
        )
    ).astype(jnp.bfloat16)
    upstream = live_rows * cotangent.astype(jnp.float32)
    upstream_low = upstream.astype(jnp.bfloat16)
    bias_grad = jnp.sum(upstream, axis=0) / tensor_size
    activation_grad = jnp.einsum(
        "sd,df->sf", upstream_low, narrow_low, preferred_element_type=jnp.float32
    )
    gelu_slope = jax.vjp(lambda inner_value: jax.nn.gelu(inner_value, approximate=False), widened)[
        1
    ](activation_grad)[0]
    widen_back = gelu_slope.astype(jnp.bfloat16)
    narrow_grad = jnp.einsum(
        "sd,sf->df", upstream_low, activated, preferred_element_type=jnp.float32
    )
    widen_grad = jnp.einsum(
        "sd,sf->df", second_norm, widen_back, preferred_element_type=jnp.float32
    )
    widen_bias_grad = jnp.sum(widen_back.astype(jnp.float32), axis=0)
    second_back = jnp.einsum("sf,df->sd", widen_back, widen_low, preferred_element_type=jnp.float32)
    mixed_grad = jnp.einsum(
        "sd,dk->sk", upstream_low, output_low, preferred_element_type=jnp.float32
    ).astype(jnp.bfloat16)
    output_grad = jnp.einsum("sd,sk->dk", upstream_low, mixture, preferred_element_type=jnp.float32)
    mixed_grad = mixed_grad.reshape(length, local_heads, HEAD_DIM)

    def backward_block(carried, block_index):
        key_grad, value_grad = carried
        first_row = block_index * BLOCK
        scores = block_scores(first_row)
        block_queries = lax.dynamic_slice_in_dim(queries, first_row, BLOCK, 0)
        block_mixed = lax.dynamic_slice_in_dim(mixed_grad, first_row, BLOCK, 0)
        softmax_rows = jnp.exp(scores - logsum[block_index])
        softmax_low = softmax_rows.astype(jnp.bfloat16)
        softmax_grad = jnp.einsum(
            "qhd,khd->hqk", block_mixed, values, preferred_element_type=jnp.float32
        )
        row_delta = jnp.sum(softmax_rows * softmax_grad, axis=-1, keepdims=True)
        score_grad = (softmax_rows * (softmax_grad - row_delta)).astype(jnp.bfloat16)
        query_grad = jnp.einsum(
            "hqk,khd->qhd", score_grad, key_heads, preferred_element_type=jnp.float32
        ) / math.sqrt(HEAD_DIM)
        key_grad = key_grad + jnp.einsum(
            "hqk,qhd->khd", score_grad, block_queries, preferred_element_type=jnp.float32
        ) / math.sqrt(HEAD_DIM)
        value_grad = value_grad + jnp.einsum(
            "hqk,qhd->khd", softmax_low, block_mixed, preferred_element_type=jnp.float32
        )
        return ((key_grad, value_grad), query_grad)

    def backward_any(carried, block_index):
        return backward_block(carried, block_index)

    zero_heads = jnp.zeros((length, local_heads, HEAD_DIM), jnp.float32)
    (key_grad, value_grad), query_blocks = lax.scan(
        backward_any, (zero_heads, zero_heads), jnp.arange(blocks, dtype=jnp.int32)
    )
    query_grad = query_blocks.reshape(length, local_heads, HEAD_DIM)
    query_back = rotate_back(
        lax.optimization_barrier(query_grad.astype(jnp.bfloat16)).astype(jnp.float32),
        cosines,
        sines,
    )
    key_back = rotate_back(
        lax.optimization_barrier(key_grad.astype(jnp.bfloat16)).astype(jnp.float32), cosines, sines
    )
    triple_grad = (
        jnp.stack([query_back, key_back, value_grad], axis=2)
        .reshape(length, triple_cols)
        .astype(jnp.bfloat16)
    )
    attend_grad = jnp.einsum(
        "sd,sk->dk", first_norm, triple_grad, preferred_element_type=jnp.float32
    )
    attend_bias_grad = jnp.sum(triple_grad.astype(jnp.float32), axis=0)
    first_back = jnp.einsum(
        "sk,dk->sd", triple_grad, attend_low, preferred_element_type=jnp.float32
    )
    row_share = length // tensor_size
    row_start = tensor_rank * row_share
    first_total, second_total = (
        lax.psum_scatter(
            first_back.astype(jnp.bfloat16), "tensor", scatter_dimension=0, tiled=True
        ).astype(jnp.float32),
        lax.psum_scatter(
            second_back.astype(jnp.bfloat16), "tensor", scatter_dimension=0, tiled=True
        ).astype(jnp.float32),
    )
    normed_share = lax.dynamic_slice_in_dim(normed, row_start, row_share, 0)
    inverse_share = lax.dynamic_slice_in_dim(inverse, row_start, row_share, 0)
    upstream_share = lax.dynamic_slice_in_dim(upstream, row_start, row_share, 0)
    input_share = upstream_share + (
        norm_backward(first_total, normed_share, inverse_share, first_gain)
        + norm_backward(second_total, normed_share, inverse_share, second_gain)
    )
    input_grad = lax.all_gather(
        input_share.astype(jnp.bfloat16), "tensor", axis=0, tiled=True
    ).astype(input_share.dtype)
    norm_rows = jnp.stack(
        [
            jnp.sum(first_total * normed_share, axis=0),
            jnp.sum(first_total, axis=0),
            jnp.sum(second_total * normed_share, axis=0),
            jnp.sum(second_total, axis=0),
        ]
    )
    attend_bias_full = lax.dynamic_update_slice_in_dim(
        jnp.zeros((3 * D,), jnp.float32), attend_bias_grad, tensor_rank * triple_cols, 0
    )
    widen_bias_full = lax.dynamic_update_slice_in_dim(
        jnp.zeros((FF,), jnp.float32), widen_bias_grad, tensor_rank * widen_cols, 0
    )
    vector_part = jnp.concatenate(
        [
            norm_rows,
            attend_bias_full.reshape(3, D),
            bias_grad[None],
            widen_bias_full.reshape(widen_rows, D),
            bias_grad[None],
        ],
        axis=0,
    )
    vector_grad = lax.psum(vector_part, ("dp", "tensor"))
    attend_sum, output_sum, widen_sum, narrow_sum = (
        lax.psum_scatter(attend_grad, "dp", scatter_dimension=0, tiled=True),
        lax.psum_scatter(output_grad, "dp", scatter_dimension=0, tiled=True),
        lax.psum_scatter(widen_grad, "dp", scatter_dimension=0, tiled=True),
        lax.psum_scatter(narrow_grad, "dp", scatter_dimension=0, tiled=True),
    )
    summed = (attend_sum, output_sum, widen_sum, narrow_sum)
    moments = (attend_moment, output_moment, widen_moment, narrow_moment)
    momenta = [MUON_BETA * previous + gradient for previous, gradient in zip(moments, summed)]
    widths = [matrix.shape[1] for matrix in momenta]
    widest = max(widths)
    rows_here = D // data_size
    owner_list = [matrix_index * data_size // 4 for matrix_index in range(4)]
    gathered = (
        lax.all_gather(momenta[0].astype(jnp.bfloat16), "dp", axis=0, tiled=True).astype(
            jnp.float32
        ),
        lax.all_gather(momenta[1].astype(jnp.bfloat16), "dp", axis=0, tiled=True).astype(
            jnp.float32
        ),
        lax.all_gather(momenta[2].astype(jnp.bfloat16), "dp", axis=0, tiled=True).astype(
            jnp.float32
        ),
        lax.all_gather(momenta[3].astype(jnp.bfloat16), "dp", axis=0, tiled=True).astype(
            jnp.float32
        ),
    )
    padded = jnp.stack(
        [jnp.pad(matrix, ((0, 0), (0, widest - matrix.shape[1]))) for matrix in gathered]
    )
    owned_slot = jnp.zeros((), jnp.int32)
    for matrix_index in range(4):
        owned_slot = owned_slot + jnp.where(
            data_rank == owner_list[matrix_index], matrix_index, 0
        ).astype(jnp.int32)
    chosen = lax.dynamic_index_in_dim(padded, owned_slot, 0, keepdims=True)
    result = newton(chosen)[0]
    orthos = [
        spread(as_sent(result[:, : widths[matrix_index]]), "dp", owner_list[matrix_index])
        for matrix_index in range(4)
    ]
    row_parts = [
        lax.dynamic_slice_in_dim(orthos[matrix_index], data_rank * rows_here, rows_here, 0)
        for matrix_index in range(4)
    ]
    updated = []
    for matrix_index in range(4):
        longest = max(D, widths[matrix_index] * tensor_size)
        updated.append(
            masters[matrix_index] * (1.0 - MUON_RATE * MUON_DECAY)
            - MUON_RATE * math.sqrt(longest) * row_parts[matrix_index]
        )
    first_new = BETA_ONE * vector_first + (1.0 - BETA_ONE) * vector_grad
    second_new = BETA_TWO * vector_second + (1.0 - BETA_TWO) * vector_grad * vector_grad
    first_hat = first_new / (1.0 - BETA_ONE**STEP)
    second_hat = second_new / (1.0 - BETA_TWO**STEP)
    vectors_new = vector_params - ADAM_RATE * first_hat / (jnp.sqrt(second_hat) + ADAM_EPS)
    return (
        block_output,
        input_grad,
        attend_sum,
        output_sum,
        widen_sum,
        narrow_sum,
        momenta[0],
        momenta[1],
        momenta[2],
        momenta[3],
        updated[0],
        updated[1],
        updated[2],
        updated[3],
        vector_grad,
        first_new,
        second_new,
        vectors_new,
    )


def solution(mesh):
    return jax.shard_map(
        shards,
        mesh=mesh,
        in_specs=(
            P("dp", None),
            P("dp", None),
            P("dp"),
            P("dp", "tensor"),
            P("dp", "tensor"),
            P("dp", "tensor"),
            P("dp", "tensor"),
            P("dp", "tensor"),
            P("dp", "tensor"),
            P("dp", "tensor"),
            P("dp", "tensor"),
            P(),
            P(),
            P(),
        ),
        out_specs=(
            P("dp", "tensor"),
            P("dp", None),
            P("dp", "tensor"),
            P("dp", "tensor"),
            P("dp", "tensor"),
            P("dp", "tensor"),
            P("dp", "tensor"),
            P("dp", "tensor"),
            P("dp", "tensor"),
            P("dp", "tensor"),
            P("dp", "tensor"),
            P("dp", "tensor"),
            P("dp", "tensor"),
            P("dp", "tensor"),
            P(),
            P(),
            P(),
            P(),
        ),
        check_vma=False,
    )
```

profile of v0, /device:TPU:0, one launch (start us, length us, event | category | flops | bytes accessed | tf_op | source)
XLA Modules:
  0.0 1548.9 jit_solution(2627935909917507351)
XLA Ops:
  20.5 49.7 %all_gather.43 = bf16[768,384]{1,0:T(8,128)(2,1)} all-gather(bf16[48,384]{1,0:T(8,128)(2,1)S(1)} %convert_element_type.174), channel_id=1, replica_groups=mesh['dp'=16,'tensor'=2] {'dp'}, dimensions={0}, use_global_device_ids=true | all-gather | bytes 626688 | tf_op jit(solution)/shard_map/all_gather | solution.py:145
  74.7 6.1 convolution_add_fusion
  80.8 6.1 copy.45
  91.1 25.3 %while.28 = (s32[]{:T(128)}, bf16[2,512,6,64]{1,3,2,0:T(8,128)(2,1)}, f32[2,6,512,1]{2,1,3,0:T(8,128)S(1)}, s32[2]{0:T(128)S(1)}, s32[1024]{0:T(1024)S(1)}, /*in...) while((s32[]{:T(128)}, ...), condition=%wide.region_6.7_spmd.clone, body=%wide.region_3.6_spmd.clone.sunk | while | flops 844822016 | bytes 42330812 | solution.py:202
  95.2 3.6 fusion.232
  98.8 4.9 fusion.233
  107.8 3.6 fusion.232
  111.5 4.9 fusion.233
  116.4 81.5 %while.29 = (s32[]{:T(128)}, f32[1024,6,64]{0,2,1:T(8,128)}, f32[1024,6,64]{0,2,1:T(8,128)}, bf16[2,512,6,64]{1,3,2,0:T(8,128)(2,1)}, s32[2]{0:T(128)S(1)}, /*in...) while((s32[]{:T(128)}, f32[1024,6,64]{0,2,1:T(8,128)}, ...), condition=%wide.region_10.11_spmd.clone, body=%wide.region_8.10_spmd.clone.sunk | while | flops 2064184832 | bytes 186227216 | solution.py:276
  118.5 6.4 fusion.243
  126.9 7.6 multiply_reduce_fusion.3
  135.6 5.0 multiply_convert_fusion.4
  140.6 5.3 bitcast_add_fusion.19
  148.8 7.8 bitcast_add_fusion.20
  158.5 6.4 fusion.243
  167.0 7.6 multiply_reduce_fusion.3
  175.6 5.0 multiply_convert_fusion.4
  180.6 5.7 bitcast_add_fusion.19
  189.3 8.2 bitcast_add_fusion.20
  204.7 4.5 fusion.151
  210.0 19.8 %multiply_convert_fusion.1 = (bf16[1024,1536]{1,0:T(8,128)(2,1)}, f32[1024,1536]{1,0:T(8,128)}, f32[1024,1536]{1,0:T(8,128)}) fusion(f32[1536]{0:T(1024)S(1)} %dynamic_slice.66, bf16[768,1536]{1,0:T(8,128)(2,1)} %all-gather.15.cloned.1.call-done, f32[768]{0:T(1024)S(1)} %copy-done.48, f32[768]{0:T(1024)S(1)} %copy-done.43, f32[1024]{0:T(1024)S(1)} %copy-done.45, ...), kind=kOutput, calls=%fused_computation.53 | convolution fusion | flops 2524446720 | bytes 19681280 | tf_op jit(solution)/shard_map/dot_general | solution.py:205
  229.8 8.4 convert_reduce_fusion
  240.0 4.6 fusion.152
  244.6 6.6 fusion.171
  256.7 85.2 %reduce-scatter.19.cloned.1.call-done = f32[48,1152]{1,0:T(8,128)} async-done(((f32[768,1152]{1,0:T(8,128)}), f32[48,1152]{1,0:T(8,128)}) %reduce-scatter.19.cloned.1.call-update) | async-done | bytes 221200 | tf_op jit(solution)/shard_map/reduce_scatter | solution.py:346
  343.6 139.4 %reduce-scatter.23.cloned.1.call-done = f32[48,1536]{1,0:T(8,128)} async-done(((f32[768,1536]{1,0:T(8,128)}), f32[48,1536]{1,0:T(8,128)}) %reduce-scatter.23.cloned.1.call-update) | async-done | bytes 294928 | tf_op jit(solution)/shard_map/reduce_scatter | solution.py:348
  485.0 141.0 %reduce-scatter.25.cloned.1.call-done = f32[48,1536]{1,0:T(8,128)} async-done(((f32[768,1536]{1,0:T(8,128)}), f32[48,1536]{1,0:T(8,128)}) %reduce-scatter.25.cloned.1.call-update) | async-done | bytes 294928 | tf_op jit(solution)/shard_map/reduce_scatter | solution.py:349
  627.9 126.1 %reduce-scatter.21.cloned.1.call-done = f32[48,384]{1,0:T(8,128)} async-done(((f32[768,384]{1,0:T(8,128)}), f32[48,384]{1,0:T(8,128)}) %reduce-scatter.21.cloned.1.call-update) | async-done | bytes 73744 | tf_op jit(solution)/shard_map/reduce_scatter | solution.py:347
  755.6 43.3 %all_gather.48 = bf16[768,384]{1,0:T(8,128)(2,1)S(1)} all-gather(bf16[48,384]{1,0:T(8,128)(2,1)S(1)} %get-tuple-element.254), channel_id=1, replica_groups=mesh['dp'=16,'tensor'=2] {'dp'}, dimensions={0}, use_global_device_ids=true | all-gather | bytes 626688 | tf_op jit(solution)/shard_map/all_gather | solution.py:362
  800.5 15.7 %all-gather.21.cloned.1.call-done = bf16[768,1152]{1,0:T(8,128)(2,1)} async-done(((bf16[48,1152]{1,0:T(8,128)(2,1)}), bf16[768,1152]{1,0:T(8,128)(2,1)}) %all-gather.21.cloned.1.call-update) | async-done | bytes 1769488 | tf_op jit(solution)/shard_map/all_gather | solution.py:359
  819.3 61.4 %all-gather.23.cloned.1.call-done = bf16[768,1536]{1,0:T(8,128)(2,1)} async-done(((bf16[48,1536]{1,0:T(8,128)(2,1)}), bf16[768,1536]{1,0:T(8,128)(2,1)}) %all-gather.23.cloned.1.call-update) | async-done | bytes 2359312 | tf_op jit(solution)/shard_map/all_gather | solution.py:365
  880.7 64.4 %all-gather.25.cloned.1.call-done = bf16[768,1536]{1,0:T(8,128)(2,1)} async-done(((bf16[48,1536]{1,0:T(8,128)(2,1)}), bf16[768,1536]{1,0:T(8,128)(2,1)}) %all-gather.25.cloned.1.call-update) | async-done | bytes 2359312 | tf_op jit(solution)/shard_map/all_gather | solution.py:368
  945.1 4.7 pad_maximum_fusion
  949.8 3.6 copy-done.7
  956.9 8.8 reduce-scatter.27.cloned.1.call-done
  965.8 13.5 all-gather.27.cloned.1.call-done
  979.3 12.2 gather_fusion
  992.9 8.5 fusion.88
  1001.4 14.7 bitcast_add_fusion.6
  1018.3 13.0 fusion.116
  1031.4 11.2 reduce-scatter.29.cloned.1.call-done
  1042.6 13.5 all-gather.29.cloned.1.call-done
  1056.1 8.4 fusion.85
  1064.5 14.8 bitcast_add_fusion.5
  1081.4 13.2 fusion.119
  1094.7 11.2 reduce-scatter.31.cloned.1.call-done
  1106.0 13.6 all-gather.31.cloned.1.call-done
  1119.5 8.4 fusion.82
  1127.9 14.7 bitcast_add_fusion.4
  1144.8 13.0 fusion.122
  1157.9 11.2 reduce-scatter.33.cloned.1.call-done
  1169.1 13.5 all-gather.33.cloned.1.call-done
  1182.6 8.4 fusion.79
  1191.0 15.0 bitcast_add_fusion.3
  1208.1 13.0 fusion.125
  1221.2 5.6 convolution_convert_fusion.1
  1226.9 7.3 convolution_convert_fusion
  1239.3 5.5 reduce-scatter.15.cloned.1.call-done
  1244.8 12.6 reduce-scatter.17.cloned.1.call-done
  1264.2 5.6 fusion.186
  1272.8 8.5 fusion.76
  1281.4 16.2 %broadcast_select_fusion = (bf16[768,1536]{1,0:T(8,128)(2,1)}, bf16[768,1536]{1,0:T(8,128)(2,1)}, bf16[768,1536]{1,0:T(8,128)(2,1)S(1)}) fusion(pred[]{:T(512)S(6)} %eq.65, pred[]{:T(512)S(6)} %eq.64, f32[1,768,1536]{2,1,0:T(8,128)} %copy-done.13, f32[768,768]{1,0:T(8,128)S(1)} %fusion.76, f32[1,768,768]{2,1,0:T(8,128)S(1)} %copy-done.17), kind=kOutput, calls=%fused_computation.143 | convolution fusion | flops 10879303680 | bytes 16515074 | tf_op jit(solution)/shard_map/mde,mek->mdk/dot_general | solution.py:116
  1302.7 43.3 %psum.39 = f32[13,768]{1,0:T(8,128)S(1)} all-reduce(f32[13,768]{1,0:T(8,128)S(1)} %concatenate.26), channel_id=1, replica_groups=mesh['dp'=16,'tensor'=2] {'dp','tensor'}, use_global_device_ids=true, to_apply=%region_38.39 | all-reduce | flops 9984 | bytes 79872 | tf_op jit(solution)/shard_map/psum | solution.py:344
  1352.7 182.9 %all-reduce.5.cloned.1.call-done = (bf16[768,1152]{1,0:T(8,128)(2,1)}, bf16[768,384]{1,0:T(8,128)(2,1)}, bf16[768,1536]{1,0:T(8,128)(2,1)}, bf16[768,1536]{1,0:T(8,128)(2,1)}) async-done(((bf16[768,1152]{1,0:T(8,128)(2,1)}, bf16[768,384]{1,0:T(8,128)(2,1)}, bf16[768,1536]{1,0:T(8,128)(2,1)}, bf16[768,1536]{1,0:T(8,128)(2,1)}), (bf16[768,1152]{1,0:T(8,128)(2,1)}, bf16[768,384]{1,0:T(8,128)(2,1)}, ...) | async-done | bytes 7077904 | tf_op jit(solution)/shard_map/psum | solution.py:38
  (316 shorter events, 111.7 us)
Async XLA Ops:
  7.2 12.6 copy-start.19
  7.2 12.0 copy-start.4
  7.2 13.3 copy-start.29
  7.2 63.3 %copy-start.10 = (bf16[1024,768]{1,0:T(8,128)(2,1)S(1)}, bf16[1024,768]{1,0:T(8,128)(2,1)}, u32[]{:S(2)}) copy-start(bf16[1024,768]{1,0:T(8,128)(2,1)} %param.19) | copy-start | bytes 4718596
  7.2 67.5 %all-gather.13.cloned.1.call-start = ((), (), s32[]{:S(2)}) async-start(), calls=%async_computation.12 | async-start | bytes 1880064 | tf_op jit(solution)/shard_map/all_gather | solution.py:144
  9.1 200.9 %all-gather.15.cloned.1.call-start = ((), (), s32[]{:S(2)}) async-start(), calls=%async_computation.13 | async-start | bytes 2506752 | tf_op jit(solution)/shard_map/all_gather | solution.py:146
  10.8 219.0 %all-gather.17.cloned.1.call-start = ((), (), s32[]{:S(2)}) async-start(), calls=%async_computation.14 | async-start | bytes 2506752 | tf_op jit(solution)/shard_map/all_gather | solution.py:147
  12.5 329.4 %reduce-scatter.19.cloned.1.call-start = ((), (), s32[]{:S(2)}) async-start(), calls=%async_computation.19 | async-start | bytes 3760128 | tf_op jit(solution)/shard_map/reduce_scatter | solution.py:346
  15.4 59.3 %copy-start.40 = (f32[768]{0:T(1024)}, f32[768]{0:T(1024)S(1)}, u32[]{:S(2)}) copy-start(f32[768]{0:T(1024)S(1)} %get-tuple-element.201) | copy-start | bytes 9220
  15.4 59.3 %copy-start.49 = (f32[768]{0:T(1024)}, f32[768]{0:T(1024)S(1)}, u32[]{:S(2)}) copy-start(f32[768]{0:T(1024)S(1)} %get-tuple-element.204) | copy-start | bytes 9220
  17.5 56.0 %copy-start.23 = (f32[1024]{0:T(1024)}, f32[1024]{0:T(1024)S(1)}, u32[]{:S(2)}) copy-start(f32[1024]{0:T(1024)S(1)} %compare_convert_fusion) | copy-start | bytes 12292
  19.2 61.7 %copy-start.38 = (f32[1024]{0:T(1024)}, f32[1024]{0:T(1024)S(1)}, u32[]{:S(2)}) copy-start(f32[1024]{0:T(1024)S(1)} %broadcast_multiply_fusion.1) | copy-start | bytes 12292
  19.8 61.0 %copy-start.44 = (f32[1024]{0:T(1024)}, f32[1024]{0:T(1024)S(1)}, u32[]{:S(2)}) copy-start(f32[1024]{0:T(1024)S(1)} %add_rsqrt_fusion) | copy-start | bytes 12292
  70.5 20.2 %copy-start.25 = (f32[1024,8]{0,1:T(8,128)}, f32[1024,8]{0,1:T(8,128)S(1)}, u32[]{:S(2)}) copy-start(f32[1024,8]{0,1:T(8,128)S(1)} %get-tuple-element.286) | copy-start | bytes 98308
  70.6 20.2 %copy-start.27 = (f32[1024,8]{0,1:T(8,128)}, f32[1024,8]{0,1:T(8,128)S(1)}, u32[]{:S(2)}) copy-start(f32[1024,8]{0,1:T(8,128)S(1)} %get-tuple-element.287) | copy-start | bytes 98308
  116.5 10.3 copy-start.2
  126.8 7.7 slice-start
  126.8 7.7 slice-start.1
  126.9 8.7 slice-start.2
  148.8 7.8 copy-start.3
  156.6 10.3 copy-start.2
  166.9 7.7 slice-start
  166.9 7.7 slice-start.1
  166.9 8.7 slice-start.2
  180.6 5.8 copy-start
  180.6 5.8 copy-start.21
  189.3 8.2 copy-start.3
  209.2 273.9 %reduce-scatter.23.cloned.1.call-start = ((), (), s32[]{:S(2)}) async-start(), calls=%async_computation.21 | async-start | bytes 5013504 | tf_op jit(solution)/shard_map/reduce_scatter | solution.py:348
  209.9 19.8 %copy-start.11 = (bf16[1024,768]{1,0:T(8,128)(2,1)S(1)}, bf16[1024,768]{1,0:T(8,128)(2,1)}, u32[]{:S(2)}) copy-start(bf16[1024,768]{1,0:T(8,128)(2,1)} %param.19) | copy-start | bytes 4718596
  210.0 19.8 %copy-start.24 = (f32[1024]{0:T(1024)S(1)}, f32[1024]{0:T(1024)}, u32[]{:S(2)}) copy-start(f32[1024]{0:T(1024)} %copy-done.23) | copy-start | bytes 12292
  244.6 381.4 %reduce-scatter.25.cloned.1.call-start = ((), (), s32[]{:S(2)}) async-start(), calls=%async_computation.22 | async-start | bytes 5013504 | tf_op jit(solution)/shard_map/reduce_scatter | solution.py:349
  251.2 502.8 %reduce-scatter.21.cloned.1.call-start = ((), (), s32[]{:S(2)}) async-start(), calls=%async_computation.20 | async-start | bytes 1253376 | tf_op jit(solution)/shard_map/reduce_scatter | solution.py:347
  253.2 88.7 %copy-start.31 = (f32[48,1152]{1,0:T(8,128)S(1)}, f32[48,1152]{1,0:T(8,128)}, u32[]{:S(2)}) copy-start(f32[48,1152]{1,0:T(8,128)} %param.25) | copy-start | bytes 663556
  256.6 497.5 %copy-start.34 = (f32[48,384]{1,0:T(8,128)S(1)}, f32[48,384]{1,0:T(8,128)}, u32[]{:S(2)}) copy-start(f32[48,384]{1,0:T(8,128)} %param.26) | copy-start | bytes 221188
  256.6 559.6 %all-gather.21.cloned.1.call-start = ((), (), s32[]{:S(2)}) async-start(), calls=%async_computation.23 | async-start | bytes 1880064 | tf_op jit(solution)/shard_map/all_gather | solution.py:359
  343.6 537.1 %all-gather.23.cloned.1.call-start = ((), (), s32[]{:S(2)}) async-start(), calls=%async_computation.24 | async-start | bytes 2506752 | tf_op jit(solution)/shard_map/all_gather | solution.py:365
  485.0 460.1 %all-gather.25.cloned.1.call-start = ((), (), s32[]{:S(2)}) async-start(), calls=%async_computation.25 | async-start | bytes 2506752 | tf_op jit(solution)/shard_map/all_gather | solution.py:368
  627.9 337.9 %reduce-scatter.27.cloned.1.call-start = ((), (), s32[]{:S(2)}) async-start(), calls=%async_computation.26 | async-start | bytes 3538944 | tf_op jit(solution)/shard_map/reduce_scatter | solution.py:100
  956.8 22.5 %all-gather.27.cloned.1.call-start = ((), (), s32[]{:S(2)}) async-start(), calls=%async_computation.27 | async-start | bytes 3538944 | tf_op jit(solution)/shard_map/all_gather | solution.py:101
  965.8 76.8 %reduce-scatter.29.cloned.1.call-start = ((), (), s32[]{:S(2)}) async-start(), calls=%async_computation.28 | async-start | bytes 3538944 | tf_op jit(solution)/shard_map/reduce_scatter | solution.py:100
  992.9 8.5 copy-start.8
  1031.3 24.8 %all-gather.29.cloned.1.call-start = ((), (), s32[]{:S(2)}) async-start(), calls=%async_computation.29 | async-start | bytes 3538944 | tf_op jit(solution)/shard_map/all_gather | solution.py:101
  1042.6 63.3 %reduce-scatter.31.cloned.1.call-start = ((), (), s32[]{:S(2)}) async-start(), calls=%async_computation.30 | async-start | bytes 3538944 | tf_op jit(solution)/shard_map/reduce_scatter | solution.py:100
  1056.1 8.4 copy-start.51
  1094.7 24.9 %all-gather.31.cloned.1.call-start = ((), (), s32[]{:S(2)}) async-start(), calls=%async_computation.31 | async-start | bytes 3538944 | tf_op jit(solution)/shard_map/all_gather | solution.py:101
  1105.9 63.2 %reduce-scatter.33.cloned.1.call-start = ((), (), s32[]{:S(2)}) async-start(), calls=%async_computation.32 | async-start | bytes 3538944 | tf_op jit(solution)/shard_map/reduce_scatter | solution.py:100
  1119.5 8.4 copy-start.52
  1157.8 24.8 %all-gather.33.cloned.1.call-start = ((), (), s32[]{:S(2)}) async-start(), calls=%async_computation.33 | async-start | bytes 3538944 | tf_op jit(solution)/shard_map/all_gather | solution.py:101
  1169.1 65.1 %reduce-scatter.35.cloned.1.call-start = ((), (), s32[]{:S(2)}) async-start(), calls=%async_computation.34 | async-start | bytes 3538944 | tf_op jit(solution)/shard_map/reduce_scatter | solution.py:100
  1182.6 8.4 copy-start.53
  1221.1 23.7 %reduce-scatter.15.cloned.1.call-start = ((), (), s32[]{:S(2)}) async-start(), calls=%async_computation.16 | async-start | bytes 2359296 | tf_op jit(solution)/shard_map/reduce_scatter | solution.py:303
  1226.8 30.6 %reduce-scatter.17.cloned.1.call-start = ((), (), s32[]{:S(2)}) async-start(), calls=%async_computation.17 | async-start | bytes 2359296 | tf_op jit(solution)/shard_map/reduce_scatter | solution.py:306
  1234.2 38.7 %all-gather.35.cloned.1.call-start = ((), (), s32[]{:S(2)}) async-start(), calls=%async_computation.35 | async-start | bytes 3538944 | tf_op jit(solution)/shard_map/all_gather | solution.py:101
  1234.9 111.8 %all-gather.19.cloned.1.call-start = ((), (), s32[]{:S(2)}) async-start(), calls=%async_computation.18 | async-start | bytes 2359296 | tf_op jit(solution)/shard_map/all_gather | solution.py:317
  1237.1 20.3 %copy-start.42 = (f32[768]{0:T(1024)S(1)}, f32[768]{0:T(1024)}, u32[]{:S(2)}) copy-start(f32[768]{0:T(1024)} %copy-done.40) | copy-start | bytes 9220
  1264.1 85.9 %reduce-scatter.13.cloned.1.call-start = ((), (), s32[]{:S(2)}) async-start(), calls=%async_computation.15 | async-start | bytes 4718592 | tf_op jit(solution)/shard_map/reduce_scatter | solution.py:208
  1272.5 263.1 %all-reduce.5.cloned.1.call-start = ((), (), s32[]{:S(2)}) async-start(), calls=%async_computation.36 | async-start | bytes 14155776 | tf_op jit(solution)/shard_map/psum | solution.py:38
  1272.8 8.6 copy-start.17
  1299.9 46.1 %copy-start.33 = (f32[13,768]{1,0:T(8,128)S(1)}, f32[13,768]{1,0:T(8,128)}, u32[]{:S(2)}) copy-start(f32[13,768]{1,0:T(8,128)} %param.29) | copy-start | bytes 119812
  1299.9 46.1 %copy-start.36 = (f32[13,768]{1,0:T(8,128)S(1)}, f32[13,768]{1,0:T(8,128)}, u32[]{:S(2)}) copy-start(f32[13,768]{1,0:T(8,128)} %param.31) | copy-start | bytes 119812
  1299.9 46.1 %copy-start.37 = (f32[13,768]{1,0:T(8,128)S(1)}, f32[13,768]{1,0:T(8,128)}, u32[]{:S(2)}) copy-start(f32[13,768]{1,0:T(8,128)} %param.30) | copy-start | bytes 119812
  1301.8 48.2 %copy-start.9 = (f32[1024,768]{1,0:T(8,128)S(1)}, f32[1024,768]{1,0:T(8,128)}, u32[]{:S(2)}) copy-start(f32[1024,768]{1,0:T(8,128)} %convert_element_type.167) | copy-start | bytes 9437188
  1350.0 185.6 %copy-start.20 = (f32[48,1536]{1,0:T(8,128)S(1)}, f32[48,1536]{1,0:T(8,128)}, u32[]{:S(2)}) copy-start(f32[48,1536]{1,0:T(8,128)} %param.24) | copy-start | bytes 884740
  1350.0 190.7 %copy-start.30 = (f32[48,384]{1,0:T(8,128)S(1)}, f32[48,384]{1,0:T(8,128)}, u32[]{:S(2)}) copy-start(f32[48,384]{1,0:T(8,128)} %param.22) | copy-start | bytes 221188
  (32 other events, 70.0 us)
Sparse Core Ops, SparseCore 0:
  11.4 63.2 all-gather.12
  78.1 61.0 all-gather.14
  142.5 61.1 all-gather.16
  209.3 132.5 reduce-scatter.18
  347.5 135.5 reduce-scatter.22
  489.5 136.4 reduce-scatter.24
  631.3 122.6 reduce-scatter.20
  757.4 58.7 all-gather.20
  819.6 61.0 all-gather.22
  883.9 61.0 all-gather.24
  957.0 8.7 reduce-scatter.26
  967.2 12.0 all-gather.26
  1031.4 11.0 reduce-scatter.28
  1043.9 12.1 all-gather.28
  1094.8 11.0 reduce-scatter.30
  1107.4 12.1 all-gather.30
  1158.0 11.0 reduce-scatter.32
  1170.5 12.1 all-gather.32
  1221.3 11.0 reduce-scatter.34
  1234.6 10.1 reduce-scatter.14
  1247.0 10.2 reduce-scatter.16
  1259.0 12.1 all-gather.34
  1272.8 10.9 all-gather.18
  1286.0 12.0 reduce-scatter.12
  1304.5 231.0 all-reduce.4
where the time goes:
time: 1560 us; the launch traced here: 1550 us
  waiting for transfers between devices  933 us (60%)
  matrix products  323 us (21%)
  blocking collectives  136 us (9%)
  other arithmetic  73.3 us (5%)
  local copies, waits for them, and re-layouts  58.8 us (4%)
  between operations  16 us (1%)
    psum x1, waiting for transfers between devices, spread(): return lax.psum(kept, axis)  183 us
    reduce_scatter x1, waiting for transfers between devices, shards(): lax.psum_scatter(narrow_grad, 'dp', scatter_dimension=0, tiled=True)  141 us
    reduce_scatter x1, waiting for transfers between devices, shards(): lax.psum_scatter(widen_grad, 'dp', scatter_dimension=0, tiled=True)  139 us
    reduce_scatter x1, waiting for transfers between devices, shards(): lax.psum_scatter(output_grad, 'dp', scatter_dimension=0, tiled=True)  126 us
    reduce_scatter x1, waiting for transfers between devices, shards(): lax.psum_scatter(attend_grad, 'dp', scatter_dimension=0, tiled=True)  85.2 us
    dot_general x5, matrix products, newton(): jnp.einsum('mde,mek->mdk', polynomial, current, precision=HIGHEST)  75.3 us
    all_gather x1, waiting for transfers between devices, shards(): lax.all_gather(momenta[3].astype(jnp.bfloat16), 'dp', axis=0, tiled=True)  64.4 us
    all_gather x1, waiting for transfers between devices, shards(): lax.all_gather(momenta[2].astype(jnp.bfloat16), 'dp', axis=0, tiled=True)  61.4 us
  transfers between devices with their start and end apart: 25, of which 19 were waited for; matrix products, arithmetic and copies ran while one was open for 17% of the time, Pallas kernels for 0%

commit v1 on v0

--- a/solution.py
+++ b/solution.py
@@ -14,7 +14,13 @@
 STEP = 10
 
 
-HIGHEST = lax.Precision.HIGHEST
+HIGH = lax.Precision.HIGH
+X_FIRST = (0, 1, 2)
+Z_THEN_X = (2, 0, 1)
+Z_THEN_Y = (2, 1, 0)
+X_THEN_Y = (0, 1, 2)
+Y_THEN_X = (1, 0, 2)
+Z_FIRST = (2, 1, 0)
 NORM_EPS = 1e-05
 POLY_ONE = 3.4445
 POLY_TWO = -4.775
@@ -29,13 +35,116 @@
 ADAM_EPS = 1e-08
 
 
-def as_sent(value):
-    return jax.tree.map(lambda a: a.astype(jnp.bfloat16) if a.dtype == jnp.float32 else a, value)
-
-
-def spread(value, axis, source):
-    kept = jnp.where(lax.axis_index(axis) == source, value, 0).astype(value.dtype)
-    return lax.psum(kept, axis)
+DATA_AXES = {16: ((1, 2), (2, 2), (4, 4)), 128: ((1, 4), (4, 8), (32, 4))}
+
+
+def data_axes(count):
+    return DATA_AXES.get(count, ((1, count), (count, 1), (count, 1)))
+
+
+def ring(count, stride, size):
+    pairs = []
+    for index in range(count):
+        place = (index // stride) % size
+        pairs.append((index, index + ((place + 1) % size - place) * stride))
+    return pairs
+
+
+def staged_gather(share, order):
+    count = lax.axis_size("dp")
+    rank = lax.axis_index("dp")
+    rows, columns = share.shape
+    held = share[None]
+    sources = [rank]
+    for axis in order:
+        stride, size = data_axes(count)[axis]
+        perm = ring(count, stride, size)
+        parts, found = [held], list(sources)
+        moving, owners = held, sources
+        for _ in range(size - 1):
+            moving = lax.ppermute(moving, "dp", perm)
+            places = [(owner // stride) % size for owner in owners]
+            owners = [
+                owner + ((place + size - 1) % size - place) * stride
+                for owner, place in zip(owners, places)
+            ]
+            parts.append(moving)
+            found += owners
+        held, sources = jnp.concatenate(parts, 0), found
+    whole = jnp.zeros((count, rows, columns), share.dtype)
+    for slot, source in enumerate(sources):
+        whole = lax.dynamic_update_slice(whole, held[slot : slot + 1], (source, 0, 0))
+    return whole.reshape(count * rows, columns)
+
+
+def staged_scatter(partial, order):
+    count = lax.axis_size("dp")
+    rank = lax.axis_index("dp")
+    axes = data_axes(count)
+    rows, columns = partial.shape[0] // count, partial.shape[1]
+    slow_first = sorted(range(len(axes)), key=lambda axis: -axes[axis][0])
+    held = partial.reshape(*[axes[axis][1] for axis in slow_first], rows, columns)
+    for axis in order:
+        stride, size = axes[axis]
+        if size == 1:
+            continue
+        perm = ring(count, stride, size)
+        place = (rank // stride) % size
+        dim = slow_first.index(axis)
+
+        def block(target):
+            return lax.dynamic_slice_in_dim(held, target % size, 1, dim)
+
+        total = block(place + size - 1)
+        for step in range(size - 1):
+            got = lax.ppermute(total.astype(jnp.bfloat16), "dp", perm)
+            total = block(place + 2 * size - 2 - step) + got.astype(jnp.float32)
+        held = total
+    return held.reshape(rows, columns)
+
+
+def other_core(value):
+    return lax.ppermute(value, "tensor", [(0, 1), (1, 0)])
+
+
+def sum_everywhere(value):
+    value = value + other_core(value)
+    count = lax.axis_size("dp")
+    distance = 1
+    while distance < count:
+        pairs = [(index, index ^ distance) for index in range(count)]
+        value = value + lax.ppermute(value, "dp", pairs)
+        distance *= 2
+    return value
+
+
+def product(left, right):
+    return jnp.dot(left, right, precision=HIGH, preferred_element_type=jnp.float32)
+
+
+def newton_rows(gram, first_row, rows):
+    factor = 1.0 / (jnp.sqrt(jnp.trace(gram)) + SCALE_EPS)
+    square = gram * (factor * factor)
+    identity = jnp.eye(D, dtype=jnp.float32)
+    kept = lax.dynamic_slice_in_dim(identity, first_row, rows, 0) * factor
+    for iteration in range(NS_STEPS - 1):
+        step = (
+            POLY_ONE * identity + POLY_TWO * square + POLY_THREE * product(square, square)
+        )
+        kept = product(kept, step) if iteration else lax.dynamic_slice_in_dim(
+            step, first_row, rows, 0
+        ) * factor
+        square = product(product(step, square), step)
+    once = product(kept, square)
+    return POLY_ONE * kept + POLY_TWO * once + POLY_THREE * product(once, square)
+
+
+def rows_product(left, right):
+    high = left.astype(jnp.bfloat16)
+    low = (left - high.astype(jnp.float32)).astype(jnp.bfloat16)
+    return jnp.dot(high, right, preferred_element_type=jnp.float32) + jnp.dot(
+        low, right, preferred_element_type=jnp.float32
+    )
 
 
 def norm_stats(values):
@@ -91,32 +200,6 @@
     frequency = jnp.exp(-math.log(10000.0) * exponent)
     angles = position[:, None] * frequency[None, :]
     return (jnp.cos(angles)[:, None, :], jnp.sin(angles)[:, None, :])
-
-
-def gram_sum(matrices):
-    square = jnp.einsum(
-        "mdk,mek->mde", matrices, matrices, precision=HIGHEST, preferred_element_type=jnp.float32
-    )
-    gram_share = lax.psum_scatter(square, "tensor", scatter_dimension=1, tiled=True)
-    return lax.all_gather(gram_share, "tensor", axis=1, tiled=True)
-
-
-def newton(matrices):
-    square = gram_sum(matrices)
-    trace_sum = jnp.sum(jnp.diagonal(square, axis1=1, axis2=2), axis=1)
-    factor = 1.0 / (jnp.sqrt(trace_sum) + SCALE_EPS)
-    current = matrices * factor[:, None, None]
-    square = square * (factor * factor)[:, None, None]
-    for iteration in range(NS_STEPS):
-        if iteration > 0:
-            square = gram_sum(current)
-        polynomial = POLY_TWO * square + POLY_THREE * jnp.einsum(
-            "mde,mef->mdf", square, square, precision=HIGHEST
-        )
-        current = POLY_ONE * current + jnp.einsum(
-            "mde,mek->mdk", polynomial, current, precision=HIGHEST
-        )
-    return current
 
 
 def shards(
@@ -140,12 +223,13 @@
     data_size = lax.axis_size("dp")
     data_rank = lax.axis_index("dp")
     masters = (attend_weight, output_weight, widen_weight, narrow_weight)
-    attend_low, output_low, widen_low, narrow_low = (
-        lax.all_gather(attend_weight.astype(jnp.bfloat16), "dp", axis=0, tiled=True),
-        lax.all_gather(output_weight.astype(jnp.bfloat16), "dp", axis=0, tiled=True),
-        lax.all_gather(widen_weight.astype(jnp.bfloat16), "dp", axis=0, tiled=True),
-        lax.all_gather(narrow_weight.astype(jnp.bfloat16), "dp", axis=0, tiled=True),
-    )
+    attend_columns = attend_weight.shape[1]
+    widen_low = staged_gather(widen_weight.astype(jnp.bfloat16), Z_THEN_X)
+    narrow_low = staged_gather(narrow_weight.astype(jnp.bfloat16), Z_THEN_Y)
+    joint_low = staged_gather(
+        jnp.concatenate([attend_weight, output_weight], 1).astype(jnp.bfloat16), X_FIRST
+    )
+    attend_low, output_low = joint_low[:, :attend_columns], joint_low[:, attend_columns:]
     length = layer_input.shape[0]
     triple_cols = attend_low.shape[1]
     local_heads = triple_cols // (3 * HEAD_DIM)
@@ -205,13 +289,17 @@
     widened = jnp.dot(second_norm, widen_low, preferred_element_type=jnp.float32) + widen_bias
     activated = jax.nn.gelu(widened, approximate=False).astype(jnp.bfloat16)
     narrowed = jnp.einsum("sf,df->sd", activated, narrow_low, preferred_element_type=jnp.float32)
-    branch = lax.psum_scatter(attended + narrowed, "tensor", scatter_dimension=1, tiled=True)
+    branch_part = attended + narrowed
     live_rows = (segment_ids >= 0).astype(jnp.float32)[:, None]
     column_start = tensor_rank * feature_share
 
     def own_columns(array):
         return lax.dynamic_slice_in_dim(array, column_start, feature_share, array.ndim - 1)
 
+    other_start = (1 - tensor_rank) * feature_share
+    branch = own_columns(branch_part) + other_core(
+        lax.dynamic_slice_in_dim(branch_part, other_start, feature_share, 1)
+    )
     block_output = (
         live_rows
         * (
@@ -299,14 +387,14 @@
     )
     row_share = length // tensor_size
     row_start = tensor_rank * row_share
-    first_total, second_total = (
-        lax.psum_scatter(
-            first_back.astype(jnp.bfloat16), "tensor", scatter_dimension=0, tiled=True
-        ).astype(jnp.float32),
-        lax.psum_scatter(
-            second_back.astype(jnp.bfloat16), "tensor", scatter_dimension=0, tiled=True
-        ).astype(jnp.float32),
-    )
+    other_row = (1 - tensor_rank) * row_share
+
+    def core_sum(part):
+        sent = lax.dynamic_slice_in_dim(part, other_row, row_share, 0).astype(jnp.bfloat16)
+        kept = lax.dynamic_slice_in_dim(part, row_start, row_share, 0)
+        return kept + other_core(sent).astype(jnp.float32)
+
+    first_total, second_total = core_sum(first_back), core_sum(second_back)
     normed_share = lax.dynamic_slice_in_dim(normed, row_start, row_share, 0)
     inverse_share = lax.dynamic_slice_in_dim(inverse, row_start, row_share, 0)
     upstream_share = lax.dynamic_slice_in_dim(upstream, row_start, row_share, 0)
@@ -314,9 +402,13 @@
         norm_backward(first_total, normed_share, inverse_share, first_gain)
         + norm_backward(second_total, normed_share, inverse_share, second_gain)
     )
-    input_grad = lax.all_gather(
-        input_share.astype(jnp.bfloat16), "tensor", axis=0, tiled=True
-    ).astype(input_share.dtype)
+    input_low = input_share.astype(jnp.bfloat16)
+    input_other = other_core(input_low)
+    input_grad = jnp.where(
+        tensor_rank == 0,
+        jnp.concatenate([input_low, input_other], 0),
+        jnp.concatenate([input_other, input_low], 0),
+    ).astype(jnp.float32)
     norm_rows = jnp.stack(
         [
             jnp.sum(first_total * normed_share, axis=0),
@@ -341,58 +433,53 @@
         ],
         axis=0,
     )
-    vector_grad = lax.psum(vector_part, ("dp", "tensor"))
-    attend_sum, output_sum, widen_sum, narrow_sum = (
-        lax.psum_scatter(attend_grad, "dp", scatter_dimension=0, tiled=True),
-        lax.psum_scatter(output_grad, "dp", scatter_dimension=0, tiled=True),
-        lax.psum_scatter(widen_grad, "dp", scatter_dimension=0, tiled=True),
-        lax.psum_scatter(narrow_grad, "dp", scatter_dimension=0, tiled=True),
-    )
+    vector_grad = sum_everywhere(vector_part)
+    widen_sum = staged_scatter(widen_grad, X_THEN_Y)
+    narrow_sum = staged_scatter(narrow_grad, Y_THEN_X)
+    joint_sum = staged_scatter(jnp.concatenate([attend_grad, output_grad], 1), Z_FIRST)
+    attend_sum, output_sum = joint_sum[:, :attend_columns], joint_sum[:, attend_columns:]
     summed = (attend_sum, output_sum, widen_sum, narrow_sum)
     moments = (attend_moment, output_moment, widen_moment, narrow_moment)
     momenta = [MUON_BETA * previous + gradient for previous, gradient in zip(moments, summed)]
     widths = [matrix.shape[1] for matrix in momenta]
-    widest = max(widths)
     rows_here = D // data_size
-    owner_list = [matrix_index * data_size // 4 for matrix_index in range(4)]
-    gathered = (
-        lax.all_gather(momenta[0].astype(jnp.bfloat16), "dp", axis=0, tiled=True).astype(
-            jnp.float32
-        ),
-        lax.all_gather(momenta[1].astype(jnp.bfloat16), "dp", axis=0, tiled=True).astype(
-            jnp.float32
-        ),
-        lax.all_gather(momenta[2].astype(jnp.bfloat16), "dp", axis=0, tiled=True).astype(
-            jnp.float32
-        ),
-        lax.all_gather(momenta[3].astype(jnp.bfloat16), "dp", axis=0, tiled=True).astype(
-            jnp.float32
-        ),
-    )
-    padded = jnp.stack(
-        [jnp.pad(matrix, ((0, 0), (0, widest - matrix.shape[1]))) for matrix in gathered]
-    )
-    owned_slot = jnp.zeros((), jnp.int32)
-    for matrix_index in range(4):
-        owned_slot = owned_slot + jnp.where(
-            data_rank == owner_list[matrix_index], matrix_index, 0
-        ).astype(jnp.int32)
-    chosen = lax.dynamic_index_in_dim(padded, owned_slot, 0, keepdims=True)
-    result = newton(chosen)[0]
-    orthos = [
-        spread(as_sent(result[:, : widths[matrix_index]]), "dp", owner_list[matrix_index])
-        for matrix_index in range(4)
+    widen_whole = staged_gather(momenta[2].astype(jnp.bfloat16), Z_THEN_X)
+    narrow_whole = staged_gather(momenta[3].astype(jnp.bfloat16), Z_THEN_Y)
+    joint_whole = staged_gather(
+        jnp.concatenate([momenta[0], momenta[1]], 1).astype(jnp.bfloat16), X_FIRST
+    )
+    wholes = [
+        joint_whole[:, :attend_columns],
+        joint_whole[:, attend_columns:],
+        widen_whole,
+        narrow_whole,
     ]
-    row_parts = [
-        lax.dynamic_slice_in_dim(orthos[matrix_index], data_rank * rows_here, rows_here, 0)
-        for matrix_index in range(4)
-    ]
+
+    def gram(matrix):
+        return jnp.einsum("dk,ek->de", matrix, matrix, preferred_element_type=jnp.float32)
+
+    def pair_rows(first, second):
+        first_gram, second_gram = gram(first), gram(second)
+        own = jnp.where(tensor_rank == 0, first_gram, second_gram)
+        sent = jnp.where(tensor_rank == 0, second_gram, first_gram)
+        rows = newton_rows(own + other_core(sent), data_rank * rows_here, rows_here)
+        other = other_core(rows)
+        return (
+            jnp.where(tensor_rank == 0, rows, other),
+            jnp.where(tensor_rank == 0, other, rows),
+        )
+
+    widen_rows_out, narrow_rows_out = pair_rows(wholes[2], wholes[3])
+    attend_rows_out, output_rows_out = pair_rows(wholes[0], wholes[1])
+    ortho_rows = (attend_rows_out, output_rows_out, widen_rows_out, narrow_rows_out)
     updated = []
     for matrix_index in range(4):
         longest = max(D, widths[matrix_index] * tensor_size)
         updated.append(
             masters[matrix_index] * (1.0 - MUON_RATE * MUON_DECAY)
-            - MUON_RATE * math.sqrt(longest) * row_parts[matrix_index]
+            - MUON_RATE
+            * math.sqrt(longest)
+            * rows_product(ortho_rows[matrix_index], wholes[matrix_index])
         )
     first_new = BETA_ONE * vector_first + (1.0 - BETA_ONE) * vector_grad
     second_new = BETA_TWO * vector_second + (1.0 - BETA_TWO) * vector_grad * vector_grad

time: 1560 us -> 685 us (0.44)
  waiting for transfers between devices: 933 us -> 170 us
  blocking collectives: 136 us -> 0 us
  local copies, waits for them, and re-layouts: 58.8 us -> 124 us
  matrix products: 323 us -> 261 us
  starting transfers between devices: 1.23 us -> 34.2 us
    reduce_scatter x12 -> x0, waiting for transfers between devices: 552 us -> none  [the longest x1 141 us: shards(): lax.psum_scatter(narrow_grad, 'dp', scatter_dimension=0, tiled=True)]
    all_gather x12 -> x0, waiting for transfers between devices: 197 us -> none  [the longest x1 64.4 us: shards(): lax.all_gather(momenta[3].astype(jnp.bfloat16), 'dp', axis=0, tiled=True)]
    psum x1 -> x0, waiting for transfers between devices: 183 us -> none  [spread(): return lax.psum(kept, axis)]
    ppermute x0 -> x58, waiting for transfers between devices: none -> 170 us  [the longest x30 101 us: staged_gather(): moving = lax.ppermute(moving, 'dp', perm)]
    all_gather x2 -> x0, blocking collectives: 93.1 us -> none  [the longest x1 49.7 us: shards(): lax.all_gather(output_weight.astype(jnp.bfloat16), 'dp', axis=0, tiled=True)]
    dynamic_update_slice x0 -> x81, local copies, waits for them, and re-layouts: none -> 64 us  [staged_gather(): whole = lax.dynamic_update_slice(whole, held[slot:slot + 1], (source, 0, 0))]
    dot_general x15 -> x46, matrix products: 173 us -> 124 us  [the longest x34 94 us: product(): jnp.dot(left, right, precision=HIGH, preferred_element_type=jnp.float32)]
    psum x1 -> x0, blocking collectives: 43.3 us -> none  [shards(): vector_grad = lax.psum(vector_part, ('dp', 'tensor'))]
  transfers between devices with their start and end apart: 25 -> 58, of which waited for: 19 -> 32; matrix products, arithmetic and copies ran while one was open for 17% -> 58% of each run, Pallas kernels for 0% -> 0%
where the time goes in v1:
time: 685 us; the launch traced here: 678 us
  matrix products  261 us (38%)
  waiting for transfers between devices  170 us (25%)
  local copies, waits for them, and re-layouts  124 us (18%)
  other arithmetic  76.9 us (11%)
  starting transfers between devices  34.2 us (5%)
  loops' own time  7.23 us (1%)
    ppermute x30, waiting for transfers between devices, staged_gather(): moving = lax.ppermute(moving, 'dp', perm)  101 us
    dot_general x34, matrix products, product(): jnp.dot(left, right, precision=HIGH, preferred_element_type=jnp.float32)  94 us
    dynamic_update_slice x81, local copies, waits for them, and re-layouts, staged_gather(): whole = lax.dynamic_update_slice(whole, held[slot:slot + 1], (source, 0, 0))  64 us
    ppermute x15, waiting for transfers between devices, staged_scatter(): got = lax.ppermute(total.astype(jnp.bfloat16), 'dp', perm)  54.8 us
    dot_general x1, matrix products, shards(): jnp.dot(second_norm, widen_low, preferred_element_type=jnp.float32)  19.5 us
    ppermute x30, starting transfers between devices, staged_gather(): moving = lax.ppermute(moving, 'dp', perm)  18.7 us
    dot_general x4, matrix products, block_scores(): jnp.einsum('qhd,khd->hqk', block_queries, key_heads, preferred_element_ty...  17.4 us
    unnamed x167, local copies, waits for them, and re-layouts  17.1 us
  transfers between devices with their start and end apart: 58, of which 32 were waited for; matrix products, arithmetic and copies ran while one was open for 58% of the time, Pallas kernels for 0%

profile of v1, /device:TPU:0, one launch (start us, length us, event | category | flops | bytes accessed | tf_op | source)
XLA Modules:
  0.0 677.6 jit_solution(10511040818030606602)
XLA Ops:
  46.2 3.6 collective-permute-done.12
  57.1 5.2 collective-permute-done.13
  63.7 3.9 collective-permute-done.8
  75.9 9.0 %collective-permute-done.3 = bf16[4,48,1536]{2,1,0:T(8,128)(2,1)S(1)} collective-permute-done((bf16[4,48,1536]{2,1,0:T(8,128)(2,1)S(1)}, bf16[4,48,1536]{2,1,0:T(8,128)(2,1)S(1)}, u32[]{:S(2)}, u32[]{:S(2)}) %collective-permute-start.3) | collective-permute-done | bytes 589856 | tf_op jit(solution)/shard_map/ppermute | solution.py:65
  93.2 19.5 %multiply_convert_fusion.1 = (bf16[1024,1536]{1,0:T(8,128)(2,1)S(1)}, f32[1024,1536]{1,0:T(8,128)}, f32[1024,1536]{1,0:T(8,128)}) fusion(f32[1536]{0:T(1024)S(1)} %dynamic_slice.146, bf16[768,1536]{1,0:T(8,128)(2,1)} %bitcast.8, f32[768]{0:T(1024)S(1)} %get-tuple-element.202, f32[768]{0:T(1024)S(1)} %get-tuple-element.203, f32[1024]{0:T(1024)S(1)} %add_rsqrt_fusion, ...), kind=kOutput, calls=%fused_computation.59 | convolution fusion | flops 2524446720 | bytes 19681280 | tf_op jit(solution)/shard_map/dot_general | solution.py:289
  123.1 6.2 convolution_add_fusion
  129.3 6.1 copy.48
  142.4 26.9 %while.28 = (s32[]{:T(128)}, bf16[2,512,6,64]{1,3,2,0:T(8,128)(2,1)}, f32[2,6,512,1]{2,1,3,0:T(8,128)}, s32[2]{0:T(128)S(1)}, s32[1024]{0:T(1024)S(1)}, /*index=...) while((s32[]{:T(128)}, ...), condition=%wide.region_6.7_spmd.clone, body=%wide.region_3.6_spmd.clone.sunk | while | flops 844822016 | bytes 42323128 | solution.py:286
  147.0 3.6 fusion.420
  151.2 4.9 fusion.421
  160.2 3.6 fusion.420
  164.4 4.9 fusion.421
  169.3 82.1 %while.29 = (s32[]{:T(128)}, f32[1024,6,64]{0,2,1:T(8,128)}, f32[1024,6,64]{0,2,1:T(8,128)}, bf16[2,512,6,64]{1,3,2,0:T(8,128)(2,1)}, s32[2]{0:T(128)S(1)}, /*in...) while((s32[]{:T(128)}, f32[1024,6,64]{0,2,1:T(8,128)}, ...), condition=%wide.region_9.10_spmd.clone, body=%wide.region_7.9_spmd.clone.sunk | while | flops 2064184832 | bytes 186227216 | solution.py:364
  171.2 6.4 fusion.431
  180.3 7.6 %multiply_reduce_fusion.9 = (f32[6,512]{1,0:T(8,128)S(1)}, f32[6,512,1024]{2,1,0:T(8,128)S(1)}) fusion(f32[6,512,1024]{2,1,0:T(8,128)} %fusion.431, f32[6,512]{1,0:T(8,128)S(1)} %dynamic-slice_bitcast_fusion.2, pred[512,1024]{1,0:T(8,128)(4,1)S(1)} %fusion.432, bf16[1024,6,64]{0,2,1:T(8,128)(2,1)} %copy-done.2, ...), kind=kOutput, calls=%fused_computation.21.clone.1 | convolution fusion | flops 418378752 | bytes 26894340 | tf_op jit(solution)/shard_map/while/body/eval_jaxpr/qhd,khd->hqk/dot_general | solution.py:344
  188.9 5.0 multiply_convert_fusion.4
  193.9 5.3 bitcast_add_fusion.4
  202.1 7.7 %bitcast_add_fusion.5 = f32[1024,6,64]{0,2,1:T(8,128)} fusion(f32[1024,6,64]{0,2,1:T(8,128)} %get-tuple-element.518, f32[6,512,1024]{2,1,0:T(8,128)} %fusion.431, f32[6,512]{1,0:T(8,128)S(1)} %dynamic-slice_bitcast_fusion.2, pred[512,1024]{1,0:T(8,128)(4,1)S(1)} %fusion.432, pred[]{:T(512)S(6)} %compare.112, ...), kind=kOutput, calls=%fused_computation.28.clone.1 | convolution fusion | flops 416022528 | bytes 16662533 | tf_op jit(solution)/shard_map/while/body/eval_jaxpr/hqk,qhd->khd/dot_general | solution.py:355
  211.7 6.4 fusion.431
  220.8 7.6 %multiply_reduce_fusion.9 = (f32[6,512]{1,0:T(8,128)S(1)}, f32[6,512,1024]{2,1,0:T(8,128)S(1)}) fusion(f32[6,512,1024]{2,1,0:T(8,128)} %fusion.431, f32[6,512]{1,0:T(8,128)S(1)} %dynamic-slice_bitcast_fusion.2, pred[512,1024]{1,0:T(8,128)(4,1)S(1)} %fusion.432, bf16[1024,6,64]{0,2,1:T(8,128)(2,1)} %copy-done.2, ...), kind=kOutput, calls=%fused_computation.21.clone.1 | convolution fusion | flops 418378752 | bytes 26894340 | tf_op jit(solution)/shard_map/while/body/eval_jaxpr/qhd,khd->hqk/dot_general | solution.py:344
  229.4 5.0 multiply_convert_fusion.4
  234.4 5.7 bitcast_add_fusion.4
  243.1 8.1 %bitcast_add_fusion.5 = f32[1024,6,64]{0,2,1:T(8,128)} fusion(f32[1024,6,64]{0,2,1:T(8,128)} %get-tuple-element.518, f32[6,512,1024]{2,1,0:T(8,128)} %fusion.431, f32[6,512]{1,0:T(8,128)S(1)} %dynamic-slice_bitcast_fusion.2, pred[512,1024]{1,0:T(8,128)(4,1)S(1)} %fusion.432, pred[]{:T(512)S(6)} %compare.112, ...), kind=kOutput, calls=%fused_computation.28.clone.1 | convolution fusion | flops 416022528 | bytes 16662533 | tf_op jit(solution)/shard_map/while/body/eval_jaxpr/hqk,qhd->khd/dot_general | solution.py:355
  267.1 4.0 fusion.107
  271.2 10.5 %collective-permute-done.19 = bf16[1,2,2,48,1536]{4,3,2,1,0:T(8,128)(2,1)S(1)} collective-permute-done((bf16[1,2,2,48,1536]{4,3,2,1,0:T(8,128)(2,1)S(1)}, bf16[1,2,2,48,1536]{4,3,2,1,0:T(8,128)(2,1)S(1)}, u32[]{:S(2)}, u32[]{:S(2)}) %collective-permute-start.19) | collective-permute-done | bytes 589856 | tf_op jit(solution)/shard_map/ppermute | solution.py:100
  287.9 6.6 collective-permute-done.20
  298.4 10.7 %collective-permute-done.21 = bf16[1,2,2,48,1536]{4,3,2,1,0:T(8,128)(2,1)S(1)} collective-permute-done((bf16[1,2,2,48,1536]{4,3,2,1,0:T(8,128)(2,1)S(1)}, bf16[1,2,2,48,1536]{4,3,2,1,0:T(8,128)(2,1)S(1)}, u32[]{:S(2)}, u32[]{:S(2)}) %collective-permute-start.21) | collective-permute-done | bytes 589856 | tf_op jit(solution)/shard_map/ppermute | solution.py:100
  312.1 7.2 %collective-permute-done.32 = bf16[1,1,1,48,1536]{4,3,2,1,0:T(8,128)(2,1)S(1)} collective-permute-done((bf16[1,1,1,48,1536]{4,3,2,1,0:T(8,128)(2,1)S(1)}, bf16[1,1,1,48,1536]{4,3,2,1,0:T(8,128)(2,1)S(1)}, u32[]{:S(2)}, u32[]{:S(2)}) %collective-permute-start.32) | collective-permute-done | bytes 147488 | tf_op jit(solution)/shard_map/ppermute | solution.py:100
  320.0 7.9 %collective-permute-done.33 = bf16[1,1,1,48,1536]{4,3,2,1,0:T(8,128)(2,1)S(1)} collective-permute-done((bf16[1,1,1,48,1536]{4,3,2,1,0:T(8,128)(2,1)S(1)}, bf16[1,1,1,48,1536]{4,3,2,1,0:T(8,128)(2,1)S(1)}, u32[]{:S(2)}, u32[]{:S(2)}) %collective-permute-start.33) | collective-permute-done | bytes 147488 | tf_op jit(solution)/shard_map/ppermute | solution.py:100
  343.9 7.9 %collective-permute-done.48 = bf16[1,48,1536]{2,1,0:T(8,128)(2,1)S(1)} collective-permute-done((bf16[1,48,1536]{2,1,0:T(8,128)(2,1)S(1)}, bf16[1,48,1536]{2,1,0:T(8,128)(2,1)S(1)}, u32[]{:S(2)}, u32[]{:S(2)}) %collective-permute-start.48) | collective-permute-done | bytes 147488 | tf_op jit(solution)/shard_map/ppermute | solution.py:65
  354.8 7.0 %collective-permute-done.49 = bf16[4,48,1536]{2,1,0:T(8,128)(2,1)S(1)} collective-permute-done((bf16[4,48,1536]{2,1,0:T(8,128)(2,1)S(1)}, bf16[4,48,1536]{2,1,0:T(8,128)(2,1)S(1)}, u32[]{:S(2)}, u32[]{:S(2)}) %collective-permute-start.49) | collective-permute-done | bytes 589856 | tf_op jit(solution)/shard_map/ppermute | solution.py:65
  365.7 4.5 collective-permute-done.36
  372.9 15.1 %collective-permute-done.37 = bf16[4,48,1536]{2,1,0:T(8,128)(2,1)} collective-permute-done((bf16[4,48,1536]{2,1,0:T(8,128)(2,1)S(1)}, bf16[4,48,1536]{2,1,0:T(8,128)(2,1)}, u32[]{:S(2)}, u32[]{:S(2)}) %collective-permute-start.37) | collective-permute-done | bytes 589856 | tf_op jit(solution)/shard_map/ppermute | solution.py:65
  408.1 6.7 convert_reduce_fusion
  414.8 4.3 fusion.317
  419.2 4.6 fusion.204
  423.7 6.0 fusion.316
  450.2 3.9 fusion.113
  454.1 5.2 broadcast_select_fusion.1
  459.7 4.0 multiply_reduce_fusion.2
  474.0 10.4 %collective-permute-done.55 = f32[13,768]{1,0:T(8,128)S(1)} collective-permute-done((f32[13,768]{1,0:T(8,128)S(1)}, f32[13,768]{1,0:T(8,128)S(1)}, u32[]{:S(2)}, u32[]{:S(2)}) %collective-permute-start.55) | collective-permute-done | bytes 39968 | tf_op jit(solution)/shard_map/ppermute | solution.py:116
  494.8 5.3 collective-permute-done.27
  502.9 4.2 collective-permute-done.28
  508.3 6.7 collective-permute-done.41
  515.7 4.0 select_reduce_fusion.1
  520.4 6.4 fusion.43
  533.0 3.3 fusion.319
  536.2 3.2 fusion.101
  545.6 3.6 fusion.95
  556.6 3.3 fusion.89
  559.9 3.9 collective-permute-done.43
  569.9 4.8 collective-permute-done.44
  576.3 19.7 %collective-permute-done.45 = bf16[8,48,1536]{2,1,0:T(8,128)(2,1)S(1)} collective-permute-done((bf16[8,48,1536]{2,1,0:T(8,128)(2,1)S(1)}, bf16[8,48,1536]{2,1,0:T(8,128)(2,1)S(1)}, u32[]{:S(2)}, u32[]{:S(2)}) %collective-permute-start.45) | collective-permute-done | bytes 1179680 | tf_op jit(solution)/shard_map/ppermute | solution.py:65
  598.2 4.4 broadcast_select_fusion
  608.2 3.5 fusion.105
  620.7 6.5 fusion.47
  633.5 3.6 fusion.325
  637.0 3.4 fusion.83
  641.4 3.2 fusion.81
  644.7 3.3 fusion.326
  648.0 3.4 fusion.77
  651.4 3.2 fusion.75
  657.8 3.6 fusion.71
  661.3 3.2 fusion.69
  (571 shorter events, 295.2 us)
Async XLA Ops:
  2.3 32.5 %collective-permute-start.10 = (bf16[1,48,1536]{2,1,0:T(8,128)(2,1)}, bf16[1,48,1536]{2,1,0:T(8,128)(2,1)}, u32[]{:S(2)}, u32[]{:S(2)}) collective-permute-start(bf16[1,48,1536]{2,1,0:T(8,128)(2,1)} %get-tuple-element.270), channel_id=1, source_target_pairs={{0,8},{2,10},{4,12},{6,14},{8,16},{10,18},{12,20},{14,22},{16,24},... | collective-permute-start | bytes 442376 | tf_op jit(solution)/shard_map/ppermute | solution.py:65
  7.0 29.5 %collective-permute-start.5 = (bf16[1,48,1536]{2,1,0:T(8,128)(2,1)S(1)}, bf16[1,48,1536]{2,1,0:T(8,128)(2,1)}, u32[]{:S(2)}, u32[]{:S(2)}) collective-permute-start(bf16[1,48,1536]{2,1,0:T(8,128)(2,1)S(1)} %get-tuple-element.274), channel_id=1, source_target_pairs={{0,8},{2,10},{4,12},{6,14},{8,16},{10,18},{12,20},{14,22},{16,24},... | collective-permute-start | bytes 442376 | tf_op jit(solution)/shard_map/ppermute | solution.py:65
  12.9 19.5 %collective-permute-start = (bf16[1,48,1536]{2,1,0:T(8,128)(2,1)}, bf16[1,48,1536]{2,1,0:T(8,128)(2,1)}, u32[]{:S(2)}, u32[]{:S(2)}) collective-permute-start(bf16[1,48,1536]{2,1,0:T(8,128)(2,1)} %get-tuple-element.305), channel_id=1, source_target_pairs={{0,2},{2,0},{4,6},{6,4},{8,10},{10,8},{12,14},{14,12},{16,18},{18,... | collective-permute-start | bytes 442376 | tf_op jit(solution)/shard_map/ppermute | solution.py:65
  15.0 108.1 %copy-start.57 = (f32[768]{0:T(1024)}, f32[768]{0:T(1024)S(1)}, u32[]{:S(2)}) copy-start(f32[768]{0:T(1024)S(1)} %get-tuple-element.201) | copy-start | bytes 9220
  15.0 124.0 %copy-start.42 = (f32[1024]{0:T(1024)}, f32[1024]{0:T(1024)S(1)}, u32[]{:S(2)}) copy-start(f32[1024]{0:T(1024)S(1)} %compare_convert_fusion) | copy-start | bytes 12292
  23.8 99.3 %copy-start.61 = (f32[1024]{0:T(1024)}, f32[1024]{0:T(1024)S(1)}, u32[]{:S(2)}) copy-start(f32[1024]{0:T(1024)S(1)} %broadcast_multiply_fusion.1) | copy-start | bytes 12292
  24.5 98.6 %copy-start.64 = (f32[1024]{0:T(1024)}, f32[1024]{0:T(1024)S(1)}, u32[]{:S(2)}) copy-start(f32[1024]{0:T(1024)S(1)} %add_rsqrt_fusion) | copy-start | bytes 12292
  32.3 109.8 %copy-start.44 = (f32[1024,8]{0,1:T(8,128)}, f32[1024,8]{0,1:T(8,128)S(1)}, u32[]{:S(2)}) copy-start(f32[1024,8]{0,1:T(8,128)S(1)} %get-tuple-element.325) | copy-start | bytes 98308
  32.3 109.8 %copy-start.46 = (f32[1024,8]{0,1:T(8,128)}, f32[1024,8]{0,1:T(8,128)S(1)}, u32[]{:S(2)}) copy-start(f32[1024,8]{0,1:T(8,128)S(1)} %get-tuple-element.326) | copy-start | bytes 98308
  33.3 20.0 %collective-permute-start.1 = (bf16[2,48,1536]{2,1,0:T(8,128)(2,1)S(1)}, bf16[2,48,1536]{2,1,0:T(8,128)(2,1)S(1)}, u32[]{:S(2)}, u32[]{:S(2)}) collective-permute-start(bf16[2,48,1536]{2,1,0:T(8,128)(2,1)S(1)} %pad_maximum_fusion.9), channel_id=1, source_target_pairs={{0,4},{2,6},{4,0},{6,2},{8,12},{10,14},{12,8},{14,10},{16,20},{18,... | collective-permute-start | bytes 884744 | tf_op jit(solution)/shard_map/ppermute | solution.py:65
  34.9 8.1 %collective-permute-start.11 = (bf16[1,48,1536]{2,1,0:T(8,128)(2,1)}, bf16[1,48,1536]{2,1,0:T(8,128)(2,1)S(1)}, u32[]{:S(2)}, u32[]{:S(2)}) collective-permute-start(bf16[1,48,1536]{2,1,0:T(8,128)(2,1)} %collective-permute-done.10), channel_id=1, source_target_pairs={{0,8},{2,10},{4,12},{6,14},{8,16},{10,18},{12,20},{14,22},{16,24},... | collective-permute-start | bytes 442376 | tf_op jit(solution)/shard_map/ppermute | solution.py:65
  36.5 8.2 %collective-permute-start.6 = (bf16[1,48,1536]{2,1,0:T(8,128)(2,1)}, bf16[1,48,1536]{2,1,0:T(8,128)(2,1)S(1)}, u32[]{:S(2)}, u32[]{:S(2)}) collective-permute-start(bf16[1,48,1536]{2,1,0:T(8,128)(2,1)} %collective-permute-done.5), channel_id=1, source_target_pairs={{0,8},{2,10},{4,12},{6,14},{8,16},{10,18},{12,20},{14,22},{16,24},... | collective-permute-start | bytes 442376 | tf_op jit(solution)/shard_map/ppermute | solution.py:65
  42.9 6.9 %collective-permute-start.12 = (bf16[1,48,1536]{2,1,0:T(8,128)(2,1)S(1)}, bf16[1,48,1536]{2,1,0:T(8,128)(2,1)S(1)}, u32[]{:S(2)}, u32[]{:S(2)}) collective-permute-start(bf16[1,48,1536]{2,1,0:T(8,128)(2,1)S(1)} %collective-permute-done.11), channel_id=1, source_target_pairs={{0,8},{2,10},{4,12},{6,14},{8,16},{10,18},{12,20},{14,22},{16,24},... | collective-permute-start | bytes 442376 | tf_op jit(solution)/shard_map/ppermute | solution.py:65
  44.7 6.9 %collective-permute-start.7 = (bf16[1,48,1536]{2,1,0:T(8,128)(2,1)S(1)}, bf16[1,48,1536]{2,1,0:T(8,128)(2,1)S(1)}, u32[]{:S(2)}, u32[]{:S(2)}) collective-permute-start(bf16[1,48,1536]{2,1,0:T(8,128)(2,1)S(1)} %collective-permute-done.6), channel_id=1, source_target_pairs={{0,8},{2,10},{4,12},{6,14},{8,16},{10,18},{12,20},{14,22},{16,24},... | collective-permute-start | bytes 442376 | tf_op jit(solution)/shard_map/ppermute | solution.py:65
  50.9 11.3 %collective-permute-start.13 = (bf16[4,48,1536]{2,1,0:T(8,128)(2,1)S(1)}, bf16[4,48,1536]{2,1,0:T(8,128)(2,1)S(1)}, u32[]{:S(2)}, u32[]{:S(2)}) collective-permute-start(bf16[4,48,1536]{2,1,0:T(8,128)(2,1)S(1)} %pad_maximum_fusion.5), channel_id=1, source_target_pairs={{0,4},{2,6},{4,0},{6,2},{8,12},{10,14},{12,8},{14,10},{16,20},{18,... | collective-permute-start | bytes 1769480 | tf_op jit(solution)/shard_map/ppermute | solution.py:65
  52.6 14.9 %collective-permute-start.8 = (bf16[4,48,1536]{2,1,0:T(8,128)(2,1)S(1)}, bf16[4,48,1536]{2,1,0:T(8,128)(2,1)S(1)}, u32[]{:S(2)}, u32[]{:S(2)}) collective-permute-start(bf16[4,48,1536]{2,1,0:T(8,128)(2,1)S(1)} %pad_maximum_fusion.4), channel_id=1, source_target_pairs={{0,2},{2,0},{4,6},{6,4},{8,10},{10,8},{12,14},{14,12},{16,18},{18,... | collective-permute-start | bytes 1769480 | tf_op jit(solution)/shard_map/ppermute | solution.py:65
  54.2 15.6 %collective-permute-start.2 = (bf16[4,48,1536]{2,1,0:T(8,128)(2,1)S(1)}, bf16[4,48,1536]{2,1,0:T(8,128)(2,1)S(1)}, u32[]{:S(2)}, u32[]{:S(2)}) collective-permute-start(bf16[4,48,1536]{2,1,0:T(8,128)(2,1)S(1)} %pad_maximum_fusion.3), channel_id=1, source_target_pairs={{0,8},{2,10},{4,12},{6,14},{8,16},{10,18},{12,20},{14,22},{16,24},... | collective-permute-start | bytes 1769480 | tf_op jit(solution)/shard_map/ppermute | solution.py:65
  63.2 331.2 %collective-permute-start.14 = (bf16[8,48,1536]{2,1,0:T(8,128)(2,1)}, bf16[8,48,1536]{2,1,0:T(8,128)(2,1)}, u32[]{:S(2)}, u32[]{:S(2)}) collective-permute-start(bf16[8,48,1536]{2,1,0:T(8,128)(2,1)} %constant_dynamic-update-slice_fusion.5), channel_id=1, source_target_pairs={{0,2},{2,0},{4,6},{6,4},{8,10},{10,8},{12,14},{14,12},{16,18},{18,... | collective-permute-start | bytes 3538952 | tf_op jit(solution)/shard_map/ppermute | solution.py:65
  67.6 20.3 %collective-permute-start.9 = (bf16[8,48,1536]{2,1,0:T(8,128)(2,1)S(1)}, bf16[8,48,1536]{2,1,0:T(8,128)(2,1)S(1)}, u32[]{:S(2)}, u32[]{:S(2)}) collective-permute-start(bf16[8,48,1536]{2,1,0:T(8,128)(2,1)S(1)} %constant_dynamic-update-slice_fusion), channel_id=1, source_target_pairs={{0,4},{2,6},{4,0},{6,2},{8,12},{10,14},{12,8},{14,10},{16,20},{18,... | collective-permute-start | bytes 3538952 | tf_op jit(solution)/shard_map/ppermute | solution.py:65
  69.9 15.0 %collective-permute-start.3 = (bf16[4,48,1536]{2,1,0:T(8,128)(2,1)S(1)}, bf16[4,48,1536]{2,1,0:T(8,128)(2,1)S(1)}, u32[]{:S(2)}, u32[]{:S(2)}) collective-permute-start(bf16[4,48,1536]{2,1,0:T(8,128)(2,1)S(1)} %collective-permute-done.2), channel_id=1, source_target_pairs={{0,8},{2,10},{4,12},{6,14},{8,16},{10,18},{12,20},{14,22},{16,24},... | collective-permute-start | bytes 1769480 | tf_op jit(solution)/shard_map/ppermute | solution.py:65
  84.9 35.5 %collective-permute-start.4 = (bf16[4,48,1536]{2,1,0:T(8,128)(2,1)S(1)}, bf16[4,48,1536]{2,1,0:T(8,128)(2,1)S(1)}, u32[]{:S(2)}, u32[]{:S(2)}) collective-permute-start(bf16[4,48,1536]{2,1,0:T(8,128)(2,1)S(1)} %collective-permute-done.3), channel_id=1, source_target_pairs={{0,8},{2,10},{4,12},{6,14},{8,16},{10,18},{12,20},{14,22},{16,24},... | collective-permute-start | bytes 1769480 | tf_op jit(solution)/shard_map/ppermute | solution.py:65
  118.9 163.7 %collective-permute-start.29 = (bf16[4,1,2,48,1536]{4,3,2,1,0:T(8,128)(2,1)}, bf16[4,1,2,48,1536]{4,3,2,1,0:T(8,128)(2,1)}, u32[]{:S(2)}, u32[]{:S(2)}) collective-permute-start(bf16[4,1,2,48,1536]{4,3,2,1,0:T(8,128)(2,1)} %dynamic-slice_convert_fusion), channel_id=1, source_target_pairs={{0,4},{2,6},{4,0},{6,2},{8,12},{10,14},{12,8},{14,10},{16,20},{18,... | collective-permute-start | bytes 3538952 | tf_op jit(solution)/shard_map/ppermute | solution.py:100
  264.4 17.2 %collective-permute-start.19 = (bf16[1,2,2,48,1536]{4,3,2,1,0:T(8,128)(2,1)S(1)}, bf16[1,2,2,48,1536]{4,3,2,1,0:T(8,128)(2,1)S(1)}, u32[]{:S(2)}, u32[]{:S(2)}) collective-permute-start(bf16[1,2,2,48,1536]{4,3,2,1,0:T(8,128)(2,1)S(1)} %dynamic-slice_convert_fusion.6), channel_id=1, source_target_pairs={{0,8},{2,10},{4,12},{6,14},{8,16},{10,18},{12,20},{14,22},{16,24},... | collective-permute-start | bytes 1769480 | tf_op jit(solution)/shard_map/ppermute | solution.py:100
  282.6 12.0 %collective-permute-start.20 = (bf16[1,2,2,48,1536]{4,3,2,1,0:T(8,128)(2,1)}, bf16[1,2,2,48,1536]{4,3,2,1,0:T(8,128)(2,1)}, u32[]{:S(2)}, u32[]{:S(2)}) collective-permute-start(bf16[1,2,2,48,1536]{4,3,2,1,0:T(8,128)(2,1)} %add_convert_fusion.4), channel_id=1, source_target_pairs={{0,8},{2,10},{4,12},{6,14},{8,16},{10,18},{12,20},{14,22},{16,24},... | collective-permute-start | bytes 1769480 | tf_op jit(solution)/shard_map/ppermute | solution.py:100
  286.6 10.2 %collective-permute-start.30 = (bf16[4,1,1,48,1536]{4,3,2,1,0:T(8,128)(2,1)}, bf16[4,1,1,48,1536]{4,3,2,1,0:T(8,128)(2,1)}, u32[]{:S(2)}, u32[]{:S(2)}) collective-permute-start(bf16[4,1,1,48,1536]{4,3,2,1,0:T(8,128)(2,1)} %dynamic-slice_convert_fusion.4), channel_id=1, source_target_pairs={{0,2},{2,0},{4,6},{6,4},{8,10},{10,8},{12,14},{14,12},{16,18},{18,... | collective-permute-start | bytes 1769480 | tf_op jit(solution)/shard_map/ppermute | solution.py:100
  287.6 172.1 %collective-permute-start.16 = (bf16[512,768]{1,0:T(8,128)(2,1)}, bf16[512,768]{1,0:T(8,128)(2,1)}, u32[]{:S(2)}, u32[]{:S(2)}) collective-permute-start(bf16[512,768]{1,0:T(8,128)(2,1)} %dynamic-slice_convert_fusion.3), channel_id=1, source_target_pairs={{0,1},{1,0},{2,3},{3,2},{4,5},{5,4},{6,7},{7,6},{8,9},{9,8},{10,11... | collective-permute-start | bytes 2359304 | tf_op jit(solution)/shard_map/ppermute | solution.py:107
  296.2 12.9 %collective-permute-start.21 = (bf16[1,2,2,48,1536]{4,3,2,1,0:T(8,128)(2,1)S(1)}, bf16[1,2,2,48,1536]{4,3,2,1,0:T(8,128)(2,1)S(1)}, u32[]{:S(2)}, u32[]{:S(2)}) collective-permute-start(bf16[1,2,2,48,1536]{4,3,2,1,0:T(8,128)(2,1)S(1)} %add_convert_fusion.3), channel_id=1, source_target_pairs={{0,8},{2,10},{4,12},{6,14},{8,16},{10,18},{12,20},{14,22},{16,24},... | collective-permute-start | bytes 1769480 | tf_op jit(solution)/shard_map/ppermute | solution.py:100
  298.0 12.9 %collective-permute-start.31 = (bf16[1,1,1,48,1536]{4,3,2,1,0:T(8,128)(2,1)S(1)}, bf16[1,1,1,48,1536]{4,3,2,1,0:T(8,128)(2,1)S(1)}, u32[]{:S(2)}, u32[]{:S(2)}) collective-permute-start(bf16[1,1,1,48,1536]{4,3,2,1,0:T(8,128)(2,1)S(1)} %dynamic-slice_convert_fusion.8), channel_id=1, source_target_pairs={{0,8},{2,10},{4,12},{6,14},{8,16},{10,18},{12,20},{14,22},{16,24},... | collective-permute-start | bytes 442376 | tf_op jit(solution)/shard_map/ppermute | solution.py:100
  310.9 8.4 %collective-permute-start.32 = (bf16[1,1,1,48,1536]{4,3,2,1,0:T(8,128)(2,1)S(1)}, bf16[1,1,1,48,1536]{4,3,2,1,0:T(8,128)(2,1)S(1)}, u32[]{:S(2)}, u32[]{:S(2)}) collective-permute-start(bf16[1,1,1,48,1536]{4,3,2,1,0:T(8,128)(2,1)S(1)} %add_convert_fusion.10), channel_id=1, source_target_pairs={{0,8},{2,10},{4,12},{6,14},{8,16},{10,18},{12,20},{14,22},{16,24},... | collective-permute-start | bytes 442376 | tf_op jit(solution)/shard_map/ppermute | solution.py:100
  311.1 8.4 %collective-permute-start.22 = (bf16[1,1,2,48,1536]{4,3,2,1,0:T(8,128)(2,1)S(1)}, bf16[1,1,2,48,1536]{4,3,2,1,0:T(8,128)(2,1)S(1)}, u32[]{:S(2)}, u32[]{:S(2)}) collective-permute-start(bf16[1,1,2,48,1536]{4,3,2,1,0:T(8,128)(2,1)S(1)} %dynamic-slice_convert_fusion.7), channel_id=1, source_target_pairs={{0,4},{2,6},{4,0},{6,2},{8,12},{10,14},{12,8},{14,10},{16,20},{18,... | collective-permute-start | bytes 884744 | tf_op jit(solution)/shard_map/ppermute | solution.py:100
  319.4 8.5 %collective-permute-start.33 = (bf16[1,1,1,48,1536]{4,3,2,1,0:T(8,128)(2,1)S(1)}, bf16[1,1,1,48,1536]{4,3,2,1,0:T(8,128)(2,1)S(1)}, u32[]{:S(2)}, u32[]{:S(2)}) collective-permute-start(bf16[1,1,1,48,1536]{4,3,2,1,0:T(8,128)(2,1)S(1)} %add_convert_fusion.9), channel_id=1, source_target_pairs={{0,8},{2,10},{4,12},{6,14},{8,16},{10,18},{12,20},{14,22},{16,24},... | collective-permute-start | bytes 442376 | tf_op jit(solution)/shard_map/ppermute | solution.py:100
  319.5 11.5 %collective-permute-start.23 = (bf16[1,1,1,48,1536]{4,3,2,1,0:T(8,128)(2,1)S(1)}, bf16[1,1,1,48,1536]{4,3,2,1,0:T(8,128)(2,1)S(1)}, u32[]{:S(2)}, u32[]{:S(2)}) collective-permute-start(bf16[1,1,1,48,1536]{4,3,2,1,0:T(8,128)(2,1)S(1)} %dynamic-slice_convert_fusion.10), channel_id=1, source_target_pairs={{0,2},{2,0},{4,6},{6,4},{8,10},{10,8},{12,14},{14,12},{16,18},{18,... | collective-permute-start | bytes 442376 | tf_op jit(solution)/shard_map/ppermute | solution.py:100
  328.8 7.1 %collective-permute-start.46 = (bf16[1,48,1536]{2,1,0:T(8,128)(2,1)S(1)}, bf16[1,48,1536]{2,1,0:T(8,128)(2,1)S(1)}, u32[]{:S(2)}, u32[]{:S(2)}) collective-permute-start(bf16[1,48,1536]{2,1,0:T(8,128)(2,1)S(1)} %get-tuple-element.252), channel_id=1, source_target_pairs={{0,8},{2,10},{4,12},{6,14},{8,16},{10,18},{12,20},{14,22},{16,24},... | collective-permute-start | bytes 442376 | tf_op jit(solution)/shard_map/ppermute | solution.py:65
  334.9 5.1 collective-permute-start.34
  335.9 7.3 %collective-permute-start.47 = (bf16[1,48,1536]{2,1,0:T(8,128)(2,1)S(1)}, bf16[1,48,1536]{2,1,0:T(8,128)(2,1)S(1)}, u32[]{:S(2)}, u32[]{:S(2)}) collective-permute-start(bf16[1,48,1536]{2,1,0:T(8,128)(2,1)S(1)} %collective-permute-done.46), channel_id=1, source_target_pairs={{0,8},{2,10},{4,12},{6,14},{8,16},{10,18},{12,20},{14,22},{16,24},... | collective-permute-start | bytes 442376 | tf_op jit(solution)/shard_map/ppermute | solution.py:65
  340.1 13.2 %collective-permute-start.35 = (bf16[2,48,1536]{2,1,0:T(8,128)(2,1)S(1)}, bf16[2,48,1536]{2,1,0:T(8,128)(2,1)S(1)}, u32[]{:S(2)}, u32[]{:S(2)}) collective-permute-start(bf16[2,48,1536]{2,1,0:T(8,128)(2,1)S(1)} %pad_maximum_fusion.10), channel_id=1, source_target_pairs={{0,4},{2,6},{4,0},{6,2},{8,12},{10,14},{12,8},{14,10},{16,20},{18,... | collective-permute-start | bytes 884744 | tf_op jit(solution)/shard_map/ppermute | solution.py:65
  343.3 8.5 %collective-permute-start.48 = (bf16[1,48,1536]{2,1,0:T(8,128)(2,1)S(1)}, bf16[1,48,1536]{2,1,0:T(8,128)(2,1)S(1)}, u32[]{:S(2)}, u32[]{:S(2)}) collective-permute-start(bf16[1,48,1536]{2,1,0:T(8,128)(2,1)S(1)} %collective-permute-done.47), channel_id=1, source_target_pairs={{0,8},{2,10},{4,12},{6,14},{8,16},{10,18},{12,20},{14,22},{16,24},... | collective-permute-start | bytes 442376 | tf_op jit(solution)/shard_map/ppermute | solution.py:65
  351.9 9.9 %collective-permute-start.49 = (bf16[4,48,1536]{2,1,0:T(8,128)(2,1)S(1)}, bf16[4,48,1536]{2,1,0:T(8,128)(2,1)S(1)}, u32[]{:S(2)}, u32[]{:S(2)}) collective-permute-start(bf16[4,48,1536]{2,1,0:T(8,128)(2,1)S(1)} %pad_maximum_fusion.8), channel_id=1, source_target_pairs={{0,4},{2,6},{4,0},{6,2},{8,12},{10,14},{12,8},{14,10},{16,20},{18,... | collective-permute-start | bytes 1769480 | tf_op jit(solution)/shard_map/ppermute | solution.py:65
  353.4 16.8 %collective-permute-start.36 = (bf16[4,48,1536]{2,1,0:T(8,128)(2,1)S(1)}, bf16[4,48,1536]{2,1,0:T(8,128)(2,1)S(1)}, u32[]{:S(2)}, u32[]{:S(2)}) collective-permute-start(bf16[4,48,1536]{2,1,0:T(8,128)(2,1)S(1)} %pad_maximum_fusion.6), channel_id=1, source_target_pairs={{0,8},{2,10},{4,12},{6,14},{8,16},{10,18},{12,20},{14,22},{16,24},... | collective-permute-start | bytes 1769480 | tf_op jit(solution)/shard_map/ppermute | solution.py:65
  361.9 32.5 %collective-permute-start.50 = (bf16[8,48,1536]{2,1,0:T(8,128)(2,1)S(1)}, bf16[8,48,1536]{2,1,0:T(8,128)(2,1)S(1)}, u32[]{:S(2)}, u32[]{:S(2)}) collective-permute-start(bf16[8,48,1536]{2,1,0:T(8,128)(2,1)S(1)} %constant_dynamic-update-slice_fusion.15), channel_id=1, source_target_pairs={{0,2},{2,0},{4,6},{6,4},{8,10},{10,8},{12,14},{14,12},{16,18},{18,... | collective-permute-start | bytes 3538952 | tf_op jit(solution)/shard_map/ppermute | solution.py:65
  370.2 17.8 %collective-permute-start.37 = (bf16[4,48,1536]{2,1,0:T(8,128)(2,1)S(1)}, bf16[4,48,1536]{2,1,0:T(8,128)(2,1)}, u32[]{:S(2)}, u32[]{:S(2)}) collective-permute-start(bf16[4,48,1536]{2,1,0:T(8,128)(2,1)S(1)} %collective-permute-done.36), channel_id=1, source_target_pairs={{0,8},{2,10},{4,12},{6,14},{8,16},{10,18},{12,20},{14,22},{16,24},... | collective-permute-start | bytes 1769480 | tf_op jit(solution)/shard_map/ppermute | solution.py:65
  388.0 55.8 %collective-permute-start.38 = (bf16[4,48,1536]{2,1,0:T(8,128)(2,1)}, bf16[4,48,1536]{2,1,0:T(8,128)(2,1)}, u32[]{:S(2)}, u32[]{:S(2)}) collective-permute-start(bf16[4,48,1536]{2,1,0:T(8,128)(2,1)} %collective-permute-done.37), channel_id=1, source_target_pairs={{0,8},{2,10},{4,12},{6,14},{8,16},{10,18},{12,20},{14,22},{16,24},... | collective-permute-start | bytes 1769480 | tf_op jit(solution)/shard_map/ppermute | solution.py:65
  430.8 28.9 %collective-permute-start.17 = (bf16[512,768]{1,0:T(8,128)(2,1)}, bf16[512,768]{1,0:T(8,128)(2,1)}, u32[]{:S(2)}, u32[]{:S(2)}) collective-permute-start(bf16[512,768]{1,0:T(8,128)(2,1)} %dynamic-slice_convert_fusion.2), channel_id=1, source_target_pairs={{0,1},{1,0},{2,3},{3,2},{4,5},{5,4},{6,7},{7,6},{8,9},{9,8},{10,11... | collective-permute-start | bytes 2359304 | tf_op jit(solution)/shard_map/ppermute | solution.py:107
  433.9 30.1 %collective-permute-start.24 = (bf16[4,2,1,48,1536]{4,3,2,1,0:T(8,128)(2,1)}, bf16[4,2,1,48,1536]{4,3,2,1,0:T(8,128)(2,1)}, u32[]{:S(2)}, u32[]{:S(2)}) collective-permute-start(bf16[4,2,1,48,1536]{4,3,2,1,0:T(8,128)(2,1)} %dynamic-slice_convert_fusion.1), channel_id=1, source_target_pairs={{0,2},{2,0},{4,6},{6,4},{8,10},{10,8},{12,14},{14,12},{16,18},{18,... | collective-permute-start | bytes 3538952 | tf_op jit(solution)/shard_map/ppermute | solution.py:100
  438.4 61.8 %collective-permute-start.15 = (f32[1024,384]{1,0:T(8,128)}, f32[1024,384]{1,0:T(8,128)}, u32[]{:S(2)}, u32[]{:S(2)}) collective-permute-start(f32[1024,384]{1,0:T(8,128)} %constant_dynamic-slice_fusion.2), channel_id=1, source_target_pairs={{0,1},{1,0},{2,3},{3,2},{4,5},{5,4},{6,7},{7,6},{8,9},{9,8},{10,11... | collective-permute-start | bytes 4718600 | tf_op jit(solution)/shard_map/ppermute | solution.py:107
  459.3 56.4 %collective-permute-start.39 = (f32[768,768]{1,0:T(8,128)}, f32[768,768]{1,0:T(8,128)}, u32[]{:S(2)}, u32[]{:S(2)}) collective-permute-start(f32[768,768]{1,0:T(8,128)} %get-tuple-element.328), channel_id=1, source_target_pairs={{0,1},{1,0},{2,3},{3,2},{4,5},{5,4},{6,7},{7,6},{8,9},{9,8},{10,11... | collective-permute-start | bytes 7077896 | tf_op jit(solution)/shard_map/ppermute | solution.py:107
  463.8 5.9 collective-permute-start.53
  466.5 18.0 %collective-permute-start.25 = (bf16[4,1,1,48,1536]{4,3,2,1,0:T(8,128)(2,1)S(1)}, bf16[4,1,1,48,1536]{4,3,2,1,0:T(8,128)(2,1)S(1)}, u32[]{:S(2)}, u32[]{:S(2)}) collective-permute-start(bf16[4,1,1,48,1536]{4,3,2,1,0:T(8,128)(2,1)S(1)} %dynamic-slice_convert_fusion.5), channel_id=1, source_target_pairs={{0,4},{2,6},{4,0},{6,2},{8,12},{10,14},{12,8},{14,10},{16,20},{18,... | collective-permute-start | bytes 1769480 | tf_op jit(solution)/shard_map/ppermute | solution.py:100
  469.8 4.2 collective-permute-start.54
  473.9 10.5 %collective-permute-start.55 = (f32[13,768]{1,0:T(8,128)S(1)}, f32[13,768]{1,0:T(8,128)S(1)}, u32[]{:S(2)}, u32[]{:S(2)}) collective-permute-start(f32[13,768]{1,0:T(8,128)S(1)} %add.1492), channel_id=1, source_target_pairs={{0,4},{2,6},{4,0},{6,2},{8,12},{10,14},{12,8},{14,10},{16,20},{18,... | collective-permute-start | bytes 119816 | tf_op jit(solution)/shard_map/ppermute | solution.py:116
  484.5 4.2 collective-permute-start.56
  484.7 8.3 %collective-permute-start.26 = (bf16[1,1,1,48,1536]{4,3,2,1,0:T(8,128)(2,1)S(1)}, bf16[1,1,1,48,1536]{4,3,2,1,0:T(8,128)(2,1)S(1)}, u32[]{:S(2)}, u32[]{:S(2)}) collective-permute-start(bf16[1,1,1,48,1536]{4,3,2,1,0:T(8,128)(2,1)S(1)} %dynamic-slice_convert_fusion.9), channel_id=1, source_target_pairs={{0,8},{2,10},{4,12},{6,14},{8,16},{10,18},{12,20},{14,22},{16,24},... | collective-permute-start | bytes 442376 | tf_op jit(solution)/shard_map/ppermute | solution.py:100
  488.7 119.5 %collective-permute-start.18 = (bf16[512,768]{1,0:T(8,128)(2,1)}, bf16[512,768]{1,0:T(8,128)(2,1)S(1)}, u32[]{:S(2)}, u32[]{:S(2)}) collective-permute-start(bf16[512,768]{1,0:T(8,128)(2,1)} %fusion.106), channel_id=1, source_target_pairs={{0,1},{1,0},{2,3},{3,2},{4,5},{5,4},{6,7},{7,6},{8,9},{9,8},{10,11... | collective-permute-start | bytes 2359304 | tf_op jit(solution)/shard_map/ppermute | solution.py:107
  488.7 5.4 collective-permute-start.57
  493.1 7.0 %collective-permute-start.27 = (bf16[1,1,1,48,1536]{4,3,2,1,0:T(8,128)(2,1)S(1)}, bf16[1,1,1,48,1536]{4,3,2,1,0:T(8,128)(2,1)S(1)}, u32[]{:S(2)}, u32[]{:S(2)}) collective-permute-start(bf16[1,1,1,48,1536]{4,3,2,1,0:T(8,128)(2,1)S(1)} %add_convert_fusion.12), channel_id=1, source_target_pairs={{0,8},{2,10},{4,12},{6,14},{8,16},{10,18},{12,20},{14,22},{16,24},... | collective-permute-start | bytes 442376 | tf_op jit(solution)/shard_map/ppermute | solution.py:100
  500.1 7.0 %collective-permute-start.28 = (bf16[1,1,1,48,1536]{4,3,2,1,0:T(8,128)(2,1)S(1)}, bf16[1,1,1,48,1536]{4,3,2,1,0:T(8,128)(2,1)S(1)}, u32[]{:S(2)}, u32[]{:S(2)}) collective-permute-start(bf16[1,1,1,48,1536]{4,3,2,1,0:T(8,128)(2,1)S(1)} %add_convert_fusion.11), channel_id=1, source_target_pairs={{0,8},{2,10},{4,12},{6,14},{8,16},{10,18},{12,20},{14,22},{16,24},... | collective-permute-start | bytes 442376 | tf_op jit(solution)/shard_map/ppermute | solution.py:100
  508.1 6.9 %collective-permute-start.41 = (bf16[1,48,1536]{2,1,0:T(8,128)(2,1)S(1)}, bf16[1,48,1536]{2,1,0:T(8,128)(2,1)S(1)}, u32[]{:S(2)}, u32[]{:S(2)}) collective-permute-start(bf16[1,48,1536]{2,1,0:T(8,128)(2,1)S(1)} %get-tuple-element.256), channel_id=1, source_target_pairs={{0,8},{2,10},{4,12},{6,14},{8,16},{10,18},{12,20},{14,22},{16,24},... | collective-permute-start | bytes 442376 | tf_op jit(solution)/shard_map/ppermute | solution.py:65
  515.0 40.5 %collective-permute-start.42 = (bf16[1,48,1536]{2,1,0:T(8,128)(2,1)S(1)}, bf16[1,48,1536]{2,1,0:T(8,128)(2,1)}, u32[]{:S(2)}, u32[]{:S(2)}) collective-permute-start(bf16[1,48,1536]{2,1,0:T(8,128)(2,1)S(1)} %collective-permute-done.41), channel_id=1, source_target_pairs={{0,8},{2,10},{4,12},{6,14},{8,16},{10,18},{12,20},{14,22},{16,24},... | collective-permute-start | bytes 442376 | tf_op jit(solution)/shard_map/ppermute | solution.py:65
  555.5 8.3 %collective-permute-start.43 = (bf16[1,48,1536]{2,1,0:T(8,128)(2,1)}, bf16[1,48,1536]{2,1,0:T(8,128)(2,1)S(1)}, u32[]{:S(2)}, u32[]{:S(2)}) collective-permute-start(bf16[1,48,1536]{2,1,0:T(8,128)(2,1)} %collective-permute-done.42), channel_id=1, source_target_pairs={{0,8},{2,10},{4,12},{6,14},{8,16},{10,18},{12,20},{14,22},{16,24},... | collective-permute-start | bytes 442376 | tf_op jit(solution)/shard_map/ppermute | solution.py:65
  564.7 9.9 %collective-permute-start.44 = (bf16[4,48,1536]{2,1,0:T(8,128)(2,1)S(1)}, bf16[4,48,1536]{2,1,0:T(8,128)(2,1)S(1)}, u32[]{:S(2)}, u32[]{:S(2)}) collective-permute-start(bf16[4,48,1536]{2,1,0:T(8,128)(2,1)S(1)} %pad_maximum_fusion.7), channel_id=1, source_target_pairs={{0,2},{2,0},{4,6},{6,4},{8,10},{10,8},{12,14},{14,12},{16,18},{18,... | collective-permute-start | bytes 1769480 | tf_op jit(solution)/shard_map/ppermute | solution.py:65
  574.7 21.2 %collective-permute-start.45 = (bf16[8,48,1536]{2,1,0:T(8,128)(2,1)S(1)}, bf16[8,48,1536]{2,1,0:T(8,128)(2,1)S(1)}, u32[]{:S(2)}, u32[]{:S(2)}) collective-permute-start(bf16[8,48,1536]{2,1,0:T(8,128)(2,1)S(1)} %constant_dynamic-update-slice_fusion.10), channel_id=1, source_target_pairs={{0,4},{2,6},{4,0},{6,2},{8,12},{10,14},{12,8},{14,10},{16,20},{18,... | collective-permute-start | bytes 3538952 | tf_op jit(solution)/shard_map/ppermute | solution.py:65
  602.6 14.9 %collective-permute-start.51 = (f32[768,768]{1,0:T(8,128)S(1)}, f32[768,768]{1,0:T(8,128)S(1)}, u32[]{:S(2)}, u32[]{:S(2)}) collective-permute-start(f32[768,768]{1,0:T(8,128)S(1)} %get-tuple-element.330), channel_id=1, source_target_pairs={{0,1},{1,0},{2,3},{3,2},{4,5},{5,4},{6,7},{7,6},{8,9},{9,8},{10,11... | collective-permute-start | bytes 7077896 | tf_op jit(solution)/shard_map/ppermute | solution.py:107
  607.6 4.0 collective-permute-start.40
  668.5 2.0 collective-permute-start.52
  (90 other events, 1111.0 us)

commit v2 on v1

v2 whole, which is shorter than its diff:
```python
import functools
import math

import jax
import jax.numpy as jnp
from jax import lax
from jax.experimental import pallas as pl
from jax.experimental.pallas import tpu as pltpu
from jax.sharding import PartitionSpec as P

D = 768
HEAD_DIM = 64
FF = 3072
ROTARY = 16
HALF = ROTARY // 2
NS_STEPS = 5
STEP = 10
QUERY_TILE = 512
VMEM_LIMIT = 48 * 1024 * 1024


HIGH = lax.Precision.HIGH
X_FIRST = (0, 1, 2)
Z_THEN_X = (2, 0, 1)
Z_THEN_Y = (2, 1, 0)
Z_ORDERS = (Z_THEN_X, Z_THEN_Y)
X_THEN_Y = (0, 1, 2)
Y_THEN_X = (1, 0, 2)
Z_FIRST = (2, 1, 0)
NORM_EPS = 1e-05
POLY_ONE = 3.4445
POLY_TWO = -4.775
POLY_THREE = 2.0315
SCALE_EPS = 1e-07
MUON_BETA = 0.9
MUON_RATE = 0.03
MUON_DECAY = 0.1
BETA_ONE = 0.9
BETA_TWO = 0.95
ADAM_RATE = 0.1
ADAM_EPS = 1e-08


DATA_AXES = {16: ((1, 2), (2, 2), (4, 4)), 128: ((1, 4), (4, 8), (32, 4))}


def data_axes(count):
    return DATA_AXES.get(count, ((1, count), (count, 1), (count, 1)))


def ring(count, stride, size):
    pairs = []
    for index in range(count):
        place = (index // stride) % size
        pairs.append((index, index + ((place + 1) % size - place) * stride))
    return pairs


def gather_sources(order, count, rank):
    sources = [rank]
    for axis in order:
        stride, size = data_axes(count)[axis]
        found, owners = list(sources), sources
        for _ in range(size - 1):
            places = [(owner // stride) % size for owner in owners]
            owners = [
                owner + ((place + size - 1) % size - place) * stride
                for owner, place in zip(owners, places)
            ]
            found += owners
        sources = found
    return sources


def place_kernel(orders, counts, width, count, *refs):
    parts, whole_ref, semaphores = list(refs[:-2]), refs[-2], refs[-1]
    copies = []
    for piece, order in enumerate(orders):
        sources = gather_sources(order, count, lax.axis_index("dp"))
        columns = pl.ds(piece * width, width)
        for part in [parts.pop(0) for _ in range(counts[piece])]:
            for row in range(part.shape[0]):
                copies.append(
                    pltpu.make_async_copy(
                        part.at[row],
                        whole_ref.at[sources.pop(0), :, columns],
                        semaphores.at[len(copies)],
                    )
                )
    for copy in copies:
        copy.start()
    for copy in copies:
        copy.wait()


def gather_stage(parts, axis):
    count = lax.axis_size("dp")
    stride, size = data_axes(count)[axis]
    perm = ring(count, stride, size)
    moving = jnp.concatenate(parts, 0) if len(parts) > 1 else parts[0]
    parts = [moving]
    for _ in range(size - 1):
        moving = lax.ppermute(moving, "dp", perm)
        parts.append(moving)
    return parts


def staged_gather(share, orders, early=(), late=()):
    count = lax.axis_size("dp")
    rows, columns = share.shape
    width = columns // len(orders)
    pieces = [
        [share[None, :, piece * width : (piece + 1) * width]] for piece in range(len(orders))
    ]
    for stage in range(3):
        pieces = [gather_stage(parts, order[stage]) for parts, order in zip(pieces, orders)]
        if stage == 0:
            pieces, early = lax.optimization_barrier((pieces, early))
    pieces, late = lax.optimization_barrier((pieces, late))
    anywhere = pl.BlockSpec(memory_space=pl.ANY)
    whole = pl.pallas_call(
        functools.partial(place_kernel, orders, [len(parts) for parts in pieces], width, count),
        in_specs=[anywhere] * sum(len(parts) for parts in pieces),
        out_specs=pl.BlockSpec(memory_space=pltpu.VMEM),
        out_shape=jax.ShapeDtypeStruct((count, rows, columns), share.dtype),
        scratch_shapes=[pltpu.SemaphoreType.DMA((count * len(orders),))],
        compiler_params=pltpu.CompilerParams(vmem_limit_bytes=VMEM_LIMIT),
        cost_estimate=pl.CostEstimate(
            flops=0, bytes_accessed=4 * count * rows * columns, transcendentals=0
        ),
    )(*[part for parts in pieces for part in parts])
    whole = whole.reshape(count * rows, columns)
    return whole, early, late


def staged_scatter(partial, order):
    count = lax.axis_size("dp")
    rank = lax.axis_index("dp")
    axes = data_axes(count)
    rows, columns = partial.shape[0] // count, partial.shape[1]
    slow_first = sorted(range(len(axes)), key=lambda axis: -axes[axis][0])
    held = partial.reshape(*[axes[axis][1] for axis in slow_first], rows, columns)
    for axis in order:
        stride, size = axes[axis]
        if size == 1:
            continue
        perm = ring(count, stride, size)
        place = (rank // stride) % size
        dim = slow_first.index(axis)

        def block(target):
            return lax.dynamic_slice_in_dim(held, target % size, 1, dim)

        total = block(place + size - 1)
        for step in range(size - 1):
            got = lax.ppermute(total.astype(jnp.bfloat16), "dp", perm)
            total = block(place + 2 * size - 2 - step) + got.astype(jnp.float32)
        held = total
    return held.reshape(rows, columns)


def other_core(value):
    return lax.ppermute(value, "tensor", [(0, 1), (1, 0)])


def sum_everywhere(value):
    value = value + other_core(value)
    count = lax.axis_size("dp")
    distance = 1
    while distance < count:
        pairs = [(index, index ^ distance) for index in range(count)]
        value = value + lax.ppermute(value, "dp", pairs)
        distance *= 2
    return value


def product(left, right):
    return jnp.dot(left, right, precision=HIGH, preferred_element_type=jnp.float32)


def newton_rows(gram, first_row, rows):
    factor = 1.0 / (jnp.sqrt(jnp.trace(gram)) + SCALE_EPS)
    square = gram * (factor * factor)
    identity = jnp.eye(D, dtype=jnp.float32)
    kept = lax.dynamic_slice_in_dim(identity, first_row, rows, 0) * factor
    for iteration in range(NS_STEPS - 1):
        step = (
            POLY_ONE * identity + POLY_TWO * square + POLY_THREE * product(square, square)
        )
        kept = product(kept, step) if iteration else lax.dynamic_slice_in_dim(
            step, first_row, rows, 0
        ) * factor
        square = product(product(step, square), step)
    once = product(kept, square)
    return POLY_ONE * kept + POLY_TWO * once + POLY_THREE * product(once, square)


def rows_product(left, right):
    high = left.astype(jnp.bfloat16)
    low = (left - high.astype(jnp.float32)).astype(jnp.bfloat16)
    return jnp.dot(high, right, preferred_element_type=jnp.float32) + jnp.dot(
        low, right, preferred_element_type=jnp.float32
    )


def norm_stats(values):
    row_mean = jnp.mean(values, axis=-1, keepdims=True)
    centered = values - row_mean
    row_var = jnp.mean(centered * centered, axis=-1, keepdims=True)
    inverse = lax.rsqrt(row_var + NORM_EPS)
    return (centered * inverse, inverse)


def norm_backward(incoming, normed, inverse, gain):
    scaled = incoming * gain
    return inverse * (
        scaled
        - jnp.mean(scaled, axis=-1, keepdims=True)
        - normed * jnp.mean(scaled * normed, axis=-1, keepdims=True)
    )


def rotary_tables(segments):
    token_index = jnp.arange(segments.shape[0], dtype=jnp.int32)
    leading = jnp.sum((segments == 0).astype(jnp.int32))
    position = (token_index - jnp.where(segments == 1, leading, 0)).astype(jnp.float32)
    exponent = jnp.arange(HALF, dtype=jnp.int32).astype(jnp.float32) * (2.0 / ROTARY)
    frequency = jnp.exp(-math.log(10000.0) * exponent)
    angles = frequency[:, None] * position[None, :]
    return (jnp.cos(angles), jnp.sin(angles))


def first_slots(segments):
    leading = jnp.sum((segments == 0).astype(jnp.int32))
    live = jnp.sum((segments >= 0).astype(jnp.int32))
    return jnp.where(segments == 0, 0, jnp.where(segments == 1, leading, live))


def matmul(left, right):
    return jnp.dot(left, right, preferred_element_type=jnp.float32)


def attention_kernel(
    triple_ref, cos_ref, sin_ref, upstream_ref, first_ref, mixture_ref, grad_ref, key_acc, value_acc
):
    length = triple_ref.shape[1]
    scale = 1.0 / math.sqrt(HEAD_DIM)
    cosines, sines = cos_ref[...], sin_ref[...]

    def turned(values, sign):
        first, second = values[:HALF], values[HALF:ROTARY]
        return jnp.concatenate(
            [
                first * cosines - sign * (second * sines),
                second * cosines + sign * (first * sines),
                values[ROTARY:],
            ],
            0,
        )

    def rounded(values):
        return values.astype(jnp.bfloat16).astype(jnp.float32)

    query_rows = rounded(turned(triple_ref[:HEAD_DIM], 1.0)) * scale
    key_rows = turned(triple_ref[HEAD_DIM : 2 * HEAD_DIM], 1.0)
    value_rows = triple_ref[2 * HEAD_DIM :]
    up_rows = upstream_ref[...]
    queries = query_rows.T.astype(jnp.bfloat16)
    keys = key_rows.T.astype(jnp.bfloat16)
    values = value_rows.T.astype(jnp.bfloat16)
    ups = up_rows.astype(jnp.float32).T.astype(jnp.bfloat16)
    query_rows = query_rows.astype(jnp.bfloat16)
    key_rows = key_rows.astype(jnp.bfloat16)
    value_rows = value_rows.astype(jnp.bfloat16)
    key_acc[...] = jnp.zeros_like(key_acc)
    value_acc[...] = jnp.zeros_like(value_acc)
    query_parts = []
    for tile in range(length // QUERY_TILE):
        start, stop = tile * QUERY_TILE, (tile + 1) * QUERY_TILE
        scores = matmul(keys[:stop], query_rows[:, start:stop])
        slot = lax.broadcasted_iota(jnp.int32, (stop, QUERY_TILE), 0)
        own = lax.broadcasted_iota(jnp.int32, (QUERY_TILE, QUERY_TILE), 1)
        keep = slot >= first_ref[:, start:stop]
        square = jnp.where(
            keep[start:] & (slot[:QUERY_TILE] <= own), scores[start:], -jnp.inf
        )
        if tile:
            scores = jnp.concatenate(
                [jnp.where(keep[:start], scores[:start], -jnp.inf), square], 0
            )
        else:
            scores = square
        top = jnp.max(scores, axis=0, keepdims=True)
        exponent = jnp.exp(scores - top)
        probs = exponent * (1.0 / jnp.sum(exponent, axis=0, keepdims=True))
        probs_low = probs.astype(jnp.bfloat16)
        mixture_ref[:, start:stop] = matmul(value_rows[:, :stop], probs_low).astype(jnp.bfloat16)
        prob_grad = matmul(values[:stop], up_rows[:, start:stop])
        delta = jnp.sum(probs * prob_grad, axis=0, keepdims=True)
        score_grad = (probs * (prob_grad - delta)).astype(jnp.bfloat16)
        query_parts.append(matmul(key_rows[:, :stop], score_grad))
        key_acc[:stop] += matmul(score_grad, queries[start:stop])
        value_acc[:stop] += matmul(probs_low, ups[start:stop])
    query_grad = rounded(jnp.concatenate(query_parts, 1) * scale)
    key_grad = rounded(key_acc[...].T)
    grad_ref[:HEAD_DIM] = turned(query_grad, -1.0).astype(jnp.bfloat16)
    grad_ref[HEAD_DIM : 2 * HEAD_DIM] = turned(key_grad, -1.0).astype(jnp.bfloat16)
    grad_ref[2 * HEAD_DIM :] = value_acc[...].T.astype(jnp.bfloat16)


def attention(triple_rows, cosines, sines, up_rows, segments):
    width, length = triple_rows.shape
    heads = width // (3 * HEAD_DIM)

    def whole(rows):
        return pl.BlockSpec((rows, length), lambda head: (0, 0))

    def own(rows):
        return pl.BlockSpec((rows, length), lambda head: (head, 0))

    return pl.pallas_call(
        attention_kernel,
        grid=(heads,),
        in_specs=[own(3 * HEAD_DIM), whole(HALF), whole(HALF), own(HEAD_DIM), whole(1)],
        out_specs=[own(HEAD_DIM), own(3 * HEAD_DIM)],
        out_shape=[
            jax.ShapeDtypeStruct((heads * HEAD_DIM, length), jnp.bfloat16),
            jax.ShapeDtypeStruct((width, length), jnp.bfloat16),
        ],
        scratch_shapes=[pltpu.VMEM((length, HEAD_DIM), jnp.float32)] * 2,
        compiler_params=pltpu.CompilerParams(vmem_limit_bytes=VMEM_LIMIT),
        cost_estimate=pl.CostEstimate(
            flops=heads * 36 * length * length * HEAD_DIM,
            bytes_accessed=width * length * 8,
            transcendentals=heads * length * length,
        ),
    )(triple_rows, cosines, sines, up_rows, first_slots(segments)[None])


def shards(
    layer_input,
    cotangent,
    segment_ids,
    attend_weight,
    output_weight,
    widen_weight,
    narrow_weight,
    attend_moment,
    output_moment,
    widen_moment,
    narrow_moment,
    vector_params,
    vector_first,
    vector_second,
):
    tensor_size = lax.axis_size("tensor")
    tensor_rank = lax.axis_index("tensor")
    data_size = lax.axis_size("dp")
    data_rank = lax.axis_index("dp")
    masters = (attend_weight, output_weight, widen_weight, narrow_weight)
    attend_columns = attend_weight.shape[1]
    attend_share = jnp.concatenate([attend_weight, output_weight], 1).astype(jnp.bfloat16)
    widen_low, narrow_share, _ = staged_gather(
        widen_weight.astype(jnp.bfloat16), Z_ORDERS, narrow_weight.astype(jnp.bfloat16)
    )
    length = layer_input.shape[0]
    triple_cols = attend_weight.shape[1]
    attend_columns = triple_cols
    widen_cols = widen_low.shape[1]
    widen_rows = FF // D
    feature_share = D // tensor_size
    float_input = layer_input.astype(jnp.float32)
    first_gain = vector_params[0]
    second_gain = vector_params[2]
    attend_bias = lax.dynamic_slice_in_dim(
        vector_params[4:7].reshape(-1), tensor_rank * triple_cols, triple_cols
    )
    widen_bias = lax.dynamic_slice_in_dim(
        vector_params[8 : 8 + widen_rows].reshape(-1), tensor_rank * widen_cols, widen_cols
    )
    normed, inverse = norm_stats(float_input)
    first_norm = (normed * first_gain + vector_params[1]).astype(jnp.bfloat16)
    second_norm = (normed * second_gain + vector_params[3]).astype(jnp.bfloat16)
    widened = jnp.dot(second_norm, widen_low, preferred_element_type=jnp.float32) + widen_bias
    activated = jax.nn.gelu(widened, approximate=False).astype(jnp.bfloat16)
    narrow_low, _, (widened, activated) = staged_gather(
        narrow_share, Z_ORDERS, late=(widened, activated)
    )
    live_rows = (segment_ids >= 0).astype(jnp.float32)[:, None]
    upstream = live_rows * cotangent.astype(jnp.float32)
    upstream_low = upstream.astype(jnp.bfloat16)
    bias_grad = jnp.sum(upstream, axis=0) / tensor_size
    activation_grad = jnp.einsum(
        "sd,df->sf", upstream_low, narrow_low, preferred_element_type=jnp.float32
    )
    gelu_slope = jax.vjp(lambda inner_value: jax.nn.gelu(inner_value, approximate=False), widened)[
        1
    ](activation_grad)[0]
    widen_back = gelu_slope.astype(jnp.bfloat16)
    narrow_grad = jnp.einsum(
        "sd,sf->df", upstream_low, activated, preferred_element_type=jnp.float32
    )
    widen_grad = jnp.einsum(
        "sd,sf->df", second_norm, widen_back, preferred_element_type=jnp.float32
    )
    widen_bias_grad = jnp.sum(widen_back.astype(jnp.float32), axis=0)
    second_back = jnp.einsum("sf,df->sd", widen_back, widen_low, preferred_element_type=jnp.float32)
    joint_low, _, (widen_grad, narrow_grad) = staged_gather(
        attend_share, (X_FIRST,), late=(widen_grad, narrow_grad)
    )
    attend_low, output_low = joint_low[:, :attend_columns], joint_low[:, attend_columns:]
    widen_sum = staged_scatter(widen_grad, X_THEN_Y)
    narrow_sum = staged_scatter(narrow_grad, Y_THEN_X)
    triple_rows = (
        jnp.einsum("dk,sd->ks", attend_low, first_norm, preferred_element_type=jnp.float32)
        + attend_bias[:, None]
    )
    mixed_rows = jnp.einsum(
        "sd,dk->ks", upstream_low, output_low, preferred_element_type=jnp.float32
    ).astype(jnp.bfloat16)
    cosines, sines = rotary_tables(segment_ids)
    mixture_rows, triple_grad = attention(triple_rows, cosines, sines, mixed_rows, segment_ids)
    output_grad = jnp.einsum(
        "sd,ks->dk", upstream_low, mixture_rows, preferred_element_type=jnp.float32
    )
    attend_grad = jnp.einsum(
        "sd,ks->dk", first_norm, triple_grad, preferred_element_type=jnp.float32
    )
    joint_sum = staged_scatter(jnp.concatenate([attend_grad, output_grad], 1), Z_FIRST)
    attend_bias_grad = jnp.sum(triple_grad.astype(jnp.float32), axis=1)
    first_back = jnp.einsum(
        "ks,dk->sd", triple_grad, attend_low, preferred_element_type=jnp.float32
    )
    attended = jnp.einsum(
        "ks,dk->sd", mixture_rows, output_low, preferred_element_type=jnp.float32
    )
    narrowed = jnp.einsum("sf,df->sd", activated, narrow_low, preferred_element_type=jnp.float32)
    branch_part = attended + narrowed
    column_start = tensor_rank * feature_share

    def own_columns(array):
        return lax.dynamic_slice_in_dim(array, column_start, feature_share, array.ndim - 1)

    other_start = (1 - tensor_rank) * feature_share
    branch = own_columns(branch_part) + other_core(
        lax.dynamic_slice_in_dim(branch_part, other_start, feature_share, 1)
    )
    block_output = (
        live_rows
        * (
            own_columns(float_input)
            + branch
            + own_columns(vector_params[7])
            + own_columns(vector_params[8 + widen_rows])
        )
    ).astype(jnp.bfloat16)
    row_share = length // tensor_size
    row_start = tensor_rank * row_share
    other_row = (1 - tensor_rank) * row_share

    def core_sum(part):
        sent = lax.dynamic_slice_in_dim(part, other_row, row_share, 0).astype(jnp.bfloat16)
        kept = lax.dynamic_slice_in_dim(part, row_start, row_share, 0)
        return kept + other_core(sent).astype(jnp.float32)

    first_total, second_total = core_sum(first_back), core_sum(second_back)
    normed_share = lax.dynamic_slice_in_dim(normed, row_start, row_share, 0)
    inverse_share = lax.dynamic_slice_in_dim(inverse, row_start, row_share, 0)
    upstream_share = lax.dynamic_slice_in_dim(upstream, row_start, row_share, 0)
    input_share = upstream_share + (
        norm_backward(first_total, normed_share, inverse_share, first_gain)
        + norm_backward(second_total, normed_share, inverse_share, second_gain)
    )
    input_low = input_share.astype(jnp.bfloat16)
    input_other = other_core(input_low)
    input_grad = jnp.where(
        tensor_rank == 0,
        jnp.concatenate([input_low, input_other], 0),
        jnp.concatenate([input_other, input_low], 0),
    ).astype(jnp.float32)
    norm_rows = jnp.stack(
        [
            jnp.sum(first_total * normed_share, axis=0),
            jnp.sum(first_total, axis=0),
            jnp.sum(second_total * normed_share, axis=0),
            jnp.sum(second_total, axis=0),
        ]
    )
    attend_bias_full = lax.dynamic_update_slice_in_dim(
        jnp.zeros((3 * D,), jnp.float32), attend_bias_grad, tensor_rank * triple_cols, 0
    )
    widen_bias_full = lax.dynamic_update_slice_in_dim(
        jnp.zeros((FF,), jnp.float32), widen_bias_grad, tensor_rank * widen_cols, 0
    )
    vector_part = jnp.concatenate(
        [
            norm_rows,
            attend_bias_full.reshape(3, D),
            bias_grad[None],
            widen_bias_full.reshape(widen_rows, D),
            bias_grad[None],
        ],
        axis=0,
    )
    vector_grad = sum_everywhere(vector_part)
    attend_sum, output_sum = joint_sum[:, :attend_columns], joint_sum[:, attend_columns:]
    summed = (attend_sum, output_sum, widen_sum, narrow_sum)
    moments = (attend_moment, output_moment, widen_moment, narrow_moment)
    momenta = [MUON_BETA * previous + gradient for previous, gradient in zip(moments, summed)]
    widths = [matrix.shape[1] for matrix in momenta]
    rows_here = D // data_size
    widen_whole, _, _ = staged_gather(momenta[2].astype(jnp.bfloat16), (Z_THEN_X,))
    narrow_whole, _, _ = staged_gather(momenta[3].astype(jnp.bfloat16), (Z_THEN_Y,))
    joint_moment = jnp.concatenate([momenta[0], momenta[1]], 1).astype(jnp.bfloat16)
    joint_moment, block_output, input_grad, vector_grad = lax.optimization_barrier(
        (joint_moment, block_output, input_grad, vector_grad)
    )
    joint_whole, _, _ = staged_gather(joint_moment, (X_FIRST,))
    wholes = [
        joint_whole[:, :attend_columns],
        joint_whole[:, attend_columns:],
        widen_whole,
        narrow_whole,
    ]

    def gram(matrix):
        return jnp.einsum("dk,ek->de", matrix, matrix, preferred_element_type=jnp.float32)

    parity = data_rank % 2
    even, low_core = parity == 0, tensor_rank == 0
    grams = [gram(matrix) for matrix in wholes]
    core_first = jnp.where(even, grams[2], grams[0])
    core_second = jnp.where(even, grams[3], grams[1])
    own_gram = jnp.where(low_core, core_first, core_second) + other_core(
        jnp.where(low_core, core_second, core_first)
    )
    pair_rows = newton_rows(own_gram, (data_rank - parity) * rows_here, 2 * rows_here)

    def rows_for(chip_parity):
        return lax.dynamic_slice_in_dim(pair_rows, chip_parity * rows_here, rows_here, 0)

    own_rows, near_rows = rows_for(parity), rows_for(1 - parity)
    devices = data_size * tensor_size

    def swapped(value, flip):
        pairs = [(index, index ^ flip) for index in range(devices)]
        return lax.ppermute(value, ("dp", "tensor"), pairs)

    core_rows, chip_rows, both_rows = (
        swapped(own_rows, 1),
        swapped(near_rows, tensor_size),
        swapped(near_rows, tensor_size + 1),
    )

    def pick(low, high):
        return jnp.where(low_core, low, high)

    here = (pick(own_rows, core_rows), pick(core_rows, own_rows))
    there = (pick(chip_rows, both_rows), pick(both_rows, chip_rows))
    ortho_rows = (
        jnp.where(even, there[0], here[0]),
        jnp.where(even, there[1], here[1]),
        jnp.where(even, here[0], there[0]),
        jnp.where(even, here[1], there[1]),
    )
    updated = []
    for matrix_index in range(4):
        longest = max(D, widths[matrix_index] * tensor_size)
        updated.append(
            masters[matrix_index] * (1.0 - MUON_RATE * MUON_DECAY)
            - MUON_RATE
            * math.sqrt(longest)
            * rows_product(ortho_rows[matrix_index], wholes[matrix_index])
        )
    first_new = BETA_ONE * vector_first + (1.0 - BETA_ONE) * vector_grad
    second_new = BETA_TWO * vector_second + (1.0 - BETA_TWO) * vector_grad * vector_grad
    first_hat = first_new / (1.0 - BETA_ONE**STEP)
    second_hat = second_new / (1.0 - BETA_TWO**STEP)
    vectors_new = vector_params - ADAM_RATE * first_hat / (jnp.sqrt(second_hat) + ADAM_EPS)
    return (
        block_output,
        input_grad,
        attend_sum,
        output_sum,
        widen_sum,
        narrow_sum,
        momenta[0],
        momenta[1],
        momenta[2],
        momenta[3],
        updated[0],
        updated[1],
        updated[2],
        updated[3],
        vector_grad,
        first_new,
        second_new,
        vectors_new,
    )


def solution(mesh):
    return jax.shard_map(
        shards,
        mesh=mesh,
        in_specs=(
            P("dp", None),
            P("dp", None),
            P("dp"),
            P("dp", "tensor"),
            P("dp", "tensor"),
            P("dp", "tensor"),
            P("dp", "tensor"),
            P("dp", "tensor"),
            P("dp", "tensor"),
            P("dp", "tensor"),
            P("dp", "tensor"),
            P(),
            P(),
            P(),
        ),
        out_specs=(
            P("dp", "tensor"),
            P("dp", None),
            P("dp", "tensor"),
            P("dp", "tensor"),
            P("dp", "tensor"),
            P("dp", "tensor"),
            P("dp", "tensor"),
            P("dp", "tensor"),
            P("dp", "tensor"),
            P("dp", "tensor"),
            P("dp", "tensor"),
            P("dp", "tensor"),
            P("dp", "tensor"),
            P("dp", "tensor"),
            P(),
            P(),
            P(),
            P(),
        ),
        check_vma=False,
    )
```

time: 685 us -> 468 us (0.68)
  matrix products: 261 us -> 115 us
  local copies, waits for them, and re-layouts: 124 us -> 21.2 us
  Pallas kernels: 0 us -> 39.5 us
  other arithmetic: 76.9 us -> 58.9 us
  waiting for transfers between devices: 170 us -> 181 us
  starting transfers between devices: 34.2 us -> 42.8 us
  loops' own time: 7.23 us -> 0 us
    dot_general x20 -> x6, matrix products: 93.5 us -> 13.4 us  [the longest x1 4.97 us: shards(): jnp.einsum('dk,sd->ks', attend_low, first_norm, preferred_element_type=jn...]
    dynamic_update_slice x81 -> x0, local copies, waits for them, and re-layouts: 64 us -> none  [staged_gather(): whole = lax.dynamic_update_slice(whole, held[slot:slot + 1], (source, 0, 0))]
    dot_general x34 -> x17, matrix products: 94 us -> 47.5 us  [product(): jnp.dot(left, right, precision=HIGH, preferred_element_type=jnp.float32)]
    pallas_call x0 -> x7, Pallas kernels: none -> 39.5 us  [the longest x1 24.9 us: attention(): pl.pallas_call(attention_kernel, grid=(heads,), in_specs=[own(3 * HEAD_DI...]
    ppermute x15, waiting for transfers between devices: 54.8 us -> 29.5 us  [staged_scatter(): got = lax.ppermute(total.astype(jnp.bfloat16), 'dp', perm)]
    ppermute x30 -> x43, waiting for transfers between devices: 101 us -> 118 us  [the longest x40 110 us: gather_stage(): moving = lax.ppermute(moving, 'dp', perm)]
    ppermute x4, waiting for transfers between devices: 13.9 us -> 29.4 us  [sum_everywhere(): value = value + lax.ppermute(value, 'dp', pairs)]
    unnamed x167 -> x144, local copies, waits for them, and re-layouts: 17.1 us -> 5.64 us
  transfers between devices with their start and end apart: 58 -> 68, of which waited for: 32 -> 38; matrix products, arithmetic and copies ran while one was open for 58% -> 27% of each run, Pallas kernels for 0% -> 8%
where the time goes in v2:
time: 468 us; the launch traced here: 463 us
  waiting for transfers between devices  181 us (39%)
  matrix products  115 us (25%)
  other arithmetic  58.9 us (13%)
  starting transfers between devices  42.8 us (9%)
  Pallas kernels  39.5 us (8%)
  local copies, waits for them, and re-layouts  21.2 us (5%)
    ppermute x40, waiting for transfers between devices, gather_stage(): moving = lax.ppermute(moving, 'dp', perm)  110 us
    dot_general x17, matrix products, product(): jnp.dot(left, right, precision=HIGH, preferred_element_type=jnp.float32)  47.5 us
    ppermute x15, waiting for transfers between devices, staged_scatter(): got = lax.ppermute(total.astype(jnp.bfloat16), 'dp', perm)  29.5 us
    ppermute x4, waiting for transfers between devices, sum_everywhere(): value = value + lax.ppermute(value, 'dp', pairs)  29.4 us
    ppermute x40, starting transfers between devices, gather_stage(): moving = lax.ppermute(moving, 'dp', perm)  25.9 us
    pallas_call x1, Pallas kernels, attention(): pl.pallas_call(attention_kernel, grid=(heads,), in_specs=[own(3 * HEAD_DI...  24.9 us
    dot_general x1, matrix products, shards(): jnp.dot(second_norm, widen_low, preferred_element_type=jnp.float32)  17.6 us
    reduce_sum x1, other arithmetic, shards(): widen_bias_grad = jnp.sum(widen_back.astype(jnp.float32), axis=0)  16 us
  transfers between devices with their start and end apart: 68, of which 38 were waited for; matrix products, arithmetic and copies ran while one was open for 27% of the time, Pallas kernels for 8%

profile of v2, /device:TPU:0, one launch (start us, length us, event | category | flops | bytes accessed | tf_op | source)
XLA Modules:
  0.0 462.5 jit_solution(2322453329575750537)
XLA Ops:
  2.7 3.0 collective-permute-start
  28.0 4.4 collective-permute-done.6
  35.5 3.1 collective-permute-done.7
  42.5 3.7 collective-permute-done.11
  47.8 4.9 %collective-permute-done.12 = bf16[1,48,768]{2,1,0:T(8,128)(2,1)S(1)} collective-permute-done((bf16[1,48,768]{2,1,0:T(8,128)(2,1)S(1)}, bf16[1,48,768]{2,1,0:T(8,128)(2,1)S(1)}, u32[]{:S(2)}, u32[]{:S(2)}) %collective-permute-start.12) | collective-permute-done | bytes 73760 | tf_op jit(solution)/shard_map/ppermute | solution.py:103
  54.8 4.9 %collective-permute-done.13 = bf16[1,48,768]{2,1,0:T(8,128)(2,1)S(1)} collective-permute-done((bf16[1,48,768]{2,1,0:T(8,128)(2,1)S(1)}, bf16[1,48,768]{2,1,0:T(8,128)(2,1)S(1)}, u32[]{:S(2)}, u32[]{:S(2)}) %collective-permute-start.13) | collective-permute-done | bytes 73760 | tf_op jit(solution)/shard_map/ppermute | solution.py:103
  66.2 3.9 collective-permute-done.17
  71.7 11.4 %collective-permute-done.19 = bf16[4,48,768]{2,1,0:T(8,128)(2,1)S(1)} collective-permute-done((bf16[4,48,768]{2,1,0:T(8,128)(2,1)S(1)}, bf16[4,48,768]{2,1,0:T(8,128)(2,1)S(1)}, u32[]{:S(2)}, u32[]{:S(2)}) %collective-permute-start.19) | collective-permute-done | bytes 294944 | tf_op jit(solution)/shard_map/ppermute | solution.py:103
  86.2 17.6 %fusion.2 = (bf16[1024,1536]{1,0:T(8,128)(2,1)}, f32[1024,1536]{1,0:T(8,128)}) fusion(f32[1536]{0:T(1024)S(1)} %dynamic_slice.121, bf16[768,1536]{1,0:T(8,128)(2,1)S(1)} %bitcast.94, f32[768]{0:T(1024)S(1)} %copy-done.51, f32[768]{0:T(1024)S(1)} %get-tuple-element.148, f32[1024]{0:T(1024)S(1)} %add_rsqrt_fusion, f32[1024]{0:T(1024)S(1)} %broadcast_multiply_fusion.1, ...), kind=kOutput, calls=%fused_computation.4 | convolution fusion | flops 2524446720 | bytes 13389824 | tf_op jit(solution)/shard_map/dot_general | solution.py:384
  105.0 4.2 fusion.179
  109.3 16.0 %convert_reduce_fusion = (f32[1536]{0:T(1024)}, bf16[1024,1536]{1,0:T(8,128)(2,1)S(1)}) fusion(f32[1024,1536]{1,0:T(8,128)S(1)} %fusion.179, f32[1024,1536]{1,0:T(8,128)S(1)} %bitcast.108), kind=kLoop, calls=%fused_computation.10 | loop fusion | flops 116390400 | bytes 15734784 | tf_op jit(solution)/shard_map/reduce_sum | solution.py:406
  125.3 2.6 fusion.185
  133.3 7.6 %fusion.114 = f32[768,1536]{1,0:T(8,128)} fusion(bf16[1024,1536]{1,0:T(8,128)(2,1)} %copy-done.18, f32[768]{0:T(1024)} %get-tuple-element.147, f32[768]{0:T(1024)S(1)} %get-tuple-element.148, bf16[1024,768]{1,0:T(8,128)(2,1)} %param.14, f32[1024]{0:T(1024)} %copy-done.43, f32[1024]{0:T(1024)} %copy-done.40), kind=kOutput, calls=%fused_computation.178 | convolution fusion | flops 2420637696 | bytes 9451520 | tf_op jit(solution)/shard_map/sd,sf->df/dot_general | solution.py:403
  141.3 4.5 fusion.177
  145.9 13.2 %collective-permute-done.4.refs_3_ = bf16[4,48,1536]{2,1,0:T(8,128)(2,1)S(1)} collective-permute-done((bf16[4,48,1536]{2,1,0:T(8,128)(2,1)}, bf16[4,48,1536]{2,1,0:T(8,128)(2,1)S(1)}, u32[]{:S(2)}, u32[]{:S(2)}) %collective-permute-start.4) | collective-permute-done | bytes 589856 | tf_op jit(solution)/shard_map/ppermute | solution.py:103
  159.1 2.8 shard_map.279
  163.3 5.0 %convolution_add_fusion.triple_ref = f32[1152,1024]{1,0:T(8,128)} fusion(f32[1152]{0:T(1024)S(1)} %copy-done.48, bf16[768,1536]{1,0:T(8,128)(2,1)S(1)} %bitcast.89, f32[768]{0:T(1024)S(1)} %copy-done.50, f32[768]{0:T(1024)S(1)} %get-tuple-element.146, bf16[1024,768]{1,0:T(8,128)(2,1)S(1)} %copy-done.9, f32[1024]{0:T(1024)S(1)} %copy-done.44, ...), kind=kOutput, calls=%fused_computation.47 | convolution fusion | flops 1817837568 | bytes 8085504 | tf_op jit(solution)/shard_map/dk,sd->ks/dot_general | solution.py:415
  168.3 24.9 %shard_map.280 = (bf16[384,1024]{1,0:T(8,128)(2,1)S(1)}, bf16[1152,1024]{1,0:T(8,128)(2,1)S(1)}) custom-call(f32[1152,1024]{1,0:T(8,128)} %convolution_add_fusion.triple_ref, f32[8,1024]{1,0:T(8,128)S(1)} %copy-done.7, f32[8,1024]{1,0:T(8,128)S(1)} %copy-done.6, bf16[384,1024]{1,0:T(8,128)(2,1)S(1)} %convolution_convert_fusion.upstream_ref, ...), custom_call_target="tpu_custom_call" | custom-call | flops 14495514624 | bytes 9437184 | tf_op jit(solution)/shard_map/pallas_call | solution.py:321
  195.5 2.8 fusion.113
  198.3 2.3 fusion.58
  202.6 2.2 copy-done.22
  204.8 2.6 convolution_add_fusion.5
  212.4 5.2 %multiply_reduce_fusion.1 = (f32[768]{0:T(1024)S(1)}, f32[512]{0:T(512)S(1)}, f32[512]{0:T(512)S(1)}, f32[768]{0:T(1024)S(1)}, f32[512]{0:T(512)S(1)}, /*index=5...) fusion(f32[1024,768]{1,0:T(8,128)} %subtract_multiply_fusion, ...), kind=kLoop, calls=%fused_computation.94 | loop fusion | flops 7072768 | bytes 9463812 | tf_op jit(solution)/shard_map/reduce_sum | solution.py:485
  224.9 16.1 %collective-permute-done.35 = f32[13,768]{1,0:T(8,128)S(1)} collective-permute-done((f32[13,768]{1,0:T(8,128)S(1)}, f32[13,768]{1,0:T(8,128)S(1)}, u32[]{:S(2)}, u32[]{:S(2)}) %collective-permute-start.35) | collective-permute-done | bytes 39968 | tf_op jit(solution)/shard_map/ppermute | solution.py:172
  242.5 6.8 %collective-permute-done.36 = f32[13,768]{1,0:T(8,128)S(1)} collective-permute-done((f32[13,768]{1,0:T(8,128)S(1)}, f32[13,768]{1,0:T(8,128)S(1)}, u32[]{:S(2)}, u32[]{:S(2)}) %collective-permute-start.36) | collective-permute-done | bytes 39968 | tf_op jit(solution)/shard_map/ppermute | solution.py:172
  249.4 4.1 collective-permute-done.37
  253.8 2.2 fusion.57
  256.0 2.5 collective-permute-done.38
  259.4 2.5 convert_add_fusion.1
  267.8 2.7 multiply_convert_fusion
  270.4 6.4 %collective-permute-done.27 = bf16[1,2,2,48,1536]{4,3,2,1,0:T(8,128)(2,1)S(1)} collective-permute-done((bf16[1,2,2,48,1536]{4,3,2,1,0:T(8,128)(2,1)S(1)}, bf16[1,2,2,48,1536]{4,3,2,1,0:T(8,128)(2,1)S(1)}, u32[]{:S(2)}, u32[]{:S(2)}) %collective-permute-start.27) | collective-permute-done | bytes 589856 | tf_op jit(solution)/shard_map/ppermute | solution.py:156
  281.4 6.1 %collective-permute-done.41 = bf16[1,1,1,48,1536]{4,3,2,1,0:T(8,128)(2,1)S(1)} collective-permute-done((bf16[1,1,1,48,1536]{4,3,2,1,0:T(8,128)(2,1)S(1)}, bf16[1,1,1,48,1536]{4,3,2,1,0:T(8,128)(2,1)S(1)}, u32[]{:S(2)}, u32[]{:S(2)}) %collective-permute-start.41) | collective-permute-done | bytes 147488 | tf_op jit(solution)/shard_map/ppermute | solution.py:156
  289.5 5.9 %collective-permute-done.42 = bf16[1,1,1,48,1536]{4,3,2,1,0:T(8,128)(2,1)S(1)} collective-permute-done((bf16[1,1,1,48,1536]{4,3,2,1,0:T(8,128)(2,1)S(1)}, bf16[1,1,1,48,1536]{4,3,2,1,0:T(8,128)(2,1)S(1)}, u32[]{:S(2)}, u32[]{:S(2)}) %collective-permute-start.42) | collective-permute-done | bytes 147488 | tf_op jit(solution)/shard_map/ppermute | solution.py:156
  295.5 2.8 collective-permute-done.47
  300.2 2.3 collective-permute-done.43
  303.4 3.6 collective-permute-done.48
  311.0 4.7 %collective-permute-done.59 = bf16[1,48,1536]{2,1,0:T(8,128)(2,1)S(1)} collective-permute-done((bf16[1,48,1536]{2,1,0:T(8,128)(2,1)S(1)}, bf16[1,48,1536]{2,1,0:T(8,128)(2,1)S(1)}, u32[]{:S(2)}, u32[]{:S(2)}) %collective-permute-start.59) | collective-permute-done | bytes 147488 | tf_op jit(solution)/shard_map/ppermute | solution.py:103
  316.7 2.5 collective-permute-done.50
  319.2 3.4 collective-permute-done.60
  322.7 3.5 collective-permute-done.51
  326.4 4.8 %collective-permute-done.61 = bf16[1,48,1536]{2,1,0:T(8,128)(2,1)S(1)} collective-permute-done((bf16[1,48,1536]{2,1,0:T(8,128)(2,1)S(1)}, bf16[1,48,1536]{2,1,0:T(8,128)(2,1)S(1)}, u32[]{:S(2)}, u32[]{:S(2)}) %collective-permute-start.61) | collective-permute-done | bytes 147488 | tf_op jit(solution)/shard_map/ppermute | solution.py:103
  332.5 7.1 %collective-permute-done.52 = bf16[4,48,1536]{2,1,0:T(8,128)(2,1)S(1)} collective-permute-done((bf16[4,48,1536]{2,1,0:T(8,128)(2,1)S(1)}, bf16[4,48,1536]{2,1,0:T(8,128)(2,1)S(1)}, u32[]{:S(2)}, u32[]{:S(2)}) %collective-permute-start.52) | collective-permute-done | bytes 589856 | tf_op jit(solution)/shard_map/ppermute | solution.py:103
  340.2 7.4 %collective-permute-done.62 = bf16[4,48,1536]{2,1,0:T(8,128)(2,1)S(1)} collective-permute-done((bf16[4,48,1536]{2,1,0:T(8,128)(2,1)S(1)}, bf16[4,48,1536]{2,1,0:T(8,128)(2,1)S(1)}, u32[]{:S(2)}, u32[]{:S(2)}) %collective-permute-start.62) | collective-permute-done | bytes 589856 | tf_op jit(solution)/shard_map/ppermute | solution.py:103
  349.5 18.3 %collective-permute-done.57.refs_2_ = bf16[4,48,1536]{2,1,0:T(8,128)(2,1)} collective-permute-done((bf16[4,48,1536]{2,1,0:T(8,128)(2,1)}, bf16[4,48,1536]{2,1,0:T(8,128)(2,1)}, u32[]{:S(2)}, u32[]{:S(2)}) %collective-permute-start.57) | collective-permute-done | bytes 589856 | tf_op jit(solution)/shard_map/ppermute | solution.py:103
  367.8 3.9 shard_map.281
  373.7 3.4 shard_map.283
  379.6 2.2 shard_map.282
  383.7 3.0 broadcast_select_fusion
  386.6 4.9 %collective-permute-done.64 = f32[768,768]{1,0:T(8,128)} collective-permute-done((f32[768,768]{1,0:T(8,128)}, f32[768,768]{1,0:T(8,128)}, u32[]{:S(2)}, u32[]{:S(2)}) %collective-permute-start.64) | collective-permute-done | bytes 2359328 | tf_op jit(solution)/shard_map/ppermute | solution.py:163
  391.5 4.8 %select_reduce_fusion = (f32[]{:T(128)}, f32[768,768]{1,0:T(8,128)}) fusion(f32[768,768]{1,0:T(8,128)} %collective-permute-done.64, f32[768,768]{1,0:T(8,128)} %copy-done.13, f32[768,768]{1,0:T(8,128)} %get-tuple-element.198, pred[]{:T(512)S(6)} %eq.66), kind=kLoop, calls=%fused_computation.58 | loop fusion | flops 2949119 | bytes 9437189 | tf_op jit(solution)/shard_map/jit(trace)/reduce_sum | solution.py:182
  397.0 6.5 %fusion.22 = f32[768,768]{1,0:T(8,128)S(1)} fusion(f32[768,768]{1,0:T(8,128)} %get-tuple-element.154, f32[]{:T(128)S(6)} %mul.405), kind=kOutput, calls=%fused_computation.54 | convolution fusion | flops 2722627584 | bytes 4718596 | tf_op jit(solution)/shard_map/dot_general | solution.py:178
  403.6 3.1 fusion.32
  406.7 3.2 fusion.188
  409.8 3.3 fusion.189
  413.2 3.3 fusion.52
  417.6 3.2 fusion.50
  420.8 3.4 fusion.190
  424.2 3.3 fusion.46
  428.6 3.2 fusion.44
  431.8 3.1 fusion.191
  434.9 3.6 fusion.40
  439.6 3.2 fusion.38
  447.7 3.6 collective-permute-done.66
  451.4 3.6 collective-permute-done.65
  (375 shorter events, 118.4 us)
Async XLA Ops:
  2.7 25.3 %collective-permute-start = (bf16[1,48,1536]{2,1,0:T(8,128)(2,1)S(1)}, bf16[1,48,1536]{2,1,0:T(8,128)(2,1)S(1)}, u32[]{:S(2)}, u32[]{:S(2)}) collective-permute-start(bf16[1,48,1536]{2,1,0:T(8,128)(2,1)S(1)} %pad_maximum_fusion.9), channel_id=1, source_target_pairs={{0,2},{2,0},{4,6},{6,4},{8,10},{10,8},{12,14},{14,12},{16,18},{18,... | collective-permute-start | bytes 442376 | tf_op jit(solution)/shard_map/ppermute | solution.py:103
  6.7 19.5 %collective-permute-start.5 = (bf16[1,48,768]{2,1,0:T(8,128)(2,1)S(1)}, bf16[1,48,768]{2,1,0:T(8,128)(2,1)S(1)}, u32[]{:S(2)}, u32[]{:S(2)}) collective-permute-start(bf16[1,48,768]{2,1,0:T(8,128)(2,1)S(1)} %get-tuple-element.88), channel_id=1, source_target_pairs={{0,8},{2,10},{4,12},{6,14},{8,16},{10,18},{12,20},{14,22},{16,24},... | collective-permute-start | bytes 221192 | tf_op jit(solution)/shard_map/ppermute | solution.py:103
  8.3 19.4 %collective-permute-start.8 = (bf16[1,48,768]{2,1,0:T(8,128)(2,1)S(1)}, bf16[1,48,768]{2,1,0:T(8,128)(2,1)S(1)}, u32[]{:S(2)}, u32[]{:S(2)}) collective-permute-start(bf16[1,48,768]{2,1,0:T(8,128)(2,1)S(1)} %get-tuple-element.92), channel_id=1, source_target_pairs={{0,8},{2,10},{4,12},{6,14},{8,16},{10,18},{12,20},{14,22},{16,24},... | collective-permute-start | bytes 221192 | tf_op jit(solution)/shard_map/ppermute | solution.py:103
  26.2 6.3 %collective-permute-start.6 = (bf16[1,48,768]{2,1,0:T(8,128)(2,1)S(1)}, bf16[1,48,768]{2,1,0:T(8,128)(2,1)S(1)}, u32[]{:S(2)}, u32[]{:S(2)}) collective-permute-start(bf16[1,48,768]{2,1,0:T(8,128)(2,1)S(1)} %collective-permute-done.5), channel_id=1, source_target_pairs={{0,8},{2,10},{4,12},{6,14},{8,16},{10,18},{12,20},{14,22},{16,24},... | collective-permute-start | bytes 221192 | tf_op jit(solution)/shard_map/ppermute | solution.py:103
  27.7 6.2 %collective-permute-start.9 = (bf16[1,48,768]{2,1,0:T(8,128)(2,1)S(1)}, bf16[1,48,768]{2,1,0:T(8,128)(2,1)S(1)}, u32[]{:S(2)}, u32[]{:S(2)}) collective-permute-start(bf16[1,48,768]{2,1,0:T(8,128)(2,1)S(1)} %collective-permute-done.8), channel_id=1, source_target_pairs={{0,8},{2,10},{4,12},{6,14},{8,16},{10,18},{12,20},{14,22},{16,24},... | collective-permute-start | bytes 221192 | tf_op jit(solution)/shard_map/ppermute | solution.py:103
  32.4 6.2 %collective-permute-start.7 = (bf16[1,48,768]{2,1,0:T(8,128)(2,1)S(1)}, bf16[1,48,768]{2,1,0:T(8,128)(2,1)S(1)}, u32[]{:S(2)}, u32[]{:S(2)}) collective-permute-start(bf16[1,48,768]{2,1,0:T(8,128)(2,1)S(1)} %collective-permute-done.6), channel_id=1, source_target_pairs={{0,8},{2,10},{4,12},{6,14},{8,16},{10,18},{12,20},{14,22},{16,24},... | collective-permute-start | bytes 221192 | tf_op jit(solution)/shard_map/ppermute | solution.py:103
  33.9 6.2 %collective-permute-start.10 = (bf16[1,48,768]{2,1,0:T(8,128)(2,1)S(1)}, bf16[1,48,768]{2,1,0:T(8,128)(2,1)S(1)}, u32[]{:S(2)}, u32[]{:S(2)}) collective-permute-start(bf16[1,48,768]{2,1,0:T(8,128)(2,1)S(1)} %collective-permute-done.9), channel_id=1, source_target_pairs={{0,8},{2,10},{4,12},{6,14},{8,16},{10,18},{12,20},{14,22},{16,24},... | collective-permute-start | bytes 221192 | tf_op jit(solution)/shard_map/ppermute | solution.py:103
  33.9 20.8 %collective-permute-start.1 = (bf16[2,48,1536]{2,1,0:T(8,128)(2,1)S(1)}, bf16[2,48,1536]{2,1,0:T(8,128)(2,1)S(1)}, u32[]{:S(2)}, u32[]{:S(2)}) collective-permute-start(bf16[2,48,1536]{2,1,0:T(8,128)(2,1)S(1)} %pad_maximum_fusion.3), channel_id=1, source_target_pairs={{0,4},{2,6},{4,0},{6,2},{8,12},{10,14},{12,8},{14,10},{16,20},{18,... | collective-permute-start | bytes 884744 | tf_op jit(solution)/shard_map/ppermute | solution.py:103
  40.1 6.2 %collective-permute-start.11 = (bf16[1,48,768]{2,1,0:T(8,128)(2,1)S(1)}, bf16[1,48,768]{2,1,0:T(8,128)(2,1)S(1)}, u32[]{:S(2)}, u32[]{:S(2)}) collective-permute-start(bf16[1,48,768]{2,1,0:T(8,128)(2,1)S(1)} %get-tuple-element.80), channel_id=1, source_target_pairs={{0,8},{2,10},{4,12},{6,14},{8,16},{10,18},{12,20},{14,22},{16,24},... | collective-permute-start | bytes 221192 | tf_op jit(solution)/shard_map/ppermute | solution.py:103
  40.1 7.6 %collective-permute-start.14 = (bf16[1,48,768]{2,1,0:T(8,128)(2,1)S(1)}, bf16[1,48,768]{2,1,0:T(8,128)(2,1)S(1)}, u32[]{:S(2)}, u32[]{:S(2)}) collective-permute-start(bf16[1,48,768]{2,1,0:T(8,128)(2,1)S(1)} %get-tuple-element.84), channel_id=1, source_target_pairs={{0,8},{2,10},{4,12},{6,14},{8,16},{10,18},{12,20},{14,22},{16,24},... | collective-permute-start | bytes 221192 | tf_op jit(solution)/shard_map/ppermute | solution.py:103
  40.3 22.1 %collective-permute-start.21 = (bf16[4,48,768]{2,1,0:T(8,128)(2,1)S(1)}, bf16[4,48,768]{2,1,0:T(8,128)(2,1)S(1)}, u32[]{:S(2)}, u32[]{:S(2)}) collective-permute-start(bf16[4,48,768]{2,1,0:T(8,128)(2,1)S(1)} %pad_maximum_fusion.6), channel_id=1, source_target_pairs={{0,2},{2,0},{4,6},{6,4},{8,10},{10,8},{12,14},{14,12},{16,18},{18,... | collective-permute-start | bytes 884744 | tf_op jit(solution)/shard_map/ppermute | solution.py:103
  40.9 23.0 %collective-permute-start.23 = (bf16[4,48,768]{2,1,0:T(8,128)(2,1)S(1)}, bf16[4,48,768]{2,1,0:T(8,128)(2,1)S(1)}, u32[]{:S(2)}, u32[]{:S(2)}) collective-permute-start(bf16[4,48,768]{2,1,0:T(8,128)(2,1)S(1)} %pad_maximum_fusion.7), channel_id=1, source_target_pairs={{0,4},{2,6},{4,0},{6,2},{8,12},{10,14},{12,8},{14,10},{16,20},{18,... | collective-permute-start | bytes 884744 | tf_op jit(solution)/shard_map/ppermute | solution.py:103
  46.3 6.4 %collective-permute-start.12 = (bf16[1,48,768]{2,1,0:T(8,128)(2,1)S(1)}, bf16[1,48,768]{2,1,0:T(8,128)(2,1)S(1)}, u32[]{:S(2)}, u32[]{:S(2)}) collective-permute-start(bf16[1,48,768]{2,1,0:T(8,128)(2,1)S(1)} %collective-permute-done.11), channel_id=1, source_target_pairs={{0,8},{2,10},{4,12},{6,14},{8,16},{10,18},{12,20},{14,22},{16,24},... | collective-permute-start | bytes 221192 | tf_op jit(solution)/shard_map/ppermute | solution.py:103
  47.7 6.9 %collective-permute-start.15 = (bf16[1,48,768]{2,1,0:T(8,128)(2,1)S(1)}, bf16[1,48,768]{2,1,0:T(8,128)(2,1)S(1)}, u32[]{:S(2)}, u32[]{:S(2)}) collective-permute-start(bf16[1,48,768]{2,1,0:T(8,128)(2,1)S(1)} %collective-permute-done.14), channel_id=1, source_target_pairs={{0,8},{2,10},{4,12},{6,14},{8,16},{10,18},{12,20},{14,22},{16,24},... | collective-permute-start | bytes 221192 | tf_op jit(solution)/shard_map/ppermute | solution.py:103
  52.6 7.0 %collective-permute-start.13 = (bf16[1,48,768]{2,1,0:T(8,128)(2,1)S(1)}, bf16[1,48,768]{2,1,0:T(8,128)(2,1)S(1)}, u32[]{:S(2)}, u32[]{:S(2)}) collective-permute-start(bf16[1,48,768]{2,1,0:T(8,128)(2,1)S(1)} %collective-permute-done.12), channel_id=1, source_target_pairs={{0,8},{2,10},{4,12},{6,14},{8,16},{10,18},{12,20},{14,22},{16,24},... | collective-permute-start | bytes 221192 | tf_op jit(solution)/shard_map/ppermute | solution.py:103
  54.7 7.0 %collective-permute-start.16 = (bf16[1,48,768]{2,1,0:T(8,128)(2,1)S(1)}, bf16[1,48,768]{2,1,0:T(8,128)(2,1)S(1)}, u32[]{:S(2)}, u32[]{:S(2)}) collective-permute-start(bf16[1,48,768]{2,1,0:T(8,128)(2,1)S(1)} %collective-permute-done.15), channel_id=1, source_target_pairs={{0,8},{2,10},{4,12},{6,14},{8,16},{10,18},{12,20},{14,22},{16,24},... | collective-permute-start | bytes 221192 | tf_op jit(solution)/shard_map/ppermute | solution.py:103
  54.7 30.1 %collective-permute-start.2 = (bf16[4,48,1536]{2,1,0:T(8,128)(2,1)S(1)}, bf16[4,48,1536]{2,1,0:T(8,128)(2,1)S(1)}, u32[]{:S(2)}, u32[]{:S(2)}) collective-permute-start(bf16[4,48,1536]{2,1,0:T(8,128)(2,1)S(1)} %constant_dynamic-update-slice_fusion.refs_0_), channel_id=1, source_target_pairs={{0,8},{2,10},{4,12},{6,14},{8,16},{10,18},{12,20},{14,22},{16,24},... | collective-permute-start | bytes 1769480 | tf_op jit(solution)/shard_map/ppermute | solution.py:103
  61.7 8.4 %collective-permute-start.17 = (bf16[4,48,768]{2,1,0:T(8,128)(2,1)S(1)}, bf16[4,48,768]{2,1,0:T(8,128)(2,1)S(1)}, u32[]{:S(2)}, u32[]{:S(2)}) collective-permute-start(bf16[4,48,768]{2,1,0:T(8,128)(2,1)S(1)} %pad_maximum_fusion.4), channel_id=1, source_target_pairs={{0,2},{2,0},{4,6},{6,4},{8,10},{10,8},{12,14},{14,12},{16,18},{18,... | collective-permute-start | bytes 884744 | tf_op jit(solution)/shard_map/ppermute | solution.py:103
  62.4 22.6 %collective-permute-start.22 = (bf16[8,48,768]{2,1,0:T(8,128)(2,1)S(1)}, bf16[8,48,768]{2,1,0:T(8,128)(2,1)S(1)}, u32[]{:S(2)}, u32[]{:S(2)}) collective-permute-start(bf16[8,48,768]{2,1,0:T(8,128)(2,1)S(1)} %constant_dynamic-update-slice_fusion.13.refs_0_), channel_id=1, source_target_pairs={{0,4},{2,6},{4,0},{6,2},{8,12},{10,14},{12,8},{14,10},{16,20},{18,... | collective-permute-start | bytes 1769480 | tf_op jit(solution)/shard_map/ppermute | solution.py:103
  64.0 21.0 %collective-permute-start.24 = (bf16[8,48,768]{2,1,0:T(8,128)(2,1)S(1)}, bf16[8,48,768]{2,1,0:T(8,128)(2,1)S(1)}, u32[]{:S(2)}, u32[]{:S(2)}) collective-permute-start(bf16[8,48,768]{2,1,0:T(8,128)(2,1)S(1)} %constant_dynamic-update-slice_fusion.18.refs_2_), channel_id=1, source_target_pairs={{0,2},{2,0},{4,6},{6,4},{8,10},{10,8},{12,14},{14,12},{16,18},{18,... | collective-permute-start | bytes 1769480 | tf_op jit(solution)/shard_map/ppermute | solution.py:103
  65.6 17.6 %collective-permute-start.19 = (bf16[4,48,768]{2,1,0:T(8,128)(2,1)S(1)}, bf16[4,48,768]{2,1,0:T(8,128)(2,1)S(1)}, u32[]{:S(2)}, u32[]{:S(2)}) collective-permute-start(bf16[4,48,768]{2,1,0:T(8,128)(2,1)S(1)} %pad_maximum_fusion.5), channel_id=1, source_target_pairs={{0,4},{2,6},{4,0},{6,2},{8,12},{10,14},{12,8},{14,10},{16,20},{18,... | collective-permute-start | bytes 884744 | tf_op jit(solution)/shard_map/ppermute | solution.py:103
  70.2 33.7 %collective-permute-start.18 = (bf16[8,48,768]{2,1,0:T(8,128)(2,1)S(1)}, bf16[8,48,768]{2,1,0:T(8,128)(2,1)S(1)}, u32[]{:S(2)}, u32[]{:S(2)}) collective-permute-start(bf16[8,48,768]{2,1,0:T(8,128)(2,1)S(1)} %constant_dynamic-update-slice_fusion.3.refs_0_), channel_id=1, source_target_pairs={{0,4},{2,6},{4,0},{6,2},{8,12},{10,14},{12,8},{14,10},{16,20},{18,... | collective-permute-start | bytes 1769480 | tf_op jit(solution)/shard_map/ppermute | solution.py:103
  83.2 20.6 %collective-permute-start.20 = (bf16[8,48,768]{2,1,0:T(8,128)(2,1)S(1)}, bf16[8,48,768]{2,1,0:T(8,128)(2,1)S(1)}, u32[]{:S(2)}, u32[]{:S(2)}) collective-permute-start(bf16[8,48,768]{2,1,0:T(8,128)(2,1)S(1)} %constant_dynamic-update-slice_fusion.8.refs_2_), channel_id=1, source_target_pairs={{0,2},{2,0},{4,6},{6,4},{8,10},{10,8},{12,14},{14,12},{16,18},{18,... | collective-permute-start | bytes 1769480 | tf_op jit(solution)/shard_map/ppermute | solution.py:103
  84.8 56.2 %collective-permute-start.3 = (bf16[4,48,1536]{2,1,0:T(8,128)(2,1)S(1)}, bf16[4,48,1536]{2,1,0:T(8,128)(2,1)}, u32[]{:S(2)}, u32[]{:S(2)}) collective-permute-start(bf16[4,48,1536]{2,1,0:T(8,128)(2,1)S(1)} %collective-permute-done.2.refs_1_), channel_id=1, source_target_pairs={{0,8},{2,10},{4,12},{6,14},{8,16},{10,18},{12,20},{14,22},{16,24},... | collective-permute-start | bytes 1769480 | tf_op jit(solution)/shard_map/ppermute | solution.py:103
  129.9 82.5 %collective-permute-start.32 = (bf16[512,768]{1,0:T(8,128)(2,1)}, bf16[512,768]{1,0:T(8,128)(2,1)}, u32[]{:S(2)}, u32[]{:S(2)}) collective-permute-start(bf16[512,768]{1,0:T(8,128)(2,1)} %dynamic-slice_convert_fusion.2), channel_id=1, source_target_pairs={{0,1},{1,0},{2,3},{3,2},{4,5},{5,4},{6,7},{7,6},{8,9},{9,8},{10,11... | collective-permute-start | bytes 2359304 | tf_op jit(solution)/shard_map/ppermute | solution.py:163
  140.9 18.2 %collective-permute-start.4 = (bf16[4,48,1536]{2,1,0:T(8,128)(2,1)}, bf16[4,48,1536]{2,1,0:T(8,128)(2,1)S(1)}, u32[]{:S(2)}, u32[]{:S(2)}) collective-permute-start(bf16[4,48,1536]{2,1,0:T(8,128)(2,1)} %collective-permute-done.3.refs_2_), channel_id=1, source_target_pairs={{0,8},{2,10},{4,12},{6,14},{8,16},{10,18},{12,20},{14,22},{16,24},... | collective-permute-start | bytes 1769480 | tf_op jit(solution)/shard_map/ppermute | solution.py:103
  202.1 20.9 %collective-permute-start.25 = (bf16[1,2,2,48,1536]{4,3,2,1,0:T(8,128)(2,1)}, bf16[1,2,2,48,1536]{4,3,2,1,0:T(8,128)(2,1)}, u32[]{:S(2)}, u32[]{:S(2)}) collective-permute-start(bf16[1,2,2,48,1536]{4,3,2,1,0:T(8,128)(2,1)} %dynamic-slice_convert_fusion.6), channel_id=1, source_target_pairs={{0,8},{2,10},{4,12},{6,14},{8,16},{10,18},{12,20},{14,22},{16,24},... | collective-permute-start | bytes 1769480 | tf_op jit(solution)/shard_map/ppermute | solution.py:156
  202.5 9.9 %collective-permute-start.31 = (bf16[512,768]{1,0:T(8,128)(2,1)S(1)}, bf16[512,768]{1,0:T(8,128)(2,1)}, u32[]{:S(2)}, u32[]{:S(2)}) collective-permute-start(bf16[512,768]{1,0:T(8,128)(2,1)S(1)} %dynamic-slice_convert_fusion.3), channel_id=1, source_target_pairs={{0,1},{1,0},{2,3},{3,2},{4,5},{5,4},{6,7},{7,6},{8,9},{9,8},{10,11... | collective-permute-start | bytes 2359304 | tf_op jit(solution)/shard_map/ppermute | solution.py:163
  208.9 58.8 %collective-permute-start.30 = (f32[1024,384]{1,0:T(8,128)}, f32[1024,384]{1,0:T(8,128)}, u32[]{:S(2)}, u32[]{:S(2)}) collective-permute-start(f32[1024,384]{1,0:T(8,128)} %constant_dynamic-slice_fusion.3), channel_id=1, source_target_pairs={{0,1},{1,0},{2,3},{3,2},{4,5},{5,4},{6,7},{7,6},{8,9},{9,8},{10,11... | collective-permute-start | bytes 4718600 | tf_op jit(solution)/shard_map/ppermute | solution.py:163
  211.8 47.6 %collective-permute-start.39 = (bf16[4,2,1,48,1536]{4,3,2,1,0:T(8,128)(2,1)S(1)}, bf16[4,2,1,48,1536]{4,3,2,1,0:T(8,128)(2,1)}, u32[]{:S(2)}, u32[]{:S(2)}) collective-permute-start(bf16[4,2,1,48,1536]{4,3,2,1,0:T(8,128)(2,1)S(1)} %dynamic-slice_convert_fusion.1), channel_id=1, source_target_pairs={{0,2},{2,0},{4,6},{6,4},{8,10},{10,8},{12,14},{14,12},{16,18},{18,... | collective-permute-start | bytes 3538952 | tf_op jit(solution)/shard_map/ppermute | solution.py:156
  219.9 43.7 %collective-permute-start.44 = (bf16[4,1,2,48,1536]{4,3,2,1,0:T(8,128)(2,1)S(1)}, bf16[4,1,2,48,1536]{4,3,2,1,0:T(8,128)(2,1)S(1)}, u32[]{:S(2)}, u32[]{:S(2)}) collective-permute-start(bf16[4,1,2,48,1536]{4,3,2,1,0:T(8,128)(2,1)S(1)} %dynamic-slice_convert_fusion), channel_id=1, source_target_pairs={{0,4},{2,6},{4,0},{6,2},{8,12},{10,14},{12,8},{14,10},{16,20},{18,... | collective-permute-start | bytes 3538952 | tf_op jit(solution)/shard_map/ppermute | solution.py:156
  221.5 19.5 %collective-permute-start.35 = (f32[13,768]{1,0:T(8,128)S(1)}, f32[13,768]{1,0:T(8,128)S(1)}, u32[]{:S(2)}, u32[]{:S(2)}) collective-permute-start(f32[13,768]{1,0:T(8,128)S(1)} %add.467), channel_id=1, source_target_pairs={{0,2},{2,0},{4,6},{6,4},{8,10},{10,8},{12,14},{14,12},{16,18},{18,... | collective-permute-start | bytes 119816 | tf_op jit(solution)/shard_map/ppermute | solution.py:172
  224.6 34.6 %collective-permute-start.26 = (bf16[1,2,2,48,1536]{4,3,2,1,0:T(8,128)(2,1)S(1)}, bf16[1,2,2,48,1536]{4,3,2,1,0:T(8,128)(2,1)S(1)}, u32[]{:S(2)}, u32[]{:S(2)}) collective-permute-start(bf16[1,2,2,48,1536]{4,3,2,1,0:T(8,128)(2,1)S(1)} %add_convert_fusion.3), channel_id=1, source_target_pairs={{0,8},{2,10},{4,12},{6,14},{8,16},{10,18},{12,20},{14,22},{16,24},... | collective-permute-start | bytes 1769480 | tf_op jit(solution)/shard_map/ppermute | solution.py:156
  241.0 8.4 %collective-permute-start.36 = (f32[13,768]{1,0:T(8,128)S(1)}, f32[13,768]{1,0:T(8,128)S(1)}, u32[]{:S(2)}, u32[]{:S(2)}) collective-permute-start(f32[13,768]{1,0:T(8,128)S(1)} %add.468), channel_id=1, source_target_pairs={{0,4},{2,6},{4,0},{6,2},{8,12},{10,14},{12,8},{14,10},{16,20},{18,... | collective-permute-start | bytes 119816 | tf_op jit(solution)/shard_map/ppermute | solution.py:172
  253.5 5.0 %collective-permute-start.38 = (f32[13,768]{1,0:T(8,128)S(1)}, f32[13,768]{1,0:T(8,128)S(1)}, u32[]{:S(2)}, u32[]{:S(2)}) collective-permute-start(f32[13,768]{1,0:T(8,128)S(1)} %add.470), channel_id=1, source_target_pairs={{0,16},{2,18},{4,20},{6,22},{8,24},{10,26},{12,28},{14,30},{16,0},... | collective-permute-start | bytes 119816 | tf_op jit(solution)/shard_map/ppermute | solution.py:172
  258.5 7.2 %collective-permute-start.33 = (bf16[512,768]{1,0:T(8,128)(2,1)S(1)}, bf16[512,768]{1,0:T(8,128)(2,1)S(1)}, u32[]{:S(2)}, u32[]{:S(2)}) collective-permute-start(bf16[512,768]{1,0:T(8,128)(2,1)S(1)} %fusion.57), channel_id=1, source_target_pairs={{0,1},{1,0},{2,3},{3,2},{4,5},{5,4},{6,7},{7,6},{8,9},{9,8},{10,11... | collective-permute-start | bytes 2359304 | tf_op jit(solution)/shard_map/ppermute | solution.py:163
  259.3 17.6 %collective-permute-start.27 = (bf16[1,2,2,48,1536]{4,3,2,1,0:T(8,128)(2,1)S(1)}, bf16[1,2,2,48,1536]{4,3,2,1,0:T(8,128)(2,1)S(1)}, u32[]{:S(2)}, u32[]{:S(2)}) collective-permute-start(bf16[1,2,2,48,1536]{4,3,2,1,0:T(8,128)(2,1)S(1)} %add_convert_fusion.2), channel_id=1, source_target_pairs={{0,8},{2,10},{4,12},{6,14},{8,16},{10,18},{12,20},{14,22},{16,24},... | collective-permute-start | bytes 1769480 | tf_op jit(solution)/shard_map/ppermute | solution.py:156
  262.0 16.7 %collective-permute-start.40 = (bf16[4,1,1,48,1536]{4,3,2,1,0:T(8,128)(2,1)S(1)}, bf16[4,1,1,48,1536]{4,3,2,1,0:T(8,128)(2,1)S(1)}, u32[]{:S(2)}, u32[]{:S(2)}) collective-permute-start(bf16[4,1,1,48,1536]{4,3,2,1,0:T(8,128)(2,1)S(1)} %dynamic-slice_convert_fusion.5), channel_id=1, source_target_pairs={{0,4},{2,6},{4,0},{6,2},{8,12},{10,14},{12,8},{14,10},{16,20},{18,... | collective-permute-start | bytes 1769480 | tf_op jit(solution)/shard_map/ppermute | solution.py:156
  264.1 15.5 %collective-permute-start.45 = (bf16[4,1,1,48,1536]{4,3,2,1,0:T(8,128)(2,1)S(1)}, bf16[4,1,1,48,1536]{4,3,2,1,0:T(8,128)(2,1)S(1)}, u32[]{:S(2)}, u32[]{:S(2)}) collective-permute-start(bf16[4,1,1,48,1536]{4,3,2,1,0:T(8,128)(2,1)S(1)} %dynamic-slice_convert_fusion.4), channel_id=1, source_target_pairs={{0,2},{2,0},{4,6},{6,4},{8,10},{10,8},{12,14},{14,12},{16,18},{18,... | collective-permute-start | bytes 1769480 | tf_op jit(solution)/shard_map/ppermute | solution.py:156
  277.1 21.4 %collective-permute-start.28 = (bf16[1,1,2,48,1536]{4,3,2,1,0:T(8,128)(2,1)S(1)}, bf16[1,1,2,48,1536]{4,3,2,1,0:T(8,128)(2,1)S(1)}, u32[]{:S(2)}, u32[]{:S(2)}) collective-permute-start(bf16[1,1,2,48,1536]{4,3,2,1,0:T(8,128)(2,1)S(1)} %dynamic-slice_convert_fusion.7), channel_id=1, source_target_pairs={{0,4},{2,6},{4,0},{6,2},{8,12},{10,14},{12,8},{14,10},{16,20},{18,... | collective-permute-start | bytes 884744 | tf_op jit(solution)/shard_map/ppermute | solution.py:156
  278.8 8.6 %collective-permute-start.41 = (bf16[1,1,1,48,1536]{4,3,2,1,0:T(8,128)(2,1)S(1)}, bf16[1,1,1,48,1536]{4,3,2,1,0:T(8,128)(2,1)S(1)}, u32[]{:S(2)}, u32[]{:S(2)}) collective-permute-start(bf16[1,1,1,48,1536]{4,3,2,1,0:T(8,128)(2,1)S(1)} %dynamic-slice_convert_fusion.9), channel_id=1, source_target_pairs={{0,8},{2,10},{4,12},{6,14},{8,16},{10,18},{12,20},{14,22},{16,24},... | collective-permute-start | bytes 442376 | tf_op jit(solution)/shard_map/ppermute | solution.py:156
  279.8 9.6 %collective-permute-start.46 = (bf16[1,1,1,48,1536]{4,3,2,1,0:T(8,128)(2,1)S(1)}, bf16[1,1,1,48,1536]{4,3,2,1,0:T(8,128)(2,1)S(1)}, u32[]{:S(2)}, u32[]{:S(2)}) collective-permute-start(bf16[1,1,1,48,1536]{4,3,2,1,0:T(8,128)(2,1)S(1)} %dynamic-slice_convert_fusion.8), channel_id=1, source_target_pairs={{0,8},{2,10},{4,12},{6,14},{8,16},{10,18},{12,20},{14,22},{16,24},... | collective-permute-start | bytes 442376 | tf_op jit(solution)/shard_map/ppermute | solution.py:156
  287.5 7.9 %collective-permute-start.42 = (bf16[1,1,1,48,1536]{4,3,2,1,0:T(8,128)(2,1)S(1)}, bf16[1,1,1,48,1536]{4,3,2,1,0:T(8,128)(2,1)S(1)}, u32[]{:S(2)}, u32[]{:S(2)}) collective-permute-start(bf16[1,1,1,48,1536]{4,3,2,1,0:T(8,128)(2,1)S(1)} %add_convert_fusion.11), channel_id=1, source_target_pairs={{0,8},{2,10},{4,12},{6,14},{8,16},{10,18},{12,20},{14,22},{16,24},... | collective-permute-start | bytes 442376 | tf_op jit(solution)/shard_map/ppermute | solution.py:156
  289.5 8.9 %collective-permute-start.47 = (bf16[1,1,1,48,1536]{4,3,2,1,0:T(8,128)(2,1)S(1)}, bf16[1,1,1,48,1536]{4,3,2,1,0:T(8,128)(2,1)S(1)}, u32[]{:S(2)}, u32[]{:S(2)}) collective-permute-start(bf16[1,1,1,48,1536]{4,3,2,1,0:T(8,128)(2,1)S(1)} %add_convert_fusion.9), channel_id=1, source_target_pairs={{0,8},{2,10},{4,12},{6,14},{8,16},{10,18},{12,20},{14,22},{16,24},... | collective-permute-start | bytes 442376 | tf_op jit(solution)/shard_map/ppermute | solution.py:156
  295.5 7.0 %collective-permute-start.43 = (bf16[1,1,1,48,1536]{4,3,2,1,0:T(8,128)(2,1)S(1)}, bf16[1,1,1,48,1536]{4,3,2,1,0:T(8,128)(2,1)S(1)}, u32[]{:S(2)}, u32[]{:S(2)}) collective-permute-start(bf16[1,1,1,48,1536]{4,3,2,1,0:T(8,128)(2,1)S(1)} %add_convert_fusion.10), channel_id=1, source_target_pairs={{0,8},{2,10},{4,12},{6,14},{8,16},{10,18},{12,20},{14,22},{16,24},... | collective-permute-start | bytes 442376 | tf_op jit(solution)/shard_map/ppermute | solution.py:156
  298.4 8.6 %collective-permute-start.48 = (bf16[1,1,1,48,1536]{4,3,2,1,0:T(8,128)(2,1)S(1)}, bf16[1,1,1,48,1536]{4,3,2,1,0:T(8,128)(2,1)S(1)}, u32[]{:S(2)}, u32[]{:S(2)}) collective-permute-start(bf16[1,1,1,48,1536]{4,3,2,1,0:T(8,128)(2,1)S(1)} %add_convert_fusion.8), channel_id=1, source_target_pairs={{0,8},{2,10},{4,12},{6,14},{8,16},{10,18},{12,20},{14,22},{16,24},... | collective-permute-start | bytes 442376 | tf_op jit(solution)/shard_map/ppermute | solution.py:156
  298.6 9.3 %collective-permute-start.29 = (bf16[1,1,1,48,1536]{4,3,2,1,0:T(8,128)(2,1)S(1)}, bf16[1,1,1,48,1536]{4,3,2,1,0:T(8,128)(2,1)S(1)}, u32[]{:S(2)}, u32[]{:S(2)}) collective-permute-start(bf16[1,1,1,48,1536]{4,3,2,1,0:T(8,128)(2,1)S(1)} %dynamic-slice_convert_fusion.10), channel_id=1, source_target_pairs={{0,2},{2,0},{4,6},{6,4},{8,10},{10,8},{12,14},{14,12},{16,18},{18,... | collective-permute-start | bytes 442376 | tf_op jit(solution)/shard_map/ppermute | solution.py:156
  303.4 7.6 %collective-permute-start.49 = (bf16[1,48,1536]{2,1,0:T(8,128)(2,1)S(1)}, bf16[1,48,1536]{2,1,0:T(8,128)(2,1)S(1)}, u32[]{:S(2)}, u32[]{:S(2)}) collective-permute-start(bf16[1,48,1536]{2,1,0:T(8,128)(2,1)S(1)} %get-tuple-element.116), channel_id=1, source_target_pairs={{0,8},{2,10},{4,12},{6,14},{8,16},{10,18},{12,20},{14,22},{16,24},... | collective-permute-start | bytes 442376 | tf_op jit(solution)/shard_map/ppermute | solution.py:103
  307.9 7.8 %collective-permute-start.59 = (bf16[1,48,1536]{2,1,0:T(8,128)(2,1)S(1)}, bf16[1,48,1536]{2,1,0:T(8,128)(2,1)S(1)}, u32[]{:S(2)}, u32[]{:S(2)}) collective-permute-start(bf16[1,48,1536]{2,1,0:T(8,128)(2,1)S(1)} %get-tuple-element.129), channel_id=1, source_target_pairs={{0,8},{2,10},{4,12},{6,14},{8,16},{10,18},{12,20},{14,22},{16,24},... | collective-permute-start | bytes 442376 | tf_op jit(solution)/shard_map/ppermute | solution.py:103
  309.4 6.3 %collective-permute-start.54 = (bf16[1,48,1536]{2,1,0:T(8,128)(2,1)S(1)}, bf16[1,48,1536]{2,1,0:T(8,128)(2,1)S(1)}, u32[]{:S(2)}, u32[]{:S(2)}) collective-permute-start(bf16[1,48,1536]{2,1,0:T(8,128)(2,1)S(1)} %bitcast.111), channel_id=1, source_target_pairs={{0,2},{2,0},{4,6},{6,4},{8,10},{10,8},{12,14},{14,12},{16,18},{18,... | collective-permute-start | bytes 442376 | tf_op jit(solution)/shard_map/ppermute | solution.py:103
  311.0 8.2 %collective-permute-start.50 = (bf16[1,48,1536]{2,1,0:T(8,128)(2,1)S(1)}, bf16[1,48,1536]{2,1,0:T(8,128)(2,1)S(1)}, u32[]{:S(2)}, u32[]{:S(2)}) collective-permute-start(bf16[1,48,1536]{2,1,0:T(8,128)(2,1)S(1)} %collective-permute-done.49), channel_id=1, source_target_pairs={{0,8},{2,10},{4,12},{6,14},{8,16},{10,18},{12,20},{14,22},{16,24},... | collective-permute-start | bytes 442376 | tf_op jit(solution)/shard_map/ppermute | solution.py:103
  315.7 7.0 %collective-permute-start.60 = (bf16[1,48,1536]{2,1,0:T(8,128)(2,1)S(1)}, bf16[1,48,1536]{2,1,0:T(8,128)(2,1)S(1)}, u32[]{:S(2)}, u32[]{:S(2)}) collective-permute-start(bf16[1,48,1536]{2,1,0:T(8,128)(2,1)S(1)} %collective-permute-done.59), channel_id=1, source_target_pairs={{0,8},{2,10},{4,12},{6,14},{8,16},{10,18},{12,20},{14,22},{16,24},... | collective-permute-start | bytes 442376 | tf_op jit(solution)/shard_map/ppermute | solution.py:103
  315.7 16.7 %collective-permute-start.55 = (bf16[2,48,1536]{2,1,0:T(8,128)(2,1)S(1)}, bf16[2,48,1536]{2,1,0:T(8,128)(2,1)S(1)}, u32[]{:S(2)}, u32[]{:S(2)}) collective-permute-start(bf16[2,48,1536]{2,1,0:T(8,128)(2,1)S(1)} %pad_maximum_fusion.8), channel_id=1, source_target_pairs={{0,4},{2,6},{4,0},{6,2},{8,12},{10,14},{12,8},{14,10},{16,20},{18,... | collective-permute-start | bytes 884744 | tf_op jit(solution)/shard_map/ppermute | solution.py:103
  319.2 6.9 %collective-permute-start.51 = (bf16[1,48,1536]{2,1,0:T(8,128)(2,1)S(1)}, bf16[1,48,1536]{2,1,0:T(8,128)(2,1)S(1)}, u32[]{:S(2)}, u32[]{:S(2)}) collective-permute-start(bf16[1,48,1536]{2,1,0:T(8,128)(2,1)S(1)} %collective-permute-done.50), channel_id=1, source_target_pairs={{0,8},{2,10},{4,12},{6,14},{8,16},{10,18},{12,20},{14,22},{16,24},... | collective-permute-start | bytes 442376 | tf_op jit(solution)/shard_map/ppermute | solution.py:103
  322.7 8.6 %collective-permute-start.61 = (bf16[1,48,1536]{2,1,0:T(8,128)(2,1)S(1)}, bf16[1,48,1536]{2,1,0:T(8,128)(2,1)S(1)}, u32[]{:S(2)}, u32[]{:S(2)}) collective-permute-start(bf16[1,48,1536]{2,1,0:T(8,128)(2,1)S(1)} %collective-permute-done.60), channel_id=1, source_target_pairs={{0,8},{2,10},{4,12},{6,14},{8,16},{10,18},{12,20},{14,22},{16,24},... | collective-permute-start | bytes 442376 | tf_op jit(solution)/shard_map/ppermute | solution.py:103
  326.3 13.3 %collective-permute-start.52 = (bf16[4,48,1536]{2,1,0:T(8,128)(2,1)S(1)}, bf16[4,48,1536]{2,1,0:T(8,128)(2,1)S(1)}, u32[]{:S(2)}, u32[]{:S(2)}) collective-permute-start(bf16[4,48,1536]{2,1,0:T(8,128)(2,1)S(1)} %pad_maximum_fusion.1), channel_id=1, source_target_pairs={{0,2},{2,0},{4,6},{6,4},{8,10},{10,8},{12,14},{14,12},{16,18},{18,... | collective-permute-start | bytes 1769480 | tf_op jit(solution)/shard_map/ppermute | solution.py:103
  331.4 16.3 %collective-permute-start.62 = (bf16[4,48,1536]{2,1,0:T(8,128)(2,1)S(1)}, bf16[4,48,1536]{2,1,0:T(8,128)(2,1)S(1)}, u32[]{:S(2)}, u32[]{:S(2)}) collective-permute-start(bf16[4,48,1536]{2,1,0:T(8,128)(2,1)S(1)} %pad_maximum_fusion.2), channel_id=1, source_target_pairs={{0,4},{2,6},{4,0},{6,2},{8,12},{10,14},{12,8},{14,10},{16,20},{18,... | collective-permute-start | bytes 1769480 | tf_op jit(solution)/shard_map/ppermute | solution.py:103
  332.4 17.0 %collective-permute-start.56 = (bf16[4,48,1536]{2,1,0:T(8,128)(2,1)S(1)}, bf16[4,48,1536]{2,1,0:T(8,128)(2,1)}, u32[]{:S(2)}, u32[]{:S(2)}) collective-permute-start(bf16[4,48,1536]{2,1,0:T(8,128)(2,1)S(1)} %constant_dynamic-update-slice_fusion.28.refs_0_), channel_id=1, source_target_pairs={{0,8},{2,10},{4,12},{6,14},{8,16},{10,18},{12,20},{14,22},{16,24},... | collective-permute-start | bytes 1769480 | tf_op jit(solution)/shard_map/ppermute | solution.py:103
  339.6 28.1 %collective-permute-start.53 = (bf16[8,48,1536]{2,1,0:T(8,128)(2,1)S(1)}, bf16[8,48,1536]{2,1,0:T(8,128)(2,1)S(1)}, u32[]{:S(2)}, u32[]{:S(2)}) collective-permute-start(bf16[8,48,1536]{2,1,0:T(8,128)(2,1)S(1)} %constant_dynamic-update-slice_fusion.23.refs_0_), channel_id=1, source_target_pairs={{0,4},{2,6},{4,0},{6,2},{8,12},{10,14},{12,8},{14,10},{16,20},{18,... | collective-permute-start | bytes 3538952 | tf_op jit(solution)/shard_map/ppermute | solution.py:103
  347.7 25.9 %collective-permute-start.63 = (bf16[8,48,1536]{2,1,0:T(8,128)(2,1)S(1)}, bf16[8,48,1536]{2,1,0:T(8,128)(2,1)}, u32[]{:S(2)}, u32[]{:S(2)}) collective-permute-start(bf16[8,48,1536]{2,1,0:T(8,128)(2,1)S(1)} %constant_dynamic-update-slice_fusion.31.refs_0_), channel_id=1, source_target_pairs={{0,2},{2,0},{4,6},{6,4},{8,10},{10,8},{12,14},{14,12},{16,18},{18,... | collective-permute-start | bytes 3538952 | tf_op jit(solution)/shard_map/ppermute | solution.py:103
  349.4 18.3 %collective-permute-start.57 = (bf16[4,48,1536]{2,1,0:T(8,128)(2,1)}, bf16[4,48,1536]{2,1,0:T(8,128)(2,1)}, u32[]{:S(2)}, u32[]{:S(2)}) collective-permute-start(bf16[4,48,1536]{2,1,0:T(8,128)(2,1)} %collective-permute-done.56.refs_1_), channel_id=1, source_target_pairs={{0,8},{2,10},{4,12},{6,14},{8,16},{10,18},{12,20},{14,22},{16,24},... | collective-permute-start | bytes 1769480 | tf_op jit(solution)/shard_map/ppermute | solution.py:103
  367.8 11.9 %collective-permute-start.58 = (bf16[4,48,1536]{2,1,0:T(8,128)(2,1)}, bf16[4,48,1536]{2,1,0:T(8,128)(2,1)S(1)}, u32[]{:S(2)}, u32[]{:S(2)}) collective-permute-start(bf16[4,48,1536]{2,1,0:T(8,128)(2,1)} %collective-permute-done.57.refs_2_), channel_id=1, source_target_pairs={{0,8},{2,10},{4,12},{6,14},{8,16},{10,18},{12,20},{14,22},{16,24},... | collective-permute-start | bytes 1769480 | tf_op jit(solution)/shard_map/ppermute | solution.py:103
  445.7 5.7 %collective-permute-start.66 = (f32[48,768]{1,0:T(8,128)S(1)}, f32[48,768]{1,0:T(8,128)S(1)}, u32[]{:S(2)}, u32[]{:S(2)}) collective-permute-start(f32[48,768]{1,0:T(8,128)S(1)} %get-tuple-element.184), channel_id=1, source_target_pairs={{0,3},{1,2},{2,1},{3,0},{4,7},{5,6},{6,5},{7,4},{8,11},{9,10},{10,... | collective-permute-start | bytes 442376 | tf_op jit(solution)/shard_map/ppermute | solution.py:547
  447.1 7.9 %collective-permute-start.65 = (f32[48,768]{1,0:T(8,128)S(1)}, f32[48,768]{1,0:T(8,128)S(1)}, u32[]{:S(2)}, u32[]{:S(2)}) collective-permute-start(f32[48,768]{1,0:T(8,128)S(1)} %get-tuple-element.184), channel_id=1, source_target_pairs={{0,2},{1,3},{2,0},{3,1},{4,6},{5,7},{6,4},{7,5},{8,10},{9,11},{10,... | collective-permute-start | bytes 442376 | tf_op jit(solution)/shard_map/ppermute | solution.py:547
  (63 other events, 613.2 us)

commit v3 on v2

--- a/solution.py
+++ b/solution.py
@@ -26,7 +26,6 @@
 Z_ORDERS = (Z_THEN_X, Z_THEN_Y)
 X_THEN_Y = (0, 1, 2)
 Y_THEN_X = (1, 0, 2)
-Z_FIRST = (2, 1, 0)
 NORM_EPS = 1e-05
 POLY_ONE = 3.4445
 POLY_TWO = -4.775
@@ -93,47 +92,34 @@
         copy.wait()
 
 
-def gather_stage(parts, axis):
+def gather_steps(share, orders):
     count = lax.axis_size("dp")
-    stride, size = data_axes(count)[axis]
-    perm = ring(count, stride, size)
-    moving = jnp.concatenate(parts, 0) if len(parts) > 1 else parts[0]
-    parts = [moving]
-    for _ in range(size - 1):
-        moving = lax.ppermute(moving, "dp", perm)
-        parts.append(moving)
-    return parts
-
-
-def staged_gather(share, orders, early=(), late=()):
-    count = lax.axis_size("dp")
-    rows, columns = share.shape
-    width = columns // len(orders)
+    width = share.shape[1] // len(orders)
     pieces = [
         [share[None, :, piece * width : (piece + 1) * width]] for piece in range(len(orders))
     ]
-    for stage in range(3):
-        pieces = [gather_stage(parts, order[stage]) for parts, order in zip(pieces, orders)]
-        if stage == 0:
-            pieces, early = lax.optimization_barrier((pieces, early))
-    pieces, late = lax.optimization_barrier((pieces, late))
-    anywhere = pl.BlockSpec(memory_space=pl.ANY)
-    whole = pl.pallas_call(
-        functools.partial(place_kernel, orders, [len(parts) for parts in pieces], width, count),
-        in_specs=[anywhere] * sum(len(parts) for parts in pieces),
-        out_specs=pl.BlockSpec(memory_space=pltpu.VMEM),
-        out_shape=jax.ShapeDtypeStruct((count, rows, columns), share.dtype),
-        scratch_shapes=[pltpu.SemaphoreType.DMA((count * len(orders),))],
-        compiler_params=pltpu.CompilerParams(vmem_limit_bytes=VMEM_LIMIT),
-        cost_estimate=pl.CostEstimate(
-            flops=0, bytes_accessed=4 * count * rows * columns, transcendentals=0
-        ),
-    )(*[part for parts in pieces for part in parts])
-    whole = whole.reshape(count * rows, columns)
-    return whole, early, late
-
-
-def staged_scatter(partial, order):
+    hops = sum(size - 1 for _, size in data_axes(count))
+    plans = [
+        [(axis, hop) for axis in order for hop in range(data_axes(count)[axis][1] - 1)]
+        for order in orders
+    ]
+    moving = [None] * len(orders)
+    for step in range(hops):
+        for piece, plan in enumerate(plans):
+            axis, hop = plan[step]
+            stride, size = data_axes(count)[axis]
+            if hop == 0:
+                parts = pieces[piece]
+                moving[piece] = jnp.concatenate(parts, 0) if len(parts) > 1 else parts[0]
+                pieces[piece] = [moving[piece]]
+            moving[piece] = lax.ppermute(moving[piece], "dp", ring(count, stride, size))
+        moving = list((yield moving))
+        for parts, part in zip(pieces, moving):
+            parts.append(part)
+    return pieces
+
+
+def scatter_steps(partial, order):
     count = lax.axis_size("dp")
     rank = lax.axis_index("dp")
     axes = data_axes(count)
@@ -153,23 +139,76 @@
 
         total = block(place + size - 1)
         for step in range(size - 1):
-            got = lax.ppermute(total.astype(jnp.bfloat16), "dp", perm)
+            (got,) = yield [lax.ppermute(total.astype(jnp.bfloat16), "dp", perm)]
             total = block(place + 2 * size - 2 - step) + got.astype(jnp.float32)
         held = total
     return held.reshape(rows, columns)
 
 
+class Travel:
+    def __init__(self, steps):
+        self.steps = steps
+        self.moving = None
+        self.result = None
+
+    def hop(self):
+        if self.result is None:
+            try:
+                self.moving = self.steps.send(self.moving)
+            except StopIteration as stop:
+                self.moving = []
+                self.result = stop.value
+
+    def finish(self):
+        while self.result is None:
+            self.hop()
+        return self.result
+
+
+def hop_all(*travels):
+    for travel in travels:
+        travel.hop()
+
+
+def arrived(travels, beside):
+    moving, beside = lax.optimization_barrier(([travel.moving for travel in travels], beside))
+    for travel, value in zip(travels, moving):
+        travel.moving = value
+    return beside
+
+
+def placed(pieces, orders):
+    count = lax.axis_size("dp")
+    rows, width = pieces[0][0].shape[1:]
+    dtype = pieces[0][0].dtype
+    anywhere = pl.BlockSpec(memory_space=pl.ANY)
+    whole = pl.pallas_call(
+        functools.partial(place_kernel, orders, [len(parts) for parts in pieces], width, count),
+        in_specs=[anywhere] * sum(len(parts) for parts in pieces),
+        out_specs=pl.BlockSpec(memory_space=pltpu.VMEM),
+        out_shape=jax.ShapeDtypeStruct((count, rows, width * len(orders)), dtype),
+        scratch_shapes=[pltpu.SemaphoreType.DMA((count * len(orders),))],
+        compiler_params=pltpu.CompilerParams(vmem_limit_bytes=VMEM_LIMIT),
+        cost_estimate=pl.CostEstimate(
+            flops=0, bytes_accessed=4 * count * rows * width * len(orders), transcendentals=0
+        ),
+    )(*[part for parts in pieces for part in parts])
+    return whole.reshape(count * rows, width * len(orders))
+
+
 def other_core(value):
     return lax.ppermute(value, "tensor", [(0, 1), (1, 0)])
 
 
-def sum_everywhere(value):
-    value = value + other_core(value)
+def sum_steps(value):
+    (got,) = yield [other_core(value)]
+    value = value + got
     count = lax.axis_size("dp")
     distance = 1
     while distance < count:
         pairs = [(index, index ^ distance) for index in range(count)]
-        value = value + lax.ppermute(value, "dp", pairs)
+        (got,) = yield [lax.ppermute(value, "dp", pairs)]
+        value = value + got
         distance *= 2
     return value
 
@@ -358,17 +397,28 @@
     data_size = lax.axis_size("dp")
     data_rank = lax.axis_index("dp")
     masters = (attend_weight, output_weight, widen_weight, narrow_weight)
-    attend_columns = attend_weight.shape[1]
-    attend_share = jnp.concatenate([attend_weight, output_weight], 1).astype(jnp.bfloat16)
-    widen_low, narrow_share, _ = staged_gather(
-        widen_weight.astype(jnp.bfloat16), Z_ORDERS, narrow_weight.astype(jnp.bfloat16)
-    )
     length = layer_input.shape[0]
     triple_cols = attend_weight.shape[1]
-    attend_columns = triple_cols
-    widen_cols = widen_low.shape[1]
+    widen_cols = widen_weight.shape[1]
     widen_rows = FF // D
     feature_share = D // tensor_size
+    widen_order, narrow_order = (Z_THEN_X,), (Z_THEN_Y,)
+
+    joint_gather = Travel(
+        gather_steps(
+            jnp.concatenate([attend_weight, output_weight], 1).astype(jnp.bfloat16), Z_ORDERS
+        )
+    )
+    joint_gather.hop()
+    widen_share, narrow_share = arrived(
+        [joint_gather], (widen_weight.astype(jnp.bfloat16), narrow_weight.astype(jnp.bfloat16))
+    )
+    widen_gather = Travel(gather_steps(widen_share, widen_order))
+    narrow_gather = Travel(gather_steps(narrow_share, narrow_order))
+    feeds = (widen_gather, narrow_gather)
+    joint_gather.hop()
+    layer_input, cotangent = arrived([joint_gather], (layer_input, cotangent))
+    joint_gather.hop()
     float_input = layer_input.astype(jnp.float32)
     first_gain = vector_params[0]
     second_gain = vector_params[2]
@@ -379,17 +429,52 @@
         vector_params[8 : 8 + widen_rows].reshape(-1), tensor_rank * widen_cols, widen_cols
     )
     normed, inverse = norm_stats(float_input)
+    inverse = arrived([joint_gather], inverse)
+    hop_all(joint_gather, *feeds)
     first_norm = (normed * first_gain + vector_params[1]).astype(jnp.bfloat16)
     second_norm = (normed * second_gain + vector_params[3]).astype(jnp.bfloat16)
-    widened = jnp.dot(second_norm, widen_low, preferred_element_type=jnp.float32) + widen_bias
-    activated = jax.nn.gelu(widened, approximate=False).astype(jnp.bfloat16)
-    narrow_low, _, (widened, activated) = staged_gather(
-        narrow_share, Z_ORDERS, late=(widened, activated)
-    )
+    first_norm, second_norm = arrived([joint_gather, *feeds], (first_norm, second_norm))
+    hop_all(joint_gather, *feeds)
+    hop_all(*feeds)
     live_rows = (segment_ids >= 0).astype(jnp.float32)[:, None]
     upstream = live_rows * cotangent.astype(jnp.float32)
     upstream_low = upstream.astype(jnp.bfloat16)
     bias_grad = jnp.sum(upstream, axis=0) / tensor_size
+    cosines, sines = rotary_tables(segment_ids)
+    upstream_low, bias_grad, cosines, sines = arrived(
+        [joint_gather, *feeds], (upstream_low, bias_grad, cosines, sines)
+    )
+    hop_all(*feeds)
+    joint_low = placed(joint_gather.finish(), Z_ORDERS)
+    attend_low, output_low = joint_low[:, :triple_cols], joint_low[:, triple_cols:]
+    triple_rows = (
+        jnp.einsum("dk,sd->ks", attend_low, first_norm, preferred_element_type=jnp.float32)
+        + attend_bias[:, None]
+    )
+    mixed_rows = jnp.einsum(
+        "sd,dk->ks", upstream_low, output_low, preferred_element_type=jnp.float32
+    ).astype(jnp.bfloat16)
+    triple_rows, mixed_rows = arrived(feeds, (triple_rows, mixed_rows))
+    hop_all(*feeds)
+    mixture_rows, triple_grad = attention(triple_rows, cosines, sines, mixed_rows, segment_ids)
+    mixture_rows, triple_grad = arrived(feeds, (mixture_rows, triple_grad))
+    output_grad = jnp.einsum(
+        "sd,ks->dk", upstream_low, mixture_rows, preferred_element_type=jnp.float32
+    )
+    attend_grad = jnp.einsum(
+        "sd,ks->dk", first_norm, triple_grad, preferred_element_type=jnp.float32
+    )
+    joint_scatter = Travel(
+        scatter_steps(jnp.concatenate([attend_grad, output_grad], 1), X_THEN_Y)
+    )
+    widen_low = placed(widen_gather.finish(), widen_order)
+    narrow_low = placed(narrow_gather.finish(), narrow_order)
+
+    joint_scatter.hop()
+    widened = jnp.dot(second_norm, widen_low, preferred_element_type=jnp.float32) + widen_bias
+    activated = jax.nn.gelu(widened, approximate=False).astype(jnp.bfloat16)
+    widened, activated = arrived([joint_scatter], (widened, activated))
+    joint_scatter.hop()
     activation_grad = jnp.einsum(
         "sd,df->sf", upstream_low, narrow_low, preferred_element_type=jnp.float32
     )
@@ -403,34 +488,29 @@
     widen_grad = jnp.einsum(
         "sd,sf->df", second_norm, widen_back, preferred_element_type=jnp.float32
     )
-    widen_bias_grad = jnp.sum(widen_back.astype(jnp.float32), axis=0)
+    widen_grad, narrow_grad, widen_back = arrived(
+        [joint_scatter], (widen_grad, narrow_grad, widen_back)
+    )
+    widen_scatter = Travel(scatter_steps(widen_grad, X_THEN_Y))
+    narrow_scatter = Travel(scatter_steps(narrow_grad, Y_THEN_X))
+    sums = (widen_scatter, narrow_scatter)
+    hop_all(*sums, joint_scatter)
+    hop_all(joint_scatter)
+    hop_all(joint_scatter)
+    row_share = length // tensor_size
+    row_start = tensor_rank * row_share
+    other_row = (1 - tensor_rank) * row_share
+
+    def core_sum(part):
+        sent = lax.dynamic_slice_in_dim(part, other_row, row_share, 0).astype(jnp.bfloat16)
+        kept = lax.dynamic_slice_in_dim(part, row_start, row_share, 0)
+        return kept + other_core(sent).astype(jnp.float32)
+
     second_back = jnp.einsum("sf,df->sd", widen_back, widen_low, preferred_element_type=jnp.float32)
-    joint_low, _, (widen_grad, narrow_grad) = staged_gather(
-        attend_share, (X_FIRST,), late=(widen_grad, narrow_grad)
-    )
-    attend_low, output_low = joint_low[:, :attend_columns], joint_low[:, attend_columns:]
-    widen_sum = staged_scatter(widen_grad, X_THEN_Y)
-    narrow_sum = staged_scatter(narrow_grad, Y_THEN_X)
-    triple_rows = (
-        jnp.einsum("dk,sd->ks", attend_low, first_norm, preferred_element_type=jnp.float32)
-        + attend_bias[:, None]
-    )
-    mixed_rows = jnp.einsum(
-        "sd,dk->ks", upstream_low, output_low, preferred_element_type=jnp.float32
-    ).astype(jnp.bfloat16)
-    cosines, sines = rotary_tables(segment_ids)
-    mixture_rows, triple_grad = attention(triple_rows, cosines, sines, mixed_rows, segment_ids)
-    output_grad = jnp.einsum(
-        "sd,ks->dk", upstream_low, mixture_rows, preferred_element_type=jnp.float32
-    )
-    attend_grad = jnp.einsum(
-        "sd,ks->dk", first_norm, triple_grad, preferred_element_type=jnp.float32
-    )
-    joint_sum = staged_scatter(jnp.concatenate([attend_grad, output_grad], 1), Z_FIRST)
-    attend_bias_grad = jnp.sum(triple_grad.astype(jnp.float32), axis=1)
     first_back = jnp.einsum(
         "ks,dk->sd", triple_grad, attend_low, preferred_element_type=jnp.float32
     )
+    first_total, second_total = core_sum(first_back), core_sum(second_back)
     attended = jnp.einsum(
         "ks,dk->sd", mixture_rows, output_low, preferred_element_type=jnp.float32
     )
@@ -454,16 +534,23 @@
             + own_columns(vector_params[8 + widen_rows])
         )
     ).astype(jnp.bfloat16)
-    row_share = length // tensor_size
-    row_start = tensor_rank * row_share
-    other_row = (1 - tensor_rank) * row_share
-
-    def core_sum(part):
-        sent = lax.dynamic_slice_in_dim(part, other_row, row_share, 0).astype(jnp.bfloat16)
-        kept = lax.dynamic_slice_in_dim(part, row_start, row_share, 0)
-        return kept + other_core(sent).astype(jnp.float32)
-
-    first_total, second_total = core_sum(first_back), core_sum(second_back)
+    widen_bias_grad = jnp.sum(widen_back.astype(jnp.float32), axis=0)
+    attend_bias_grad = jnp.sum(triple_grad.astype(jnp.float32), axis=1)
+    first_total, second_total, block_output, widen_bias_grad, attend_bias_grad = arrived(
+        [*sums, joint_scatter],
+        (first_total, second_total, block_output, widen_bias_grad, attend_bias_grad),
+    )
+    joint_sum = joint_scatter.finish()
+    attend_sum, output_sum = joint_sum[:, :triple_cols], joint_sum[:, triple_cols:]
+    attend_momentum = MUON_BETA * attend_moment + attend_sum
+    output_momentum = MUON_BETA * output_moment + output_sum
+    joint_gather = Travel(
+        gather_steps(
+            jnp.concatenate([attend_momentum, output_momentum], 1).astype(jnp.bfloat16), Z_ORDERS
+        )
+    )
+    hop_all(*sums, joint_gather)
+    hop_all(joint_gather)
     normed_share = lax.dynamic_slice_in_dim(normed, row_start, row_share, 0)
     inverse_share = lax.dynamic_slice_in_dim(inverse, row_start, row_share, 0)
     upstream_share = lax.dynamic_slice_in_dim(upstream, row_start, row_share, 0)
@@ -502,33 +589,43 @@
         ],
         axis=0,
     )
-    vector_grad = sum_everywhere(vector_part)
-    attend_sum, output_sum = joint_sum[:, :attend_columns], joint_sum[:, attend_columns:]
+    input_grad, vector_part = arrived([*sums, joint_gather], (input_grad, vector_part))
+    vector_sum = Travel(sum_steps(vector_part))
+    for _ in range(3):
+        hop_all(*sums, joint_gather, vector_sum)
+        arrived([*sums, joint_gather, vector_sum], ())
+    widen_sum, narrow_sum = widen_scatter.finish(), narrow_scatter.finish()
+    widen_momentum = MUON_BETA * widen_moment + widen_sum
+    narrow_momentum = MUON_BETA * narrow_moment + narrow_sum
+    widen_gather = Travel(gather_steps(widen_momentum.astype(jnp.bfloat16), widen_order))
+    narrow_gather = Travel(gather_steps(narrow_momentum.astype(jnp.bfloat16), narrow_order))
+    feeds = (widen_gather, narrow_gather)
+    hop_all(*feeds, vector_sum)
+
+    def gram(matrix):
+        return jnp.einsum("dk,ek->de", matrix, matrix, preferred_element_type=jnp.float32)
+
+    joint_whole = placed(joint_gather.finish(), Z_ORDERS)
+    attend_whole, output_whole = joint_whole[:, :triple_cols], joint_whole[:, triple_cols:]
+    attend_gram, output_gram = gram(attend_whole), gram(output_whole)
+    attend_gram, output_gram = arrived([*feeds, vector_sum], (attend_gram, output_gram))
+    hop_all(*feeds, vector_sum)
+    arrived([*feeds, vector_sum], ())
+    hop_all(*feeds)
+    vector_grad = arrived(feeds, vector_sum.finish())
+    hop_all(*feeds)
+    arrived(feeds, ())
+    hop_all(*feeds)
+    widen_whole = placed(widen_gather.finish(), widen_order)
+    narrow_whole = placed(narrow_gather.finish(), narrow_order)
+    grams = (attend_gram, output_gram, gram(widen_whole), gram(narrow_whole))
     summed = (attend_sum, output_sum, widen_sum, narrow_sum)
-    moments = (attend_moment, output_moment, widen_moment, narrow_moment)
-    momenta = [MUON_BETA * previous + gradient for previous, gradient in zip(moments, summed)]
+    momenta = (attend_momentum, output_momentum, widen_momentum, narrow_momentum)
     widths = [matrix.shape[1] for matrix in momenta]
     rows_here = D // data_size
-    widen_whole, _, _ = staged_gather(momenta[2].astype(jnp.bfloat16), (Z_THEN_X,))
-    narrow_whole, _, _ = staged_gather(momenta[3].astype(jnp.bfloat16), (Z_THEN_Y,))
-    joint_moment = jnp.concatenate([momenta[0], momenta[1]], 1).astype(jnp.bfloat16)
-    joint_moment, block_output, input_grad, vector_grad = lax.optimization_barrier(
-        (joint_moment, block_output, input_grad, vector_grad)
-    )
-    joint_whole, _, _ = staged_gather(joint_moment, (X_FIRST,))
-    wholes = [
-        joint_whole[:, :attend_columns],
-        joint_whole[:, attend_columns:],
-        widen_whole,
-        narrow_whole,
-    ]
-
-    def gram(matrix):
-        return jnp.einsum("dk,ek->de", matrix, matrix, preferred_element_type=jnp.float32)
-
+    wholes = (attend_whole, output_whole, widen_whole, narrow_whole)
     parity = data_rank % 2
     even, low_core = parity == 0, tensor_rank == 0
-    grams = [gram(matrix) for matrix in wholes]
     core_first = jnp.where(even, grams[2], grams[0])
     core_second = jnp.where(even, grams[3], grams[1])
     own_gram = jnp.where(low_core, core_first, core_second) + other_core(

time: 468 us -> 453 us (0.968)
  waiting for transfers between devices: 181 us -> 134 us
  starting transfers between devices: 42.8 us -> 66.6 us
  matrix products: 115 us -> 128 us
  other arithmetic: 58.9 us -> 46.4 us
    ppermute x59, waiting for transfers between devices: 169 us -> 122 us  [the longest x40 71.9 us: gather_steps(): moving[piece] = lax.ppermute(moving[piece], 'dp', ring(count, stride, size))]
    ppermute x59, starting transfers between devices: 40.5 us -> 63.9 us  [the longest x40 48 us: gather_steps(): moving[piece] = lax.ppermute(moving[piece], 'dp', ring(count, stride, size))]
    reduce_sum x1, other arithmetic: 16 us -> 1.09 us  [shards(): widen_bias_grad = jnp.sum(widen_back.astype(jnp.float32), axis=0)]
    dot_general x1, matrix products: 4.23 us -> 18.9 us  [shards(): jnp.einsum('sd,df->sf', upstream_low, narrow_low, preferred_element_type=...]
    dot_general x1, matrix products: 7.64 us -> 2.64 us  [shards(): jnp.einsum('sd,sf->df', second_norm, widen_back, preferred_element_type=j...]
  transfers between devices with their start and end apart: 68 -> 68, of which waited for: 38 -> 34; matrix products, arithmetic and copies ran while one was open for 27% -> 25% of each run, Pallas kernels for 8% -> 8%
where the time goes in v3:
time: 453 us; the launch traced here: 447 us
  waiting for transfers between devices  134 us (30%)
  matrix products  128 us (28%)
  starting transfers between devices  66.6 us (15%)
  other arithmetic  46.4 us (10%)
  Pallas kernels  42.5 us (9%)
  local copies, waits for them, and re-layouts  25.6 us (6%)
    ppermute x40, waiting for transfers between devices, gather_steps(): moving[piece] = lax.ppermute(moving[piece], 'dp', ring(count, stride, size))  71.9 us
    ppermute x40, starting transfers between devices, gather_steps(): moving[piece] = lax.ppermute(moving[piece], 'dp', ring(count, stride, size))  48 us
    dot_general x17, matrix products, product(): jnp.dot(left, right, precision=HIGH, preferred_element_type=jnp.float32)  47.6 us
    ppermute x15, waiting for transfers between devices, scatter_steps(): got, = (yield [lax.ppermute(total.astype(jnp.bfloat16), 'dp', perm)])  26.9 us
    pallas_call x1, Pallas kernels, attention(): pl.pallas_call(attention_kernel, grid=(heads,), in_specs=[own(3 * HEAD_DI...  24.8 us
    ppermute x4, waiting for transfers between devices, sum_steps(): got, = (yield [lax.ppermute(value, 'dp', pairs)])  23.3 us
    dot_general x1, matrix products, shards(): jnp.einsum('sd,df->sf', upstream_low, narrow_low, preferred_element_type=...  18.9 us
    dot_general x1, matrix products, shards(): jnp.dot(second_norm, widen_low, preferred_element_type=jnp.float32)  18.3 us
  transfers between devices with their start and end apart: 68, of which 34 were waited for; matrix products, arithmetic and copies ran while one was open for 25% of the time, Pallas kernels for 8%

profile of v3, /device:TPU:0, one launch (start us, length us, event | category | flops | bytes accessed | tf_op | source)
XLA Modules:
  0.0 446.9 jit_solution(366913481731287746)
XLA Ops:
  1.8 3.1 collective-permute-start
  28.5 2.1 convert_multiply_fusion
  31.3 3.1 subtract_multiply_fusion
  38.5 3.1 collective-permute-done.7
  44.2 4.6 %collective-permute-start.14 = (bf16[1,48,1536]{2,1,0:T(8,128)(2,1)S(1)}, bf16[1,48,1536]{2,1,0:T(8,128)(2,1)S(1)}, u32[]{:S(2)}, u32[]{:S(2)}) collective-permute-start(bf16[1,48,1536]{2,1,0:T(8,128)(2,1)S(1)} %collective-permute-done.9), channel_id=1, source_target_pairs={{0,8},{2,10},{4,12},{6,14},{8,16},{10,18},{12,20},{14,22},{16,24},... | collective-permute-start | bytes 442376 | tf_op jit(solution)/shard_map/ppermute | solution.py:115
  55.5 2.9 collective-permute-done.13
  58.4 2.2 collective-permute-done.15
  60.5 2.9 collective-permute-done.11.refs_1_
  66.9 4.5 %convolution_add_fusion.triple_ref = f32[1152,1024]{1,0:T(8,128)} fusion(bf16[1024,768]{1,0:T(8,128)(2,1)S(1)} %get-tuple-element.111, f32[1152]{0:T(1024)S(1)} %dynamic_slice.123, bf16[768,1536]{1,0:T(8,128)(2,1)S(1)} %bitcast.106), kind=kOutput, calls=%fused_computation.47 | convolution fusion | flops 1813118976 | bytes 8069120 | tf_op jit(solution)/shard_map/dk,sd->ks/dot_general | solution.py:451
  71.4 5.0 %collective-permute-done.17 = bf16[4,48,1536]{2,1,0:T(8,128)(2,1)S(1)} collective-permute-done((bf16[4,48,1536]{2,1,0:T(8,128)(2,1)S(1)}, bf16[4,48,1536]{2,1,0:T(8,128)(2,1)S(1)}, u32[]{:S(2)}, u32[]{:S(2)}) %collective-permute-start.17) | collective-permute-done | bytes 589856 | tf_op jit(solution)/shard_map/ppermute | solution.py:115
  76.4 3.3 collective-permute-done.16
  81.5 24.8 %shard_map.278 = (bf16[384,1024]{1,0:T(8,128)(2,1)S(1)}, bf16[1152,1024]{1,0:T(8,128)(2,1)S(1)}) custom-call(f32[1152,1024]{1,0:T(8,128)} %convolution_add_fusion.triple_ref, f32[8,1024]{1,0:T(8,128)S(1)} %get-tuple-element.125.cos_ref, f32[8,1024]{1,0:T(8,128)S(1)} %get-tuple-element.126.sin_ref, ...), custom_call_target="tpu_custom_call" | custom-call | flops 14495514624 | bytes 9437184 | tf_op jit(solution)/shard_map/pallas_call | solution.py:360
  106.3 4.0 fusion.180
  110.3 3.9 fusion.58
  114.2 4.2 shard_map.279
  119.5 2.4 dynamic-slice_convert_fusion.4
  125.1 18.3 %fusion.2 = (bf16[1024,1536]{1,0:T(8,128)(2,1)}, f32[1024,1536]{1,0:T(8,128)}) fusion(f32[1536]{0:T(1024)S(1)} %dynamic_slice.126, bf16[1024,768]{1,0:T(8,128)(2,1)S(1)} %copy-done.15, bf16[768,1536]{1,0:T(8,128)(2,1)S(1)} %bitcast.109), kind=kOutput, calls=%fused_computation.4 | convolution fusion | flops 2519728128 | bytes 13375488 | tf_op jit(solution)/shard_map/dot_general | solution.py:474
  143.4 3.8 shard_map.280
  148.2 2.2 convert_add_fusion.4
  153.8 2.6 fusion.183
  156.4 2.6 fusion.185
  159.1 18.9 %fusion.7 = bf16[1024,1536]{1,0:T(8,128)(2,1)S(1)} fusion(f32[1024,1536]{1,0:T(8,128)} %get-tuple-element.135, bf16[1024,768]{1,0:T(8,128)(2,1)S(1)} %copy-done.18, bf16[768,1536]{1,0:T(8,128)(2,1)S(1)} %bitcast.112), kind=kOutput, calls=%fused_computation.9 | convolution fusion | flops 2529165312 | bytes 13369344 | tf_op jit(solution)/shard_map/sd,df->sf/dot_general | solution.py:478
  179.2 2.6 fusion.182
  181.8 2.6 fusion.184
  189.9 2.8 collective-permute-done.24
  193.9 6.1 %collective-permute-done.25 = bf16[1,1,1,48,1536]{4,3,2,1,0:T(8,128)(2,1)S(1)} collective-permute-done((bf16[1,1,1,48,1536]{4,3,2,1,0:T(8,128)(2,1)S(1)}, bf16[1,1,1,48,1536]{4,3,2,1,0:T(8,128)(2,1)S(1)}, u32[]{:S(2)}, u32[]{:S(2)}) %collective-permute-start.25) | collective-permute-done | bytes 147488 | tf_op jit(solution)/shard_map/ppermute | solution.py:142
  201.6 5.4 %collective-permute-done.26 = bf16[1,1,1,48,1536]{4,3,2,1,0:T(8,128)(2,1)S(1)} collective-permute-done((bf16[1,1,1,48,1536]{4,3,2,1,0:T(8,128)(2,1)S(1)}, bf16[1,1,1,48,1536]{4,3,2,1,0:T(8,128)(2,1)S(1)}, u32[]{:S(2)}, u32[]{:S(2)}) %collective-permute-start.26) | collective-permute-done | bytes 147488 | tf_op jit(solution)/shard_map/ppermute | solution.py:142
  207.1 8.1 %collective-permute-done.22 = bf16[4,2,1,48,1536]{4,3,2,1,0:T(8,128)(2,1)S(1)} collective-permute-done((bf16[4,2,1,48,1536]{4,3,2,1,0:T(8,128)(2,1)S(1)}, bf16[4,2,1,48,1536]{4,3,2,1,0:T(8,128)(2,1)S(1)}, u32[]{:S(2)}, u32[]{:S(2)}) %collective-permute-start.22) | collective-permute-done | bytes 1179680 | tf_op jit(solution)/shard_map/ppermute | solution.py:142
  217.2 2.3 copy-done.7
  235.5 2.7 concatenate.89
  238.2 2.5 collective-permute-start.33
  240.6 2.4 collective-permute-start.35
  244.9 4.0 fusion.56
  251.6 2.4 collective-permute-start.37
  254.1 2.9 collective-permute-start.40
  258.4 6.0 %collective-permute-done.40 = bf16[1,48,768]{2,1,0:T(8,128)(2,1)S(1)} collective-permute-done((bf16[1,48,768]{2,1,0:T(8,128)(2,1)S(1)}, bf16[1,48,768]{2,1,0:T(8,128)(2,1)S(1)}, u32[]{:S(2)}, u32[]{:S(2)}) %collective-permute-start.40) | collective-permute-done | bytes 73760 | tf_op jit(solution)/shard_map/ppermute | solution.py:115
  269.4 5.6 %collective-permute-done.46 = f32[13,768]{1,0:T(8,128)S(1)} collective-permute-done((f32[13,768]{1,0:T(8,128)S(1)}, f32[13,768]{1,0:T(8,128)S(1)}, u32[]{:S(2)}, u32[]{:S(2)}) %collective-permute-start.46) | collective-permute-done | bytes 39968 | tf_op jit(solution)/shard_map/ppermute | solution.py:210
  280.8 9.4 %collective-permute-done.51 = f32[13,768]{1,0:T(8,128)S(1)} collective-permute-done((f32[13,768]{1,0:T(8,128)S(1)}, f32[13,768]{1,0:T(8,128)S(1)}, u32[]{:S(2)}, u32[]{:S(2)}) %collective-permute-start.51) | collective-permute-done | bytes 39968 | tf_op jit(solution)/shard_map/ppermute | solution.py:210
  295.7 3.1 fusion.64
  298.9 2.3 fusion.112
  301.5 2.1 collective-permute-start.56
  305.6 8.3 %collective-permute-done.57 = f32[13,768]{1,0:T(8,128)S(1)} collective-permute-done((f32[13,768]{1,0:T(8,128)S(1)}, f32[13,768]{1,0:T(8,128)S(1)}, u32[]{:S(2)}, u32[]{:S(2)}) %collective-permute-start.57) | collective-permute-done | bytes 39968 | tf_op jit(solution)/shard_map/ppermute | solution.py:210
  314.8 6.2 %collective-permute-done.58 = bf16[1,48,1536]{2,1,0:T(8,128)(2,1)S(1)} collective-permute-done((bf16[1,48,1536]{2,1,0:T(8,128)(2,1)S(1)}, bf16[1,48,1536]{2,1,0:T(8,128)(2,1)S(1)}, u32[]{:S(2)}, u32[]{:S(2)}) %collective-permute-start.58) | collective-permute-done | bytes 147488 | tf_op jit(solution)/shard_map/ppermute | solution.py:115
  324.7 14.2 %collective-permute-done.61 = bf16[4,48,1536]{2,1,0:T(8,128)(2,1)S(1)} collective-permute-done((bf16[4,48,1536]{2,1,0:T(8,128)(2,1)S(1)}, bf16[4,48,1536]{2,1,0:T(8,128)(2,1)S(1)}, u32[]{:S(2)}, u32[]{:S(2)}) %collective-permute-start.61) | collective-permute-done | bytes 589856 | tf_op jit(solution)/shard_map/ppermute | solution.py:115
  341.8 15.8 %collective-permute-done.62.refs_1_ = bf16[8,48,1536]{2,1,0:T(8,128)(2,1)S(1)} collective-permute-done((bf16[8,48,1536]{2,1,0:T(8,128)(2,1)S(1)}, bf16[8,48,1536]{2,1,0:T(8,128)(2,1)S(1)}, u32[]{:S(2)}, u32[]{:S(2)}) %collective-permute-start.62) | collective-permute-done | bytes 1179680 | tf_op jit(solution)/shard_map/ppermute | solution.py:115
  357.6 3.8 shard_map.282
  363.5 3.4 shard_map.283
  366.9 4.1 broadcast_select_fusion
  371.1 4.9 %collective-permute-done.64 = f32[768,768]{1,0:T(8,128)} collective-permute-done((f32[768,768]{1,0:T(8,128)}, f32[768,768]{1,0:T(8,128)}, u32[]{:S(2)}, u32[]{:S(2)}) %collective-permute-start.64) | collective-permute-done | bytes 2359328 | tf_op jit(solution)/shard_map/ppermute | solution.py:200
  376.0 4.8 %select_reduce_fusion = (f32[]{:T(128)}, f32[768,768]{1,0:T(8,128)}) fusion(f32[768,768]{1,0:T(8,128)} %collective-permute-done.64, f32[768,768]{1,0:T(8,128)} %copy-done.8, f32[768,768]{1,0:T(8,128)} %get-tuple-element.252, pred[]{:T(512)S(6)} %eq.66), kind=kLoop, calls=%fused_computation.58 | loop fusion | flops 2949119 | bytes 9437189 | tf_op jit(solution)/shard_map/jit(trace)/reduce_sum | solution.py:221
  381.5 6.5 %fusion.22 = f32[768,768]{1,0:T(8,128)S(1)} fusion(f32[768,768]{1,0:T(8,128)} %get-tuple-element.204, f32[]{:T(128)S(6)} %mul.408), kind=kOutput, calls=%fused_computation.54 | convolution fusion | flops 2722627584 | bytes 4718596 | tf_op jit(solution)/shard_map/dot_general | solution.py:217
  388.1 3.1 fusion.32
  391.1 3.2 fusion.186
  394.3 3.3 fusion.187
  397.7 3.3 fusion.52
  402.1 3.2 fusion.50
  405.3 3.4 fusion.188
  408.7 3.4 fusion.46
  413.1 3.2 fusion.44
  416.3 3.1 fusion.189
  419.5 3.6 fusion.40
  424.1 3.2 fusion.38
  432.2 3.7 collective-permute-done.66
  435.9 3.6 collective-permute-done.65
  (351 shorter events, 128.1 us)
Async XLA Ops:
  1.8 15.2 %collective-permute-start = (bf16[1,48,768]{2,1,0:T(8,128)(2,1)S(1)}, bf16[1,48,768]{2,1,0:T(8,128)(2,1)S(1)}, u32[]{:S(2)}, u32[]{:S(2)}) collective-permute-start(bf16[1,48,768]{2,1,0:T(8,128)(2,1)S(1)} %slice_bitcast_fusion.1), channel_id=1, source_target_pairs={{0,8},{2,10},{4,12},{6,14},{8,16},{10,18},{12,20},{14,22},{16,24},... | collective-permute-start | bytes 221192 | tf_op jit(solution)/shard_map/ppermute | solution.py:115
  5.7 11.3 %collective-permute-start.1 = (bf16[1,48,768]{2,1,0:T(8,128)(2,1)S(1)}, bf16[1,48,768]{2,1,0:T(8,128)(2,1)S(1)}, u32[]{:S(2)}, u32[]{:S(2)}) collective-permute-start(bf16[1,48,768]{2,1,0:T(8,128)(2,1)S(1)} %get-tuple-element.228), channel_id=1, source_target_pairs={{0,8},{2,10},{4,12},{6,14},{8,16},{10,18},{12,20},{14,22},{16,24},... | collective-permute-start | bytes 221192 | tf_op jit(solution)/shard_map/ppermute | solution.py:115
  17.0 6.9 %collective-permute-start.2 = (bf16[1,48,768]{2,1,0:T(8,128)(2,1)S(1)}, bf16[1,48,768]{2,1,0:T(8,128)(2,1)S(1)}, u32[]{:S(2)}, u32[]{:S(2)}) collective-permute-start(bf16[1,48,768]{2,1,0:T(8,128)(2,1)S(1)} %collective-permute-done), channel_id=1, source_target_pairs={{0,8},{2,10},{4,12},{6,14},{8,16},{10,18},{12,20},{14,22},{16,24},... | collective-permute-start | bytes 221192 | tf_op jit(solution)/shard_map/ppermute | solution.py:115
  18.6 7.0 %collective-permute-start.3 = (bf16[1,48,768]{2,1,0:T(8,128)(2,1)S(1)}, bf16[1,48,768]{2,1,0:T(8,128)(2,1)S(1)}, u32[]{:S(2)}, u32[]{:S(2)}) collective-permute-start(bf16[1,48,768]{2,1,0:T(8,128)(2,1)S(1)} %collective-permute-done.1), channel_id=1, source_target_pairs={{0,8},{2,10},{4,12},{6,14},{8,16},{10,18},{12,20},{14,22},{16,24},... | collective-permute-start | bytes 221192 | tf_op jit(solution)/shard_map/ppermute | solution.py:115
  18.7 19.8 %collective-permute-start.9 = (bf16[1,48,1536]{2,1,0:T(8,128)(2,1)S(1)}, bf16[1,48,1536]{2,1,0:T(8,128)(2,1)S(1)}, u32[]{:S(2)}, u32[]{:S(2)}) collective-permute-start(bf16[1,48,1536]{2,1,0:T(8,128)(2,1)S(1)} %bitcast.122), channel_id=1, source_target_pairs={{0,8},{2,10},{4,12},{6,14},{8,16},{10,18},{12,20},{14,22},{16,24},... | collective-permute-start | bytes 442376 | tf_op jit(solution)/shard_map/ppermute | solution.py:115
  20.5 18.0 %collective-permute-start.8 = (bf16[1,48,1536]{2,1,0:T(8,128)(2,1)S(1)}, bf16[1,48,1536]{2,1,0:T(8,128)(2,1)S(1)}, u32[]{:S(2)}, u32[]{:S(2)}) collective-permute-start(bf16[1,48,1536]{2,1,0:T(8,128)(2,1)S(1)} %bitcast.120), channel_id=1, source_target_pairs={{0,8},{2,10},{4,12},{6,14},{8,16},{10,18},{12,20},{14,22},{16,24},... | collective-permute-start | bytes 442376 | tf_op jit(solution)/shard_map/ppermute | solution.py:115
  27.8 6.6 %collective-permute-start.4 = (bf16[1,48,768]{2,1,0:T(8,128)(2,1)S(1)}, bf16[1,48,768]{2,1,0:T(8,128)(2,1)S(1)}, u32[]{:S(2)}, u32[]{:S(2)}) collective-permute-start(bf16[1,48,768]{2,1,0:T(8,128)(2,1)S(1)} %collective-permute-done.2), channel_id=1, source_target_pairs={{0,8},{2,10},{4,12},{6,14},{8,16},{10,18},{12,20},{14,22},{16,24},... | collective-permute-start | bytes 221192 | tf_op jit(solution)/shard_map/ppermute | solution.py:115
  28.4 6.3 %collective-permute-start.5 = (bf16[1,48,768]{2,1,0:T(8,128)(2,1)S(1)}, bf16[1,48,768]{2,1,0:T(8,128)(2,1)S(1)}, u32[]{:S(2)}, u32[]{:S(2)}) collective-permute-start(bf16[1,48,768]{2,1,0:T(8,128)(2,1)S(1)} %collective-permute-done.3), channel_id=1, source_target_pairs={{0,8},{2,10},{4,12},{6,14},{8,16},{10,18},{12,20},{14,22},{16,24},... | collective-permute-start | bytes 221192 | tf_op jit(solution)/shard_map/ppermute | solution.py:115
  34.8 6.8 %collective-permute-start.7 = (bf16[4,48,768]{2,1,0:T(8,128)(2,1)S(1)}, bf16[4,48,768]{2,1,0:T(8,128)(2,1)S(1)}, u32[]{:S(2)}, u32[]{:S(2)}) collective-permute-start(bf16[4,48,768]{2,1,0:T(8,128)(2,1)S(1)} %pad_maximum_fusion.6), channel_id=1, source_target_pairs={{0,4},{2,6},{4,0},{6,2},{8,12},{10,14},{12,8},{14,10},{16,20},{18,... | collective-permute-start | bytes 884744 | tf_op jit(solution)/shard_map/ppermute | solution.py:115
  36.4 6.7 %collective-permute-start.6 = (bf16[4,48,768]{2,1,0:T(8,128)(2,1)S(1)}, bf16[4,48,768]{2,1,0:T(8,128)(2,1)S(1)}, u32[]{:S(2)}, u32[]{:S(2)}) collective-permute-start(bf16[4,48,768]{2,1,0:T(8,128)(2,1)S(1)} %pad_maximum_fusion.5), channel_id=1, source_target_pairs={{0,2},{2,0},{4,6},{6,4},{8,10},{10,8},{12,14},{14,12},{16,18},{18,... | collective-permute-start | bytes 884744 | tf_op jit(solution)/shard_map/ppermute | solution.py:115
  43.1 8.3 %collective-permute-start.10 = (bf16[1,48,1536]{2,1,0:T(8,128)(2,1)S(1)}, bf16[1,48,1536]{2,1,0:T(8,128)(2,1)S(1)}, u32[]{:S(2)}, u32[]{:S(2)}) collective-permute-start(bf16[1,48,1536]{2,1,0:T(8,128)(2,1)S(1)} %collective-permute-done.8), channel_id=1, source_target_pairs={{0,8},{2,10},{4,12},{6,14},{8,16},{10,18},{12,20},{14,22},{16,24},... | collective-permute-start | bytes 442376 | tf_op jit(solution)/shard_map/ppermute | solution.py:115
  44.2 9.3 %collective-permute-start.14 = (bf16[1,48,1536]{2,1,0:T(8,128)(2,1)S(1)}, bf16[1,48,1536]{2,1,0:T(8,128)(2,1)S(1)}, u32[]{:S(2)}, u32[]{:S(2)}) collective-permute-start(bf16[1,48,1536]{2,1,0:T(8,128)(2,1)S(1)} %collective-permute-done.9), channel_id=1, source_target_pairs={{0,8},{2,10},{4,12},{6,14},{8,16},{10,18},{12,20},{14,22},{16,24},... | collective-permute-start | bytes 442376 | tf_op jit(solution)/shard_map/ppermute | solution.py:115
  48.9 11.6 %collective-permute-start.12 = (bf16[8,48,768]{2,1,0:T(8,128)(2,1)S(1)}, bf16[8,48,768]{2,1,0:T(8,128)(2,1)S(1)}, u32[]{:S(2)}, u32[]{:S(2)}) collective-permute-start(bf16[8,48,768]{2,1,0:T(8,128)(2,1)S(1)} %constant_dynamic-update-slice_fusion.5.refs_2_), channel_id=1, source_target_pairs={{0,2},{2,0},{4,6},{6,4},{8,10},{10,8},{12,14},{14,12},{16,18},{18,... | collective-permute-start | bytes 1769480 | tf_op jit(solution)/shard_map/ppermute | solution.py:115
  50.5 12.9 %collective-permute-start.11 = (bf16[8,48,768]{2,1,0:T(8,128)(2,1)S(1)}, bf16[8,48,768]{2,1,0:T(8,128)(2,1)S(1)}, u32[]{:S(2)}, u32[]{:S(2)}) collective-permute-start(bf16[8,48,768]{2,1,0:T(8,128)(2,1)S(1)} %constant_dynamic-update-slice_fusion.refs_0_), channel_id=1, source_target_pairs={{0,4},{2,6},{4,0},{6,2},{8,12},{10,14},{12,8},{14,10},{16,20},{18,... | collective-permute-start | bytes 1769480 | tf_op jit(solution)/shard_map/ppermute | solution.py:115
  51.4 7.0 %collective-permute-start.13 = (bf16[1,48,1536]{2,1,0:T(8,128)(2,1)S(1)}, bf16[1,48,1536]{2,1,0:T(8,128)(2,1)S(1)}, u32[]{:S(2)}, u32[]{:S(2)}) collective-permute-start(bf16[1,48,1536]{2,1,0:T(8,128)(2,1)S(1)} %collective-permute-done.10), channel_id=1, source_target_pairs={{0,8},{2,10},{4,12},{6,14},{8,16},{10,18},{12,20},{14,22},{16,24},... | collective-permute-start | bytes 442376 | tf_op jit(solution)/shard_map/ppermute | solution.py:115
  53.6 6.9 %collective-permute-start.15 = (bf16[1,48,1536]{2,1,0:T(8,128)(2,1)S(1)}, bf16[1,48,1536]{2,1,0:T(8,128)(2,1)S(1)}, u32[]{:S(2)}, u32[]{:S(2)}) collective-permute-start(bf16[1,48,1536]{2,1,0:T(8,128)(2,1)S(1)} %collective-permute-done.14), channel_id=1, source_target_pairs={{0,8},{2,10},{4,12},{6,14},{8,16},{10,18},{12,20},{14,22},{16,24},... | collective-permute-start | bytes 442376 | tf_op jit(solution)/shard_map/ppermute | solution.py:115
  63.5 12.9 %collective-permute-start.17 = (bf16[4,48,1536]{2,1,0:T(8,128)(2,1)S(1)}, bf16[4,48,1536]{2,1,0:T(8,128)(2,1)S(1)}, u32[]{:S(2)}, u32[]{:S(2)}) collective-permute-start(bf16[4,48,1536]{2,1,0:T(8,128)(2,1)S(1)} %pad_maximum_fusion.2), channel_id=1, source_target_pairs={{0,4},{2,6},{4,0},{6,2},{8,12},{10,14},{12,8},{14,10},{16,20},{18,... | collective-permute-start | bytes 1769480 | tf_op jit(solution)/shard_map/ppermute | solution.py:115
  64.6 15.2 %collective-permute-start.16 = (bf16[4,48,1536]{2,1,0:T(8,128)(2,1)S(1)}, bf16[4,48,1536]{2,1,0:T(8,128)(2,1)S(1)}, u32[]{:S(2)}, u32[]{:S(2)}) collective-permute-start(bf16[4,48,1536]{2,1,0:T(8,128)(2,1)S(1)} %pad_maximum_fusion.1), channel_id=1, source_target_pairs={{0,2},{2,0},{4,6},{6,4},{8,10},{10,8},{12,14},{14,12},{16,18},{18,... | collective-permute-start | bytes 1769480 | tf_op jit(solution)/shard_map/ppermute | solution.py:115
  79.8 26.5 %collective-permute-start.19 = (bf16[8,48,1536]{2,1,0:T(8,128)(2,1)S(1)}, bf16[8,48,1536]{2,1,0:T(8,128)(2,1)S(1)}, u32[]{:S(2)}, u32[]{:S(2)}) collective-permute-start(bf16[8,48,1536]{2,1,0:T(8,128)(2,1)S(1)} %constant_dynamic-update-slice_fusion.15.refs_0_), channel_id=1, source_target_pairs={{0,2},{2,0},{4,6},{6,4},{8,10},{10,8},{12,14},{14,12},{16,18},{18,... | collective-permute-start | bytes 3538952 | tf_op jit(solution)/shard_map/ppermute | solution.py:115
  79.9 26.4 %collective-permute-start.18 = (bf16[8,48,1536]{2,1,0:T(8,128)(2,1)S(1)}, bf16[8,48,1536]{2,1,0:T(8,128)(2,1)S(1)}, u32[]{:S(2)}, u32[]{:S(2)}) collective-permute-start(bf16[8,48,1536]{2,1,0:T(8,128)(2,1)S(1)} %constant_dynamic-update-slice_fusion.10.refs_0_), channel_id=1, source_target_pairs={{0,4},{2,6},{4,0},{6,2},{8,12},{10,14},{12,8},{14,10},{16,20},{18,... | collective-permute-start | bytes 3538952 | tf_op jit(solution)/shard_map/ppermute | solution.py:115
  121.9 26.3 %collective-permute-start.27 = (bf16[512,768]{1,0:T(8,128)(2,1)}, bf16[512,768]{1,0:T(8,128)(2,1)}, u32[]{:S(2)}, u32[]{:S(2)}) collective-permute-start(bf16[512,768]{1,0:T(8,128)(2,1)} %dynamic-slice_convert_fusion.4), channel_id=1, source_target_pairs={{0,1},{1,0},{2,3},{3,2},{4,5},{5,4},{6,7},{7,6},{8,9},{9,8},{10,11... | collective-permute-start | bytes 2359304 | tf_op jit(solution)/shard_map/ppermute | solution.py:200
  122.7 28.7 %collective-permute-start.20 = (bf16[4,2,1,48,1536]{4,3,2,1,0:T(8,128)(2,1)S(1)}, bf16[4,2,1,48,1536]{4,3,2,1,0:T(8,128)(2,1)S(1)}, u32[]{:S(2)}, u32[]{:S(2)}) collective-permute-start(bf16[4,2,1,48,1536]{4,3,2,1,0:T(8,128)(2,1)S(1)} %dynamic-slice_convert_fusion.2), channel_id=1, source_target_pairs={{0,2},{2,0},{4,6},{6,4},{8,10},{10,8},{12,14},{14,12},{16,18},{18,... | collective-permute-start | bytes 3538952 | tf_op jit(solution)/shard_map/ppermute | solution.py:142
  151.9 30.0 %collective-permute-start.21 = (bf16[4,1,1,48,1536]{4,3,2,1,0:T(8,128)(2,1)S(1)}, bf16[4,1,1,48,1536]{4,3,2,1,0:T(8,128)(2,1)S(1)}, u32[]{:S(2)}, u32[]{:S(2)}) collective-permute-start(bf16[4,1,1,48,1536]{4,3,2,1,0:T(8,128)(2,1)S(1)} %dynamic-slice_convert_fusion.7), channel_id=1, source_target_pairs={{0,4},{2,6},{4,0},{6,2},{8,12},{10,14},{12,8},{14,10},{16,20},{18,... | collective-permute-start | bytes 1769480 | tf_op jit(solution)/shard_map/ppermute | solution.py:142
  179.1 21.3 %collective-permute-start.29 = (f32[1024,384]{1,0:T(8,128)S(1)}, f32[1024,384]{1,0:T(8,128)S(1)}, u32[]{:S(2)}, u32[]{:S(2)}) collective-permute-start(f32[1024,384]{1,0:T(8,128)S(1)} %constant_dynamic-slice_fusion.4), channel_id=1, source_target_pairs={{0,1},{1,0},{2,3},{3,2},{4,5},{5,4},{6,7},{7,6},{8,9},{9,8},{10,11... | collective-permute-start | bytes 4718600 | tf_op jit(solution)/shard_map/ppermute | solution.py:200
  184.6 8.1 %collective-permute-start.24 = (bf16[1,1,1,48,1536]{4,3,2,1,0:T(8,128)(2,1)S(1)}, bf16[1,1,1,48,1536]{4,3,2,1,0:T(8,128)(2,1)S(1)}, u32[]{:S(2)}, u32[]{:S(2)}) collective-permute-start(bf16[1,1,1,48,1536]{4,3,2,1,0:T(8,128)(2,1)S(1)} %dynamic-slice_convert_fusion.10), channel_id=1, source_target_pairs={{0,8},{2,10},{4,12},{6,14},{8,16},{10,18},{12,20},{14,22},{16,24},... | collective-permute-start | bytes 442376 | tf_op jit(solution)/shard_map/ppermute | solution.py:142
  186.3 13.8 %collective-permute-start.28 = (bf16[512,768]{1,0:T(8,128)(2,1)S(1)}, bf16[512,768]{1,0:T(8,128)(2,1)S(1)}, u32[]{:S(2)}, u32[]{:S(2)}) collective-permute-start(bf16[512,768]{1,0:T(8,128)(2,1)S(1)} %dynamic-slice_convert_fusion.3), channel_id=1, source_target_pairs={{0,1},{1,0},{2,3},{3,2},{4,5},{5,4},{6,7},{7,6},{8,9},{9,8},{10,11... | collective-permute-start | bytes 2359304 | tf_op jit(solution)/shard_map/ppermute | solution.py:200
  186.9 28.2 %collective-permute-start.22 = (bf16[4,2,1,48,1536]{4,3,2,1,0:T(8,128)(2,1)S(1)}, bf16[4,2,1,48,1536]{4,3,2,1,0:T(8,128)(2,1)S(1)}, u32[]{:S(2)}, u32[]{:S(2)}) collective-permute-start(bf16[4,2,1,48,1536]{4,3,2,1,0:T(8,128)(2,1)S(1)} %dynamic-slice_convert_fusion.1), channel_id=1, source_target_pairs={{0,2},{2,0},{4,6},{6,4},{8,10},{10,8},{12,14},{14,12},{16,18},{18,... | collective-permute-start | bytes 3538952 | tf_op jit(solution)/shard_map/ppermute | solution.py:142
  188.5 27.9 %collective-permute-start.23 = (bf16[4,1,2,48,1536]{4,3,2,1,0:T(8,128)(2,1)S(1)}, bf16[4,1,2,48,1536]{4,3,2,1,0:T(8,128)(2,1)S(1)}, u32[]{:S(2)}, u32[]{:S(2)}) collective-permute-start(bf16[4,1,2,48,1536]{4,3,2,1,0:T(8,128)(2,1)S(1)} %dynamic-slice_convert_fusion), channel_id=1, source_target_pairs={{0,4},{2,6},{4,0},{6,2},{8,12},{10,14},{12,8},{14,10},{16,20},{18,... | collective-permute-start | bytes 3538952 | tf_op jit(solution)/shard_map/ppermute | solution.py:142
  192.7 7.3 %collective-permute-start.25 = (bf16[1,1,1,48,1536]{4,3,2,1,0:T(8,128)(2,1)S(1)}, bf16[1,1,1,48,1536]{4,3,2,1,0:T(8,128)(2,1)S(1)}, u32[]{:S(2)}, u32[]{:S(2)}) collective-permute-start(bf16[1,1,1,48,1536]{4,3,2,1,0:T(8,128)(2,1)S(1)} %add_convert_fusion.7), channel_id=1, source_target_pairs={{0,8},{2,10},{4,12},{6,14},{8,16},{10,18},{12,20},{14,22},{16,24},... | collective-permute-start | bytes 442376 | tf_op jit(solution)/shard_map/ppermute | solution.py:142
  200.1 7.0 %collective-permute-start.26 = (bf16[1,1,1,48,1536]{4,3,2,1,0:T(8,128)(2,1)S(1)}, bf16[1,1,1,48,1536]{4,3,2,1,0:T(8,128)(2,1)S(1)}, u32[]{:S(2)}, u32[]{:S(2)}) collective-permute-start(bf16[1,1,1,48,1536]{4,3,2,1,0:T(8,128)(2,1)S(1)} %add_convert_fusion.6), channel_id=1, source_target_pairs={{0,8},{2,10},{4,12},{6,14},{8,16},{10,18},{12,20},{14,22},{16,24},... | collective-permute-start | bytes 442376 | tf_op jit(solution)/shard_map/ppermute | solution.py:142
  222.5 15.7 %collective-permute-start.32 = (bf16[1,48,768]{2,1,0:T(8,128)(2,1)}, bf16[1,48,768]{2,1,0:T(8,128)(2,1)}, u32[]{:S(2)}, u32[]{:S(2)}) collective-permute-start(bf16[1,48,768]{2,1,0:T(8,128)(2,1)} %slice_bitcast_fusion), channel_id=1, source_target_pairs={{0,8},{2,10},{4,12},{6,14},{8,16},{10,18},{12,20},{14,22},{16,24},... | collective-permute-start | bytes 221192 | tf_op jit(solution)/shard_map/ppermute | solution.py:115
  225.0 19.9 %collective-permute-start.36 = (bf16[512,768]{1,0:T(8,128)(2,1)}, bf16[512,768]{1,0:T(8,128)(2,1)}, u32[]{:S(2)}, u32[]{:S(2)}) collective-permute-start(bf16[512,768]{1,0:T(8,128)(2,1)} %fusion.57), channel_id=1, source_target_pairs={{0,1},{1,0},{2,3},{3,2},{4,5},{5,4},{6,7},{7,6},{8,9},{9,8},{10,11... | collective-permute-start | bytes 2359304 | tf_op jit(solution)/shard_map/ppermute | solution.py:200
  225.9 23.0 %collective-permute-start.31 = (bf16[4,1,1,48,1536]{4,3,2,1,0:T(8,128)(2,1)}, bf16[4,1,1,48,1536]{4,3,2,1,0:T(8,128)(2,1)}, u32[]{:S(2)}, u32[]{:S(2)}) collective-permute-start(bf16[4,1,1,48,1536]{4,3,2,1,0:T(8,128)(2,1)} %dynamic-slice_convert_fusion.5), channel_id=1, source_target_pairs={{0,2},{2,0},{4,6},{6,4},{8,10},{10,8},{12,14},{14,12},{16,18},{18,... | collective-permute-start | bytes 1769480 | tf_op jit(solution)/shard_map/ppermute | solution.py:142
  226.4 22.4 %collective-permute-start.30 = (bf16[4,1,1,48,1536]{4,3,2,1,0:T(8,128)(2,1)}, bf16[4,1,1,48,1536]{4,3,2,1,0:T(8,128)(2,1)}, u32[]{:S(2)}, u32[]{:S(2)}) collective-permute-start(bf16[4,1,1,48,1536]{4,3,2,1,0:T(8,128)(2,1)} %dynamic-slice_convert_fusion.6), channel_id=1, source_target_pairs={{0,4},{2,6},{4,0},{6,2},{8,12},{10,14},{12,8},{14,10},{16,20},{18,... | collective-permute-start | bytes 1769480 | tf_op jit(solution)/shard_map/ppermute | solution.py:142
  229.1 11.5 %collective-permute-start.34 = (bf16[1,48,768]{2,1,0:T(8,128)(2,1)}, bf16[1,48,768]{2,1,0:T(8,128)(2,1)}, u32[]{:S(2)}, u32[]{:S(2)}) collective-permute-start(bf16[1,48,768]{2,1,0:T(8,128)(2,1)} %get-tuple-element.214), channel_id=1, source_target_pairs={{0,8},{2,10},{4,12},{6,14},{8,16},{10,18},{12,20},{14,22},{16,24},... | collective-permute-start | bytes 221192 | tf_op jit(solution)/shard_map/ppermute | solution.py:115
  238.2 10.7 %collective-permute-start.33 = (bf16[1,48,768]{2,1,0:T(8,128)(2,1)}, bf16[1,48,768]{2,1,0:T(8,128)(2,1)S(1)}, u32[]{:S(2)}, u32[]{:S(2)}) collective-permute-start(bf16[1,48,768]{2,1,0:T(8,128)(2,1)} %collective-permute-done.32), channel_id=1, source_target_pairs={{0,8},{2,10},{4,12},{6,14},{8,16},{10,18},{12,20},{14,22},{16,24},... | collective-permute-start | bytes 221192 | tf_op jit(solution)/shard_map/ppermute | solution.py:115
  240.6 8.2 %collective-permute-start.35 = (bf16[1,48,768]{2,1,0:T(8,128)(2,1)}, bf16[1,48,768]{2,1,0:T(8,128)(2,1)S(1)}, u32[]{:S(2)}, u32[]{:S(2)}) collective-permute-start(bf16[1,48,768]{2,1,0:T(8,128)(2,1)} %collective-permute-done.34), channel_id=1, source_target_pairs={{0,8},{2,10},{4,12},{6,14},{8,16},{10,18},{12,20},{14,22},{16,24},... | collective-permute-start | bytes 221192 | tf_op jit(solution)/shard_map/ppermute | solution.py:115
  251.3 7.1 %collective-permute-start.39 = (bf16[1,48,768]{2,1,0:T(8,128)(2,1)S(1)}, bf16[1,48,768]{2,1,0:T(8,128)(2,1)S(1)}, u32[]{:S(2)}, u32[]{:S(2)}) collective-permute-start(bf16[1,48,768]{2,1,0:T(8,128)(2,1)S(1)} %collective-permute-done.33), channel_id=1, source_target_pairs={{0,8},{2,10},{4,12},{6,14},{8,16},{10,18},{12,20},{14,22},{16,24},... | collective-permute-start | bytes 221192 | tf_op jit(solution)/shard_map/ppermute | solution.py:115
  251.5 12.9 %collective-permute-start.38 = (bf16[1,1,1,48,1536]{4,3,2,1,0:T(8,128)(2,1)S(1)}, bf16[1,1,1,48,1536]{4,3,2,1,0:T(8,128)(2,1)S(1)}, u32[]{:S(2)}, u32[]{:S(2)}) collective-permute-start(bf16[1,1,1,48,1536]{4,3,2,1,0:T(8,128)(2,1)S(1)} %dynamic-slice_convert_fusion.8), channel_id=1, source_target_pairs={{0,8},{2,10},{4,12},{6,14},{8,16},{10,18},{12,20},{14,22},{16,24},... | collective-permute-start | bytes 442376 | tf_op jit(solution)/shard_map/ppermute | solution.py:142
  251.6 12.8 %collective-permute-start.37 = (bf16[1,1,1,48,1536]{4,3,2,1,0:T(8,128)(2,1)S(1)}, bf16[1,1,1,48,1536]{4,3,2,1,0:T(8,128)(2,1)S(1)}, u32[]{:S(2)}, u32[]{:S(2)}) collective-permute-start(bf16[1,1,1,48,1536]{4,3,2,1,0:T(8,128)(2,1)S(1)} %dynamic-slice_convert_fusion.9), channel_id=1, source_target_pairs={{0,8},{2,10},{4,12},{6,14},{8,16},{10,18},{12,20},{14,22},{16,24},... | collective-permute-start | bytes 442376 | tf_op jit(solution)/shard_map/ppermute | solution.py:142
  254.1 10.2 %collective-permute-start.40 = (bf16[1,48,768]{2,1,0:T(8,128)(2,1)S(1)}, bf16[1,48,768]{2,1,0:T(8,128)(2,1)S(1)}, u32[]{:S(2)}, u32[]{:S(2)}) collective-permute-start(bf16[1,48,768]{2,1,0:T(8,128)(2,1)S(1)} %collective-permute-done.35), channel_id=1, source_target_pairs={{0,8},{2,10},{4,12},{6,14},{8,16},{10,18},{12,20},{14,22},{16,24},... | collective-permute-start | bytes 221192 | tf_op jit(solution)/shard_map/ppermute | solution.py:115
  265.4 11.8 %collective-permute-start.45 = (bf16[4,48,768]{2,1,0:T(8,128)(2,1)S(1)}, bf16[4,48,768]{2,1,0:T(8,128)(2,1)S(1)}, u32[]{:S(2)}, u32[]{:S(2)}) collective-permute-start(bf16[4,48,768]{2,1,0:T(8,128)(2,1)S(1)} %pad_maximum_fusion.8), channel_id=1, source_target_pairs={{0,4},{2,6},{4,0},{6,2},{8,12},{10,14},{12,8},{14,10},{16,20},{18,... | collective-permute-start | bytes 884744 | tf_op jit(solution)/shard_map/ppermute | solution.py:115
  267.1 10.2 %collective-permute-start.44 = (bf16[4,48,768]{2,1,0:T(8,128)(2,1)S(1)}, bf16[4,48,768]{2,1,0:T(8,128)(2,1)S(1)}, u32[]{:S(2)}, u32[]{:S(2)}) collective-permute-start(bf16[4,48,768]{2,1,0:T(8,128)(2,1)S(1)} %pad_maximum_fusion.7), channel_id=1, source_target_pairs={{0,2},{2,0},{4,6},{6,4},{8,10},{10,8},{12,14},{14,12},{16,18},{18,... | collective-permute-start | bytes 884744 | tf_op jit(solution)/shard_map/ppermute | solution.py:115
  268.7 7.0 %collective-permute-start.43 = (bf16[1,1,1,48,1536]{4,3,2,1,0:T(8,128)(2,1)S(1)}, bf16[1,1,1,48,1536]{4,3,2,1,0:T(8,128)(2,1)S(1)}, u32[]{:S(2)}, u32[]{:S(2)}) collective-permute-start(bf16[1,1,1,48,1536]{4,3,2,1,0:T(8,128)(2,1)S(1)} %add_convert_fusion.4), channel_id=1, source_target_pairs={{0,8},{2,10},{4,12},{6,14},{8,16},{10,18},{12,20},{14,22},{16,24},... | collective-permute-start | bytes 442376 | tf_op jit(solution)/shard_map/ppermute | solution.py:142
  268.7 8.5 %collective-permute-start.42 = (bf16[1,1,1,48,1536]{4,3,2,1,0:T(8,128)(2,1)S(1)}, bf16[1,1,1,48,1536]{4,3,2,1,0:T(8,128)(2,1)S(1)}, u32[]{:S(2)}, u32[]{:S(2)}) collective-permute-start(bf16[1,1,1,48,1536]{4,3,2,1,0:T(8,128)(2,1)S(1)} %add_convert_fusion.5), channel_id=1, source_target_pairs={{0,8},{2,10},{4,12},{6,14},{8,16},{10,18},{12,20},{14,22},{16,24},... | collective-permute-start | bytes 442376 | tf_op jit(solution)/shard_map/ppermute | solution.py:142
  268.8 6.2 %collective-permute-start.46 = (f32[13,768]{1,0:T(8,128)S(1)}, f32[13,768]{1,0:T(8,128)S(1)}, u32[]{:S(2)}, u32[]{:S(2)}) collective-permute-start(f32[13,768]{1,0:T(8,128)S(1)} %add.473), channel_id=1, source_target_pairs={{0,2},{2,0},{4,6},{6,4},{8,10},{10,8},{12,14},{14,12},{16,18},{18,... | collective-permute-start | bytes 119816 | tf_op jit(solution)/shard_map/ppermute | solution.py:210
  277.3 12.8 %collective-permute-start.49 = (bf16[8,48,768]{2,1,0:T(8,128)(2,1)S(1)}, bf16[8,48,768]{2,1,0:T(8,128)(2,1)S(1)}, u32[]{:S(2)}, u32[]{:S(2)}) collective-permute-start(bf16[8,48,768]{2,1,0:T(8,128)(2,1)S(1)} %constant_dynamic-update-slice_fusion.20.refs_0_), channel_id=1, source_target_pairs={{0,4},{2,6},{4,0},{6,2},{8,12},{10,14},{12,8},{14,10},{16,20},{18,... | collective-permute-start | bytes 1769480 | tf_op jit(solution)/shard_map/ppermute | solution.py:115
  278.8 11.5 %collective-permute-start.50 = (bf16[8,48,768]{2,1,0:T(8,128)(2,1)S(1)}, bf16[8,48,768]{2,1,0:T(8,128)(2,1)S(1)}, u32[]{:S(2)}, u32[]{:S(2)}) collective-permute-start(bf16[8,48,768]{2,1,0:T(8,128)(2,1)S(1)} %constant_dynamic-update-slice_fusion.25.refs_2_), channel_id=1, source_target_pairs={{0,2},{2,0},{4,6},{6,4},{8,10},{10,8},{12,14},{14,12},{16,18},{18,... | collective-permute-start | bytes 1769480 | tf_op jit(solution)/shard_map/ppermute | solution.py:115
  279.4 10.7 %collective-permute-start.48 = (bf16[1,1,1,48,1536]{4,3,2,1,0:T(8,128)(2,1)S(1)}, bf16[1,1,1,48,1536]{4,3,2,1,0:T(8,128)(2,1)S(1)}, u32[]{:S(2)}, u32[]{:S(2)}) collective-permute-start(bf16[1,1,1,48,1536]{4,3,2,1,0:T(8,128)(2,1)S(1)} %add_convert_fusion.2), channel_id=1, source_target_pairs={{0,8},{2,10},{4,12},{6,14},{8,16},{10,18},{12,20},{14,22},{16,24},... | collective-permute-start | bytes 442376 | tf_op jit(solution)/shard_map/ppermute | solution.py:142
  279.5 10.6 %collective-permute-start.47 = (bf16[1,1,1,48,1536]{4,3,2,1,0:T(8,128)(2,1)S(1)}, bf16[1,1,1,48,1536]{4,3,2,1,0:T(8,128)(2,1)S(1)}, u32[]{:S(2)}, u32[]{:S(2)}) collective-permute-start(bf16[1,1,1,48,1536]{4,3,2,1,0:T(8,128)(2,1)S(1)} %add_convert_fusion.3), channel_id=1, source_target_pairs={{0,8},{2,10},{4,12},{6,14},{8,16},{10,18},{12,20},{14,22},{16,24},... | collective-permute-start | bytes 442376 | tf_op jit(solution)/shard_map/ppermute | solution.py:142
  280.2 9.9 %collective-permute-start.51 = (f32[13,768]{1,0:T(8,128)S(1)}, f32[13,768]{1,0:T(8,128)S(1)}, u32[]{:S(2)}, u32[]{:S(2)}) collective-permute-start(f32[13,768]{1,0:T(8,128)S(1)} %add.476), channel_id=1, source_target_pairs={{0,4},{2,6},{4,0},{6,2},{8,12},{10,14},{12,8},{14,10},{16,20},{18,... | collective-permute-start | bytes 119816 | tf_op jit(solution)/shard_map/ppermute | solution.py:210
  290.3 10.8 %collective-permute-start.54 = (f32[13,768]{1,0:T(8,128)S(1)}, f32[13,768]{1,0:T(8,128)S(1)}, u32[]{:S(2)}, u32[]{:S(2)}) collective-permute-start(f32[13,768]{1,0:T(8,128)S(1)} %add.481), channel_id=1, source_target_pairs={{0,8},{2,10},{4,12},{6,14},{8,0},{10,2},{12,4},{14,6},{16,24},{18,... | collective-permute-start | bytes 119816 | tf_op jit(solution)/shard_map/ppermute | solution.py:210
  291.3 9.8 %collective-permute-start.52 = (bf16[1,48,1536]{2,1,0:T(8,128)(2,1)S(1)}, bf16[1,48,1536]{2,1,0:T(8,128)(2,1)S(1)}, u32[]{:S(2)}, u32[]{:S(2)}) collective-permute-start(bf16[1,48,1536]{2,1,0:T(8,128)(2,1)S(1)} %get-tuple-element.206), channel_id=1, source_target_pairs={{0,8},{2,10},{4,12},{6,14},{8,16},{10,18},{12,20},{14,22},{16,24},... | collective-permute-start | bytes 442376 | tf_op jit(solution)/shard_map/ppermute | solution.py:115
  294.2 7.1 %collective-permute-start.53 = (bf16[1,48,1536]{2,1,0:T(8,128)(2,1)S(1)}, bf16[1,48,1536]{2,1,0:T(8,128)(2,1)S(1)}, u32[]{:S(2)}, u32[]{:S(2)}) collective-permute-start(bf16[1,48,1536]{2,1,0:T(8,128)(2,1)S(1)} %get-tuple-element.210), channel_id=1, source_target_pairs={{0,8},{2,10},{4,12},{6,14},{8,16},{10,18},{12,20},{14,22},{16,24},... | collective-permute-start | bytes 442376 | tf_op jit(solution)/shard_map/ppermute | solution.py:115
  301.2 12.7 %collective-permute-start.55 = (bf16[1,48,1536]{2,1,0:T(8,128)(2,1)S(1)}, bf16[1,48,1536]{2,1,0:T(8,128)(2,1)S(1)}, u32[]{:S(2)}, u32[]{:S(2)}) collective-permute-start(bf16[1,48,1536]{2,1,0:T(8,128)(2,1)S(1)} %collective-permute-done.52), channel_id=1, source_target_pairs={{0,8},{2,10},{4,12},{6,14},{8,16},{10,18},{12,20},{14,22},{16,24},... | collective-permute-start | bytes 442376 | tf_op jit(solution)/shard_map/ppermute | solution.py:115
  301.5 12.5 %collective-permute-start.56 = (bf16[1,48,1536]{2,1,0:T(8,128)(2,1)S(1)}, bf16[1,48,1536]{2,1,0:T(8,128)(2,1)S(1)}, u32[]{:S(2)}, u32[]{:S(2)}) collective-permute-start(bf16[1,48,1536]{2,1,0:T(8,128)(2,1)S(1)} %collective-permute-done.53), channel_id=1, source_target_pairs={{0,8},{2,10},{4,12},{6,14},{8,16},{10,18},{12,20},{14,22},{16,24},... | collective-permute-start | bytes 442376 | tf_op jit(solution)/shard_map/ppermute | solution.py:115
  303.6 10.3 %collective-permute-start.57 = (f32[13,768]{1,0:T(8,128)S(1)}, f32[13,768]{1,0:T(8,128)S(1)}, u32[]{:S(2)}, u32[]{:S(2)}) collective-permute-start(f32[13,768]{1,0:T(8,128)S(1)} %add.482), channel_id=1, source_target_pairs={{0,16},{2,18},{4,20},{6,22},{8,24},{10,26},{12,28},{14,30},{16,0},... | collective-permute-start | bytes 119816 | tf_op jit(solution)/shard_map/ppermute | solution.py:210
  314.0 6.9 %collective-permute-start.58 = (bf16[1,48,1536]{2,1,0:T(8,128)(2,1)S(1)}, bf16[1,48,1536]{2,1,0:T(8,128)(2,1)S(1)}, u32[]{:S(2)}, u32[]{:S(2)}) collective-permute-start(bf16[1,48,1536]{2,1,0:T(8,128)(2,1)S(1)} %collective-permute-done.55), channel_id=1, source_target_pairs={{0,8},{2,10},{4,12},{6,14},{8,16},{10,18},{12,20},{14,22},{16,24},... | collective-permute-start | bytes 442376 | tf_op jit(solution)/shard_map/ppermute | solution.py:115
  314.0 8.5 %collective-permute-start.59 = (bf16[1,48,1536]{2,1,0:T(8,128)(2,1)S(1)}, bf16[1,48,1536]{2,1,0:T(8,128)(2,1)S(1)}, u32[]{:S(2)}, u32[]{:S(2)}) collective-permute-start(bf16[1,48,1536]{2,1,0:T(8,128)(2,1)S(1)} %collective-permute-done.56), channel_id=1, source_target_pairs={{0,8},{2,10},{4,12},{6,14},{8,16},{10,18},{12,20},{14,22},{16,24},... | collective-permute-start | bytes 442376 | tf_op jit(solution)/shard_map/ppermute | solution.py:115
  322.7 16.3 %collective-permute-start.61 = (bf16[4,48,1536]{2,1,0:T(8,128)(2,1)S(1)}, bf16[4,48,1536]{2,1,0:T(8,128)(2,1)S(1)}, u32[]{:S(2)}, u32[]{:S(2)}) collective-permute-start(bf16[4,48,1536]{2,1,0:T(8,128)(2,1)S(1)} %pad_maximum_fusion.4), channel_id=1, source_target_pairs={{0,4},{2,6},{4,0},{6,2},{8,12},{10,14},{12,8},{14,10},{16,20},{18,... | collective-permute-start | bytes 1769480 | tf_op jit(solution)/shard_map/ppermute | solution.py:115
  324.0 16.2 %collective-permute-start.60 = (bf16[4,48,1536]{2,1,0:T(8,128)(2,1)S(1)}, bf16[4,48,1536]{2,1,0:T(8,128)(2,1)S(1)}, u32[]{:S(2)}, u32[]{:S(2)}) collective-permute-start(bf16[4,48,1536]{2,1,0:T(8,128)(2,1)S(1)} %pad_maximum_fusion.3), channel_id=1, source_target_pairs={{0,2},{2,0},{4,6},{6,4},{8,10},{10,8},{12,14},{14,12},{16,18},{18,... | collective-permute-start | bytes 1769480 | tf_op jit(solution)/shard_map/ppermute | solution.py:115
  340.2 17.4 %collective-permute-start.62 = (bf16[8,48,1536]{2,1,0:T(8,128)(2,1)S(1)}, bf16[8,48,1536]{2,1,0:T(8,128)(2,1)S(1)}, u32[]{:S(2)}, u32[]{:S(2)}) collective-permute-start(bf16[8,48,1536]{2,1,0:T(8,128)(2,1)S(1)} %constant_dynamic-update-slice_fusion.30.refs_0_), channel_id=1, source_target_pairs={{0,4},{2,6},{4,0},{6,2},{8,12},{10,14},{12,8},{14,10},{16,20},{18,... | collective-permute-start | bytes 3538952 | tf_op jit(solution)/shard_map/ppermute | solution.py:115
  341.1 22.4 %collective-permute-start.63 = (bf16[8,48,1536]{2,1,0:T(8,128)(2,1)S(1)}, bf16[8,48,1536]{2,1,0:T(8,128)(2,1)}, u32[]{:S(2)}, u32[]{:S(2)}) collective-permute-start(bf16[8,48,1536]{2,1,0:T(8,128)(2,1)S(1)} %constant_dynamic-update-slice_fusion.35.refs_0_), channel_id=1, source_target_pairs={{0,2},{2,0},{4,6},{6,4},{8,10},{10,8},{12,14},{14,12},{16,18},{18,... | collective-permute-start | bytes 3538952 | tf_op jit(solution)/shard_map/ppermute | solution.py:115
  430.9 8.6 %collective-permute-start.65 = (f32[48,768]{1,0:T(8,128)S(1)}, f32[48,768]{1,0:T(8,128)S(1)}, u32[]{:S(2)}, u32[]{:S(2)}) collective-permute-start(f32[48,768]{1,0:T(8,128)S(1)} %get-tuple-element.240), channel_id=1, source_target_pairs={{0,2},{1,3},{2,0},{3,1},{4,6},{5,7},{6,4},{7,5},{8,10},{9,11},{10,... | collective-permute-start | bytes 442376 | tf_op jit(solution)/shard_map/ppermute | solution.py:644
  (52 other events, 390.2 us)

commit v4 on v3

--- a/solution.py
+++ b/solution.py
@@ -16,10 +16,11 @@
 NS_STEPS = 5
 STEP = 10
 QUERY_TILE = 512
+FEED_TILE = 512
+NEWTON_TILE = 256
 VMEM_LIMIT = 48 * 1024 * 1024
 
 
-HIGH = lax.Precision.HIGH
 X_FIRST = (0, 1, 2)
 Z_THEN_X = (2, 0, 1)
 Z_THEN_Y = (2, 1, 0)
@@ -211,27 +212,6 @@
         value = value + got
         distance *= 2
     return value
-
-
-def product(left, right):
-    return jnp.dot(left, right, precision=HIGH, preferred_element_type=jnp.float32)
-
-
-def newton_rows(gram, first_row, rows):
-    factor = 1.0 / (jnp.sqrt(jnp.trace(gram)) + SCALE_EPS)
-    square = gram * (factor * factor)
-    identity = jnp.eye(D, dtype=jnp.float32)
-    kept = lax.dynamic_slice_in_dim(identity, first_row, rows, 0) * factor
-    for iteration in range(NS_STEPS - 1):
-        step = (
-            POLY_ONE * identity + POLY_TWO * square + POLY_THREE * product(square, square)
-        )
-        kept = product(kept, step) if iteration else lax.dynamic_slice_in_dim(
-            step, first_row, rows, 0
-        ) * factor
-        square = product(product(step, square), step)
-    once = product(kept, square)
-    return POLY_ONE * kept + POLY_TWO * once + POLY_THREE * product(once, square)
 
 
 def rows_product(left, right):
@@ -376,6 +356,151 @@
     )(triple_rows, cosines, sines, up_rows, first_slots(segments)[None])
 
 
+def split(value):
+    high = value.astype(jnp.bfloat16)
+    return high, (value - high.astype(jnp.float32)).astype(jnp.bfloat16)
+
+
+def newton_kernel(first_ref, second_ref, rows_ref, out_ref, square, square_parts, step, left):
+    wanted = rows_ref.shape[0]
+    tiles = D // NEWTON_TILE
+
+    def store_split(ref, rows, columns, value):
+        high, low = split(value)
+        ref[0, rows, columns] = high
+        ref[1, rows, columns] = low
+
+    def product(left_ref, rows, right_ref, columns):
+        left_high, left_low = left_ref[0, rows, :], left_ref[1, rows, :]
+        right_high, right_low = right_ref[0, :, columns], right_ref[1, :, columns]
+        return matmul(left_high, right_high) + (
+            matmul(left_high, right_low) + matmul(left_low, right_high)
+        )
+
+    def part(tile):
+        return slice(tile * NEWTON_TILE, (tile + 1) * NEWTON_TILE)
+
+    def both(store, row, column, value):
+        store(part(row), part(column), value)
+        if row != column:
+            store(part(column), part(row), value.T)
+
+    def put(rows, columns, value):
+        square[rows, columns] = value
+        store_split(square_parts, rows, columns, value)
+
+    def diagonal(size):
+        return lax.broadcasted_iota(jnp.int32, (size, size), 0) == lax.broadcasted_iota(
+            jnp.int32, (size, size), 1
+        )
+
+    whole, extra = slice(None), slice(D, D + wanted)
+    gram = first_ref[...] + second_ref[...]
+    trace = jnp.sum(jnp.where(diagonal(D), gram, 0.0), axis=0, keepdims=True)
+    trace = jnp.sum(trace, axis=1, keepdims=True)
+    factor = 1.0 / (jnp.sqrt(trace) + SCALE_EPS)
+    put(whole, whole, gram * (factor * factor))
+    rows_value = rows_ref[...] * factor
+    store_split(left, extra, whole, rows_value)
+    identity = jnp.where(diagonal(NEWTON_TILE), POLY_ONE, 0.0)
+    for _ in range(NS_STEPS - 1):
+        for column in range(tiles):
+            top = slice(0, (column + 1) * NEWTON_TILE)
+            value = POLY_TWO * square[top, part(column)] + POLY_THREE * product(
+                square_parts, top, square_parts, part(column)
+            )
+            for row in range(column + 1):
+                block = value[part(row)]
+                if row == column:
+                    block = block + identity
+                both(functools.partial(store_split, step), row, column, block)
+        for column in range(tiles):
+            top = slice(0, (column + 1) * NEWTON_TILE)
+            value = product(step, top, square_parts, part(column))
+            for row in range(column + 1):
+                both(functools.partial(store_split, left), row, column, value[part(row)])
+        rows_parts = []
+        for column in range(tiles):
+            top = slice(0, (column + 1) * NEWTON_TILE)
+            value = product(left, top, step, part(column))
+            rows_parts.append(product(left, extra, step, part(column)))
+            for row in range(column + 1):
+                both(put, row, column, value[part(row)])
+        rows_value = jnp.concatenate(rows_parts, 1)
+        store_split(left, extra, whole, rows_value)
+
+    def by_square():
+        return jnp.concatenate(
+            [product(left, extra, square_parts, part(column)) for column in range(tiles)], 1
+        )
+
+    once = by_square()
+    store_split(left, extra, whole, once)
+    out_ref[...] = POLY_ONE * rows_value + POLY_TWO * once + POLY_THREE * by_square()
+
+
+def newton_rows(own_gram, other_gram, first_row, rows):
+    wanted = -(-rows // 16) * 16
+    index = lax.broadcasted_iota(jnp.int32, (wanted, D), 0)
+    chosen = lax.broadcasted_iota(jnp.int32, (wanted, D), 1) == index + first_row
+    rows_out = pl.pallas_call(
+        newton_kernel,
+        in_specs=[pl.BlockSpec(memory_space=pltpu.VMEM)] * 3,
+        out_specs=pl.BlockSpec(memory_space=pltpu.VMEM),
+        out_shape=jax.ShapeDtypeStruct((wanted, D), jnp.float32),
+        scratch_shapes=[
+            pltpu.VMEM((D, D), jnp.float32),
+            pltpu.VMEM((2, D, D), jnp.bfloat16),
+            pltpu.VMEM((2, D, D), jnp.bfloat16),
+            pltpu.VMEM((2, D + wanted, D), jnp.bfloat16),
+        ],
+        compiler_params=pltpu.CompilerParams(vmem_limit_bytes=VMEM_LIMIT),
+        cost_estimate=pl.CostEstimate(
+            flops=(NS_STEPS - 1) * 12 * D * D * D, bytes_accessed=8 * D * D, transcendentals=0
+        ),
+    )(own_gram, other_gram, chosen.astype(jnp.float32))
+    return rows_out[:rows]
+
+
+def feed_kernel(
+    norm_ref, upstream_ref, widen_ref, narrow_ref, bias_ref, activated_ref, back_ref, sum_ref
+):
+    widened = matmul(norm_ref[...], widen_ref[...]) + bias_ref[...]
+    incoming = matmul(upstream_ref[...], narrow_ref[...])
+    area = 0.5 + 0.5 * lax.erf(widened * math.sqrt(0.5))
+    density = jnp.exp(widened * widened * -0.5) * (1.0 / math.sqrt(2.0 * math.pi))
+    activated_ref[...] = (widened * area).astype(jnp.bfloat16)
+    back = (incoming * (area + widened * density)).astype(jnp.bfloat16)
+    back_ref[...] = back
+    sum_ref[...] = jnp.sum(back.astype(jnp.float32), axis=0, keepdims=True)
+
+
+def feed_forward(norm, upstream, widen, narrow, bias):
+    length, width = norm.shape
+    hidden = widen.shape[1]
+
+    def whole():
+        return pl.BlockSpec((length, width), lambda tile: (0, 0))
+
+    def columns(rows):
+        return pl.BlockSpec((rows, FEED_TILE), lambda tile: (0, tile))
+
+    return pl.pallas_call(
+        feed_kernel,
+        grid=(hidden // FEED_TILE,),
+        in_specs=[whole(), whole(), columns(width), columns(width), columns(1)],
+        out_specs=[columns(length), columns(length), columns(1)],
+        out_shape=[jax.ShapeDtypeStruct((length, hidden), jnp.bfloat16)] * 2
+        + [jax.ShapeDtypeStruct((1, hidden), jnp.float32)],
+        compiler_params=pltpu.CompilerParams(vmem_limit_bytes=VMEM_LIMIT),
+        cost_estimate=pl.CostEstimate(
+            flops=4 * length * width * hidden,
+            bytes_accessed=4 * length * (width + hidden) + 4 * width * hidden,
+            transcendentals=4 * length * hidden,
+        ),
+    )(norm, upstream, widen, narrow, bias[None])
+
+
 def shards(
     layer_input,
     cotangent,
@@ -471,17 +596,11 @@
     narrow_low = placed(narrow_gather.finish(), narrow_order)
 
     joint_scatter.hop()
-    widened = jnp.dot(second_norm, widen_low, preferred_element_type=jnp.float32) + widen_bias
-    activated = jax.nn.gelu(widened, approximate=False).astype(jnp.bfloat16)
-    widened, activated = arrived([joint_scatter], (widened, activated))
+    activated, widen_back, widen_bias_grad = feed_forward(
+        second_norm, upstream_low, widen_low, narrow_low, widen_bias
+    )
+    activated, widen_back = arrived([joint_scatter], (activated, widen_back))
     joint_scatter.hop()
-    activation_grad = jnp.einsum(
-        "sd,df->sf", upstream_low, narrow_low, preferred_element_type=jnp.float32
-    )
-    gelu_slope = jax.vjp(lambda inner_value: jax.nn.gelu(inner_value, approximate=False), widened)[
-        1
-    ](activation_grad)[0]
-    widen_back = gelu_slope.astype(jnp.bfloat16)
     narrow_grad = jnp.einsum(
         "sd,sf->df", upstream_low, activated, preferred_element_type=jnp.float32
     )
@@ -534,11 +653,9 @@
             + own_columns(vector_params[8 + widen_rows])
         )
     ).astype(jnp.bfloat16)
-    widen_bias_grad = jnp.sum(widen_back.astype(jnp.float32), axis=0)
     attend_bias_grad = jnp.sum(triple_grad.astype(jnp.float32), axis=1)
-    first_total, second_total, block_output, widen_bias_grad, attend_bias_grad = arrived(
-        [*sums, joint_scatter],
-        (first_total, second_total, block_output, widen_bias_grad, attend_bias_grad),
+    first_total, second_total, block_output, attend_bias_grad = arrived(
+        [*sums, joint_scatter], (first_total, second_total, block_output, attend_bias_grad)
     )
     joint_sum = joint_scatter.finish()
     attend_sum, output_sum = joint_sum[:, :triple_cols], joint_sum[:, triple_cols:]
@@ -577,7 +694,7 @@
         jnp.zeros((3 * D,), jnp.float32), attend_bias_grad, tensor_rank * triple_cols, 0
     )
     widen_bias_full = lax.dynamic_update_slice_in_dim(
-        jnp.zeros((FF,), jnp.float32), widen_bias_grad, tensor_rank * widen_cols, 0
+        jnp.zeros((FF,), jnp.float32), widen_bias_grad[0], tensor_rank * widen_cols, 0
     )
     vector_part = jnp.concatenate(
         [
@@ -628,10 +745,12 @@
     even, low_core = parity == 0, tensor_rank == 0
     core_first = jnp.where(even, grams[2], grams[0])
     core_second = jnp.where(even, grams[3], grams[1])
-    own_gram = jnp.where(low_core, core_first, core_second) + other_core(
-        jnp.where(low_core, core_second, core_first)
-    )
-    pair_rows = newton_rows(own_gram, (data_rank - parity) * rows_here, 2 * rows_here)
+    pair_rows = newton_rows(
+        jnp.where(low_core, core_first, core_second),
+        other_core(jnp.where(low_core, core_second, core_first)),
+        (data_rank - parity) * rows_here,
+        2 * rows_here,
+    )
 
     def rows_for(chip_parity):
         return lax.dynamic_slice_in_dim(pair_rows, chip_parity * rows_here, rows_here, 0)

time: 453 us -> 401 us (0.89)
  matrix products: 128 us -> 42.2 us
  Pallas kernels: 42.5 us -> 81.9 us
  waiting for transfers between devices: 134 us -> 148 us
  other arithmetic: 46.4 us -> 34.8 us
    dot_general x19 -> x0, matrix products: 84.7 us -> none  [the longest x17 47.6 us: product(): jnp.dot(left, right, precision=HIGH, preferred_element_type=jnp.float32)]
    pallas_call x0 -> x2, Pallas kernels: none -> 39.9 us  [the longest x1 30.7 us: newton_rows(): pl.pallas_call(newton_kernel, in_specs=[pl.BlockSpec(memory_space=pltpu.V...]
    unnamed x120 -> x110, local copies, waits for them, and re-layouts: 6.96 us -> 16.3 us
    ppermute x40, waiting for transfers between devices: 71.9 us -> 79.6 us  [gather_steps(): moving[piece] = lax.ppermute(moving[piece], 'dp', ring(count, stride, size))]
    ppermute x15, waiting for transfers between devices: 26.9 us -> 33 us  [scatter_steps(): got, = (yield [lax.ppermute(total.astype(jnp.bfloat16), 'dp', perm)])]
    reduce_sum x2 -> x0, other arithmetic: 5.9 us -> none  [the longest x1 4.8 us: newton_rows(): factor = 1.0 / (jnp.sqrt(jnp.trace(gram)) + SCALE_EPS)]
  transfers between devices with their start and end apart: 68 -> 68, of which waited for: 34 -> 39; matrix products, arithmetic and copies ran while one was open for 25% -> 16% of each run, Pallas kernels for 8% -> 10%
where the time goes in v4:
time: 401 us; the launch traced here: 396 us
  waiting for transfers between devices  148 us (37%)
  Pallas kernels  81.9 us (20%)
  starting transfers between devices  65.2 us (16%)
  matrix products  42.2 us (11%)
  other arithmetic  34.8 us (9%)
  local copies, waits for them, and re-layouts  22 us (5%)
    ppermute x40, waiting for transfers between devices, gather_steps(): moving[piece] = lax.ppermute(moving[piece], 'dp', ring(count, stride, size))  79.6 us
    ppermute x40, starting transfers between devices, gather_steps(): moving[piece] = lax.ppermute(moving[piece], 'dp', ring(count, stride, size))  43.7 us
    ppermute x15, waiting for transfers between devices, scatter_steps(): got, = (yield [lax.ppermute(total.astype(jnp.bfloat16), 'dp', perm)])  33 us
    pallas_call x1, Pallas kernels, newton_rows(): pl.pallas_call(newton_kernel, in_specs=[pl.BlockSpec(memory_space=pltpu.V...  30.7 us
    pallas_call x1, Pallas kernels, attention(): pl.pallas_call(attention_kernel, grid=(heads,), in_specs=[own(3 * HEAD_DI...  24.6 us
    ppermute x4, waiting for transfers between devices, sum_steps(): got, = (yield [lax.ppermute(value, 'dp', pairs)])  21.8 us
    pallas_call x6, Pallas kernels, placed(): pl.pallas_call(functools.partial(place_kernel, orders, [len(parts) for pa...  17.4 us
    unnamed x110, local copies, waits for them, and re-layouts  16.3 us
  transfers between devices with their start and end apart: 68, of which 39 were waited for; matrix products, arithmetic and copies ran while one was open for 16% of the time, Pallas kernels for 10%

profile of v4, /device:TPU:0, one launch (start us, length us, event | category | flops | bytes accessed | tf_op | source)
XLA Modules:
  0.0 396.3 jit_solution(4709966701338228444)
XLA Ops:
  1.7 3.1 collective-permute-start
  8.7 2.0 select_select_fusion
  15.5 1.8 collective-permute-start.9
  18.9 1.7 collective-permute-done.2
  20.7 1.7 collective-permute-done.3
  24.1 3.4 convert_element_type.207
  28.9 2.2 convert_multiply_fusion
  31.0 2.6 subtract_multiply_fusion
  37.6 3.7 collective-permute-done.7
  42.8 4.0 collective-permute-start.14
  51.0 2.8 collective-permute-done.14
  54.1 3.5 collective-permute-done.13
  57.7 3.4 collective-permute-done.15
  61.7 1.9 collective-permute-start.16
  65.6 4.5 %convolution_add_fusion.triple_ref = f32[1152,1024]{1,0:T(8,128)} fusion(bf16[1024,768]{1,0:T(8,128)(2,1)S(1)} %get-tuple-element.113, f32[1152]{0:T(1024)S(1)} %dynamic_slice.120, bf16[768,1536]{1,0:T(8,128)(2,1)S(1)} %bitcast.81), kind=kOutput, calls=%fused_computation.2 | convolution fusion | flops 1813118976 | bytes 8069120 | tf_op jit(solution)/shard_map/dk,sd->ks/dot_general | solution.py:576
  70.1 4.4 %collective-permute-done.17 = bf16[4,48,1536]{2,1,0:T(8,128)(2,1)S(1)} collective-permute-done((bf16[4,48,1536]{2,1,0:T(8,128)(2,1)S(1)}, bf16[4,48,1536]{2,1,0:T(8,128)(2,1)S(1)}, u32[]{:S(2)}, u32[]{:S(2)}) %collective-permute-start.17) | collective-permute-done | bytes 589856 | tf_op jit(solution)/shard_map/ppermute | solution.py:116
  74.4 2.4 collective-permute-done.16
  76.9 2.5 collective-permute-start.19
  80.4 24.6 %shard_map.278 = (bf16[384,1024]{1,0:T(8,128)(2,1)S(1)}, bf16[1152,1024]{1,0:T(8,128)(2,1)S(1)}) custom-call(f32[1152,1024]{1,0:T(8,128)} %convolution_add_fusion.triple_ref, f32[8,1024]{1,0:T(8,128)S(1)} %get-tuple-element.127.cos_ref, f32[8,1024]{1,0:T(8,128)S(1)} %get-tuple-element.128.sin_ref, ...), custom_call_target="tpu_custom_call" | custom-call | flops 14495514624 | bytes 9437184 | tf_op jit(solution)/shard_map/pallas_call | solution.py:340
  106.1 3.8 shard_map.279
  112.5 4.1 %shard_map.280 = bf16[16,48,1536]{2,1,0:T(8,128)(2,1)S(1)} custom-call(bf16[8,48,1536]{2,1,0:T(8,128)(2,1)S(1)} %copy-done.8, bf16[8,48,1536]{2,1,0:T(8,128)(2,1)S(1)} %copy-done.10), custom_call_target="tpu_custom_call" | custom-call | bytes 4718592 | tf_op jit(solution)/shard_map/pallas_call | solution.py:186
  118.8 2.3 fusion.52
  122.0 2.3 fusion.8
  125.9 9.2 %shard_map.281 = (bf16[1024,1536]{1,0:T(8,128)(2,1)}, bf16[1024,1536]{1,0:T(8,128)(2,1)}, f32[1,1536]{1,0:T(1,128)S(1)}) custom-call(bf16[1024,768]{1,0:T(8,128)(2,1)S(1)} %get-tuple-element.134.norm_ref, bf16[1024,768]{1,0:T(8,128)(2,1)S(1)} %get-tuple-element.123.upstream_ref, bf16[768,1536]{1,0:T(8,128)(2,1)S(1)} %bitcast.84, bf16[768,1536]{1,0:T(8,128)(2,1)} %bitcast.86, ...), custom_call_target="tpu_custom_call" | custom-call | flops 4831838208 | bytes 14155776 | tf_op jit(solution)/shard_map/pallas_call | solution.py:488
  135.1 3.0 collective-permute-done.20
  138.2 4.7 %fusion.57 = f32[1024,768]{1,0:T(8,128)S(1)} fusion(bf16[1024,1536]{1,0:T(8,128)(2,1)} %get-tuple-element.141, bf16[768,1536]{1,0:T(8,128)(2,1)S(1)} %bitcast.87), kind=kOutput, calls=%fused_computation.204 | convolution fusion | flops 2415919104 | bytes 8650752 | tf_op jit(solution)/shard_map/sf,df->sd/dot_general | solution.py:636
  142.8 2.7 fusion.55
  145.5 2.0 convert_add_fusion.2
  150.1 1.7 copy-done.21
  151.8 2.7 fusion.54
  154.5 4.8 %collective-permute-done.21 = bf16[4,1,1,48,1536]{4,3,2,1,0:T(8,128)(2,1)S(1)} collective-permute-done((bf16[4,1,1,48,1536]{4,3,2,1,0:T(8,128)(2,1)S(1)}, bf16[4,1,1,48,1536]{4,3,2,1,0:T(8,128)(2,1)S(1)}, u32[]{:S(2)}, u32[]{:S(2)}) %collective-permute-start.21) | collective-permute-done | bytes 589856 | tf_op jit(solution)/shard_map/ppermute | solution.py:143
  159.5 2.0 collective-permute-start.24
  161.5 2.6 fusion.56
  169.1 5.6 %collective-permute-done.25 = bf16[1,1,1,48,1536]{4,3,2,1,0:T(8,128)(2,1)S(1)} collective-permute-done((bf16[1,1,1,48,1536]{4,3,2,1,0:T(8,128)(2,1)S(1)}, bf16[1,1,1,48,1536]{4,3,2,1,0:T(8,128)(2,1)S(1)}, u32[]{:S(2)}, u32[]{:S(2)}) %collective-permute-start.25) | collective-permute-done | bytes 147488 | tf_op jit(solution)/shard_map/ppermute | solution.py:143
  177.8 3.9 collective-permute-done.26
  181.8 11.2 %collective-permute-done.22 = bf16[4,2,1,48,1536]{4,3,2,1,0:T(8,128)(2,1)S(1)} collective-permute-done((bf16[4,2,1,48,1536]{4,3,2,1,0:T(8,128)(2,1)S(1)}, bf16[4,2,1,48,1536]{4,3,2,1,0:T(8,128)(2,1)S(1)}, u32[]{:S(2)}, u32[]{:S(2)}) %collective-permute-start.22) | collective-permute-done | bytes 1179680 | tf_op jit(solution)/shard_map/ppermute | solution.py:143
  193.8 3.2 copy-done.13
  205.4 4.3 %collective-permute-start.33 = (bf16[1,48,768]{2,1,0:T(8,128)(2,1)S(1)}, bf16[1,48,768]{2,1,0:T(8,128)(2,1)S(1)}, u32[]{:S(2)}, u32[]{:S(2)}) collective-permute-start(bf16[1,48,768]{2,1,0:T(8,128)(2,1)S(1)} %collective-permute-done.32), channel_id=1, source_target_pairs={{0,8},{2,10},{4,12},{6,14},{8,16},{10,18},{12,20},{14,22},{16,24},... | collective-permute-start | bytes 221192 | tf_op jit(solution)/shard_map/ppermute | solution.py:116
  209.7 1.7 collective-permute-done.34
  211.4 2.1 fusion.6
  213.5 4.0 %collective-permute-done.35 = bf16[1,48,768]{2,1,0:T(8,128)(2,1)S(1)} collective-permute-done((bf16[1,48,768]{2,1,0:T(8,128)(2,1)S(1)}, bf16[1,48,768]{2,1,0:T(8,128)(2,1)S(1)}, u32[]{:S(2)}, u32[]{:S(2)}) %collective-permute-start.35) | collective-permute-done | bytes 73760 | tf_op jit(solution)/shard_map/ppermute | solution.py:116
  221.8 3.4 collective-permute-start.38
  228.7 6.5 %collective-permute-done.40 = bf16[1,48,768]{2,1,0:T(8,128)(2,1)S(1)} collective-permute-done((bf16[1,48,768]{2,1,0:T(8,128)(2,1)S(1)}, bf16[1,48,768]{2,1,0:T(8,128)(2,1)S(1)}, u32[]{:S(2)}, u32[]{:S(2)}) %collective-permute-start.40) | collective-permute-done | bytes 73760 | tf_op jit(solution)/shard_map/ppermute | solution.py:116
  238.0 1.8 collective-permute-start.42
  240.4 4.1 %collective-permute-done.46 = f32[13,768]{1,0:T(8,128)S(1)} collective-permute-done((f32[13,768]{1,0:T(8,128)S(1)}, f32[13,768]{1,0:T(8,128)S(1)}, u32[]{:S(2)}, u32[]{:S(2)}) %collective-permute-start.46) | collective-permute-done | bytes 39968 | tf_op jit(solution)/shard_map/ppermute | solution.py:211
  245.7 1.8 collective-permute-start.49
  250.2 9.3 %collective-permute-done.51 = f32[13,768]{1,0:T(8,128)S(1)} collective-permute-done((f32[13,768]{1,0:T(8,128)S(1)}, f32[13,768]{1,0:T(8,128)S(1)}, u32[]{:S(2)}, u32[]{:S(2)}) %collective-permute-start.51) | collective-permute-done | bytes 39968 | tf_op jit(solution)/shard_map/ppermute | solution.py:211
  261.0 2.0 collective-permute-start.52
  264.9 3.2 fusion.14
  268.1 2.2 fusion.23
  271.4 1.9 collective-permute-start.56
  273.3 2.2 collective-permute-start.57
  275.5 8.3 %collective-permute-done.57 = f32[13,768]{1,0:T(8,128)S(1)} collective-permute-done((f32[13,768]{1,0:T(8,128)S(1)}, f32[13,768]{1,0:T(8,128)S(1)}, u32[]{:S(2)}, u32[]{:S(2)}) %collective-permute-start.57) | collective-permute-done | bytes 39968 | tf_op jit(solution)/shard_map/ppermute | solution.py:211
  284.6 6.2 %collective-permute-done.58 = bf16[1,48,1536]{2,1,0:T(8,128)(2,1)S(1)} collective-permute-done((bf16[1,48,1536]{2,1,0:T(8,128)(2,1)S(1)}, bf16[1,48,1536]{2,1,0:T(8,128)(2,1)S(1)}, u32[]{:S(2)}, u32[]{:S(2)}) %collective-permute-start.58) | collective-permute-done | bytes 147488 | tf_op jit(solution)/shard_map/ppermute | solution.py:116
  294.9 13.9 %collective-permute-done.61 = bf16[4,48,1536]{2,1,0:T(8,128)(2,1)S(1)} collective-permute-done((bf16[4,48,1536]{2,1,0:T(8,128)(2,1)S(1)}, bf16[4,48,1536]{2,1,0:T(8,128)(2,1)S(1)}, u32[]{:S(2)}, u32[]{:S(2)}) %collective-permute-start.61) | collective-permute-done | bytes 589856 | tf_op jit(solution)/shard_map/ppermute | solution.py:116
  311.9 15.3 %collective-permute-done.62.refs_1_ = bf16[8,48,1536]{2,1,0:T(8,128)(2,1)S(1)} collective-permute-done((bf16[8,48,1536]{2,1,0:T(8,128)(2,1)S(1)}, bf16[8,48,1536]{2,1,0:T(8,128)(2,1)S(1)}, u32[]{:S(2)}, u32[]{:S(2)}) %collective-permute-start.62) | collective-permute-done | bytes 1179680 | tf_op jit(solution)/shard_map/ppermute | solution.py:116
  327.2 3.8 shard_map.283
  331.1 2.0 convolution_select_fusion.1
  333.1 3.6 shard_map.284
  336.8 4.2 %broadcast_select_fusion = (f32[768,768]{1,0:T(8,128)}, f32[768,768]{1,0:T(8,128)}) fusion(f32[768,768]{1,0:T(8,128)S(1)} %convolution_select_fusion.1, pred[]{:T(512)S(6)} %eq.56, f32[768,768]{1,0:T(8,128)S(1)} %copy-done.14, bf16[768,1536]{1,0:T(8,128)(2,1)S(1)} %bitcast.68, pred[]{:T(512)S(6)} %eq.57), kind=kOutput, calls=%fused_computation.57 | convolution fusion | flops 1813708800 | bytes 11796482 | tf_op jit(solution)/shard_map/dk,ek->de/dot_general | solution.py:723
  341.1 4.8 %collective-permute-done.64.second_ref = f32[768,768]{1,0:T(8,128)} collective-permute-done((f32[768,768]{1,0:T(8,128)}, f32[768,768]{1,0:T(8,128)}, u32[]{:S(2)}, u32[]{:S(2)}) %collective-permute-start.64) | collective-permute-done | bytes 2359328 | tf_op jit(solution)/shard_map/ppermute | solution.py:201
  347.6 30.7 %shard_map.285 = f32[96,768]{1,0:T(8,128)S(1)} custom-call(f32[768,768]{1,0:T(8,128)S(1)} %copy-done.4, f32[768,768]{1,0:T(8,128)} %collective-permute-done.64.second_ref, f32[96,768]{1,0:T(8,128)S(1)} %fusion.25.rows_ref), custom_call_target="tpu_custom_call" | custom-call | flops 21743271936 | bytes 4718592 | tf_op jit(solution)/shard_map/pallas_call | solution.py:446
  381.3 3.7 collective-permute-done.66
  384.9 3.6 collective-permute-done.65
  (327 shorter events, 95.2 us)
Async XLA Ops:
  1.7 12.0 %collective-permute-start = (bf16[1,48,768]{2,1,0:T(8,128)(2,1)S(1)}, bf16[1,48,768]{2,1,0:T(8,128)(2,1)S(1)}, u32[]{:S(2)}, u32[]{:S(2)}) collective-permute-start(bf16[1,48,768]{2,1,0:T(8,128)(2,1)S(1)} %slice_bitcast_fusion.1), channel_id=1, source_target_pairs={{0,8},{2,10},{4,12},{6,14},{8,16},{10,18},{12,20},{14,22},{16,24},... | collective-permute-start | bytes 221192 | tf_op jit(solution)/shard_map/ppermute | solution.py:116
  5.7 8.0 %collective-permute-start.1 = (bf16[1,48,768]{2,1,0:T(8,128)(2,1)S(1)}, bf16[1,48,768]{2,1,0:T(8,128)(2,1)S(1)}, u32[]{:S(2)}, u32[]{:S(2)}) collective-permute-start(bf16[1,48,768]{2,1,0:T(8,128)(2,1)S(1)} %get-tuple-element.230), channel_id=1, source_target_pairs={{0,8},{2,10},{4,12},{6,14},{8,16},{10,18},{12,20},{14,22},{16,24},... | collective-permute-start | bytes 221192 | tf_op jit(solution)/shard_map/ppermute | solution.py:116
  13.8 6.9 %collective-permute-start.2 = (bf16[1,48,768]{2,1,0:T(8,128)(2,1)S(1)}, bf16[1,48,768]{2,1,0:T(8,128)(2,1)S(1)}, u32[]{:S(2)}, u32[]{:S(2)}) collective-permute-start(bf16[1,48,768]{2,1,0:T(8,128)(2,1)S(1)} %collective-permute-done), channel_id=1, source_target_pairs={{0,8},{2,10},{4,12},{6,14},{8,16},{10,18},{12,20},{14,22},{16,24},... | collective-permute-start | bytes 221192 | tf_op jit(solution)/shard_map/ppermute | solution.py:116
  15.4 7.0 %collective-permute-start.3 = (bf16[1,48,768]{2,1,0:T(8,128)(2,1)S(1)}, bf16[1,48,768]{2,1,0:T(8,128)(2,1)S(1)}, u32[]{:S(2)}, u32[]{:S(2)}) collective-permute-start(bf16[1,48,768]{2,1,0:T(8,128)(2,1)S(1)} %collective-permute-done.1), channel_id=1, source_target_pairs={{0,8},{2,10},{4,12},{6,14},{8,16},{10,18},{12,20},{14,22},{16,24},... | collective-permute-start | bytes 221192 | tf_op jit(solution)/shard_map/ppermute | solution.py:116
  15.5 22.2 %collective-permute-start.9 = (bf16[1,48,1536]{2,1,0:T(8,128)(2,1)S(1)}, bf16[1,48,1536]{2,1,0:T(8,128)(2,1)S(1)}, u32[]{:S(2)}, u32[]{:S(2)}) collective-permute-start(bf16[1,48,1536]{2,1,0:T(8,128)(2,1)S(1)} %bitcast.97), channel_id=1, source_target_pairs={{0,8},{2,10},{4,12},{6,14},{8,16},{10,18},{12,20},{14,22},{16,24},... | collective-permute-start | bytes 442376 | tf_op jit(solution)/shard_map/ppermute | solution.py:116
  17.3 20.4 %collective-permute-start.8 = (bf16[1,48,1536]{2,1,0:T(8,128)(2,1)S(1)}, bf16[1,48,1536]{2,1,0:T(8,128)(2,1)S(1)}, u32[]{:S(2)}, u32[]{:S(2)}) collective-permute-start(bf16[1,48,1536]{2,1,0:T(8,128)(2,1)S(1)} %bitcast.95), channel_id=1, source_target_pairs={{0,8},{2,10},{4,12},{6,14},{8,16},{10,18},{12,20},{14,22},{16,24},... | collective-permute-start | bytes 442376 | tf_op jit(solution)/shard_map/ppermute | solution.py:116
  27.5 6.2 %collective-permute-start.4 = (bf16[1,48,768]{2,1,0:T(8,128)(2,1)S(1)}, bf16[1,48,768]{2,1,0:T(8,128)(2,1)S(1)}, u32[]{:S(2)}, u32[]{:S(2)}) collective-permute-start(bf16[1,48,768]{2,1,0:T(8,128)(2,1)S(1)} %collective-permute-done.2), channel_id=1, source_target_pairs={{0,8},{2,10},{4,12},{6,14},{8,16},{10,18},{12,20},{14,22},{16,24},... | collective-permute-start | bytes 221192 | tf_op jit(solution)/shard_map/ppermute | solution.py:116
  28.1 6.3 %collective-permute-start.5 = (bf16[1,48,768]{2,1,0:T(8,128)(2,1)S(1)}, bf16[1,48,768]{2,1,0:T(8,128)(2,1)S(1)}, u32[]{:S(2)}, u32[]{:S(2)}) collective-permute-start(bf16[1,48,768]{2,1,0:T(8,128)(2,1)S(1)} %collective-permute-done.3), channel_id=1, source_target_pairs={{0,8},{2,10},{4,12},{6,14},{8,16},{10,18},{12,20},{14,22},{16,24},... | collective-permute-start | bytes 221192 | tf_op jit(solution)/shard_map/ppermute | solution.py:116
  34.5 6.8 %collective-permute-start.7 = (bf16[4,48,768]{2,1,0:T(8,128)(2,1)S(1)}, bf16[4,48,768]{2,1,0:T(8,128)(2,1)S(1)}, u32[]{:S(2)}, u32[]{:S(2)}) collective-permute-start(bf16[4,48,768]{2,1,0:T(8,128)(2,1)S(1)} %pad_maximum_fusion.6), channel_id=1, source_target_pairs={{0,4},{2,6},{4,0},{6,2},{8,12},{10,14},{12,8},{14,10},{16,20},{18,... | collective-permute-start | bytes 884744 | tf_op jit(solution)/shard_map/ppermute | solution.py:116
  36.1 6.7 %collective-permute-start.6 = (bf16[4,48,768]{2,1,0:T(8,128)(2,1)S(1)}, bf16[4,48,768]{2,1,0:T(8,128)(2,1)S(1)}, u32[]{:S(2)}, u32[]{:S(2)}) collective-permute-start(bf16[4,48,768]{2,1,0:T(8,128)(2,1)S(1)} %pad_maximum_fusion.5), channel_id=1, source_target_pairs={{0,2},{2,0},{4,6},{6,4},{8,10},{10,8},{12,14},{14,12},{16,18},{18,... | collective-permute-start | bytes 884744 | tf_op jit(solution)/shard_map/ppermute | solution.py:116
  42.8 7.9 %collective-permute-start.10 = (bf16[1,48,1536]{2,1,0:T(8,128)(2,1)S(1)}, bf16[1,48,1536]{2,1,0:T(8,128)(2,1)S(1)}, u32[]{:S(2)}, u32[]{:S(2)}) collective-permute-start(bf16[1,48,1536]{2,1,0:T(8,128)(2,1)S(1)} %collective-permute-done.8), channel_id=1, source_target_pairs={{0,8},{2,10},{4,12},{6,14},{8,16},{10,18},{12,20},{14,22},{16,24},... | collective-permute-start | bytes 442376 | tf_op jit(solution)/shard_map/ppermute | solution.py:116
  42.8 11.1 %collective-permute-start.14 = (bf16[1,48,1536]{2,1,0:T(8,128)(2,1)S(1)}, bf16[1,48,1536]{2,1,0:T(8,128)(2,1)S(1)}, u32[]{:S(2)}, u32[]{:S(2)}) collective-permute-start(bf16[1,48,1536]{2,1,0:T(8,128)(2,1)S(1)} %collective-permute-done.9), channel_id=1, source_target_pairs={{0,8},{2,10},{4,12},{6,14},{8,16},{10,18},{12,20},{14,22},{16,24},... | collective-permute-start | bytes 442376 | tf_op jit(solution)/shard_map/ppermute | solution.py:116
  46.8 14.2 %collective-permute-start.12 = (bf16[8,48,768]{2,1,0:T(8,128)(2,1)S(1)}, bf16[8,48,768]{2,1,0:T(8,128)(2,1)S(1)}, u32[]{:S(2)}, u32[]{:S(2)}) collective-permute-start(bf16[8,48,768]{2,1,0:T(8,128)(2,1)S(1)} %constant_dynamic-update-slice_fusion.5.refs_2_), channel_id=1, source_target_pairs={{0,2},{2,0},{4,6},{6,4},{8,10},{10,8},{12,14},{14,12},{16,18},{18,... | collective-permute-start | bytes 1769480 | tf_op jit(solution)/shard_map/ppermute | solution.py:116
  48.4 12.6 %collective-permute-start.11 = (bf16[8,48,768]{2,1,0:T(8,128)(2,1)S(1)}, bf16[8,48,768]{2,1,0:T(8,128)(2,1)S(1)}, u32[]{:S(2)}, u32[]{:S(2)}) collective-permute-start(bf16[8,48,768]{2,1,0:T(8,128)(2,1)S(1)} %constant_dynamic-update-slice_fusion.refs_0_), channel_id=1, source_target_pairs={{0,4},{2,6},{4,0},{6,2},{8,12},{10,14},{12,8},{14,10},{16,20},{18,... | collective-permute-start | bytes 1769480 | tf_op jit(solution)/shard_map/ppermute | solution.py:116
  50.7 6.9 %collective-permute-start.13 = (bf16[1,48,1536]{2,1,0:T(8,128)(2,1)S(1)}, bf16[1,48,1536]{2,1,0:T(8,128)(2,1)S(1)}, u32[]{:S(2)}, u32[]{:S(2)}) collective-permute-start(bf16[1,48,1536]{2,1,0:T(8,128)(2,1)S(1)} %collective-permute-done.10), channel_id=1, source_target_pairs={{0,8},{2,10},{4,12},{6,14},{8,16},{10,18},{12,20},{14,22},{16,24},... | collective-permute-start | bytes 442376 | tf_op jit(solution)/shard_map/ppermute | solution.py:116
  53.9 7.1 %collective-permute-start.15 = (bf16[1,48,1536]{2,1,0:T(8,128)(2,1)S(1)}, bf16[1,48,1536]{2,1,0:T(8,128)(2,1)S(1)}, u32[]{:S(2)}, u32[]{:S(2)}) collective-permute-start(bf16[1,48,1536]{2,1,0:T(8,128)(2,1)S(1)} %collective-permute-done.14), channel_id=1, source_target_pairs={{0,8},{2,10},{4,12},{6,14},{8,16},{10,18},{12,20},{14,22},{16,24},... | collective-permute-start | bytes 442376 | tf_op jit(solution)/shard_map/ppermute | solution.py:116
  61.1 13.3 %collective-permute-start.17 = (bf16[4,48,1536]{2,1,0:T(8,128)(2,1)S(1)}, bf16[4,48,1536]{2,1,0:T(8,128)(2,1)S(1)}, u32[]{:S(2)}, u32[]{:S(2)}) collective-permute-start(bf16[4,48,1536]{2,1,0:T(8,128)(2,1)S(1)} %pad_maximum_fusion.2), channel_id=1, source_target_pairs={{0,4},{2,6},{4,0},{6,2},{8,12},{10,14},{12,8},{14,10},{16,20},{18,... | collective-permute-start | bytes 1769480 | tf_op jit(solution)/shard_map/ppermute | solution.py:116
  61.7 15.1 %collective-permute-start.16 = (bf16[4,48,1536]{2,1,0:T(8,128)(2,1)S(1)}, bf16[4,48,1536]{2,1,0:T(8,128)(2,1)S(1)}, u32[]{:S(2)}, u32[]{:S(2)}) collective-permute-start(bf16[4,48,1536]{2,1,0:T(8,128)(2,1)S(1)} %pad_maximum_fusion.1), channel_id=1, source_target_pairs={{0,2},{2,0},{4,6},{6,4},{8,10},{10,8},{12,14},{14,12},{16,18},{18,... | collective-permute-start | bytes 1769480 | tf_op jit(solution)/shard_map/ppermute | solution.py:116
  76.9 28.1 %collective-permute-start.19 = (bf16[8,48,1536]{2,1,0:T(8,128)(2,1)S(1)}, bf16[8,48,1536]{2,1,0:T(8,128)(2,1)S(1)}, u32[]{:S(2)}, u32[]{:S(2)}) collective-permute-start(bf16[8,48,1536]{2,1,0:T(8,128)(2,1)S(1)} %constant_dynamic-update-slice_fusion.15.refs_0_), channel_id=1, source_target_pairs={{0,2},{2,0},{4,6},{6,4},{8,10},{10,8},{12,14},{14,12},{16,18},{18,... | collective-permute-start | bytes 3538952 | tf_op jit(solution)/shard_map/ppermute | solution.py:116
  79.5 26.6 %collective-permute-start.18 = (bf16[8,48,1536]{2,1,0:T(8,128)(2,1)S(1)}, bf16[8,48,1536]{2,1,0:T(8,128)(2,1)S(1)}, u32[]{:S(2)}, u32[]{:S(2)}) collective-permute-start(bf16[8,48,1536]{2,1,0:T(8,128)(2,1)S(1)} %constant_dynamic-update-slice_fusion.10.refs_0_), channel_id=1, source_target_pairs={{0,4},{2,6},{4,0},{6,2},{8,12},{10,14},{12,8},{14,10},{16,20},{18,... | collective-permute-start | bytes 3538952 | tf_op jit(solution)/shard_map/ppermute | solution.py:116
  121.9 16.3 %collective-permute-start.20 = (bf16[4,2,1,48,1536]{4,3,2,1,0:T(8,128)(2,1)S(1)}, bf16[4,2,1,48,1536]{4,3,2,1,0:T(8,128)(2,1)S(1)}, u32[]{:S(2)}, u32[]{:S(2)}) collective-permute-start(bf16[4,2,1,48,1536]{4,3,2,1,0:T(8,128)(2,1)S(1)} %dynamic-slice_convert_fusion.2), channel_id=1, source_target_pairs={{0,2},{2,0},{4,6},{6,4},{8,10},{10,8},{12,14},{14,12},{16,18},{18,... | collective-permute-start | bytes 3538952 | tf_op jit(solution)/shard_map/ppermute | solution.py:143
  124.4 43.4 %collective-permute-start.27 = (bf16[512,768]{1,0:T(8,128)(2,1)S(1)}, bf16[512,768]{1,0:T(8,128)(2,1)}, u32[]{:S(2)}, u32[]{:S(2)}) collective-permute-start(bf16[512,768]{1,0:T(8,128)(2,1)S(1)} %dynamic-slice_convert_fusion.4), channel_id=1, source_target_pairs={{0,1},{1,0},{2,3},{3,2},{4,5},{5,4},{6,7},{7,6},{8,9},{9,8},{10,11... | collective-permute-start | bytes 2359304 | tf_op jit(solution)/shard_map/ppermute | solution.py:201
  147.6 11.7 %collective-permute-start.21 = (bf16[4,1,1,48,1536]{4,3,2,1,0:T(8,128)(2,1)S(1)}, bf16[4,1,1,48,1536]{4,3,2,1,0:T(8,128)(2,1)S(1)}, u32[]{:S(2)}, u32[]{:S(2)}) collective-permute-start(bf16[4,1,1,48,1536]{4,3,2,1,0:T(8,128)(2,1)S(1)} %dynamic-slice_convert_fusion.7), channel_id=1, source_target_pairs={{0,4},{2,6},{4,0},{6,2},{8,12},{10,14},{12,8},{14,10},{16,20},{18,... | collective-permute-start | bytes 1769480 | tf_op jit(solution)/shard_map/ppermute | solution.py:143
  150.0 25.0 %collective-permute-start.29 = (f32[1024,384]{1,0:T(8,128)S(1)}, f32[1024,384]{1,0:T(8,128)S(1)}, u32[]{:S(2)}, u32[]{:S(2)}) collective-permute-start(f32[1024,384]{1,0:T(8,128)S(1)} %constant_dynamic-slice_fusion.4), channel_id=1, source_target_pairs={{0,1},{1,0},{2,3},{3,2},{4,5},{5,4},{6,7},{7,6},{8,9},{9,8},{10,11... | collective-permute-start | bytes 4718600 | tf_op jit(solution)/shard_map/ppermute | solution.py:201
  159.5 7.0 %collective-permute-start.24 = (bf16[1,1,1,48,1536]{4,3,2,1,0:T(8,128)(2,1)S(1)}, bf16[1,1,1,48,1536]{4,3,2,1,0:T(8,128)(2,1)S(1)}, u32[]{:S(2)}, u32[]{:S(2)}) collective-permute-start(bf16[1,1,1,48,1536]{4,3,2,1,0:T(8,128)(2,1)S(1)} %dynamic-slice_convert_fusion.10), channel_id=1, source_target_pairs={{0,8},{2,10},{4,12},{6,14},{8,16},{10,18},{12,20},{14,22},{16,24},... | collective-permute-start | bytes 442376 | tf_op jit(solution)/shard_map/ppermute | solution.py:143
  164.2 10.7 %collective-permute-start.28 = (bf16[512,768]{1,0:T(8,128)(2,1)S(1)}, bf16[512,768]{1,0:T(8,128)(2,1)S(1)}, u32[]{:S(2)}, u32[]{:S(2)}) collective-permute-start(bf16[512,768]{1,0:T(8,128)(2,1)S(1)} %dynamic-slice_convert_fusion.3), channel_id=1, source_target_pairs={{0,1},{1,0},{2,3},{3,2},{4,5},{5,4},{6,7},{7,6},{8,9},{9,8},{10,11... | collective-permute-start | bytes 2359304 | tf_op jit(solution)/shard_map/ppermute | solution.py:201
  164.6 28.4 %collective-permute-start.22 = (bf16[4,2,1,48,1536]{4,3,2,1,0:T(8,128)(2,1)S(1)}, bf16[4,2,1,48,1536]{4,3,2,1,0:T(8,128)(2,1)S(1)}, u32[]{:S(2)}, u32[]{:S(2)}) collective-permute-start(bf16[4,2,1,48,1536]{4,3,2,1,0:T(8,128)(2,1)S(1)} %dynamic-slice_convert_fusion.1), channel_id=1, source_target_pairs={{0,2},{2,0},{4,6},{6,4},{8,10},{10,8},{12,14},{14,12},{16,18},{18,... | collective-permute-start | bytes 3538952 | tf_op jit(solution)/shard_map/ppermute | solution.py:143
  166.5 26.6 %collective-permute-start.23 = (bf16[4,1,2,48,1536]{4,3,2,1,0:T(8,128)(2,1)S(1)}, bf16[4,1,2,48,1536]{4,3,2,1,0:T(8,128)(2,1)S(1)}, u32[]{:S(2)}, u32[]{:S(2)}) collective-permute-start(bf16[4,1,2,48,1536]{4,3,2,1,0:T(8,128)(2,1)S(1)} %dynamic-slice_convert_fusion), channel_id=1, source_target_pairs={{0,4},{2,6},{4,0},{6,2},{8,12},{10,14},{12,8},{14,10},{16,20},{18,... | collective-permute-start | bytes 3538952 | tf_op jit(solution)/shard_map/ppermute | solution.py:143
  167.7 7.0 %collective-permute-start.25 = (bf16[1,1,1,48,1536]{4,3,2,1,0:T(8,128)(2,1)S(1)}, bf16[1,1,1,48,1536]{4,3,2,1,0:T(8,128)(2,1)S(1)}, u32[]{:S(2)}, u32[]{:S(2)}) collective-permute-start(bf16[1,1,1,48,1536]{4,3,2,1,0:T(8,128)(2,1)S(1)} %add_convert_fusion.7), channel_id=1, source_target_pairs={{0,8},{2,10},{4,12},{6,14},{8,16},{10,18},{12,20},{14,22},{16,24},... | collective-permute-start | bytes 442376 | tf_op jit(solution)/shard_map/ppermute | solution.py:143
  174.8 7.0 %collective-permute-start.26 = (bf16[1,1,1,48,1536]{4,3,2,1,0:T(8,128)(2,1)S(1)}, bf16[1,1,1,48,1536]{4,3,2,1,0:T(8,128)(2,1)S(1)}, u32[]{:S(2)}, u32[]{:S(2)}) collective-permute-start(bf16[1,1,1,48,1536]{4,3,2,1,0:T(8,128)(2,1)S(1)} %add_convert_fusion.6), channel_id=1, source_target_pairs={{0,8},{2,10},{4,12},{6,14},{8,16},{10,18},{12,20},{14,22},{16,24},... | collective-permute-start | bytes 442376 | tf_op jit(solution)/shard_map/ppermute | solution.py:143
  199.0 6.4 %collective-permute-start.32 = (bf16[1,48,768]{2,1,0:T(8,128)(2,1)S(1)}, bf16[1,48,768]{2,1,0:T(8,128)(2,1)S(1)}, u32[]{:S(2)}, u32[]{:S(2)}) collective-permute-start(bf16[1,48,768]{2,1,0:T(8,128)(2,1)S(1)} %slice_bitcast_fusion), channel_id=1, source_target_pairs={{0,8},{2,10},{4,12},{6,14},{8,16},{10,18},{12,20},{14,22},{16,24},... | collective-permute-start | bytes 221192 | tf_op jit(solution)/shard_map/ppermute | solution.py:116
  200.9 10.6 %collective-permute-start.36 = (bf16[512,768]{1,0:T(8,128)(2,1)S(1)}, bf16[512,768]{1,0:T(8,128)(2,1)S(1)}, u32[]{:S(2)}, u32[]{:S(2)}) collective-permute-start(bf16[512,768]{1,0:T(8,128)(2,1)S(1)} %fusion.7), channel_id=1, source_target_pairs={{0,1},{1,0},{2,3},{3,2},{4,5},{5,4},{6,7},{7,6},{8,9},{9,8},{10,11... | collective-permute-start | bytes 2359304 | tf_op jit(solution)/shard_map/ppermute | solution.py:201
  201.8 16.0 %collective-permute-start.31 = (bf16[4,1,1,48,1536]{4,3,2,1,0:T(8,128)(2,1)}, bf16[4,1,1,48,1536]{4,3,2,1,0:T(8,128)(2,1)}, u32[]{:S(2)}, u32[]{:S(2)}) collective-permute-start(bf16[4,1,1,48,1536]{4,3,2,1,0:T(8,128)(2,1)} %dynamic-slice_convert_fusion.5), channel_id=1, source_target_pairs={{0,2},{2,0},{4,6},{6,4},{8,10},{10,8},{12,14},{14,12},{16,18},{18,... | collective-permute-start | bytes 1769480 | tf_op jit(solution)/shard_map/ppermute | solution.py:143
  203.5 15.8 %collective-permute-start.30 = (bf16[4,1,1,48,1536]{4,3,2,1,0:T(8,128)(2,1)}, bf16[4,1,1,48,1536]{4,3,2,1,0:T(8,128)(2,1)}, u32[]{:S(2)}, u32[]{:S(2)}) collective-permute-start(bf16[4,1,1,48,1536]{4,3,2,1,0:T(8,128)(2,1)} %dynamic-slice_convert_fusion.6), channel_id=1, source_target_pairs={{0,4},{2,6},{4,0},{6,2},{8,12},{10,14},{12,8},{14,10},{16,20},{18,... | collective-permute-start | bytes 1769480 | tf_op jit(solution)/shard_map/ppermute | solution.py:143
  204.5 6.9 %collective-permute-start.34 = (bf16[1,48,768]{2,1,0:T(8,128)(2,1)S(1)}, bf16[1,48,768]{2,1,0:T(8,128)(2,1)S(1)}, u32[]{:S(2)}, u32[]{:S(2)}) collective-permute-start(bf16[1,48,768]{2,1,0:T(8,128)(2,1)S(1)} %get-tuple-element.216), channel_id=1, source_target_pairs={{0,8},{2,10},{4,12},{6,14},{8,16},{10,18},{12,20},{14,22},{16,24},... | collective-permute-start | bytes 221192 | tf_op jit(solution)/shard_map/ppermute | solution.py:116
  205.4 8.1 %collective-permute-start.33 = (bf16[1,48,768]{2,1,0:T(8,128)(2,1)S(1)}, bf16[1,48,768]{2,1,0:T(8,128)(2,1)S(1)}, u32[]{:S(2)}, u32[]{:S(2)}) collective-permute-start(bf16[1,48,768]{2,1,0:T(8,128)(2,1)S(1)} %collective-permute-done.32), channel_id=1, source_target_pairs={{0,8},{2,10},{4,12},{6,14},{8,16},{10,18},{12,20},{14,22},{16,24},... | collective-permute-start | bytes 221192 | tf_op jit(solution)/shard_map/ppermute | solution.py:116
  211.4 6.2 %collective-permute-start.35 = (bf16[1,48,768]{2,1,0:T(8,128)(2,1)S(1)}, bf16[1,48,768]{2,1,0:T(8,128)(2,1)S(1)}, u32[]{:S(2)}, u32[]{:S(2)}) collective-permute-start(bf16[1,48,768]{2,1,0:T(8,128)(2,1)S(1)} %collective-permute-done.34), channel_id=1, source_target_pairs={{0,8},{2,10},{4,12},{6,14},{8,16},{10,18},{12,20},{14,22},{16,24},... | collective-permute-start | bytes 221192 | tf_op jit(solution)/shard_map/ppermute | solution.py:116
  221.7 7.0 %collective-permute-start.39 = (bf16[1,48,768]{2,1,0:T(8,128)(2,1)S(1)}, bf16[1,48,768]{2,1,0:T(8,128)(2,1)S(1)}, u32[]{:S(2)}, u32[]{:S(2)}) collective-permute-start(bf16[1,48,768]{2,1,0:T(8,128)(2,1)S(1)} %collective-permute-done.33), channel_id=1, source_target_pairs={{0,8},{2,10},{4,12},{6,14},{8,16},{10,18},{12,20},{14,22},{16,24},... | collective-permute-start | bytes 221192 | tf_op jit(solution)/shard_map/ppermute | solution.py:116
  221.8 13.4 %collective-permute-start.38 = (bf16[1,1,1,48,1536]{4,3,2,1,0:T(8,128)(2,1)S(1)}, bf16[1,1,1,48,1536]{4,3,2,1,0:T(8,128)(2,1)S(1)}, u32[]{:S(2)}, u32[]{:S(2)}) collective-permute-start(bf16[1,1,1,48,1536]{4,3,2,1,0:T(8,128)(2,1)S(1)} %dynamic-slice_convert_fusion.8), channel_id=1, source_target_pairs={{0,8},{2,10},{4,12},{6,14},{8,16},{10,18},{12,20},{14,22},{16,24},... | collective-permute-start | bytes 442376 | tf_op jit(solution)/shard_map/ppermute | solution.py:143
  225.2 10.1 %collective-permute-start.37 = (bf16[1,1,1,48,1536]{4,3,2,1,0:T(8,128)(2,1)S(1)}, bf16[1,1,1,48,1536]{4,3,2,1,0:T(8,128)(2,1)S(1)}, u32[]{:S(2)}, u32[]{:S(2)}) collective-permute-start(bf16[1,1,1,48,1536]{4,3,2,1,0:T(8,128)(2,1)S(1)} %dynamic-slice_convert_fusion.9), channel_id=1, source_target_pairs={{0,8},{2,10},{4,12},{6,14},{8,16},{10,18},{12,20},{14,22},{16,24},... | collective-permute-start | bytes 442376 | tf_op jit(solution)/shard_map/ppermute | solution.py:143
  226.8 8.5 %collective-permute-start.40 = (bf16[1,48,768]{2,1,0:T(8,128)(2,1)S(1)}, bf16[1,48,768]{2,1,0:T(8,128)(2,1)S(1)}, u32[]{:S(2)}, u32[]{:S(2)}) collective-permute-start(bf16[1,48,768]{2,1,0:T(8,128)(2,1)S(1)} %collective-permute-done.35), channel_id=1, source_target_pairs={{0,8},{2,10},{4,12},{6,14},{8,16},{10,18},{12,20},{14,22},{16,24},... | collective-permute-start | bytes 221192 | tf_op jit(solution)/shard_map/ppermute | solution.py:116
  235.3 10.3 %collective-permute-start.45 = (bf16[4,48,768]{2,1,0:T(8,128)(2,1)S(1)}, bf16[4,48,768]{2,1,0:T(8,128)(2,1)S(1)}, u32[]{:S(2)}, u32[]{:S(2)}) collective-permute-start(bf16[4,48,768]{2,1,0:T(8,128)(2,1)S(1)} %pad_maximum_fusion.8), channel_id=1, source_target_pairs={{0,4},{2,6},{4,0},{6,2},{8,12},{10,14},{12,8},{14,10},{16,20},{18,... | collective-permute-start | bytes 884744 | tf_op jit(solution)/shard_map/ppermute | solution.py:116
  235.7 9.9 %collective-permute-start.44 = (bf16[4,48,768]{2,1,0:T(8,128)(2,1)S(1)}, bf16[4,48,768]{2,1,0:T(8,128)(2,1)S(1)}, u32[]{:S(2)}, u32[]{:S(2)}) collective-permute-start(bf16[4,48,768]{2,1,0:T(8,128)(2,1)S(1)} %pad_maximum_fusion.7), channel_id=1, source_target_pairs={{0,2},{2,0},{4,6},{6,4},{8,10},{10,8},{12,14},{14,12},{16,18},{18,... | collective-permute-start | bytes 884744 | tf_op jit(solution)/shard_map/ppermute | solution.py:116
  236.9 7.7 %collective-permute-start.43 = (bf16[1,1,1,48,1536]{4,3,2,1,0:T(8,128)(2,1)S(1)}, bf16[1,1,1,48,1536]{4,3,2,1,0:T(8,128)(2,1)S(1)}, u32[]{:S(2)}, u32[]{:S(2)}) collective-permute-start(bf16[1,1,1,48,1536]{4,3,2,1,0:T(8,128)(2,1)S(1)} %add_convert_fusion.4), channel_id=1, source_target_pairs={{0,8},{2,10},{4,12},{6,14},{8,16},{10,18},{12,20},{14,22},{16,24},... | collective-permute-start | bytes 442376 | tf_op jit(solution)/shard_map/ppermute | solution.py:143
  238.0 7.6 %collective-permute-start.42 = (bf16[1,1,1,48,1536]{4,3,2,1,0:T(8,128)(2,1)S(1)}, bf16[1,1,1,48,1536]{4,3,2,1,0:T(8,128)(2,1)S(1)}, u32[]{:S(2)}, u32[]{:S(2)}) collective-permute-start(bf16[1,1,1,48,1536]{4,3,2,1,0:T(8,128)(2,1)S(1)} %add_convert_fusion.5), channel_id=1, source_target_pairs={{0,8},{2,10},{4,12},{6,14},{8,16},{10,18},{12,20},{14,22},{16,24},... | collective-permute-start | bytes 442376 | tf_op jit(solution)/shard_map/ppermute | solution.py:143
  245.7 13.8 %collective-permute-start.49 = (bf16[8,48,768]{2,1,0:T(8,128)(2,1)S(1)}, bf16[8,48,768]{2,1,0:T(8,128)(2,1)S(1)}, u32[]{:S(2)}, u32[]{:S(2)}) collective-permute-start(bf16[8,48,768]{2,1,0:T(8,128)(2,1)S(1)} %constant_dynamic-update-slice_fusion.20.refs_0_), channel_id=1, source_target_pairs={{0,4},{2,6},{4,0},{6,2},{8,12},{10,14},{12,8},{14,10},{16,20},{18,... | collective-permute-start | bytes 1769480 | tf_op jit(solution)/shard_map/ppermute | solution.py:116
  247.5 12.5 %collective-permute-start.50 = (bf16[8,48,768]{2,1,0:T(8,128)(2,1)S(1)}, bf16[8,48,768]{2,1,0:T(8,128)(2,1)S(1)}, u32[]{:S(2)}, u32[]{:S(2)}) collective-permute-start(bf16[8,48,768]{2,1,0:T(8,128)(2,1)S(1)} %constant_dynamic-update-slice_fusion.25.refs_2_), channel_id=1, source_target_pairs={{0,2},{2,0},{4,6},{6,4},{8,10},{10,8},{12,14},{14,12},{16,18},{18,... | collective-permute-start | bytes 1769480 | tf_op jit(solution)/shard_map/ppermute | solution.py:116
  248.8 10.7 %collective-permute-start.48 = (bf16[1,1,1,48,1536]{4,3,2,1,0:T(8,128)(2,1)S(1)}, bf16[1,1,1,48,1536]{4,3,2,1,0:T(8,128)(2,1)S(1)}, u32[]{:S(2)}, u32[]{:S(2)}) collective-permute-start(bf16[1,1,1,48,1536]{4,3,2,1,0:T(8,128)(2,1)S(1)} %add_convert_fusion.2), channel_id=1, source_target_pairs={{0,8},{2,10},{4,12},{6,14},{8,16},{10,18},{12,20},{14,22},{16,24},... | collective-permute-start | bytes 442376 | tf_op jit(solution)/shard_map/ppermute | solution.py:143
  248.9 10.6 %collective-permute-start.47 = (bf16[1,1,1,48,1536]{4,3,2,1,0:T(8,128)(2,1)S(1)}, bf16[1,1,1,48,1536]{4,3,2,1,0:T(8,128)(2,1)S(1)}, u32[]{:S(2)}, u32[]{:S(2)}) collective-permute-start(bf16[1,1,1,48,1536]{4,3,2,1,0:T(8,128)(2,1)S(1)} %add_convert_fusion.3), channel_id=1, source_target_pairs={{0,8},{2,10},{4,12},{6,14},{8,16},{10,18},{12,20},{14,22},{16,24},... | collective-permute-start | bytes 442376 | tf_op jit(solution)/shard_map/ppermute | solution.py:143
  249.2 10.3 %collective-permute-start.51 = (f32[13,768]{1,0:T(8,128)S(1)}, f32[13,768]{1,0:T(8,128)S(1)}, u32[]{:S(2)}, u32[]{:S(2)}) collective-permute-start(f32[13,768]{1,0:T(8,128)S(1)} %add.434), channel_id=1, source_target_pairs={{0,4},{2,6},{4,0},{6,2},{8,12},{10,14},{12,8},{14,10},{16,20},{18,... | collective-permute-start | bytes 119816 | tf_op jit(solution)/shard_map/ppermute | solution.py:211
  260.0 10.3 %collective-permute-start.54 = (f32[13,768]{1,0:T(8,128)S(1)}, f32[13,768]{1,0:T(8,128)S(1)}, u32[]{:S(2)}, u32[]{:S(2)}) collective-permute-start(f32[13,768]{1,0:T(8,128)S(1)} %add.439), channel_id=1, source_target_pairs={{0,8},{2,10},{4,12},{6,14},{8,0},{10,2},{12,4},{14,6},{16,24},{18,... | collective-permute-start | bytes 119816 | tf_op jit(solution)/shard_map/ppermute | solution.py:211
  261.0 9.4 %collective-permute-start.52 = (bf16[1,48,1536]{2,1,0:T(8,128)(2,1)S(1)}, bf16[1,48,1536]{2,1,0:T(8,128)(2,1)S(1)}, u32[]{:S(2)}, u32[]{:S(2)}) collective-permute-start(bf16[1,48,1536]{2,1,0:T(8,128)(2,1)S(1)} %get-tuple-element.212), channel_id=1, source_target_pairs={{0,8},{2,10},{4,12},{6,14},{8,16},{10,18},{12,20},{14,22},{16,24},... | collective-permute-start | bytes 442376 | tf_op jit(solution)/shard_map/ppermute | solution.py:116
  263.9 7.2 %collective-permute-start.53 = (bf16[1,48,1536]{2,1,0:T(8,128)(2,1)S(1)}, bf16[1,48,1536]{2,1,0:T(8,128)(2,1)S(1)}, u32[]{:S(2)}, u32[]{:S(2)}) collective-permute-start(bf16[1,48,1536]{2,1,0:T(8,128)(2,1)S(1)} %get-tuple-element.208), channel_id=1, source_target_pairs={{0,8},{2,10},{4,12},{6,14},{8,16},{10,18},{12,20},{14,22},{16,24},... | collective-permute-start | bytes 442376 | tf_op jit(solution)/shard_map/ppermute | solution.py:116
  271.1 12.7 %collective-permute-start.55 = (bf16[1,48,1536]{2,1,0:T(8,128)(2,1)S(1)}, bf16[1,48,1536]{2,1,0:T(8,128)(2,1)S(1)}, u32[]{:S(2)}, u32[]{:S(2)}) collective-permute-start(bf16[1,48,1536]{2,1,0:T(8,128)(2,1)S(1)} %collective-permute-done.52), channel_id=1, source_target_pairs={{0,8},{2,10},{4,12},{6,14},{8,16},{10,18},{12,20},{14,22},{16,24},... | collective-permute-start | bytes 442376 | tf_op jit(solution)/shard_map/ppermute | solution.py:116
  271.4 12.4 %collective-permute-start.56 = (bf16[1,48,1536]{2,1,0:T(8,128)(2,1)S(1)}, bf16[1,48,1536]{2,1,0:T(8,128)(2,1)S(1)}, u32[]{:S(2)}, u32[]{:S(2)}) collective-permute-start(bf16[1,48,1536]{2,1,0:T(8,128)(2,1)S(1)} %collective-permute-done.53), channel_id=1, source_target_pairs={{0,8},{2,10},{4,12},{6,14},{8,16},{10,18},{12,20},{14,22},{16,24},... | collective-permute-start | bytes 442376 | tf_op jit(solution)/shard_map/ppermute | solution.py:116
  273.3 10.5 %collective-permute-start.57 = (f32[13,768]{1,0:T(8,128)S(1)}, f32[13,768]{1,0:T(8,128)S(1)}, u32[]{:S(2)}, u32[]{:S(2)}) collective-permute-start(f32[13,768]{1,0:T(8,128)S(1)} %add.440), channel_id=1, source_target_pairs={{0,16},{2,18},{4,20},{6,22},{8,24},{10,26},{12,28},{14,30},{16,0},... | collective-permute-start | bytes 119816 | tf_op jit(solution)/shard_map/ppermute | solution.py:211
  283.8 6.9 %collective-permute-start.58 = (bf16[1,48,1536]{2,1,0:T(8,128)(2,1)S(1)}, bf16[1,48,1536]{2,1,0:T(8,128)(2,1)S(1)}, u32[]{:S(2)}, u32[]{:S(2)}) collective-permute-start(bf16[1,48,1536]{2,1,0:T(8,128)(2,1)S(1)} %collective-permute-done.55), channel_id=1, source_target_pairs={{0,8},{2,10},{4,12},{6,14},{8,16},{10,18},{12,20},{14,22},{16,24},... | collective-permute-start | bytes 442376 | tf_op jit(solution)/shard_map/ppermute | solution.py:116
  283.8 8.5 %collective-permute-start.59 = (bf16[1,48,1536]{2,1,0:T(8,128)(2,1)S(1)}, bf16[1,48,1536]{2,1,0:T(8,128)(2,1)S(1)}, u32[]{:S(2)}, u32[]{:S(2)}) collective-permute-start(bf16[1,48,1536]{2,1,0:T(8,128)(2,1)S(1)} %collective-permute-done.56), channel_id=1, source_target_pairs={{0,8},{2,10},{4,12},{6,14},{8,16},{10,18},{12,20},{14,22},{16,24},... | collective-permute-start | bytes 442376 | tf_op jit(solution)/shard_map/ppermute | solution.py:116
  292.5 16.2 %collective-permute-start.61 = (bf16[4,48,1536]{2,1,0:T(8,128)(2,1)S(1)}, bf16[4,48,1536]{2,1,0:T(8,128)(2,1)S(1)}, u32[]{:S(2)}, u32[]{:S(2)}) collective-permute-start(bf16[4,48,1536]{2,1,0:T(8,128)(2,1)S(1)} %pad_maximum_fusion.4), channel_id=1, source_target_pairs={{0,4},{2,6},{4,0},{6,2},{8,12},{10,14},{12,8},{14,10},{16,20},{18,... | collective-permute-start | bytes 1769480 | tf_op jit(solution)/shard_map/ppermute | solution.py:116
  293.6 16.2 %collective-permute-start.60 = (bf16[4,48,1536]{2,1,0:T(8,128)(2,1)S(1)}, bf16[4,48,1536]{2,1,0:T(8,128)(2,1)S(1)}, u32[]{:S(2)}, u32[]{:S(2)}) collective-permute-start(bf16[4,48,1536]{2,1,0:T(8,128)(2,1)S(1)} %pad_maximum_fusion.3), channel_id=1, source_target_pairs={{0,2},{2,0},{4,6},{6,4},{8,10},{10,8},{12,14},{14,12},{16,18},{18,... | collective-permute-start | bytes 1769480 | tf_op jit(solution)/shard_map/ppermute | solution.py:116
  309.8 17.4 %collective-permute-start.62 = (bf16[8,48,1536]{2,1,0:T(8,128)(2,1)S(1)}, bf16[8,48,1536]{2,1,0:T(8,128)(2,1)S(1)}, u32[]{:S(2)}, u32[]{:S(2)}) collective-permute-start(bf16[8,48,1536]{2,1,0:T(8,128)(2,1)S(1)} %constant_dynamic-update-slice_fusion.30.refs_0_), channel_id=1, source_target_pairs={{0,4},{2,6},{4,0},{6,2},{8,12},{10,14},{12,8},{14,10},{16,20},{18,... | collective-permute-start | bytes 3538952 | tf_op jit(solution)/shard_map/ppermute | solution.py:116
  311.0 22.1 %collective-permute-start.63 = (bf16[8,48,1536]{2,1,0:T(8,128)(2,1)S(1)}, bf16[8,48,1536]{2,1,0:T(8,128)(2,1)}, u32[]{:S(2)}, u32[]{:S(2)}) collective-permute-start(bf16[8,48,1536]{2,1,0:T(8,128)(2,1)S(1)} %constant_dynamic-update-slice_fusion.35.refs_0_), channel_id=1, source_target_pairs={{0,2},{2,0},{4,6},{6,4},{8,10},{10,8},{12,14},{14,12},{16,18},{18,... | collective-permute-start | bytes 3538952 | tf_op jit(solution)/shard_map/ppermute | solution.py:116
  379.2 5.7 %collective-permute-start.66 = (f32[48,768]{1,0:T(8,128)S(1)}, f32[48,768]{1,0:T(8,128)S(1)}, u32[]{:S(2)}, u32[]{:S(2)}) collective-permute-start(f32[48,768]{1,0:T(8,128)S(1)} %get-tuple-element.244), channel_id=1, source_target_pairs={{0,3},{1,2},{2,1},{3,0},{4,7},{5,6},{6,5},{7,4},{8,11},{9,10},{10,... | collective-permute-start | bytes 442376 | tf_op jit(solution)/shard_map/ppermute | solution.py:763
  380.4 8.1 %collective-permute-start.65 = (f32[48,768]{1,0:T(8,128)S(1)}, f32[48,768]{1,0:T(8,128)S(1)}, u32[]{:S(2)}, u32[]{:S(2)}) collective-permute-start(f32[48,768]{1,0:T(8,128)S(1)} %get-tuple-element.244), channel_id=1, source_target_pairs={{0,2},{1,3},{2,0},{3,1},{4,6},{5,7},{6,4},{7,5},{8,10},{9,11},{10,... | collective-permute-start | bytes 442376 | tf_op jit(solution)/shard_map/ppermute | solution.py:763
  (48 other events, 433.9 us)

commit v5 on v4

--- a/solution.py
+++ b/solution.py
@@ -18,7 +18,11 @@
 QUERY_TILE = 512
 FEED_TILE = 512
 NEWTON_TILE = 256
-VMEM_LIMIT = 48 * 1024 * 1024
+MEBIBYTE = 1024 * 1024
+PLACE_VMEM = 8 * MEBIBYTE
+ATTENTION_VMEM = 26 * MEBIBYTE
+FEED_VMEM = 26 * MEBIBYTE
+NEWTON_VMEM = 32 * MEBIBYTE
 
 
 X_FIRST = (0, 1, 2)
@@ -48,11 +52,11 @@
     return DATA_AXES.get(count, ((1, count), (count, 1), (count, 1)))
 
 
-def ring(count, stride, size):
+def ring(count, stride, size, distance):
     pairs = []
     for index in range(count):
         place = (index // stride) % size
-        pairs.append((index, index + ((place + 1) % size - place) * stride))
+        pairs.append((index, index + ((place + distance) % size - place) * stride))
     return pairs
 
 
@@ -96,31 +100,53 @@
 def gather_steps(share, orders):
     count = lax.axis_size("dp")
     width = share.shape[1] // len(orders)
+    pieces = [[share[None]]]
+    for stage in range(len(orders[0])):
+        if stage == 1:
+            pieces = [
+                [part[:, :, piece * width : (piece + 1) * width] for part in pieces[0]]
+                for piece in range(len(orders))
+            ]
+        heads, sends = [], []
+        for parts, order in zip(pieces, orders):
+            stride, size = data_axes(count)[order[stage]]
+            heads.append(jnp.concatenate(parts, 0) if len(parts) > 1 else parts[0])
+            sends.append([ring(count, stride, size, step) for step in range(1, size)])
+        got = yield [(head, perm) for head, perms in zip(heads, sends) for perm in perms]
+        pieces = []
+        for head, perms in zip(heads, sends):
+            pieces.append([head] + got[: len(perms)])
+            got = got[len(perms) :]
+    return pieces
+
+
+def ring_gather_steps(share, orders):
+    count = lax.axis_size("dp")
+    width = share.shape[1] // len(orders)
     pieces = [
         [share[None, :, piece * width : (piece + 1) * width]] for piece in range(len(orders))
     ]
-    hops = sum(size - 1 for _, size in data_axes(count))
     plans = [
         [(axis, hop) for axis in order for hop in range(data_axes(count)[axis][1] - 1)]
         for order in orders
     ]
     moving = [None] * len(orders)
-    for step in range(hops):
+    for step in range(len(plans[0])):
+        sends = []
         for piece, plan in enumerate(plans):
             axis, hop = plan[step]
-            stride, size = data_axes(count)[axis]
             if hop == 0:
                 parts = pieces[piece]
                 moving[piece] = jnp.concatenate(parts, 0) if len(parts) > 1 else parts[0]
                 pieces[piece] = [moving[piece]]
-            moving[piece] = lax.ppermute(moving[piece], "dp", ring(count, stride, size))
-        moving = list((yield moving))
+            sends.append((moving[piece], ring(count, *data_axes(count)[axis], 1)))
+        moving = yield sends
         for parts, part in zip(pieces, moving):
             parts.append(part)
     return pieces
 
 
-def scatter_steps(partial, order):
+def ring_scatter_steps(partial, order):
     count = lax.axis_size("dp")
     rank = lax.axis_index("dp")
     axes = data_axes(count)
@@ -131,7 +157,6 @@
         stride, size = axes[axis]
         if size == 1:
             continue
-        perm = ring(count, stride, size)
         place = (rank // stride) % size
         dim = slow_first.index(axis)
 
@@ -140,7 +165,7 @@
 
         total = block(place + size - 1)
         for step in range(size - 1):
-            (got,) = yield [lax.ppermute(total.astype(jnp.bfloat16), "dp", perm)]
+            (got,) = yield [(total.astype(jnp.bfloat16), ring(count, stride, size, 1))]
             total = block(place + 2 * size - 2 - step) + got.astype(jnp.float32)
         held = total
     return held.reshape(rows, columns)
@@ -150,32 +175,60 @@
     def __init__(self, steps):
         self.steps = steps
         self.moving = None
+        self.perms = []
         self.result = None
 
+    def load(self):
+        if self.result is not None:
+            return
+        try:
+            sends = self.steps.send(self.moving)
+            self.moving = [value for value, _ in sends]
+            self.perms = [perm for _, perm in sends]
+        except StopIteration as stop:
+            self.moving, self.perms = [], []
+            self.result = stop.value
+
+    def send(self):
+        self.moving = [
+            lax.ppermute(value, "dp", perm) for value, perm in zip(self.moving, self.perms)
+        ]
+
     def hop(self):
-        if self.result is None:
-            try:
-                self.moving = self.steps.send(self.moving)
-            except StopIteration as stop:
-                self.moving = []
-                self.result = stop.value
+        self.load()
+        self.send()
 
     def finish(self):
-        while self.result is None:
-            self.hop()
-        return self.result
-
-
-def hop_all(*travels):
-    for travel in travels:
-        travel.hop()
-
-
-def arrived(travels, beside):
+        while True:
+            self.load()
+            if self.result is not None:
+                return self.result
+            self.send()
+
+
+def joined(travels, beside):
     moving, beside = lax.optimization_barrier(([travel.moving for travel in travels], beside))
     for travel, value in zip(travels, moving):
         travel.moving = value
     return beside
+
+
+def depart(travels, beside=()):
+    for travel in travels:
+        travel.load()
+    beside = joined(travels, beside)
+    for travel in travels:
+        travel.send()
+    return beside
+
+
+def hop_all(*travels):
+    for travel in travels:
+        travel.hop()
+
+
+def arrive(travels, beside=()):
+    return joined(travels, beside)
 
 
 def placed(pieces, orders):
@@ -189,7 +242,7 @@
         out_specs=pl.BlockSpec(memory_space=pltpu.VMEM),
         out_shape=jax.ShapeDtypeStruct((count, rows, width * len(orders)), dtype),
         scratch_shapes=[pltpu.SemaphoreType.DMA((count * len(orders),))],
-        compiler_params=pltpu.CompilerParams(vmem_limit_bytes=VMEM_LIMIT),
+        compiler_params=pltpu.CompilerParams(vmem_limit_bytes=PLACE_VMEM),
         cost_estimate=pl.CostEstimate(
             flops=0, bytes_accessed=4 * count * rows * width * len(orders), transcendentals=0
         ),
@@ -202,13 +255,10 @@
 
 
 def sum_steps(value):
-    (got,) = yield [other_core(value)]
-    value = value + got
     count = lax.axis_size("dp")
     distance = 1
     while distance < count:
-        pairs = [(index, index ^ distance) for index in range(count)]
-        (got,) = yield [lax.ppermute(value, "dp", pairs)]
+        (got,) = yield [(value, [(index, index ^ distance) for index in range(count)])]
         value = value + got
         distance *= 2
     return value
@@ -347,7 +397,7 @@
             jax.ShapeDtypeStruct((width, length), jnp.bfloat16),
         ],
         scratch_shapes=[pltpu.VMEM((length, HEAD_DIM), jnp.float32)] * 2,
-        compiler_params=pltpu.CompilerParams(vmem_limit_bytes=VMEM_LIMIT),
+        compiler_params=pltpu.CompilerParams(vmem_limit_bytes=ATTENTION_VMEM),
         cost_estimate=pl.CostEstimate(
             flops=heads * 36 * length * length * HEAD_DIM,
             bytes_accessed=width * length * 8,
@@ -454,7 +504,7 @@
             pltpu.VMEM((2, D, D), jnp.bfloat16),
             pltpu.VMEM((2, D + wanted, D), jnp.bfloat16),
         ],
-        compiler_params=pltpu.CompilerParams(vmem_limit_bytes=VMEM_LIMIT),
+        compiler_params=pltpu.CompilerParams(vmem_limit_bytes=NEWTON_VMEM),
         cost_estimate=pl.CostEstimate(
             flops=(NS_STEPS - 1) * 12 * D * D * D, bytes_accessed=8 * D * D, transcendentals=0
         ),
@@ -475,30 +525,31 @@
     sum_ref[...] = jnp.sum(back.astype(jnp.float32), axis=0, keepdims=True)
 
 
-def feed_forward(norm, upstream, widen, narrow, bias):
+def feed_forward(norm, upstream, weights, bias):
     length, width = norm.shape
-    hidden = widen.shape[1]
+    hidden = weights.shape[1] // 2
+    tiles = hidden // FEED_TILE
 
     def whole():
         return pl.BlockSpec((length, width), lambda tile: (0, 0))
 
-    def columns(rows):
-        return pl.BlockSpec((rows, FEED_TILE), lambda tile: (0, tile))
+    def columns(rows, first=0):
+        return pl.BlockSpec((rows, FEED_TILE), lambda tile: (0, tile + first))
 
     return pl.pallas_call(
         feed_kernel,
-        grid=(hidden // FEED_TILE,),
-        in_specs=[whole(), whole(), columns(width), columns(width), columns(1)],
+        grid=(tiles,),
+        in_specs=[whole(), whole(), columns(width), columns(width, tiles), columns(1)],
         out_specs=[columns(length), columns(length), columns(1)],
         out_shape=[jax.ShapeDtypeStruct((length, hidden), jnp.bfloat16)] * 2
         + [jax.ShapeDtypeStruct((1, hidden), jnp.float32)],
-        compiler_params=pltpu.CompilerParams(vmem_limit_bytes=VMEM_LIMIT),
+        compiler_params=pltpu.CompilerParams(vmem_limit_bytes=FEED_VMEM),
         cost_estimate=pl.CostEstimate(
             flops=4 * length * width * hidden,
             bytes_accessed=4 * length * (width + hidden) + 4 * width * hidden,
             transcendentals=4 * length * hidden,
         ),
-    )(norm, upstream, widen, narrow, bias[None])
+    )(norm, upstream, weights, weights, bias[None])
 
 
 def shards(
@@ -527,23 +578,16 @@
     widen_cols = widen_weight.shape[1]
     widen_rows = FF // D
     feature_share = D // tensor_size
-    widen_order, narrow_order = (Z_THEN_X,), (Z_THEN_Y,)
 
     joint_gather = Travel(
         gather_steps(
             jnp.concatenate([attend_weight, output_weight], 1).astype(jnp.bfloat16), Z_ORDERS
         )
     )
-    joint_gather.hop()
-    widen_share, narrow_share = arrived(
-        [joint_gather], (widen_weight.astype(jnp.bfloat16), narrow_weight.astype(jnp.bfloat16))
-    )
-    widen_gather = Travel(gather_steps(widen_share, widen_order))
-    narrow_gather = Travel(gather_steps(narrow_share, narrow_order))
-    feeds = (widen_gather, narrow_gather)
-    joint_gather.hop()
-    layer_input, cotangent = arrived([joint_gather], (layer_input, cotangent))
-    joint_gather.hop()
+    layer_input, cotangent, widen_weight, narrow_weight = depart(
+        [joint_gather], (layer_input, cotangent, widen_weight, narrow_weight)
+    )
+    feed_share = jnp.concatenate([widen_weight, narrow_weight], 1).astype(jnp.bfloat16)
     float_input = layer_input.astype(jnp.float32)
     first_gain = vector_params[0]
     second_gain = vector_params[2]
@@ -554,23 +598,25 @@
         vector_params[8 : 8 + widen_rows].reshape(-1), tensor_rank * widen_cols, widen_cols
     )
     normed, inverse = norm_stats(float_input)
-    inverse = arrived([joint_gather], inverse)
-    hop_all(joint_gather, *feeds)
+    inverse, feed_share = arrive([joint_gather], (inverse, feed_share))
+    feed_gather = Travel(gather_steps(feed_share, Z_ORDERS))
+    depart([joint_gather])
+    depart([feed_gather])
     first_norm = (normed * first_gain + vector_params[1]).astype(jnp.bfloat16)
     second_norm = (normed * second_gain + vector_params[3]).astype(jnp.bfloat16)
-    first_norm, second_norm = arrived([joint_gather, *feeds], (first_norm, second_norm))
-    hop_all(joint_gather, *feeds)
-    hop_all(*feeds)
+    first_norm, second_norm, cotangent = arrive(
+        [joint_gather], (first_norm, second_norm, cotangent)
+    )
+    cotangent, segment_ids = depart([joint_gather], (cotangent, segment_ids))
     live_rows = (segment_ids >= 0).astype(jnp.float32)[:, None]
     upstream = live_rows * cotangent.astype(jnp.float32)
     upstream_low = upstream.astype(jnp.bfloat16)
-    bias_grad = jnp.sum(upstream, axis=0) / tensor_size
     cosines, sines = rotary_tables(segment_ids)
-    upstream_low, bias_grad, cosines, sines = arrived(
-        [joint_gather, *feeds], (upstream_low, bias_grad, cosines, sines)
-    )
-    hop_all(*feeds)
+    upstream_low, cosines, sines = arrive(
+        [joint_gather, feed_gather], (upstream_low, cosines, sines)
+    )
     joint_low = placed(joint_gather.finish(), Z_ORDERS)
+    (joint_low,) = depart([feed_gather], (joint_low,))
     attend_low, output_low = joint_low[:, :triple_cols], joint_low[:, triple_cols:]
     triple_rows = (
         jnp.einsum("dk,sd->ks", attend_low, first_norm, preferred_element_type=jnp.float32)
@@ -579,10 +625,10 @@
     mixed_rows = jnp.einsum(
         "sd,dk->ks", upstream_low, output_low, preferred_element_type=jnp.float32
     ).astype(jnp.bfloat16)
-    triple_rows, mixed_rows = arrived(feeds, (triple_rows, mixed_rows))
-    hop_all(*feeds)
+    triple_rows, mixed_rows = arrive([feed_gather], (triple_rows, mixed_rows))
+    triple_rows, mixed_rows = depart([feed_gather], (triple_rows, mixed_rows))
     mixture_rows, triple_grad = attention(triple_rows, cosines, sines, mixed_rows, segment_ids)
-    mixture_rows, triple_grad = arrived(feeds, (mixture_rows, triple_grad))
+    mixture_rows, triple_grad = arrive([feed_gather], (mixture_rows, triple_grad))
     output_grad = jnp.einsum(
         "sd,ks->dk", upstream_low, mixture_rows, preferred_element_type=jnp.float32
     )
@@ -590,32 +636,29 @@
         "sd,ks->dk", first_norm, triple_grad, preferred_element_type=jnp.float32
     )
     joint_scatter = Travel(
-        scatter_steps(jnp.concatenate([attend_grad, output_grad], 1), X_THEN_Y)
-    )
-    widen_low = placed(widen_gather.finish(), widen_order)
-    narrow_low = placed(narrow_gather.finish(), narrow_order)
+        ring_scatter_steps(jnp.concatenate([attend_grad, output_grad], 1), Z_THEN_Y)
+    )
 
     joint_scatter.hop()
+    feed_low = placed(feed_gather.finish(), Z_ORDERS)
+    widen_low, narrow_low = feed_low[:, :widen_cols], feed_low[:, widen_cols:]
     activated, widen_back, widen_bias_grad = feed_forward(
-        second_norm, upstream_low, widen_low, narrow_low, widen_bias
-    )
-    activated, widen_back = arrived([joint_scatter], (activated, widen_back))
-    joint_scatter.hop()
+        second_norm, upstream_low, feed_low, widen_bias
+    )
     narrow_grad = jnp.einsum(
         "sd,sf->df", upstream_low, activated, preferred_element_type=jnp.float32
     )
     widen_grad = jnp.einsum(
         "sd,sf->df", second_norm, widen_back, preferred_element_type=jnp.float32
     )
-    widen_grad, narrow_grad, widen_back = arrived(
-        [joint_scatter], (widen_grad, narrow_grad, widen_back)
-    )
-    widen_scatter = Travel(scatter_steps(widen_grad, X_THEN_Y))
-    narrow_scatter = Travel(scatter_steps(narrow_grad, Y_THEN_X))
+    widen_grad, narrow_grad, widen_back, activated, mixture_rows, triple_grad = arrive(
+        [joint_scatter],
+        (widen_grad, narrow_grad, widen_back, activated, mixture_rows, triple_grad),
+    )
+    widen_scatter = Travel(ring_scatter_steps(widen_grad, X_THEN_Y))
+    narrow_scatter = Travel(ring_scatter_steps(narrow_grad, Y_THEN_X))
     sums = (widen_scatter, narrow_scatter)
     hop_all(*sums, joint_scatter)
-    hop_all(joint_scatter)
-    hop_all(joint_scatter)
     row_share = length // tensor_size
     row_start = tensor_rank * row_share
     other_row = (1 - tensor_rank) * row_share
@@ -654,20 +697,11 @@
         )
     ).astype(jnp.bfloat16)
     attend_bias_grad = jnp.sum(triple_grad.astype(jnp.float32), axis=1)
-    first_total, second_total, block_output, attend_bias_grad = arrived(
-        [*sums, joint_scatter], (first_total, second_total, block_output, attend_bias_grad)
-    )
-    joint_sum = joint_scatter.finish()
-    attend_sum, output_sum = joint_sum[:, :triple_cols], joint_sum[:, triple_cols:]
-    attend_momentum = MUON_BETA * attend_moment + attend_sum
-    output_momentum = MUON_BETA * output_moment + output_sum
-    joint_gather = Travel(
-        gather_steps(
-            jnp.concatenate([attend_momentum, output_momentum], 1).astype(jnp.bfloat16), Z_ORDERS
-        )
-    )
-    hop_all(*sums, joint_gather)
-    hop_all(joint_gather)
+    bias_grad = jnp.sum(upstream, axis=0) / tensor_size
+    first_total, second_total, block_output = arrive(
+        [*sums, joint_scatter], (first_total, second_total, block_output)
+    )
+    hop_all(*sums, joint_scatter)
     normed_share = lax.dynamic_slice_in_dim(normed, row_start, row_share, 0)
     inverse_share = lax.dynamic_slice_in_dim(inverse, row_start, row_share, 0)
     upstream_share = lax.dynamic_slice_in_dim(upstream, row_start, row_share, 0)
@@ -706,35 +740,48 @@
         ],
         axis=0,
     )
-    input_grad, vector_part = arrived([*sums, joint_gather], (input_grad, vector_part))
+    input_grad, vector_part = arrive([*sums, joint_scatter], (input_grad, vector_part))
+    hop_all(*sums, joint_scatter)
+    vector_part = vector_part + other_core(vector_part)
+    (vector_part,) = arrive([*sums, joint_scatter], (vector_part,))
     vector_sum = Travel(sum_steps(vector_part))
-    for _ in range(3):
-        hop_all(*sums, joint_gather, vector_sum)
-        arrived([*sums, joint_gather, vector_sum], ())
+    hop_all(*sums, joint_scatter, vector_sum)
+    arrive([*sums, joint_scatter, vector_sum])
+    joint_sum = joint_scatter.finish()
+    attend_sum, output_sum = joint_sum[:, :triple_cols], joint_sum[:, triple_cols:]
+    attend_momentum = MUON_BETA * attend_moment + attend_sum
+    output_momentum = MUON_BETA * output_moment + output_sum
+    joint_gather = Travel(
+        ring_gather_steps(
+            jnp.concatenate([attend_momentum, output_momentum], 1).astype(jnp.bfloat16), Z_ORDERS
+        )
+    )
+    hop_all(*sums, joint_gather, vector_sum)
+    arrive([*sums, joint_gather, vector_sum])
     widen_sum, narrow_sum = widen_scatter.finish(), narrow_scatter.finish()
     widen_momentum = MUON_BETA * widen_moment + widen_sum
     narrow_momentum = MUON_BETA * narrow_moment + narrow_sum
-    widen_gather = Travel(gather_steps(widen_momentum.astype(jnp.bfloat16), widen_order))
-    narrow_gather = Travel(gather_steps(narrow_momentum.astype(jnp.bfloat16), narrow_order))
+    widen_gather = Travel(ring_gather_steps(widen_momentum.astype(jnp.bfloat16), (Z_THEN_X,)))
+    narrow_gather = Travel(ring_gather_steps(narrow_momentum.astype(jnp.bfloat16), (Z_THEN_Y,)))
     feeds = (widen_gather, narrow_gather)
-    hop_all(*feeds, vector_sum)
 
     def gram(matrix):
         return jnp.einsum("dk,ek->de", matrix, matrix, preferred_element_type=jnp.float32)
 
+    for _ in range(2):
+        hop_all(*feeds, joint_gather, vector_sum)
+        arrive([*feeds, joint_gather, vector_sum])
+    for _ in range(2):
+        hop_all(*feeds, joint_gather)
+        arrive([*feeds, joint_gather])
+    hop_all(*feeds)
     joint_whole = placed(joint_gather.finish(), Z_ORDERS)
     attend_whole, output_whole = joint_whole[:, :triple_cols], joint_whole[:, triple_cols:]
     attend_gram, output_gram = gram(attend_whole), gram(output_whole)
-    attend_gram, output_gram = arrived([*feeds, vector_sum], (attend_gram, output_gram))
-    hop_all(*feeds, vector_sum)
-    arrived([*feeds, vector_sum], ())
-    hop_all(*feeds)
-    vector_grad = arrived(feeds, vector_sum.finish())
-    hop_all(*feeds)
-    arrived(feeds, ())
-    hop_all(*feeds)
-    widen_whole = placed(widen_gather.finish(), widen_order)
-    narrow_whole = placed(narrow_gather.finish(), narrow_order)
+    attend_gram, output_gram = arrive(feeds, (attend_gram, output_gram))
+    vector_grad = vector_sum.finish()
+    widen_whole = placed(widen_gather.finish(), (Z_THEN_X,))
+    narrow_whole = placed(narrow_gather.finish(), (Z_THEN_Y,))
     grams = (attend_gram, output_gram, gram(widen_whole), gram(narrow_whole))
     summed = (attend_sum, output_sum, widen_sum, narrow_sum)
     momenta = (attend_momentum, output_momentum, widen_momentum, narrow_momentum)

time: 401 us -> 390 us (0.973)
  Pallas kernels: 81.9 us -> 70.2 us
  waiting for transfers between devices: 148 us -> 140 us
  starting transfers between devices: 65.2 us -> 73.1 us
  matrix products: 42.2 us -> 36.9 us
  other arithmetic: 34.8 us -> 39.4 us
    pallas_call x6 -> x5, Pallas kernels: 17.4 us -> 9.57 us  [placed(): pl.pallas_call(functools.partial(place_kernel, orders, [len(parts) for pa...]
    ppermute x59 -> x53, starting transfers between devices: 62.7 us -> 70.4 us  [send(): lax.ppermute(value, 'dp', perm)]
    ppermute x59 -> x53, waiting for transfers between devices: 134 us -> 127 us  [send(): lax.ppermute(value, 'dp', perm)]
    dot_general x4, matrix products: 11.6 us -> 6.55 us  [gram(): jnp.einsum('dk,ek->de', matrix, matrix, preferred_element_type=jnp.float32)]
    unnamed x110 -> x113, local copies, waits for them, and re-layouts: 16.3 us -> 17.4 us
  transfers between devices with their start and end apart: 68 -> 62, of which waited for: 39 -> 34; matrix products, arithmetic and copies ran while one was open for 16% -> 12% of each run, Pallas kernels for 10% -> 6%
where the time goes in v5:
time: 390 us; the launch traced here: 385 us
  waiting for transfers between devices  140 us (36%)
  starting transfers between devices  73.1 us (19%)
  Pallas kernels  70.2 us (18%)
  other arithmetic  39.4 us (10%)
  matrix products  36.9 us (9%)
  local copies, waits for them, and re-layouts  23.3 us (6%)
    ppermute x53, waiting for transfers between devices, send(): lax.ppermute(value, 'dp', perm)  127 us
    ppermute x53, starting transfers between devices, send(): lax.ppermute(value, 'dp', perm)  70.4 us
    pallas_call x1, Pallas kernels, newton_rows(): pl.pallas_call(newton_kernel, in_specs=[pl.BlockSpec(memory_space=pltpu.V...  30.7 us
    pallas_call x1, Pallas kernels, attention(): pl.pallas_call(attention_kernel, grid=(heads,), in_specs=[own(3 * HEAD_DI...  23.4 us
    unnamed x113, local copies, waits for them, and re-layouts  17.4 us
    pallas_call x5, Pallas kernels, placed(): pl.pallas_call(functools.partial(place_kernel, orders, [len(parts) for pa...  9.57 us
  transfers between devices with their start and end apart: 62, of which 34 were waited for; matrix products, arithmetic and copies ran while one was open for 12% of the time, Pallas kernels for 6%

profile of v5, /device:TPU:0, one launch (start us, length us, event | category | flops | bytes accessed | tf_op | source)
XLA Modules:
  0.0 385.4 jit_solution(9873062415448740397)
XLA Ops:
  3.3 3.0 collective-permute-start
  6.3 2.6 collective-permute-start.1
  10.3 1.7 convert_reduce_fusion.1
  12.8 3.1 subtract_multiply_fusion
  16.0 3.4 convert_element_type.207
  21.8 1.6 collective-permute-start.3
  24.8 2.7 collective-permute-start.7
  27.6 1.7 collective-permute-start.8
  33.8 2.0 fusion.49
  38.1 9.0 %collective-permute-done.8 = bf16[1,48,3072]{2,1,0:T(8,128)(2,1)S(1)} collective-permute-done((bf16[1,48,3072]{2,1,0:T(8,128)(2,1)S(1)}, bf16[1,48,3072]{2,1,0:T(8,128)(2,1)S(1)}, u32[]{:S(2)}, u32[]{:S(2)}) %collective-permute-start.8) | collective-permute-done | bytes 294944 | tf_op jit(solution)/shard_map/ppermute | solution.py:194
  50.7 2.4 convolution_add_fusion.triple_ref
  53.1 10.9 %collective-permute-done.10 = bf16[4,48,1536]{2,1,0:T(8,128)(2,1)S(1)} collective-permute-done((bf16[4,48,1536]{2,1,0:T(8,128)(2,1)S(1)}, bf16[4,48,1536]{2,1,0:T(8,128)(2,1)S(1)}, u32[]{:S(2)}, u32[]{:S(2)}) %collective-permute-start.10) | collective-permute-done | bytes 589856 | tf_op jit(solution)/shard_map/ppermute | solution.py:194
  66.4 23.4 %shard_map.278 = (bf16[384,1024]{1,0:T(8,128)(2,1)S(1)}, bf16[1152,1024]{1,0:T(8,128)(2,1)S(1)}) custom-call(f32[1152,1024]{1,0:T(8,128)S(1)} %convolution_add_fusion.triple_ref, f32[8,1024]{1,0:T(8,128)S(1)} %get-tuple-element.165.cos_ref, f32[8,1024]{1,0:T(8,128)S(1)} %get-tuple-element.166.sin_ref, ...), custom_call_target="tpu_custom_call" | custom-call | flops 14495514624 | bytes 9437184 | tf_op jit(solution)/shard_map/pallas_call | solution.py:390
  91.3 1.6 shard_map.279
  93.0 6.5 %shard_map.280 = (bf16[1024,1536]{1,0:T(8,128)(2,1)S(1)}, bf16[1024,1536]{1,0:T(8,128)(2,1)S(1)}, f32[1,1536]{1,0:T(1,128)S(1)}) custom-call(bf16[1024,768]{1,0:T(8,128)(2,1)S(1)} %get-tuple-element.172.norm_ref, bf16[1024,768]{1,0:T(8,128)(2,1)S(1)} %get-tuple-element.157.upstream_ref, bf16[768,3072]{1,0:T(8,128)(2,1)S(1)} %bitcast.71, ...), custom_call_target="tpu_custom_call" | custom-call | flops 4831838208 | bytes 14155776 | tf_op jit(solution)/shard_map/pallas_call | solution.py:539
  99.5 4.8 %fusion.59 = f32[768,1536]{1,0:T(8,128)} fusion(bf16[1024,768]{1,0:T(8,128)(2,1)S(1)} %get-tuple-element.157.upstream_ref, bf16[1024,1536]{1,0:T(8,128)(2,1)S(1)} %get-tuple-element.183), kind=kOutput, calls=%fused_computation.210 | convolution fusion | flops 2415919104 | bytes 9437184 | tf_op jit(solution)/shard_map/sd,sf->df/dot_general | solution.py:648
  104.4 4.0 %fusion.56 = f32[768,1152]{1,0:T(8,128)} fusion(bf16[1024,768]{1,0:T(8,128)(2,1)S(1)} %copy-done.25, bf16[1152,1024]{1,0:T(8,128)(2,1)S(1)} %get-tuple-element.180), kind=kOutput, calls=%fused_computation.207 | convolution fusion | flops 1811939328 | bytes 7471104 | tf_op jit(solution)/shard_map/sd,ks->dk/dot_general | solution.py:635
  109.4 2.6 pad_maximum_fusion
  112.1 6.9 %collective-permute-start.14 = (bf16[1,2,2,48,1536]{4,3,2,1,0:T(8,128)(2,1)S(1)}, bf16[1,2,2,48,1536]{4,3,2,1,0:T(8,128)(2,1)S(1)}, u32[]{:S(2)}, u32[]{:S(2)}) collective-permute-start(bf16[1,2,2,48,1536]{4,3,2,1,0:T(8,128)(2,1)S(1)} %dynamic-slice_convert_fusion.6), channel_id=1, source_target_pairs={{0,8},{2,10},{4,12},{6,14},{8,16},{10,18},{12,20},{14,22},{16,24},... | collective-permute-start | bytes 1769480 | tf_op jit(solution)/shard_map/ppermute | solution.py:194
  119.0 2.6 fusion.58
  121.7 7.9 %collective-permute-done.14 = bf16[1,2,2,48,1536]{4,3,2,1,0:T(8,128)(2,1)S(1)} collective-permute-done((bf16[1,2,2,48,1536]{4,3,2,1,0:T(8,128)(2,1)S(1)}, bf16[1,2,2,48,1536]{4,3,2,1,0:T(8,128)(2,1)S(1)}, u32[]{:S(2)}, u32[]{:S(2)}) %collective-permute-start.14) | collective-permute-done | bytes 589856 | tf_op jit(solution)/shard_map/ppermute | solution.py:194
  129.5 2.6 fusion
  134.5 2.6 fusion.2
  137.8 2.3 fusion.12
  143.6 2.7 collective-permute-start.17
  146.7 1.7 copy-done.22
  149.7 11.1 %collective-permute-done.17 = bf16[1,2,2,48,1536]{4,3,2,1,0:T(8,128)(2,1)S(1)} collective-permute-done((bf16[1,2,2,48,1536]{4,3,2,1,0:T(8,128)(2,1)S(1)}, bf16[1,2,2,48,1536]{4,3,2,1,0:T(8,128)(2,1)S(1)}, u32[]{:S(2)}, u32[]{:S(2)}) %collective-permute-start.17) | collective-permute-done | bytes 589856 | tf_op jit(solution)/shard_map/ppermute | solution.py:194
  160.8 8.0 %collective-permute-done.16 = bf16[4,1,2,48,1536]{4,3,2,1,0:T(8,128)(2,1)S(1)} collective-permute-done((bf16[4,1,2,48,1536]{4,3,2,1,0:T(8,128)(2,1)S(1)}, bf16[4,1,2,48,1536]{4,3,2,1,0:T(8,128)(2,1)S(1)}, u32[]{:S(2)}, u32[]{:S(2)}) %collective-permute-start.16) | collective-permute-done | bytes 1179680 | tf_op jit(solution)/shard_map/ppermute | solution.py:194
  173.8 2.5 collective-permute-start.23
  182.8 3.4 fusion.10
  186.2 5.5 %collective-permute-done.23 = bf16[1,2,2,48,1536]{4,3,2,1,0:T(8,128)(2,1)} collective-permute-done((bf16[1,2,2,48,1536]{4,3,2,1,0:T(8,128)(2,1)}, bf16[1,2,2,48,1536]{4,3,2,1,0:T(8,128)(2,1)}, u32[]{:S(2)}, u32[]{:S(2)}) %collective-permute-start.23) | collective-permute-done | bytes 589856 | tf_op jit(solution)/shard_map/ppermute | solution.py:194
  191.6 1.7 collective-permute-done.22
  193.4 3.1 collective-permute-done.21
  196.5 1.6 convert_add_fusion.6
  203.2 4.9 %collective-permute-done.26 = bf16[1,1,1,48,1536]{4,3,2,1,0:T(8,128)(2,1)S(1)} collective-permute-done((bf16[1,1,1,48,1536]{4,3,2,1,0:T(8,128)(2,1)S(1)}, bf16[1,1,1,48,1536]{4,3,2,1,0:T(8,128)(2,1)S(1)}, u32[]{:S(2)}, u32[]{:S(2)}) %collective-permute-start.26) | collective-permute-done | bytes 147488 | tf_op jit(solution)/shard_map/ppermute | solution.py:194
  208.2 1.6 collective-permute-done.25
  212.2 3.4 collective-permute-done.32
  215.6 2.0 collective-permute-done.30
  217.7 1.6 collective-permute-done.29
  222.7 3.3 collective-permute-start.35
  227.2 2.8 collective-permute-done.37
  232.9 2.0 collective-permute-start.39
  235.9 2.9 collective-permute-start.41
  240.0 5.3 %collective-permute-done.40 = bf16[1,48,768]{2,1,0:T(8,128)(2,1)S(1)} collective-permute-done((bf16[1,48,768]{2,1,0:T(8,128)(2,1)S(1)}, bf16[1,48,768]{2,1,0:T(8,128)(2,1)S(1)}, u32[]{:S(2)}, u32[]{:S(2)}) %collective-permute-start.40) | collective-permute-done | bytes 73760 | tf_op jit(solution)/shard_map/ppermute | solution.py:194
  245.3 1.6 collective-permute-done.41
  247.5 2.9 collective-permute-start.44
  252.7 3.9 %collective-permute-done.45 = bf16[1,48,768]{2,1,0:T(8,128)(2,1)S(1)} collective-permute-done((bf16[1,48,768]{2,1,0:T(8,128)(2,1)S(1)}, bf16[1,48,768]{2,1,0:T(8,128)(2,1)S(1)}, u32[]{:S(2)}, u32[]{:S(2)}) %collective-permute-start.45) | collective-permute-done | bytes 73760 | tf_op jit(solution)/shard_map/ppermute | solution.py:194
  259.4 2.0 collective-permute-start.50
  262.6 2.1 collective-permute-start.48
  264.7 5.2 %collective-permute-done.48 = bf16[1,48,1536]{2,1,0:T(8,128)(2,1)S(1)} collective-permute-done((bf16[1,48,1536]{2,1,0:T(8,128)(2,1)S(1)}, bf16[1,48,1536]{2,1,0:T(8,128)(2,1)S(1)}, u32[]{:S(2)}, u32[]{:S(2)}) %collective-permute-start.48) | collective-permute-done | bytes 147488 | tf_op jit(solution)/shard_map/ppermute | solution.py:194
  275.9 9.3 %collective-permute-done.55.refs_3_ = bf16[8,48,768]{2,1,0:T(8,128)(2,1)S(1)} collective-permute-done((bf16[8,48,768]{2,1,0:T(8,128)(2,1)S(1)}, bf16[8,48,768]{2,1,0:T(8,128)(2,1)S(1)}, u32[]{:S(2)}, u32[]{:S(2)}) %collective-permute-start.55) | collective-permute-done | bytes 589856 | tf_op jit(solution)/shard_map/ppermute | solution.py:194
  285.2 10.1 %collective-permute-done.52 = bf16[4,48,1536]{2,1,0:T(8,128)(2,1)S(1)} collective-permute-done((bf16[4,48,1536]{2,1,0:T(8,128)(2,1)S(1)}, bf16[4,48,1536]{2,1,0:T(8,128)(2,1)S(1)}, u32[]{:S(2)}, u32[]{:S(2)}) %collective-permute-start.52) | collective-permute-done | bytes 589856 | tf_op jit(solution)/shard_map/ppermute | solution.py:194
  305.2 1.7 fusion.18
  306.9 9.9 %collective-permute-done.57.refs_1_ = bf16[8,48,1536]{2,1,0:T(8,128)(2,1)} collective-permute-done((bf16[8,48,1536]{2,1,0:T(8,128)(2,1)S(1)}, bf16[8,48,1536]{2,1,0:T(8,128)(2,1)}, u32[]{:S(2)}, u32[]{:S(2)}) %collective-permute-start.57) | collective-permute-done | bytes 1179680 | tf_op jit(solution)/shard_map/ppermute | solution.py:194
  316.9 3.7 shard_map.283
  320.6 2.0 fusion.61
  322.6 1.9 shard_map.282
  325.9 2.0 fusion.60
  327.9 2.8 broadcast_select_fusion.2
  330.8 4.8 %collective-permute-done.58.second_ref = f32[768,768]{1,0:T(8,128)} collective-permute-done((f32[768,768]{1,0:T(8,128)}, f32[768,768]{1,0:T(8,128)}, u32[]{:S(2)}, u32[]{:S(2)}) %collective-permute-start.58) | collective-permute-done | bytes 2359328 | tf_op jit(solution)/shard_map/ppermute | solution.py:254
  335.6 1.7 copy-done.4
  337.3 30.7 %shard_map.284 = f32[96,768]{1,0:T(8,128)S(1)} custom-call(f32[768,768]{1,0:T(8,128)S(1)} %copy-done.4, f32[768,768]{1,0:T(8,128)} %collective-permute-done.58.second_ref, f32[96,768]{1,0:T(8,128)S(1)} %fusion.29.rows_ref), custom_call_target="tpu_custom_call" | custom-call | flops 21743271936 | bytes 4718592 | tf_op jit(solution)/shard_map/pallas_call | solution.py:496
  370.7 4.9 %collective-permute-done.59 = f32[48,768]{1,0:T(8,128)S(1)} collective-permute-done((f32[48,768]{1,0:T(8,128)S(1)}, f32[48,768]{1,0:T(8,128)S(1)}, u32[]{:S(2)}, u32[]{:S(2)}) %collective-permute-start.59) | collective-permute-done | bytes 147488 | tf_op jit(solution)/shard_map/ppermute | solution.py:810
  375.6 2.0 collective-permute-done.60
  (318 shorter events, 94.8 us)
Async XLA Ops:
  3.3 16.4 %collective-permute-start = (bf16[1,48,1536]{2,1,0:T(8,128)(2,1)}, bf16[1,48,1536]{2,1,0:T(8,128)(2,1)}, u32[]{:S(2)}, u32[]{:S(2)}) collective-permute-start(bf16[1,48,1536]{2,1,0:T(8,128)(2,1)} %pad_maximum_fusion.10), channel_id=1, source_target_pairs={{0,8},{2,10},{4,12},{6,14},{8,16},{10,18},{12,20},{14,22},{16,24},... | collective-permute-start | bytes 442376 | tf_op jit(solution)/shard_map/ppermute | solution.py:194
  6.3 13.4 %collective-permute-start.1 = (bf16[1,48,1536]{2,1,0:T(8,128)(2,1)}, bf16[1,48,1536]{2,1,0:T(8,128)(2,1)}, u32[]{:S(2)}, u32[]{:S(2)}) collective-permute-start(bf16[1,48,1536]{2,1,0:T(8,128)(2,1)} %pad_maximum_fusion.10), channel_id=1, source_target_pairs={{0,16},{2,18},{4,20},{6,22},{8,24},{10,26},{12,28},{14,30},{16,0},... | collective-permute-start | bytes 442376 | tf_op jit(solution)/shard_map/ppermute | solution.py:194
  8.9 10.8 %collective-permute-start.2 = (bf16[1,48,1536]{2,1,0:T(8,128)(2,1)}, bf16[1,48,1536]{2,1,0:T(8,128)(2,1)S(1)}, u32[]{:S(2)}, u32[]{:S(2)}) collective-permute-start(bf16[1,48,1536]{2,1,0:T(8,128)(2,1)} %pad_maximum_fusion.10), channel_id=1, source_target_pairs={{0,24},{2,26},{4,28},{6,30},{8,0},{10,2},{12,4},{14,6},{16,8},{18,... | collective-permute-start | bytes 442376 | tf_op jit(solution)/shard_map/ppermute | solution.py:194
  21.8 8.2 %collective-permute-start.3 = (bf16[4,48,768]{2,1,0:T(8,128)(2,1)S(1)}, bf16[4,48,768]{2,1,0:T(8,128)(2,1)S(1)}, u32[]{:S(2)}, u32[]{:S(2)}) collective-permute-start(bf16[4,48,768]{2,1,0:T(8,128)(2,1)S(1)} %get-tuple-element.134), channel_id=1, source_target_pairs={{0,2},{2,0},{4,6},{6,4},{8,10},{10,8},{12,14},{14,12},{16,18},{18,... | collective-permute-start | bytes 884744 | tf_op jit(solution)/shard_map/ppermute | solution.py:194
  23.3 7.8 %collective-permute-start.4 = (bf16[4,48,768]{2,1,0:T(8,128)(2,1)S(1)}, bf16[4,48,768]{2,1,0:T(8,128)(2,1)S(1)}, u32[]{:S(2)}, u32[]{:S(2)}) collective-permute-start(bf16[4,48,768]{2,1,0:T(8,128)(2,1)S(1)} %get-tuple-element.135), channel_id=1, source_target_pairs={{0,4},{2,6},{4,0},{6,2},{8,12},{10,14},{12,8},{14,10},{16,20},{18,... | collective-permute-start | bytes 884744 | tf_op jit(solution)/shard_map/ppermute | solution.py:194
  24.8 13.2 %collective-permute-start.7 = (bf16[1,48,3072]{2,1,0:T(8,128)(2,1)S(1)}, bf16[1,48,3072]{2,1,0:T(8,128)(2,1)S(1)}, u32[]{:S(2)}, u32[]{:S(2)}) collective-permute-start(bf16[1,48,3072]{2,1,0:T(8,128)(2,1)S(1)} %bitcast.90), channel_id=1, source_target_pairs={{0,8},{2,10},{4,12},{6,14},{8,16},{10,18},{12,20},{14,22},{16,24},... | collective-permute-start | bytes 884744 | tf_op jit(solution)/shard_map/ppermute | solution.py:194
  27.6 19.5 %collective-permute-start.8 = (bf16[1,48,3072]{2,1,0:T(8,128)(2,1)S(1)}, bf16[1,48,3072]{2,1,0:T(8,128)(2,1)S(1)}, u32[]{:S(2)}, u32[]{:S(2)}) collective-permute-start(bf16[1,48,3072]{2,1,0:T(8,128)(2,1)S(1)} %bitcast.91), channel_id=1, source_target_pairs={{0,16},{2,18},{4,20},{6,22},{8,24},{10,26},{12,28},{14,30},{16,0},... | collective-permute-start | bytes 884744 | tf_op jit(solution)/shard_map/ppermute | solution.py:194
  29.3 17.8 %collective-permute-start.9 = (bf16[1,48,3072]{2,1,0:T(8,128)(2,1)S(1)}, bf16[1,48,3072]{2,1,0:T(8,128)(2,1)S(1)}, u32[]{:S(2)}, u32[]{:S(2)}) collective-permute-start(bf16[1,48,3072]{2,1,0:T(8,128)(2,1)S(1)} %bitcast.92), channel_id=1, source_target_pairs={{0,24},{2,26},{4,28},{6,30},{8,0},{10,2},{12,4},{14,6},{16,8},{18,... | collective-permute-start | bytes 884744 | tf_op jit(solution)/shard_map/ppermute | solution.py:194
  31.8 15.3 %collective-permute-start.5 = (bf16[8,48,768]{2,1,0:T(8,128)(2,1)S(1)}, bf16[8,48,768]{2,1,0:T(8,128)(2,1)S(1)}, u32[]{:S(2)}, u32[]{:S(2)}) collective-permute-start(bf16[8,48,768]{2,1,0:T(8,128)(2,1)S(1)} %constant_dynamic-update-slice_fusion.refs_0_), channel_id=1, source_target_pairs={{0,4},{2,6},{4,0},{6,2},{8,12},{10,14},{12,8},{14,10},{16,20},{18,... | collective-permute-start | bytes 1769480 | tf_op jit(solution)/shard_map/ppermute | solution.py:194
  33.3 13.8 %collective-permute-start.6 = (bf16[8,48,768]{2,1,0:T(8,128)(2,1)S(1)}, bf16[8,48,768]{2,1,0:T(8,128)(2,1)S(1)}, u32[]{:S(2)}, u32[]{:S(2)}) collective-permute-start(bf16[8,48,768]{2,1,0:T(8,128)(2,1)S(1)} %constant_dynamic-update-slice_fusion.5.refs_2_), channel_id=1, source_target_pairs={{0,2},{2,0},{4,6},{6,4},{8,10},{10,8},{12,14},{14,12},{16,18},{18,... | collective-permute-start | bytes 1769480 | tf_op jit(solution)/shard_map/ppermute | solution.py:194
  48.8 15.2 %collective-permute-start.10 = (bf16[4,48,1536]{2,1,0:T(8,128)(2,1)S(1)}, bf16[4,48,1536]{2,1,0:T(8,128)(2,1)S(1)}, u32[]{:S(2)}, u32[]{:S(2)}) collective-permute-start(bf16[4,48,1536]{2,1,0:T(8,128)(2,1)S(1)} %pad_maximum_fusion.1), channel_id=1, source_target_pairs={{0,2},{2,0},{4,6},{6,4},{8,10},{10,8},{12,14},{14,12},{16,18},{18,... | collective-permute-start | bytes 1769480 | tf_op jit(solution)/shard_map/ppermute | solution.py:194
  49.4 14.9 %collective-permute-start.11 = (bf16[4,48,1536]{2,1,0:T(8,128)(2,1)S(1)}, bf16[4,48,1536]{2,1,0:T(8,128)(2,1)S(1)}, u32[]{:S(2)}, u32[]{:S(2)}) collective-permute-start(bf16[4,48,1536]{2,1,0:T(8,128)(2,1)S(1)} %pad_maximum_fusion.2), channel_id=1, source_target_pairs={{0,4},{2,6},{4,0},{6,2},{8,12},{10,14},{12,8},{14,10},{16,20},{18,... | collective-permute-start | bytes 1769480 | tf_op jit(solution)/shard_map/ppermute | solution.py:194
  64.4 26.7 %collective-permute-start.12 = (bf16[8,48,1536]{2,1,0:T(8,128)(2,1)S(1)}, bf16[8,48,1536]{2,1,0:T(8,128)(2,1)S(1)}, u32[]{:S(2)}, u32[]{:S(2)}) collective-permute-start(bf16[8,48,1536]{2,1,0:T(8,128)(2,1)S(1)} %constant_dynamic-update-slice_fusion.10.refs_0_), channel_id=1, source_target_pairs={{0,4},{2,6},{4,0},{6,2},{8,12},{10,14},{12,8},{14,10},{16,20},{18,... | collective-permute-start | bytes 3538952 | tf_op jit(solution)/shard_map/ppermute | solution.py:194
  64.9 26.4 %collective-permute-start.13 = (bf16[8,48,1536]{2,1,0:T(8,128)(2,1)S(1)}, bf16[8,48,1536]{2,1,0:T(8,128)(2,1)S(1)}, u32[]{:S(2)}, u32[]{:S(2)}) collective-permute-start(bf16[8,48,1536]{2,1,0:T(8,128)(2,1)S(1)} %constant_dynamic-update-slice_fusion.15.refs_2_), channel_id=1, source_target_pairs={{0,2},{2,0},{4,6},{6,4},{8,10},{10,8},{12,14},{14,12},{16,18},{18,... | collective-permute-start | bytes 3538952 | tf_op jit(solution)/shard_map/ppermute | solution.py:194
  89.9 47.9 %copy-start.5 = (bf16[1152,1024]{1,0:T(8,128)(2,1)}, bf16[1152,1024]{1,0:T(8,128)(2,1)S(1)}, u32[]{:S(2)}) copy-start(bf16[1152,1024]{1,0:T(8,128)(2,1)S(1)} %get-tuple-element.180) | copy-start | bytes 7077892
  112.0 60.8 %copy-start.16 = (f32[768,1536]{1,0:T(8,128)}, f32[768,1536]{1,0:T(8,128)S(1)}, u32[]{:S(2)}) copy-start(f32[768,1536]{1,0:T(8,128)S(1)} %pad_maximum_fusion) | copy-start | bytes 14155780
  112.1 17.4 %collective-permute-start.14 = (bf16[1,2,2,48,1536]{4,3,2,1,0:T(8,128)(2,1)S(1)}, bf16[1,2,2,48,1536]{4,3,2,1,0:T(8,128)(2,1)S(1)}, u32[]{:S(2)}, u32[]{:S(2)}) collective-permute-start(bf16[1,2,2,48,1536]{4,3,2,1,0:T(8,128)(2,1)S(1)} %dynamic-slice_convert_fusion.6), channel_id=1, source_target_pairs={{0,8},{2,10},{4,12},{6,14},{8,16},{10,18},{12,20},{14,22},{16,24},... | collective-permute-start | bytes 1769480 | tf_op jit(solution)/shard_map/ppermute | solution.py:194
  134.5 12.2 %collective-permute-start.20 = (f32[1024,384]{1,0:T(8,128)}, f32[1024,384]{1,0:T(8,128)S(1)}, u32[]{:S(2)}, u32[]{:S(2)}) collective-permute-start(f32[1024,384]{1,0:T(8,128)} %constant_dynamic-slice_fusion.4), channel_id=1, source_target_pairs={{0,1},{1,0},{2,3},{3,2},{4,5},{5,4},{6,7},{7,6},{8,9},{9,8},{10,11... | collective-permute-start | bytes 4718600 | tf_op jit(solution)/shard_map/ppermute | solution.py:254
  137.2 6.4 %collective-permute-start.19 = (bf16[512,768]{1,0:T(8,128)(2,1)S(1)}, bf16[512,768]{1,0:T(8,128)(2,1)S(1)}, u32[]{:S(2)}, u32[]{:S(2)}) collective-permute-start(bf16[512,768]{1,0:T(8,128)(2,1)S(1)} %dynamic-slice_convert_fusion.2), channel_id=1, source_target_pairs={{0,1},{1,0},{2,3},{3,2},{4,5},{5,4},{6,7},{7,6},{8,9},{9,8},{10,11... | collective-permute-start | bytes 2359304 | tf_op jit(solution)/shard_map/ppermute | solution.py:254
  140.2 6.3 %collective-permute-start.18 = (bf16[512,768]{1,0:T(8,128)(2,1)S(1)}, bf16[512,768]{1,0:T(8,128)(2,1)S(1)}, u32[]{:S(2)}, u32[]{:S(2)}) collective-permute-start(bf16[512,768]{1,0:T(8,128)(2,1)S(1)} %dynamic-slice_convert_fusion.3), channel_id=1, source_target_pairs={{0,1},{1,0},{2,3},{3,2},{4,5},{5,4},{6,7},{7,6},{8,9},{9,8},{10,11... | collective-permute-start | bytes 2359304 | tf_op jit(solution)/shard_map/ppermute | solution.py:254
  140.4 28.4 %collective-permute-start.16 = (bf16[4,1,2,48,1536]{4,3,2,1,0:T(8,128)(2,1)S(1)}, bf16[4,1,2,48,1536]{4,3,2,1,0:T(8,128)(2,1)S(1)}, u32[]{:S(2)}, u32[]{:S(2)}) collective-permute-start(bf16[4,1,2,48,1536]{4,3,2,1,0:T(8,128)(2,1)S(1)} %dynamic-slice_convert_fusion), channel_id=1, source_target_pairs={{0,4},{2,6},{4,0},{6,2},{8,12},{10,14},{12,8},{14,10},{16,20},{18,... | collective-permute-start | bytes 3538952 | tf_op jit(solution)/shard_map/ppermute | solution.py:194
  142.1 28.1 %collective-permute-start.15 = (bf16[4,2,1,48,1536]{4,3,2,1,0:T(8,128)(2,1)S(1)}, bf16[4,2,1,48,1536]{4,3,2,1,0:T(8,128)(2,1)S(1)}, u32[]{:S(2)}, u32[]{:S(2)}) collective-permute-start(bf16[4,2,1,48,1536]{4,3,2,1,0:T(8,128)(2,1)S(1)} %dynamic-slice_convert_fusion.1), channel_id=1, source_target_pairs={{0,2},{2,0},{4,6},{6,4},{8,10},{10,8},{12,14},{14,12},{16,18},{18,... | collective-permute-start | bytes 3538952 | tf_op jit(solution)/shard_map/ppermute | solution.py:194
  143.6 17.2 %collective-permute-start.17 = (bf16[1,2,2,48,1536]{4,3,2,1,0:T(8,128)(2,1)S(1)}, bf16[1,2,2,48,1536]{4,3,2,1,0:T(8,128)(2,1)S(1)}, u32[]{:S(2)}, u32[]{:S(2)}) collective-permute-start(bf16[1,2,2,48,1536]{4,3,2,1,0:T(8,128)(2,1)S(1)} %add_convert_fusion.3), channel_id=1, source_target_pairs={{0,8},{2,10},{4,12},{6,14},{8,16},{10,18},{12,20},{14,22},{16,24},... | collective-permute-start | bytes 1769480 | tf_op jit(solution)/shard_map/ppermute | solution.py:194
  172.8 10.1 %collective-permute-start.24 = (bf16[512,768]{1,0:T(8,128)(2,1)S(1)}, bf16[512,768]{1,0:T(8,128)(2,1)}, u32[]{:S(2)}, u32[]{:S(2)}) collective-permute-start(bf16[512,768]{1,0:T(8,128)(2,1)S(1)} %fusion.11), channel_id=1, source_target_pairs={{0,1},{1,0},{2,3},{3,2},{4,5},{5,4},{6,7},{7,6},{8,9},{9,8},{10,11... | collective-permute-start | bytes 2359304 | tf_op jit(solution)/shard_map/ppermute | solution.py:254
  173.8 17.8 %collective-permute-start.23 = (bf16[1,2,2,48,1536]{4,3,2,1,0:T(8,128)(2,1)}, bf16[1,2,2,48,1536]{4,3,2,1,0:T(8,128)(2,1)}, u32[]{:S(2)}, u32[]{:S(2)}) collective-permute-start(bf16[1,2,2,48,1536]{4,3,2,1,0:T(8,128)(2,1)} %add_convert_fusion.2), channel_id=1, source_target_pairs={{0,8},{2,10},{4,12},{6,14},{8,16},{10,18},{12,20},{14,22},{16,24},... | collective-permute-start | bytes 1769480 | tf_op jit(solution)/shard_map/ppermute | solution.py:194
  177.6 15.8 %collective-permute-start.22 = (bf16[4,1,1,48,1536]{4,3,2,1,0:T(8,128)(2,1)}, bf16[4,1,1,48,1536]{4,3,2,1,0:T(8,128)(2,1)}, u32[]{:S(2)}, u32[]{:S(2)}) collective-permute-start(bf16[4,1,1,48,1536]{4,3,2,1,0:T(8,128)(2,1)} %dynamic-slice_convert_fusion.4), channel_id=1, source_target_pairs={{0,2},{2,0},{4,6},{6,4},{8,10},{10,8},{12,14},{14,12},{16,18},{18,... | collective-permute-start | bytes 1769480 | tf_op jit(solution)/shard_map/ppermute | solution.py:194
  181.0 15.5 %collective-permute-start.21 = (bf16[4,1,1,48,1536]{4,3,2,1,0:T(8,128)(2,1)}, bf16[4,1,1,48,1536]{4,3,2,1,0:T(8,128)(2,1)}, u32[]{:S(2)}, u32[]{:S(2)}) collective-permute-start(bf16[4,1,1,48,1536]{4,3,2,1,0:T(8,128)(2,1)} %dynamic-slice_convert_fusion.5), channel_id=1, source_target_pairs={{0,4},{2,6},{4,0},{6,2},{8,12},{10,14},{12,8},{14,10},{16,20},{18,... | collective-permute-start | bytes 1769480 | tf_op jit(solution)/shard_map/ppermute | solution.py:194
  198.1 11.6 %collective-permute-start.27 = (bf16[1,1,2,48,1536]{4,3,2,1,0:T(8,128)(2,1)S(1)}, bf16[1,1,2,48,1536]{4,3,2,1,0:T(8,128)(2,1)S(1)}, u32[]{:S(2)}, u32[]{:S(2)}) collective-permute-start(bf16[1,1,2,48,1536]{4,3,2,1,0:T(8,128)(2,1)S(1)} %dynamic-slice_convert_fusion.7), channel_id=1, source_target_pairs={{0,4},{2,6},{4,0},{6,2},{8,12},{10,14},{12,8},{14,10},{16,20},{18,... | collective-permute-start | bytes 884744 | tf_op jit(solution)/shard_map/ppermute | solution.py:194
  200.1 8.1 %collective-permute-start.26 = (bf16[1,1,1,48,1536]{4,3,2,1,0:T(8,128)(2,1)S(1)}, bf16[1,1,1,48,1536]{4,3,2,1,0:T(8,128)(2,1)S(1)}, u32[]{:S(2)}, u32[]{:S(2)}) collective-permute-start(bf16[1,1,1,48,1536]{4,3,2,1,0:T(8,128)(2,1)S(1)} %dynamic-slice_convert_fusion.9), channel_id=1, source_target_pairs={{0,8},{2,10},{4,12},{6,14},{8,16},{10,18},{12,20},{14,22},{16,24},... | collective-permute-start | bytes 442376 | tf_op jit(solution)/shard_map/ppermute | solution.py:194
  201.7 8.1 %collective-permute-start.25 = (bf16[1,1,1,48,1536]{4,3,2,1,0:T(8,128)(2,1)S(1)}, bf16[1,1,1,48,1536]{4,3,2,1,0:T(8,128)(2,1)S(1)}, u32[]{:S(2)}, u32[]{:S(2)}) collective-permute-start(bf16[1,1,1,48,1536]{4,3,2,1,0:T(8,128)(2,1)S(1)} %dynamic-slice_convert_fusion.10), channel_id=1, source_target_pairs={{0,8},{2,10},{4,12},{6,14},{8,16},{10,18},{12,20},{14,22},{16,24},... | collective-permute-start | bytes 442376 | tf_op jit(solution)/shard_map/ppermute | solution.py:194
  202.0 1.2 collective-permute-start.28
  209.9 5.7 %collective-permute-start.31 = (bf16[1,1,1,48,1536]{4,3,2,1,0:T(8,128)(2,1)S(1)}, bf16[1,1,1,48,1536]{4,3,2,1,0:T(8,128)(2,1)S(1)}, u32[]{:S(2)}, u32[]{:S(2)}) collective-permute-start(bf16[1,1,1,48,1536]{4,3,2,1,0:T(8,128)(2,1)S(1)} %dynamic-slice_convert_fusion.8), channel_id=1, source_target_pairs={{0,2},{2,0},{4,6},{6,4},{8,10},{10,8},{12,14},{14,12},{16,18},{18,... | collective-permute-start | bytes 442376 | tf_op jit(solution)/shard_map/ppermute | solution.py:194
  210.7 7.0 %collective-permute-start.30 = (bf16[1,1,1,48,1536]{4,3,2,1,0:T(8,128)(2,1)S(1)}, bf16[1,1,1,48,1536]{4,3,2,1,0:T(8,128)(2,1)S(1)}, u32[]{:S(2)}, u32[]{:S(2)}) collective-permute-start(bf16[1,1,1,48,1536]{4,3,2,1,0:T(8,128)(2,1)S(1)} %add_convert_fusion.6), channel_id=1, source_target_pairs={{0,8},{2,10},{4,12},{6,14},{8,16},{10,18},{12,20},{14,22},{16,24},... | collective-permute-start | bytes 442376 | tf_op jit(solution)/shard_map/ppermute | solution.py:194
  210.8 8.5 %collective-permute-start.29 = (bf16[1,1,1,48,1536]{4,3,2,1,0:T(8,128)(2,1)S(1)}, bf16[1,1,1,48,1536]{4,3,2,1,0:T(8,128)(2,1)S(1)}, u32[]{:S(2)}, u32[]{:S(2)}) collective-permute-start(bf16[1,1,1,48,1536]{4,3,2,1,0:T(8,128)(2,1)S(1)} %add_convert_fusion.7), channel_id=1, source_target_pairs={{0,8},{2,10},{4,12},{6,14},{8,16},{10,18},{12,20},{14,22},{16,24},... | collective-permute-start | bytes 442376 | tf_op jit(solution)/shard_map/ppermute | solution.py:194
  210.8 4.8 %collective-permute-start.32 = (f32[13,768]{1,0:T(8,128)S(1)}, f32[13,768]{1,0:T(8,128)S(1)}, u32[]{:S(2)}, u32[]{:S(2)}) collective-permute-start(f32[13,768]{1,0:T(8,128)S(1)} %add.425), channel_id=1, source_target_pairs={{0,2},{2,0},{4,6},{6,4},{8,10},{10,8},{12,14},{14,12},{16,18},{18,... | collective-permute-start | bytes 119816 | tf_op jit(solution)/shard_map/ppermute | solution.py:194
  220.8 11.1 %collective-permute-start.34 = (bf16[1,1,1,48,1536]{4,3,2,1,0:T(8,128)(2,1)S(1)}, bf16[1,1,1,48,1536]{4,3,2,1,0:T(8,128)(2,1)S(1)}, u32[]{:S(2)}, u32[]{:S(2)}) collective-permute-start(bf16[1,1,1,48,1536]{4,3,2,1,0:T(8,128)(2,1)S(1)} %add_convert_fusion.4), channel_id=1, source_target_pairs={{0,8},{2,10},{4,12},{6,14},{8,16},{10,18},{12,20},{14,22},{16,24},... | collective-permute-start | bytes 442376 | tf_op jit(solution)/shard_map/ppermute | solution.py:194
  220.9 11.0 %collective-permute-start.33 = (bf16[1,1,1,48,1536]{4,3,2,1,0:T(8,128)(2,1)S(1)}, bf16[1,1,1,48,1536]{4,3,2,1,0:T(8,128)(2,1)S(1)}, u32[]{:S(2)}, u32[]{:S(2)}) collective-permute-start(bf16[1,1,1,48,1536]{4,3,2,1,0:T(8,128)(2,1)S(1)} %add_convert_fusion.5), channel_id=1, source_target_pairs={{0,8},{2,10},{4,12},{6,14},{8,16},{10,18},{12,20},{14,22},{16,24},... | collective-permute-start | bytes 442376 | tf_op jit(solution)/shard_map/ppermute | solution.py:194
  221.6 9.5 %collective-permute-start.36 = (bf16[1,48,768]{2,1,0:T(8,128)(2,1)S(1)}, bf16[1,48,768]{2,1,0:T(8,128)(2,1)S(1)}, u32[]{:S(2)}, u32[]{:S(2)}) collective-permute-start(bf16[1,48,768]{2,1,0:T(8,128)(2,1)S(1)} %get-tuple-element.259), channel_id=1, source_target_pairs={{0,8},{2,10},{4,12},{6,14},{8,16},{10,18},{12,20},{14,22},{16,24},... | collective-permute-start | bytes 221192 | tf_op jit(solution)/shard_map/ppermute | solution.py:194
  222.7 9.2 %collective-permute-start.35 = (bf16[1,48,768]{2,1,0:T(8,128)(2,1)S(1)}, bf16[1,48,768]{2,1,0:T(8,128)(2,1)S(1)}, u32[]{:S(2)}, u32[]{:S(2)}) collective-permute-start(bf16[1,48,768]{2,1,0:T(8,128)(2,1)S(1)} %slice_bitcast_fusion), channel_id=1, source_target_pairs={{0,8},{2,10},{4,12},{6,14},{8,16},{10,18},{12,20},{14,22},{16,24},... | collective-permute-start | bytes 221192 | tf_op jit(solution)/shard_map/ppermute | solution.py:194
  226.0 4.1 %collective-permute-start.37 = (f32[13,768]{1,0:T(8,128)S(1)}, f32[13,768]{1,0:T(8,128)S(1)}, u32[]{:S(2)}, u32[]{:S(2)}) collective-permute-start(f32[13,768]{1,0:T(8,128)S(1)} %add.434), channel_id=1, source_target_pairs={{0,4},{2,6},{4,0},{6,2},{8,12},{10,14},{12,8},{14,10},{16,20},{18,... | collective-permute-start | bytes 119816 | tf_op jit(solution)/shard_map/ppermute | solution.py:194
  232.0 8.0 %collective-permute-start.42 = (f32[13,768]{1,0:T(8,128)S(1)}, f32[13,768]{1,0:T(8,128)S(1)}, u32[]{:S(2)}, u32[]{:S(2)}) collective-permute-start(f32[13,768]{1,0:T(8,128)S(1)} %add.439), channel_id=1, source_target_pairs={{0,8},{2,10},{4,12},{6,14},{8,0},{10,2},{12,4},{14,6},{16,24},{18,... | collective-permute-start | bytes 119816 | tf_op jit(solution)/shard_map/ppermute | solution.py:194
  232.9 13.9 %collective-permute-start.39 = (bf16[1,48,1536]{2,1,0:T(8,128)(2,1)S(1)}, bf16[1,48,1536]{2,1,0:T(8,128)(2,1)S(1)}, u32[]{:S(2)}, u32[]{:S(2)}) collective-permute-start(bf16[1,48,1536]{2,1,0:T(8,128)(2,1)S(1)} %get-tuple-element.251), channel_id=1, source_target_pairs={{0,8},{2,10},{4,12},{6,14},{8,16},{10,18},{12,20},{14,22},{16,24},... | collective-permute-start | bytes 442376 | tf_op jit(solution)/shard_map/ppermute | solution.py:194
  235.9 11.0 %collective-permute-start.38 = (bf16[1,48,1536]{2,1,0:T(8,128)(2,1)S(1)}, bf16[1,48,1536]{2,1,0:T(8,128)(2,1)S(1)}, u32[]{:S(2)}, u32[]{:S(2)}) collective-permute-start(bf16[1,48,1536]{2,1,0:T(8,128)(2,1)S(1)} %get-tuple-element.255), channel_id=1, source_target_pairs={{0,8},{2,10},{4,12},{6,14},{8,16},{10,18},{12,20},{14,22},{16,24},... | collective-permute-start | bytes 442376 | tf_op jit(solution)/shard_map/ppermute | solution.py:194
  235.9 9.4 %collective-permute-start.40 = (bf16[1,48,768]{2,1,0:T(8,128)(2,1)S(1)}, bf16[1,48,768]{2,1,0:T(8,128)(2,1)S(1)}, u32[]{:S(2)}, u32[]{:S(2)}) collective-permute-start(bf16[1,48,768]{2,1,0:T(8,128)(2,1)S(1)} %collective-permute-done.35), channel_id=1, source_target_pairs={{0,8},{2,10},{4,12},{6,14},{8,16},{10,18},{12,20},{14,22},{16,24},... | collective-permute-start | bytes 221192 | tf_op jit(solution)/shard_map/ppermute | solution.py:194
  235.9 10.9 %collective-permute-start.41 = (bf16[1,48,768]{2,1,0:T(8,128)(2,1)S(1)}, bf16[1,48,768]{2,1,0:T(8,128)(2,1)S(1)}, u32[]{:S(2)}, u32[]{:S(2)}) collective-permute-start(bf16[1,48,768]{2,1,0:T(8,128)(2,1)S(1)} %collective-permute-done.36), channel_id=1, source_target_pairs={{0,8},{2,10},{4,12},{6,14},{8,16},{10,18},{12,20},{14,22},{16,24},... | collective-permute-start | bytes 221192 | tf_op jit(solution)/shard_map/ppermute | solution.py:194
  246.9 5.8 %collective-permute-start.47 = (f32[13,768]{1,0:T(8,128)S(1)}, f32[13,768]{1,0:T(8,128)S(1)}, u32[]{:S(2)}, u32[]{:S(2)}) collective-permute-start(f32[13,768]{1,0:T(8,128)S(1)} %add.440), channel_id=1, source_target_pairs={{0,16},{2,18},{4,20},{6,22},{8,24},{10,26},{12,28},{14,30},{16,0},... | collective-permute-start | bytes 119816 | tf_op jit(solution)/shard_map/ppermute | solution.py:194
  246.9 10.9 %collective-permute-start.43 = (bf16[1,48,1536]{2,1,0:T(8,128)(2,1)S(1)}, bf16[1,48,1536]{2,1,0:T(8,128)(2,1)S(1)}, u32[]{:S(2)}, u32[]{:S(2)}) collective-permute-start(bf16[1,48,1536]{2,1,0:T(8,128)(2,1)S(1)} %collective-permute-done.38), channel_id=1, source_target_pairs={{0,8},{2,10},{4,12},{6,14},{8,16},{10,18},{12,20},{14,22},{16,24},... | collective-permute-start | bytes 442376 | tf_op jit(solution)/shard_map/ppermute | solution.py:194
  247.5 10.4 %collective-permute-start.44 = (bf16[1,48,1536]{2,1,0:T(8,128)(2,1)S(1)}, bf16[1,48,1536]{2,1,0:T(8,128)(2,1)S(1)}, u32[]{:S(2)}, u32[]{:S(2)}) collective-permute-start(bf16[1,48,1536]{2,1,0:T(8,128)(2,1)S(1)} %collective-permute-done.39), channel_id=1, source_target_pairs={{0,8},{2,10},{4,12},{6,14},{8,16},{10,18},{12,20},{14,22},{16,24},... | collective-permute-start | bytes 442376 | tf_op jit(solution)/shard_map/ppermute | solution.py:194
  250.4 6.2 %collective-permute-start.45 = (bf16[1,48,768]{2,1,0:T(8,128)(2,1)S(1)}, bf16[1,48,768]{2,1,0:T(8,128)(2,1)S(1)}, u32[]{:S(2)}, u32[]{:S(2)}) collective-permute-start(bf16[1,48,768]{2,1,0:T(8,128)(2,1)S(1)} %collective-permute-done.40), channel_id=1, source_target_pairs={{0,8},{2,10},{4,12},{6,14},{8,16},{10,18},{12,20},{14,22},{16,24},... | collective-permute-start | bytes 221192 | tf_op jit(solution)/shard_map/ppermute | solution.py:194
  250.5 7.4 %collective-permute-start.46 = (bf16[1,48,768]{2,1,0:T(8,128)(2,1)S(1)}, bf16[1,48,768]{2,1,0:T(8,128)(2,1)S(1)}, u32[]{:S(2)}, u32[]{:S(2)}) collective-permute-start(bf16[1,48,768]{2,1,0:T(8,128)(2,1)S(1)} %collective-permute-done.41), channel_id=1, source_target_pairs={{0,8},{2,10},{4,12},{6,14},{8,16},{10,18},{12,20},{14,22},{16,24},... | collective-permute-start | bytes 221192 | tf_op jit(solution)/shard_map/ppermute | solution.py:194
  257.9 12.0 %collective-permute-start.51 = (bf16[4,48,768]{2,1,0:T(8,128)(2,1)S(1)}, bf16[4,48,768]{2,1,0:T(8,128)(2,1)S(1)}, u32[]{:S(2)}, u32[]{:S(2)}) collective-permute-start(bf16[4,48,768]{2,1,0:T(8,128)(2,1)S(1)} %pad_maximum_fusion.9), channel_id=1, source_target_pairs={{0,4},{2,6},{4,0},{6,2},{8,12},{10,14},{12,8},{14,10},{16,20},{18,... | collective-permute-start | bytes 884744 | tf_op jit(solution)/shard_map/ppermute | solution.py:194
  259.4 10.5 %collective-permute-start.50 = (bf16[4,48,768]{2,1,0:T(8,128)(2,1)S(1)}, bf16[4,48,768]{2,1,0:T(8,128)(2,1)S(1)}, u32[]{:S(2)}, u32[]{:S(2)}) collective-permute-start(bf16[4,48,768]{2,1,0:T(8,128)(2,1)S(1)} %pad_maximum_fusion.8), channel_id=1, source_target_pairs={{0,2},{2,0},{4,6},{6,4},{8,10},{10,8},{12,14},{14,12},{16,18},{18,... | collective-permute-start | bytes 884744 | tf_op jit(solution)/shard_map/ppermute | solution.py:194
  261.4 8.5 %collective-permute-start.49 = (bf16[1,48,1536]{2,1,0:T(8,128)(2,1)S(1)}, bf16[1,48,1536]{2,1,0:T(8,128)(2,1)S(1)}, u32[]{:S(2)}, u32[]{:S(2)}) collective-permute-start(bf16[1,48,1536]{2,1,0:T(8,128)(2,1)S(1)} %collective-permute-done.44), channel_id=1, source_target_pairs={{0,8},{2,10},{4,12},{6,14},{8,16},{10,18},{12,20},{14,22},{16,24},... | collective-permute-start | bytes 442376 | tf_op jit(solution)/shard_map/ppermute | solution.py:194
  262.6 7.4 %collective-permute-start.48 = (bf16[1,48,1536]{2,1,0:T(8,128)(2,1)S(1)}, bf16[1,48,1536]{2,1,0:T(8,128)(2,1)S(1)}, u32[]{:S(2)}, u32[]{:S(2)}) collective-permute-start(bf16[1,48,1536]{2,1,0:T(8,128)(2,1)S(1)} %collective-permute-done.43), channel_id=1, source_target_pairs={{0,8},{2,10},{4,12},{6,14},{8,16},{10,18},{12,20},{14,22},{16,24},... | collective-permute-start | bytes 442376 | tf_op jit(solution)/shard_map/ppermute | solution.py:194
  270.0 15.2 %collective-permute-start.55 = (bf16[8,48,768]{2,1,0:T(8,128)(2,1)S(1)}, bf16[8,48,768]{2,1,0:T(8,128)(2,1)S(1)}, u32[]{:S(2)}, u32[]{:S(2)}) collective-permute-start(bf16[8,48,768]{2,1,0:T(8,128)(2,1)S(1)} %constant_dynamic-update-slice_fusion.25.refs_2_), channel_id=1, source_target_pairs={{0,2},{2,0},{4,6},{6,4},{8,10},{10,8},{12,14},{14,12},{16,18},{18,... | collective-permute-start | bytes 1769480 | tf_op jit(solution)/shard_map/ppermute | solution.py:194
  271.4 13.7 %collective-permute-start.53 = (bf16[4,48,1536]{2,1,0:T(8,128)(2,1)S(1)}, bf16[4,48,1536]{2,1,0:T(8,128)(2,1)S(1)}, u32[]{:S(2)}, u32[]{:S(2)}) collective-permute-start(bf16[4,48,1536]{2,1,0:T(8,128)(2,1)S(1)} %pad_maximum_fusion.4), channel_id=1, source_target_pairs={{0,4},{2,6},{4,0},{6,2},{8,12},{10,14},{12,8},{14,10},{16,20},{18,... | collective-permute-start | bytes 1769480 | tf_op jit(solution)/shard_map/ppermute | solution.py:194
  272.3 22.9 %collective-permute-start.52 = (bf16[4,48,1536]{2,1,0:T(8,128)(2,1)S(1)}, bf16[4,48,1536]{2,1,0:T(8,128)(2,1)S(1)}, u32[]{:S(2)}, u32[]{:S(2)}) collective-permute-start(bf16[4,48,1536]{2,1,0:T(8,128)(2,1)S(1)} %pad_maximum_fusion.3), channel_id=1, source_target_pairs={{0,2},{2,0},{4,6},{6,4},{8,10},{10,8},{12,14},{14,12},{16,18},{18,... | collective-permute-start | bytes 1769480 | tf_op jit(solution)/shard_map/ppermute | solution.py:194
  273.1 22.1 %collective-permute-start.54 = (bf16[8,48,768]{2,1,0:T(8,128)(2,1)S(1)}, bf16[8,48,768]{2,1,0:T(8,128)(2,1)S(1)}, u32[]{:S(2)}, u32[]{:S(2)}) collective-permute-start(bf16[8,48,768]{2,1,0:T(8,128)(2,1)S(1)} %constant_dynamic-update-slice_fusion.20.refs_0_), channel_id=1, source_target_pairs={{0,4},{2,6},{4,0},{6,2},{8,12},{10,14},{12,8},{14,10},{16,20},{18,... | collective-permute-start | bytes 1769480 | tf_op jit(solution)/shard_map/ppermute | solution.py:194
  296.1 20.7 %collective-permute-start.57 = (bf16[8,48,1536]{2,1,0:T(8,128)(2,1)S(1)}, bf16[8,48,1536]{2,1,0:T(8,128)(2,1)}, u32[]{:S(2)}, u32[]{:S(2)}) collective-permute-start(bf16[8,48,1536]{2,1,0:T(8,128)(2,1)S(1)} %constant_dynamic-update-slice_fusion.35.refs_0_), channel_id=1, source_target_pairs={{0,2},{2,0},{4,6},{6,4},{8,10},{10,8},{12,14},{14,12},{16,18},{18,... | collective-permute-start | bytes 3538952 | tf_op jit(solution)/shard_map/ppermute | solution.py:194
  298.4 18.5 %collective-permute-start.56 = (bf16[8,48,1536]{2,1,0:T(8,128)(2,1)}, bf16[8,48,1536]{2,1,0:T(8,128)(2,1)}, u32[]{:S(2)}, u32[]{:S(2)}) collective-permute-start(bf16[8,48,1536]{2,1,0:T(8,128)(2,1)} %constant_dynamic-update-slice_fusion.30.refs_0_), channel_id=1, source_target_pairs={{0,4},{2,6},{4,0},{6,2},{8,12},{10,14},{12,8},{14,10},{16,20},{18,... | collective-permute-start | bytes 3538952 | tf_op jit(solution)/shard_map/ppermute | solution.py:194
  330.7 4.9 %collective-permute-start.58 = (f32[768,768]{1,0:T(8,128)}, f32[768,768]{1,0:T(8,128)}, u32[]{:S(2)}, u32[]{:S(2)}) collective-permute-start(f32[768,768]{1,0:T(8,128)} %get-tuple-element.274), channel_id=1, source_target_pairs={{0,1},{1,0},{2,3},{3,2},{4,5},{5,4},{6,7},{7,6},{8,9},{9,8},{10,11... | collective-permute-start | bytes 7077896 | tf_op jit(solution)/shard_map/ppermute | solution.py:254
  368.0 2.6 collective-permute-start.61
  368.9 6.7 %collective-permute-start.59 = (f32[48,768]{1,0:T(8,128)S(1)}, f32[48,768]{1,0:T(8,128)S(1)}, u32[]{:S(2)}, u32[]{:S(2)}) collective-permute-start(f32[48,768]{1,0:T(8,128)S(1)} %get-tuple-element.287), channel_id=1, source_target_pairs={{0,2},{1,3},{2,0},{3,1},{4,6},{5,7},{6,4},{7,5},{8,10},{9,11},{10,... | collective-permute-start | bytes 442376 | tf_op jit(solution)/shard_map/ppermute | solution.py:810
  370.3 7.4 %collective-permute-start.60 = (f32[48,768]{1,0:T(8,128)S(1)}, f32[48,768]{1,0:T(8,128)S(1)}, u32[]{:S(2)}, u32[]{:S(2)}) collective-permute-start(f32[48,768]{1,0:T(8,128)S(1)} %get-tuple-element.287), channel_id=1, source_target_pairs={{0,3},{1,2},{2,1},{3,0},{4,7},{5,6},{6,5},{7,4},{8,11},{9,10},{10,... | collective-permute-start | bytes 442376 | tf_op jit(solution)/shard_map/ppermute | solution.py:810
  (46 other events, 460.8 us)

commit v6 on v5

--- a/solution.py
+++ b/solution.py
@@ -639,8 +639,7 @@
         ring_scatter_steps(jnp.concatenate([attend_grad, output_grad], 1), Z_THEN_Y)
     )
 
-    joint_scatter.hop()
-    feed_low = placed(feed_gather.finish(), Z_ORDERS)
+    feed_low = placed(depart([joint_scatter], feed_gather.finish()), Z_ORDERS)
     widen_low, narrow_low = feed_low[:, :widen_cols], feed_low[:, widen_cols:]
     activated, widen_back, widen_bias_grad = feed_forward(
         second_norm, upstream_low, feed_low, widen_bias

time: 390 us -> 386 us (0.990)
  matrix products: 36.9 us -> 32.9 us
    unnamed x113 -> x109, local copies, waits for them, and re-layouts: 17.4 us -> 18.8 us
where the time goes in v6:
time: 386 us; the launch traced here: 382 us
  waiting for transfers between devices  140 us (36%)
  starting transfers between devices  73.2 us (19%)
  Pallas kernels  70.8 us (18%)
  other arithmetic  37.7 us (10%)
  matrix products  32.9 us (9%)
  local copies, waits for them, and re-layouts  24.8 us (6%)
    ppermute x53, waiting for transfers between devices, send(): lax.ppermute(value, 'dp', perm)  127 us
    ppermute x53, starting transfers between devices, send(): lax.ppermute(value, 'dp', perm)  70.6 us
    pallas_call x1, Pallas kernels, newton_rows(): pl.pallas_call(newton_kernel, in_specs=[pl.BlockSpec(memory_space=pltpu.V...  30.7 us
    pallas_call x1, Pallas kernels, attention(): pl.pallas_call(attention_kernel, grid=(heads,), in_specs=[own(3 * HEAD_DI...  23.5 us
    unnamed x109, local copies, waits for them, and re-layouts  18.8 us
    pallas_call x5, Pallas kernels, placed(): pl.pallas_call(functools.partial(place_kernel, orders, [len(parts) for pa...  9.74 us
  transfers between devices with their start and end apart: 62, of which 34 were waited for; matrix products, arithmetic and copies ran while one was open for 12% of the time, Pallas kernels for 6%

profile of v6, /device:TPU:0, one launch (start us, length us, event | category | flops | bytes accessed | tf_op | source)
XLA Modules:
  0.0 381.6 jit_solution(15946714579871892084)
XLA Ops:
  3.3 3.0 collective-permute-start
  6.3 2.6 collective-permute-start.1
  10.3 1.7 convert_reduce_fusion.1
  12.8 3.1 subtract_multiply_fusion
  16.1 3.4 convert_element_type.207
  21.8 1.6 collective-permute-start.3
  24.8 2.7 collective-permute-start.7
  27.6 1.7 collective-permute-start.8
  33.8 2.2 fusion.49
  38.2 8.9 %collective-permute-done.8 = bf16[1,48,3072]{2,1,0:T(8,128)(2,1)S(1)} collective-permute-done((bf16[1,48,3072]{2,1,0:T(8,128)(2,1)S(1)}, bf16[1,48,3072]{2,1,0:T(8,128)(2,1)S(1)}, u32[]{:S(2)}, u32[]{:S(2)}) %collective-permute-start.8) | collective-permute-done | bytes 294944 | tf_op jit(solution)/shard_map/ppermute | solution.py:194
  50.7 2.4 convolution_add_fusion.triple_ref
  53.1 10.9 %collective-permute-done.10 = bf16[4,48,1536]{2,1,0:T(8,128)(2,1)S(1)} collective-permute-done((bf16[4,48,1536]{2,1,0:T(8,128)(2,1)S(1)}, bf16[4,48,1536]{2,1,0:T(8,128)(2,1)S(1)}, u32[]{:S(2)}, u32[]{:S(2)}) %collective-permute-start.10) | collective-permute-done | bytes 589856 | tf_op jit(solution)/shard_map/ppermute | solution.py:194
  66.4 23.5 %shard_map.278 = (bf16[384,1024]{1,0:T(8,128)(2,1)S(1)}, bf16[1152,1024]{1,0:T(8,128)(2,1)S(1)}) custom-call(f32[1152,1024]{1,0:T(8,128)S(1)} %convolution_add_fusion.triple_ref, f32[8,1024]{1,0:T(8,128)S(1)} %get-tuple-element.170.cos_ref, f32[8,1024]{1,0:T(8,128)S(1)} %get-tuple-element.171.sin_ref, ...), custom_call_target="tpu_custom_call" | custom-call | flops 14495514624 | bytes 9437184 | tf_op jit(solution)/shard_map/pallas_call | solution.py:390
  91.3 2.3 fusion.56
  95.4 1.8 shard_map.279
  97.2 6.9 %shard_map.280 = (bf16[1024,1536]{1,0:T(8,128)(2,1)S(1)}, bf16[1024,1536]{1,0:T(8,128)(2,1)S(1)}, f32[1,1536]{1,0:T(1,128)S(1)}) custom-call(bf16[1024,768]{1,0:T(8,128)(2,1)S(1)} %get-tuple-element.180.norm_ref, bf16[1024,768]{1,0:T(8,128)(2,1)S(1)} %get-tuple-element.162.upstream_ref, bf16[768,3072]{1,0:T(8,128)(2,1)S(1)} %bitcast.71, ...), custom_call_target="tpu_custom_call" | custom-call | flops 4831838208 | bytes 14155776 | tf_op jit(solution)/shard_map/pallas_call | solution.py:539
  104.1 2.6 fusion.59
  106.8 6.9 %collective-permute-start.14 = (bf16[1,2,2,48,1536]{4,3,2,1,0:T(8,128)(2,1)S(1)}, bf16[1,2,2,48,1536]{4,3,2,1,0:T(8,128)(2,1)S(1)}, u32[]{:S(2)}, u32[]{:S(2)}) collective-permute-start(bf16[1,2,2,48,1536]{4,3,2,1,0:T(8,128)(2,1)S(1)} %dynamic-slice_convert_fusion.6), channel_id=1, source_target_pairs={{0,8},{2,10},{4,12},{6,14},{8,16},{10,18},{12,20},{14,22},{16,24},... | collective-permute-start | bytes 1769480 | tf_op jit(solution)/shard_map/ppermute | solution.py:194
  113.6 2.6 fusion.58
  116.3 7.9 %collective-permute-done.14 = bf16[1,2,2,48,1536]{4,3,2,1,0:T(8,128)(2,1)S(1)} collective-permute-done((bf16[1,2,2,48,1536]{4,3,2,1,0:T(8,128)(2,1)S(1)}, bf16[1,2,2,48,1536]{4,3,2,1,0:T(8,128)(2,1)S(1)}, u32[]{:S(2)}, u32[]{:S(2)}) %collective-permute-start.14) | collective-permute-done | bytes 589856 | tf_op jit(solution)/shard_map/ppermute | solution.py:194
  124.2 2.6 fusion
  129.1 2.6 fusion.2
  132.4 2.3 fusion.12
  138.2 2.7 collective-permute-start.17
  141.3 1.7 copy-done.22
  144.3 11.1 %collective-permute-done.17 = bf16[1,2,2,48,1536]{4,3,2,1,0:T(8,128)(2,1)S(1)} collective-permute-done((bf16[1,2,2,48,1536]{4,3,2,1,0:T(8,128)(2,1)S(1)}, bf16[1,2,2,48,1536]{4,3,2,1,0:T(8,128)(2,1)S(1)}, u32[]{:S(2)}, u32[]{:S(2)}) %collective-permute-start.17) | collective-permute-done | bytes 589856 | tf_op jit(solution)/shard_map/ppermute | solution.py:194
  155.4 8.0 %collective-permute-done.16 = bf16[4,1,2,48,1536]{4,3,2,1,0:T(8,128)(2,1)S(1)} collective-permute-done((bf16[4,1,2,48,1536]{4,3,2,1,0:T(8,128)(2,1)S(1)}, bf16[4,1,2,48,1536]{4,3,2,1,0:T(8,128)(2,1)S(1)}, u32[]{:S(2)}, u32[]{:S(2)}) %collective-permute-start.16) | collective-permute-done | bytes 1179680 | tf_op jit(solution)/shard_map/ppermute | solution.py:194
  168.5 2.5 collective-permute-start.23
  179.0 3.4 fusion.10
  182.3 4.0 %collective-permute-done.23 = bf16[1,2,2,48,1536]{4,3,2,1,0:T(8,128)(2,1)} collective-permute-done((bf16[1,2,2,48,1536]{4,3,2,1,0:T(8,128)(2,1)}, bf16[1,2,2,48,1536]{4,3,2,1,0:T(8,128)(2,1)}, u32[]{:S(2)}, u32[]{:S(2)}) %collective-permute-start.23) | collective-permute-done | bytes 589856 | tf_op jit(solution)/shard_map/ppermute | solution.py:194
  186.3 2.5 collective-permute-done.22
  188.8 3.8 %collective-permute-done.21 = bf16[4,1,1,48,1536]{4,3,2,1,0:T(8,128)(2,1)} collective-permute-done((bf16[4,1,1,48,1536]{4,3,2,1,0:T(8,128)(2,1)}, bf16[4,1,1,48,1536]{4,3,2,1,0:T(8,128)(2,1)}, u32[]{:S(2)}, u32[]{:S(2)}) %collective-permute-start.21) | collective-permute-done | bytes 589856 | tf_op jit(solution)/shard_map/ppermute | solution.py:194
  192.7 1.6 convert_add_fusion.6
  199.4 4.9 %collective-permute-done.26 = bf16[1,1,1,48,1536]{4,3,2,1,0:T(8,128)(2,1)S(1)} collective-permute-done((bf16[1,1,1,48,1536]{4,3,2,1,0:T(8,128)(2,1)S(1)}, bf16[1,1,1,48,1536]{4,3,2,1,0:T(8,128)(2,1)S(1)}, u32[]{:S(2)}, u32[]{:S(2)}) %collective-permute-start.26) | collective-permute-done | bytes 147488 | tf_op jit(solution)/shard_map/ppermute | solution.py:194
  204.3 1.6 collective-permute-done.25
  208.4 3.4 collective-permute-done.32
  211.8 2.0 collective-permute-done.30
  213.8 1.6 collective-permute-done.29
  218.8 3.3 collective-permute-start.35
  223.4 2.8 collective-permute-done.37
  229.1 2.0 collective-permute-start.39
  232.0 2.9 collective-permute-start.41
  236.1 5.3 %collective-permute-done.40 = bf16[1,48,768]{2,1,0:T(8,128)(2,1)S(1)} collective-permute-done((bf16[1,48,768]{2,1,0:T(8,128)(2,1)S(1)}, bf16[1,48,768]{2,1,0:T(8,128)(2,1)S(1)}, u32[]{:S(2)}, u32[]{:S(2)}) %collective-permute-start.40) | collective-permute-done | bytes 73760 | tf_op jit(solution)/shard_map/ppermute | solution.py:194
  241.3 1.6 collective-permute-done.41
  243.6 2.9 collective-permute-start.44
  248.8 3.9 %collective-permute-done.45 = bf16[1,48,768]{2,1,0:T(8,128)(2,1)S(1)} collective-permute-done((bf16[1,48,768]{2,1,0:T(8,128)(2,1)S(1)}, bf16[1,48,768]{2,1,0:T(8,128)(2,1)S(1)}, u32[]{:S(2)}, u32[]{:S(2)}) %collective-permute-start.45) | collective-permute-done | bytes 73760 | tf_op jit(solution)/shard_map/ppermute | solution.py:194
  253.9 1.6 collective-permute-start.51
  255.6 2.1 collective-permute-start.50
  258.8 2.0 collective-permute-start.48
  260.8 5.3 %collective-permute-done.48 = bf16[1,48,1536]{2,1,0:T(8,128)(2,1)S(1)} collective-permute-done((bf16[1,48,1536]{2,1,0:T(8,128)(2,1)S(1)}, bf16[1,48,1536]{2,1,0:T(8,128)(2,1)S(1)}, u32[]{:S(2)}, u32[]{:S(2)}) %collective-permute-start.48) | collective-permute-done | bytes 147488 | tf_op jit(solution)/shard_map/ppermute | solution.py:194
  272.1 9.2 %collective-permute-done.55.refs_3_ = bf16[8,48,768]{2,1,0:T(8,128)(2,1)S(1)} collective-permute-done((bf16[8,48,768]{2,1,0:T(8,128)(2,1)S(1)}, bf16[8,48,768]{2,1,0:T(8,128)(2,1)S(1)}, u32[]{:S(2)}, u32[]{:S(2)}) %collective-permute-start.55) | collective-permute-done | bytes 589856 | tf_op jit(solution)/shard_map/ppermute | solution.py:194
  281.3 10.2 %collective-permute-done.52 = bf16[4,48,1536]{2,1,0:T(8,128)(2,1)S(1)} collective-permute-done((bf16[4,48,1536]{2,1,0:T(8,128)(2,1)S(1)}, bf16[4,48,1536]{2,1,0:T(8,128)(2,1)S(1)}, u32[]{:S(2)}, u32[]{:S(2)}) %collective-permute-start.52) | collective-permute-done | bytes 589856 | tf_op jit(solution)/shard_map/ppermute | solution.py:194
  301.4 1.7 fusion.18
  303.2 9.8 %collective-permute-done.57.refs_1_ = bf16[8,48,1536]{2,1,0:T(8,128)(2,1)} collective-permute-done((bf16[8,48,1536]{2,1,0:T(8,128)(2,1)S(1)}, bf16[8,48,1536]{2,1,0:T(8,128)(2,1)}, u32[]{:S(2)}, u32[]{:S(2)}) %collective-permute-start.57) | collective-permute-done | bytes 1179680 | tf_op jit(solution)/shard_map/ppermute | solution.py:194
  313.0 3.7 shard_map.283
  316.7 2.0 fusion.61
  318.7 1.9 shard_map.282
  322.1 2.0 fusion.60
  324.1 2.8 broadcast_select_fusion.2
  327.0 4.8 %collective-permute-done.58.second_ref = f32[768,768]{1,0:T(8,128)} collective-permute-done((f32[768,768]{1,0:T(8,128)}, f32[768,768]{1,0:T(8,128)}, u32[]{:S(2)}, u32[]{:S(2)}) %collective-permute-start.58) | collective-permute-done | bytes 2359328 | tf_op jit(solution)/shard_map/ppermute | solution.py:254
  331.8 1.7 copy-done.4
  333.5 30.7 %shard_map.284 = f32[96,768]{1,0:T(8,128)S(1)} custom-call(f32[768,768]{1,0:T(8,128)S(1)} %copy-done.4, f32[768,768]{1,0:T(8,128)} %collective-permute-done.58.second_ref, f32[96,768]{1,0:T(8,128)S(1)} %fusion.29.rows_ref), custom_call_target="tpu_custom_call" | custom-call | flops 21743271936 | bytes 4718592 | tf_op jit(solution)/shard_map/pallas_call | solution.py:496
  366.8 4.9 %collective-permute-done.59 = f32[48,768]{1,0:T(8,128)S(1)} collective-permute-done((f32[48,768]{1,0:T(8,128)S(1)}, f32[48,768]{1,0:T(8,128)S(1)}, u32[]{:S(2)}, u32[]{:S(2)}) %collective-permute-start.59) | collective-permute-done | bytes 147488 | tf_op jit(solution)/shard_map/ppermute | solution.py:809
  371.8 2.1 collective-permute-done.60
  (313 shorter events, 95.5 us)
Async XLA Ops:
  3.3 16.4 %collective-permute-start = (bf16[1,48,1536]{2,1,0:T(8,128)(2,1)}, bf16[1,48,1536]{2,1,0:T(8,128)(2,1)}, u32[]{:S(2)}, u32[]{:S(2)}) collective-permute-start(bf16[1,48,1536]{2,1,0:T(8,128)(2,1)} %pad_maximum_fusion.10), channel_id=1, source_target_pairs={{0,8},{2,10},{4,12},{6,14},{8,16},{10,18},{12,20},{14,22},{16,24},... | collective-permute-start | bytes 442376 | tf_op jit(solution)/shard_map/ppermute | solution.py:194
  6.3 13.4 %collective-permute-start.1 = (bf16[1,48,1536]{2,1,0:T(8,128)(2,1)}, bf16[1,48,1536]{2,1,0:T(8,128)(2,1)}, u32[]{:S(2)}, u32[]{:S(2)}) collective-permute-start(bf16[1,48,1536]{2,1,0:T(8,128)(2,1)} %pad_maximum_fusion.10), channel_id=1, source_target_pairs={{0,16},{2,18},{4,20},{6,22},{8,24},{10,26},{12,28},{14,30},{16,0},... | collective-permute-start | bytes 442376 | tf_op jit(solution)/shard_map/ppermute | solution.py:194
  8.9 10.8 %collective-permute-start.2 = (bf16[1,48,1536]{2,1,0:T(8,128)(2,1)}, bf16[1,48,1536]{2,1,0:T(8,128)(2,1)S(1)}, u32[]{:S(2)}, u32[]{:S(2)}) collective-permute-start(bf16[1,48,1536]{2,1,0:T(8,128)(2,1)} %pad_maximum_fusion.10), channel_id=1, source_target_pairs={{0,24},{2,26},{4,28},{6,30},{8,0},{10,2},{12,4},{14,6},{16,8},{18,... | collective-permute-start | bytes 442376 | tf_op jit(solution)/shard_map/ppermute | solution.py:194
  21.8 8.2 %collective-permute-start.3 = (bf16[4,48,768]{2,1,0:T(8,128)(2,1)S(1)}, bf16[4,48,768]{2,1,0:T(8,128)(2,1)S(1)}, u32[]{:S(2)}, u32[]{:S(2)}) collective-permute-start(bf16[4,48,768]{2,1,0:T(8,128)(2,1)S(1)} %get-tuple-element.139), channel_id=1, source_target_pairs={{0,2},{2,0},{4,6},{6,4},{8,10},{10,8},{12,14},{14,12},{16,18},{18,... | collective-permute-start | bytes 884744 | tf_op jit(solution)/shard_map/ppermute | solution.py:194
  23.3 7.8 %collective-permute-start.4 = (bf16[4,48,768]{2,1,0:T(8,128)(2,1)S(1)}, bf16[4,48,768]{2,1,0:T(8,128)(2,1)S(1)}, u32[]{:S(2)}, u32[]{:S(2)}) collective-permute-start(bf16[4,48,768]{2,1,0:T(8,128)(2,1)S(1)} %get-tuple-element.140), channel_id=1, source_target_pairs={{0,4},{2,6},{4,0},{6,2},{8,12},{10,14},{12,8},{14,10},{16,20},{18,... | collective-permute-start | bytes 884744 | tf_op jit(solution)/shard_map/ppermute | solution.py:194
  24.8 13.3 %collective-permute-start.7 = (bf16[1,48,3072]{2,1,0:T(8,128)(2,1)S(1)}, bf16[1,48,3072]{2,1,0:T(8,128)(2,1)S(1)}, u32[]{:S(2)}, u32[]{:S(2)}) collective-permute-start(bf16[1,48,3072]{2,1,0:T(8,128)(2,1)S(1)} %bitcast.88), channel_id=1, source_target_pairs={{0,8},{2,10},{4,12},{6,14},{8,16},{10,18},{12,20},{14,22},{16,24},... | collective-permute-start | bytes 884744 | tf_op jit(solution)/shard_map/ppermute | solution.py:194
  27.6 19.5 %collective-permute-start.8 = (bf16[1,48,3072]{2,1,0:T(8,128)(2,1)S(1)}, bf16[1,48,3072]{2,1,0:T(8,128)(2,1)S(1)}, u32[]{:S(2)}, u32[]{:S(2)}) collective-permute-start(bf16[1,48,3072]{2,1,0:T(8,128)(2,1)S(1)} %bitcast.89), channel_id=1, source_target_pairs={{0,16},{2,18},{4,20},{6,22},{8,24},{10,26},{12,28},{14,30},{16,0},... | collective-permute-start | bytes 884744 | tf_op jit(solution)/shard_map/ppermute | solution.py:194
  29.3 17.8 %collective-permute-start.9 = (bf16[1,48,3072]{2,1,0:T(8,128)(2,1)S(1)}, bf16[1,48,3072]{2,1,0:T(8,128)(2,1)S(1)}, u32[]{:S(2)}, u32[]{:S(2)}) collective-permute-start(bf16[1,48,3072]{2,1,0:T(8,128)(2,1)S(1)} %bitcast.90), channel_id=1, source_target_pairs={{0,24},{2,26},{4,28},{6,30},{8,0},{10,2},{12,4},{14,6},{16,8},{18,... | collective-permute-start | bytes 884744 | tf_op jit(solution)/shard_map/ppermute | solution.py:194
  31.8 15.3 %collective-permute-start.5 = (bf16[8,48,768]{2,1,0:T(8,128)(2,1)S(1)}, bf16[8,48,768]{2,1,0:T(8,128)(2,1)S(1)}, u32[]{:S(2)}, u32[]{:S(2)}) collective-permute-start(bf16[8,48,768]{2,1,0:T(8,128)(2,1)S(1)} %constant_dynamic-update-slice_fusion.refs_0_), channel_id=1, source_target_pairs={{0,4},{2,6},{4,0},{6,2},{8,12},{10,14},{12,8},{14,10},{16,20},{18,... | collective-permute-start | bytes 1769480 | tf_op jit(solution)/shard_map/ppermute | solution.py:194
  33.3 13.8 %collective-permute-start.6 = (bf16[8,48,768]{2,1,0:T(8,128)(2,1)S(1)}, bf16[8,48,768]{2,1,0:T(8,128)(2,1)S(1)}, u32[]{:S(2)}, u32[]{:S(2)}) collective-permute-start(bf16[8,48,768]{2,1,0:T(8,128)(2,1)S(1)} %constant_dynamic-update-slice_fusion.5.refs_2_), channel_id=1, source_target_pairs={{0,2},{2,0},{4,6},{6,4},{8,10},{10,8},{12,14},{14,12},{16,18},{18,... | collective-permute-start | bytes 1769480 | tf_op jit(solution)/shard_map/ppermute | solution.py:194
  48.8 15.2 %collective-permute-start.10 = (bf16[4,48,1536]{2,1,0:T(8,128)(2,1)S(1)}, bf16[4,48,1536]{2,1,0:T(8,128)(2,1)S(1)}, u32[]{:S(2)}, u32[]{:S(2)}) collective-permute-start(bf16[4,48,1536]{2,1,0:T(8,128)(2,1)S(1)} %pad_maximum_fusion.1), channel_id=1, source_target_pairs={{0,2},{2,0},{4,6},{6,4},{8,10},{10,8},{12,14},{14,12},{16,18},{18,... | collective-permute-start | bytes 1769480 | tf_op jit(solution)/shard_map/ppermute | solution.py:194
  49.4 14.9 %collective-permute-start.11 = (bf16[4,48,1536]{2,1,0:T(8,128)(2,1)S(1)}, bf16[4,48,1536]{2,1,0:T(8,128)(2,1)S(1)}, u32[]{:S(2)}, u32[]{:S(2)}) collective-permute-start(bf16[4,48,1536]{2,1,0:T(8,128)(2,1)S(1)} %pad_maximum_fusion.2), channel_id=1, source_target_pairs={{0,4},{2,6},{4,0},{6,2},{8,12},{10,14},{12,8},{14,10},{16,20},{18,... | collective-permute-start | bytes 1769480 | tf_op jit(solution)/shard_map/ppermute | solution.py:194
  64.4 26.7 %collective-permute-start.12 = (bf16[8,48,1536]{2,1,0:T(8,128)(2,1)S(1)}, bf16[8,48,1536]{2,1,0:T(8,128)(2,1)S(1)}, u32[]{:S(2)}, u32[]{:S(2)}) collective-permute-start(bf16[8,48,1536]{2,1,0:T(8,128)(2,1)S(1)} %constant_dynamic-update-slice_fusion.10.refs_0_), channel_id=1, source_target_pairs={{0,4},{2,6},{4,0},{6,2},{8,12},{10,14},{12,8},{14,10},{16,20},{18,... | collective-permute-start | bytes 3538952 | tf_op jit(solution)/shard_map/ppermute | solution.py:194
  64.9 26.4 %collective-permute-start.13 = (bf16[8,48,1536]{2,1,0:T(8,128)(2,1)S(1)}, bf16[8,48,1536]{2,1,0:T(8,128)(2,1)S(1)}, u32[]{:S(2)}, u32[]{:S(2)}) collective-permute-start(bf16[8,48,1536]{2,1,0:T(8,128)(2,1)S(1)} %constant_dynamic-update-slice_fusion.15.refs_2_), channel_id=1, source_target_pairs={{0,2},{2,0},{4,6},{6,4},{8,10},{10,8},{12,14},{14,12},{16,18},{18,... | collective-permute-start | bytes 3538952 | tf_op jit(solution)/shard_map/ppermute | solution.py:194
  89.9 42.5 %copy-start.5 = (bf16[1152,1024]{1,0:T(8,128)(2,1)}, bf16[1152,1024]{1,0:T(8,128)(2,1)S(1)}, u32[]{:S(2)}) copy-start(bf16[1152,1024]{1,0:T(8,128)(2,1)S(1)} %get-tuple-element.190) | copy-start | bytes 7077892
  95.3 72.2 %copy-start.16 = (f32[768,1536]{1,0:T(8,128)}, f32[768,1536]{1,0:T(8,128)S(1)}, u32[]{:S(2)}) copy-start(f32[768,1536]{1,0:T(8,128)S(1)} %pad_maximum_fusion) | copy-start | bytes 14155780
  106.8 17.4 %collective-permute-start.14 = (bf16[1,2,2,48,1536]{4,3,2,1,0:T(8,128)(2,1)S(1)}, bf16[1,2,2,48,1536]{4,3,2,1,0:T(8,128)(2,1)S(1)}, u32[]{:S(2)}, u32[]{:S(2)}) collective-permute-start(bf16[1,2,2,48,1536]{4,3,2,1,0:T(8,128)(2,1)S(1)} %dynamic-slice_convert_fusion.6), channel_id=1, source_target_pairs={{0,8},{2,10},{4,12},{6,14},{8,16},{10,18},{12,20},{14,22},{16,24},... | collective-permute-start | bytes 1769480 | tf_op jit(solution)/shard_map/ppermute | solution.py:194
  129.1 12.2 %collective-permute-start.20 = (f32[1024,384]{1,0:T(8,128)}, f32[1024,384]{1,0:T(8,128)S(1)}, u32[]{:S(2)}, u32[]{:S(2)}) collective-permute-start(f32[1024,384]{1,0:T(8,128)} %constant_dynamic-slice_fusion.4), channel_id=1, source_target_pairs={{0,1},{1,0},{2,3},{3,2},{4,5},{5,4},{6,7},{7,6},{8,9},{9,8},{10,11... | collective-permute-start | bytes 4718600 | tf_op jit(solution)/shard_map/ppermute | solution.py:254
  131.9 6.4 %collective-permute-start.19 = (bf16[512,768]{1,0:T(8,128)(2,1)S(1)}, bf16[512,768]{1,0:T(8,128)(2,1)S(1)}, u32[]{:S(2)}, u32[]{:S(2)}) collective-permute-start(bf16[512,768]{1,0:T(8,128)(2,1)S(1)} %dynamic-slice_convert_fusion.2), channel_id=1, source_target_pairs={{0,1},{1,0},{2,3},{3,2},{4,5},{5,4},{6,7},{7,6},{8,9},{9,8},{10,11... | collective-permute-start | bytes 2359304 | tf_op jit(solution)/shard_map/ppermute | solution.py:254
  134.8 6.3 %collective-permute-start.18 = (bf16[512,768]{1,0:T(8,128)(2,1)S(1)}, bf16[512,768]{1,0:T(8,128)(2,1)S(1)}, u32[]{:S(2)}, u32[]{:S(2)}) collective-permute-start(bf16[512,768]{1,0:T(8,128)(2,1)S(1)} %dynamic-slice_convert_fusion.3), channel_id=1, source_target_pairs={{0,1},{1,0},{2,3},{3,2},{4,5},{5,4},{6,7},{7,6},{8,9},{9,8},{10,11... | collective-permute-start | bytes 2359304 | tf_op jit(solution)/shard_map/ppermute | solution.py:254
  135.0 28.4 %collective-permute-start.16 = (bf16[4,1,2,48,1536]{4,3,2,1,0:T(8,128)(2,1)S(1)}, bf16[4,1,2,48,1536]{4,3,2,1,0:T(8,128)(2,1)S(1)}, u32[]{:S(2)}, u32[]{:S(2)}) collective-permute-start(bf16[4,1,2,48,1536]{4,3,2,1,0:T(8,128)(2,1)S(1)} %dynamic-slice_convert_fusion), channel_id=1, source_target_pairs={{0,4},{2,6},{4,0},{6,2},{8,12},{10,14},{12,8},{14,10},{16,20},{18,... | collective-permute-start | bytes 3538952 | tf_op jit(solution)/shard_map/ppermute | solution.py:194
  136.7 28.1 %collective-permute-start.15 = (bf16[4,2,1,48,1536]{4,3,2,1,0:T(8,128)(2,1)S(1)}, bf16[4,2,1,48,1536]{4,3,2,1,0:T(8,128)(2,1)S(1)}, u32[]{:S(2)}, u32[]{:S(2)}) collective-permute-start(bf16[4,2,1,48,1536]{4,3,2,1,0:T(8,128)(2,1)S(1)} %dynamic-slice_convert_fusion.1), channel_id=1, source_target_pairs={{0,2},{2,0},{4,6},{6,4},{8,10},{10,8},{12,14},{14,12},{16,18},{18,... | collective-permute-start | bytes 3538952 | tf_op jit(solution)/shard_map/ppermute | solution.py:194
  138.2 17.2 %collective-permute-start.17 = (bf16[1,2,2,48,1536]{4,3,2,1,0:T(8,128)(2,1)S(1)}, bf16[1,2,2,48,1536]{4,3,2,1,0:T(8,128)(2,1)S(1)}, u32[]{:S(2)}, u32[]{:S(2)}) collective-permute-start(bf16[1,2,2,48,1536]{4,3,2,1,0:T(8,128)(2,1)S(1)} %add_convert_fusion.3), channel_id=1, source_target_pairs={{0,8},{2,10},{4,12},{6,14},{8,16},{10,18},{12,20},{14,22},{16,24},... | collective-permute-start | bytes 1769480 | tf_op jit(solution)/shard_map/ppermute | solution.py:194
  167.4 11.6 %collective-permute-start.24 = (bf16[512,768]{1,0:T(8,128)(2,1)S(1)}, bf16[512,768]{1,0:T(8,128)(2,1)}, u32[]{:S(2)}, u32[]{:S(2)}) collective-permute-start(bf16[512,768]{1,0:T(8,128)(2,1)S(1)} %fusion.11), channel_id=1, source_target_pairs={{0,1},{1,0},{2,3},{3,2},{4,5},{5,4},{6,7},{7,6},{8,9},{9,8},{10,11... | collective-permute-start | bytes 2359304 | tf_op jit(solution)/shard_map/ppermute | solution.py:254
  168.5 17.8 %collective-permute-start.23 = (bf16[1,2,2,48,1536]{4,3,2,1,0:T(8,128)(2,1)}, bf16[1,2,2,48,1536]{4,3,2,1,0:T(8,128)(2,1)}, u32[]{:S(2)}, u32[]{:S(2)}) collective-permute-start(bf16[1,2,2,48,1536]{4,3,2,1,0:T(8,128)(2,1)} %add_convert_fusion.2), channel_id=1, source_target_pairs={{0,8},{2,10},{4,12},{6,14},{8,16},{10,18},{12,20},{14,22},{16,24},... | collective-permute-start | bytes 1769480 | tf_op jit(solution)/shard_map/ppermute | solution.py:194
  173.1 15.8 %collective-permute-start.22 = (bf16[4,1,1,48,1536]{4,3,2,1,0:T(8,128)(2,1)}, bf16[4,1,1,48,1536]{4,3,2,1,0:T(8,128)(2,1)}, u32[]{:S(2)}, u32[]{:S(2)}) collective-permute-start(bf16[4,1,1,48,1536]{4,3,2,1,0:T(8,128)(2,1)} %dynamic-slice_convert_fusion.4), channel_id=1, source_target_pairs={{0,2},{2,0},{4,6},{6,4},{8,10},{10,8},{12,14},{14,12},{16,18},{18,... | collective-permute-start | bytes 1769480 | tf_op jit(solution)/shard_map/ppermute | solution.py:194
  177.2 15.5 %collective-permute-start.21 = (bf16[4,1,1,48,1536]{4,3,2,1,0:T(8,128)(2,1)}, bf16[4,1,1,48,1536]{4,3,2,1,0:T(8,128)(2,1)}, u32[]{:S(2)}, u32[]{:S(2)}) collective-permute-start(bf16[4,1,1,48,1536]{4,3,2,1,0:T(8,128)(2,1)} %dynamic-slice_convert_fusion.5), channel_id=1, source_target_pairs={{0,4},{2,6},{4,0},{6,2},{8,12},{10,14},{12,8},{14,10},{16,20},{18,... | collective-permute-start | bytes 1769480 | tf_op jit(solution)/shard_map/ppermute | solution.py:194
  194.3 11.6 %collective-permute-start.27 = (bf16[1,1,2,48,1536]{4,3,2,1,0:T(8,128)(2,1)S(1)}, bf16[1,1,2,48,1536]{4,3,2,1,0:T(8,128)(2,1)S(1)}, u32[]{:S(2)}, u32[]{:S(2)}) collective-permute-start(bf16[1,1,2,48,1536]{4,3,2,1,0:T(8,128)(2,1)S(1)} %dynamic-slice_convert_fusion.7), channel_id=1, source_target_pairs={{0,4},{2,6},{4,0},{6,2},{8,12},{10,14},{12,8},{14,10},{16,20},{18,... | collective-permute-start | bytes 884744 | tf_op jit(solution)/shard_map/ppermute | solution.py:194
  196.2 8.1 %collective-permute-start.26 = (bf16[1,1,1,48,1536]{4,3,2,1,0:T(8,128)(2,1)S(1)}, bf16[1,1,1,48,1536]{4,3,2,1,0:T(8,128)(2,1)S(1)}, u32[]{:S(2)}, u32[]{:S(2)}) collective-permute-start(bf16[1,1,1,48,1536]{4,3,2,1,0:T(8,128)(2,1)S(1)} %dynamic-slice_convert_fusion.9), channel_id=1, source_target_pairs={{0,8},{2,10},{4,12},{6,14},{8,16},{10,18},{12,20},{14,22},{16,24},... | collective-permute-start | bytes 442376 | tf_op jit(solution)/shard_map/ppermute | solution.py:194
  197.8 8.1 %collective-permute-start.25 = (bf16[1,1,1,48,1536]{4,3,2,1,0:T(8,128)(2,1)S(1)}, bf16[1,1,1,48,1536]{4,3,2,1,0:T(8,128)(2,1)S(1)}, u32[]{:S(2)}, u32[]{:S(2)}) collective-permute-start(bf16[1,1,1,48,1536]{4,3,2,1,0:T(8,128)(2,1)S(1)} %dynamic-slice_convert_fusion.10), channel_id=1, source_target_pairs={{0,8},{2,10},{4,12},{6,14},{8,16},{10,18},{12,20},{14,22},{16,24},... | collective-permute-start | bytes 442376 | tf_op jit(solution)/shard_map/ppermute | solution.py:194
  198.2 1.2 collective-permute-start.28
  206.0 5.7 %collective-permute-start.31 = (bf16[1,1,1,48,1536]{4,3,2,1,0:T(8,128)(2,1)S(1)}, bf16[1,1,1,48,1536]{4,3,2,1,0:T(8,128)(2,1)S(1)}, u32[]{:S(2)}, u32[]{:S(2)}) collective-permute-start(bf16[1,1,1,48,1536]{4,3,2,1,0:T(8,128)(2,1)S(1)} %dynamic-slice_convert_fusion.8), channel_id=1, source_target_pairs={{0,2},{2,0},{4,6},{6,4},{8,10},{10,8},{12,14},{14,12},{16,18},{18,... | collective-permute-start | bytes 442376 | tf_op jit(solution)/shard_map/ppermute | solution.py:194
  206.8 7.0 %collective-permute-start.30 = (bf16[1,1,1,48,1536]{4,3,2,1,0:T(8,128)(2,1)S(1)}, bf16[1,1,1,48,1536]{4,3,2,1,0:T(8,128)(2,1)S(1)}, u32[]{:S(2)}, u32[]{:S(2)}) collective-permute-start(bf16[1,1,1,48,1536]{4,3,2,1,0:T(8,128)(2,1)S(1)} %add_convert_fusion.6), channel_id=1, source_target_pairs={{0,8},{2,10},{4,12},{6,14},{8,16},{10,18},{12,20},{14,22},{16,24},... | collective-permute-start | bytes 442376 | tf_op jit(solution)/shard_map/ppermute | solution.py:194
  206.9 8.5 %collective-permute-start.29 = (bf16[1,1,1,48,1536]{4,3,2,1,0:T(8,128)(2,1)S(1)}, bf16[1,1,1,48,1536]{4,3,2,1,0:T(8,128)(2,1)S(1)}, u32[]{:S(2)}, u32[]{:S(2)}) collective-permute-start(bf16[1,1,1,48,1536]{4,3,2,1,0:T(8,128)(2,1)S(1)} %add_convert_fusion.7), channel_id=1, source_target_pairs={{0,8},{2,10},{4,12},{6,14},{8,16},{10,18},{12,20},{14,22},{16,24},... | collective-permute-start | bytes 442376 | tf_op jit(solution)/shard_map/ppermute | solution.py:194
  207.0 4.8 %collective-permute-start.32 = (f32[13,768]{1,0:T(8,128)S(1)}, f32[13,768]{1,0:T(8,128)S(1)}, u32[]{:S(2)}, u32[]{:S(2)}) collective-permute-start(f32[13,768]{1,0:T(8,128)S(1)} %add.425), channel_id=1, source_target_pairs={{0,2},{2,0},{4,6},{6,4},{8,10},{10,8},{12,14},{14,12},{16,18},{18,... | collective-permute-start | bytes 119816 | tf_op jit(solution)/shard_map/ppermute | solution.py:194
  216.9 11.1 %collective-permute-start.34 = (bf16[1,1,1,48,1536]{4,3,2,1,0:T(8,128)(2,1)S(1)}, bf16[1,1,1,48,1536]{4,3,2,1,0:T(8,128)(2,1)S(1)}, u32[]{:S(2)}, u32[]{:S(2)}) collective-permute-start(bf16[1,1,1,48,1536]{4,3,2,1,0:T(8,128)(2,1)S(1)} %add_convert_fusion.4), channel_id=1, source_target_pairs={{0,8},{2,10},{4,12},{6,14},{8,16},{10,18},{12,20},{14,22},{16,24},... | collective-permute-start | bytes 442376 | tf_op jit(solution)/shard_map/ppermute | solution.py:194
  217.1 11.0 %collective-permute-start.33 = (bf16[1,1,1,48,1536]{4,3,2,1,0:T(8,128)(2,1)S(1)}, bf16[1,1,1,48,1536]{4,3,2,1,0:T(8,128)(2,1)S(1)}, u32[]{:S(2)}, u32[]{:S(2)}) collective-permute-start(bf16[1,1,1,48,1536]{4,3,2,1,0:T(8,128)(2,1)S(1)} %add_convert_fusion.5), channel_id=1, source_target_pairs={{0,8},{2,10},{4,12},{6,14},{8,16},{10,18},{12,20},{14,22},{16,24},... | collective-permute-start | bytes 442376 | tf_op jit(solution)/shard_map/ppermute | solution.py:194
  217.8 9.5 %collective-permute-start.36 = (bf16[1,48,768]{2,1,0:T(8,128)(2,1)S(1)}, bf16[1,48,768]{2,1,0:T(8,128)(2,1)S(1)}, u32[]{:S(2)}, u32[]{:S(2)}) collective-permute-start(bf16[1,48,768]{2,1,0:T(8,128)(2,1)S(1)} %get-tuple-element.269), channel_id=1, source_target_pairs={{0,8},{2,10},{4,12},{6,14},{8,16},{10,18},{12,20},{14,22},{16,24},... | collective-permute-start | bytes 221192 | tf_op jit(solution)/shard_map/ppermute | solution.py:194
  218.8 9.2 %collective-permute-start.35 = (bf16[1,48,768]{2,1,0:T(8,128)(2,1)S(1)}, bf16[1,48,768]{2,1,0:T(8,128)(2,1)S(1)}, u32[]{:S(2)}, u32[]{:S(2)}) collective-permute-start(bf16[1,48,768]{2,1,0:T(8,128)(2,1)S(1)} %slice_bitcast_fusion), channel_id=1, source_target_pairs={{0,8},{2,10},{4,12},{6,14},{8,16},{10,18},{12,20},{14,22},{16,24},... | collective-permute-start | bytes 221192 | tf_op jit(solution)/shard_map/ppermute | solution.py:194
  222.1 4.1 %collective-permute-start.37 = (f32[13,768]{1,0:T(8,128)S(1)}, f32[13,768]{1,0:T(8,128)S(1)}, u32[]{:S(2)}, u32[]{:S(2)}) collective-permute-start(f32[13,768]{1,0:T(8,128)S(1)} %add.434), channel_id=1, source_target_pairs={{0,4},{2,6},{4,0},{6,2},{8,12},{10,14},{12,8},{14,10},{16,20},{18,... | collective-permute-start | bytes 119816 | tf_op jit(solution)/shard_map/ppermute | solution.py:194
  228.1 8.0 %collective-permute-start.42 = (f32[13,768]{1,0:T(8,128)S(1)}, f32[13,768]{1,0:T(8,128)S(1)}, u32[]{:S(2)}, u32[]{:S(2)}) collective-permute-start(f32[13,768]{1,0:T(8,128)S(1)} %add.439), channel_id=1, source_target_pairs={{0,8},{2,10},{4,12},{6,14},{8,0},{10,2},{12,4},{14,6},{16,24},{18,... | collective-permute-start | bytes 119816 | tf_op jit(solution)/shard_map/ppermute | solution.py:194
  229.1 13.9 %collective-permute-start.39 = (bf16[1,48,1536]{2,1,0:T(8,128)(2,1)S(1)}, bf16[1,48,1536]{2,1,0:T(8,128)(2,1)S(1)}, u32[]{:S(2)}, u32[]{:S(2)}) collective-permute-start(bf16[1,48,1536]{2,1,0:T(8,128)(2,1)S(1)} %get-tuple-element.261), channel_id=1, source_target_pairs={{0,8},{2,10},{4,12},{6,14},{8,16},{10,18},{12,20},{14,22},{16,24},... | collective-permute-start | bytes 442376 | tf_op jit(solution)/shard_map/ppermute | solution.py:194
  232.0 10.9 %collective-permute-start.38 = (bf16[1,48,1536]{2,1,0:T(8,128)(2,1)S(1)}, bf16[1,48,1536]{2,1,0:T(8,128)(2,1)S(1)}, u32[]{:S(2)}, u32[]{:S(2)}) collective-permute-start(bf16[1,48,1536]{2,1,0:T(8,128)(2,1)S(1)} %get-tuple-element.265), channel_id=1, source_target_pairs={{0,8},{2,10},{4,12},{6,14},{8,16},{10,18},{12,20},{14,22},{16,24},... | collective-permute-start | bytes 442376 | tf_op jit(solution)/shard_map/ppermute | solution.py:194
  232.0 9.4 %collective-permute-start.40 = (bf16[1,48,768]{2,1,0:T(8,128)(2,1)S(1)}, bf16[1,48,768]{2,1,0:T(8,128)(2,1)S(1)}, u32[]{:S(2)}, u32[]{:S(2)}) collective-permute-start(bf16[1,48,768]{2,1,0:T(8,128)(2,1)S(1)} %collective-permute-done.35), channel_id=1, source_target_pairs={{0,8},{2,10},{4,12},{6,14},{8,16},{10,18},{12,20},{14,22},{16,24},... | collective-permute-start | bytes 221192 | tf_op jit(solution)/shard_map/ppermute | solution.py:194
  232.0 10.9 %collective-permute-start.41 = (bf16[1,48,768]{2,1,0:T(8,128)(2,1)S(1)}, bf16[1,48,768]{2,1,0:T(8,128)(2,1)S(1)}, u32[]{:S(2)}, u32[]{:S(2)}) collective-permute-start(bf16[1,48,768]{2,1,0:T(8,128)(2,1)S(1)} %collective-permute-done.36), channel_id=1, source_target_pairs={{0,8},{2,10},{4,12},{6,14},{8,16},{10,18},{12,20},{14,22},{16,24},... | collective-permute-start | bytes 221192 | tf_op jit(solution)/shard_map/ppermute | solution.py:194
  242.9 5.8 %collective-permute-start.47 = (f32[13,768]{1,0:T(8,128)S(1)}, f32[13,768]{1,0:T(8,128)S(1)}, u32[]{:S(2)}, u32[]{:S(2)}) collective-permute-start(f32[13,768]{1,0:T(8,128)S(1)} %add.440), channel_id=1, source_target_pairs={{0,16},{2,18},{4,20},{6,22},{8,24},{10,26},{12,28},{14,30},{16,0},... | collective-permute-start | bytes 119816 | tf_op jit(solution)/shard_map/ppermute | solution.py:194
  243.0 10.8 %collective-permute-start.43 = (bf16[1,48,1536]{2,1,0:T(8,128)(2,1)S(1)}, bf16[1,48,1536]{2,1,0:T(8,128)(2,1)S(1)}, u32[]{:S(2)}, u32[]{:S(2)}) collective-permute-start(bf16[1,48,1536]{2,1,0:T(8,128)(2,1)S(1)} %collective-permute-done.38), channel_id=1, source_target_pairs={{0,8},{2,10},{4,12},{6,14},{8,16},{10,18},{12,20},{14,22},{16,24},... | collective-permute-start | bytes 442376 | tf_op jit(solution)/shard_map/ppermute | solution.py:194
  243.6 10.2 %collective-permute-start.44 = (bf16[1,48,1536]{2,1,0:T(8,128)(2,1)S(1)}, bf16[1,48,1536]{2,1,0:T(8,128)(2,1)S(1)}, u32[]{:S(2)}, u32[]{:S(2)}) collective-permute-start(bf16[1,48,1536]{2,1,0:T(8,128)(2,1)S(1)} %collective-permute-done.39), channel_id=1, source_target_pairs={{0,8},{2,10},{4,12},{6,14},{8,16},{10,18},{12,20},{14,22},{16,24},... | collective-permute-start | bytes 442376 | tf_op jit(solution)/shard_map/ppermute | solution.py:194
  246.5 6.2 %collective-permute-start.45 = (bf16[1,48,768]{2,1,0:T(8,128)(2,1)S(1)}, bf16[1,48,768]{2,1,0:T(8,128)(2,1)S(1)}, u32[]{:S(2)}, u32[]{:S(2)}) collective-permute-start(bf16[1,48,768]{2,1,0:T(8,128)(2,1)S(1)} %collective-permute-done.40), channel_id=1, source_target_pairs={{0,8},{2,10},{4,12},{6,14},{8,16},{10,18},{12,20},{14,22},{16,24},... | collective-permute-start | bytes 221192 | tf_op jit(solution)/shard_map/ppermute | solution.py:194
  246.6 7.3 %collective-permute-start.46 = (bf16[1,48,768]{2,1,0:T(8,128)(2,1)S(1)}, bf16[1,48,768]{2,1,0:T(8,128)(2,1)S(1)}, u32[]{:S(2)}, u32[]{:S(2)}) collective-permute-start(bf16[1,48,768]{2,1,0:T(8,128)(2,1)S(1)} %collective-permute-done.41), channel_id=1, source_target_pairs={{0,8},{2,10},{4,12},{6,14},{8,16},{10,18},{12,20},{14,22},{16,24},... | collective-permute-start | bytes 221192 | tf_op jit(solution)/shard_map/ppermute | solution.py:194
  253.9 12.3 %collective-permute-start.51 = (bf16[4,48,768]{2,1,0:T(8,128)(2,1)S(1)}, bf16[4,48,768]{2,1,0:T(8,128)(2,1)S(1)}, u32[]{:S(2)}, u32[]{:S(2)}) collective-permute-start(bf16[4,48,768]{2,1,0:T(8,128)(2,1)S(1)} %pad_maximum_fusion.9), channel_id=1, source_target_pairs={{0,4},{2,6},{4,0},{6,2},{8,12},{10,14},{12,8},{14,10},{16,20},{18,... | collective-permute-start | bytes 884744 | tf_op jit(solution)/shard_map/ppermute | solution.py:194
  255.6 10.6 %collective-permute-start.50 = (bf16[4,48,768]{2,1,0:T(8,128)(2,1)S(1)}, bf16[4,48,768]{2,1,0:T(8,128)(2,1)S(1)}, u32[]{:S(2)}, u32[]{:S(2)}) collective-permute-start(bf16[4,48,768]{2,1,0:T(8,128)(2,1)S(1)} %pad_maximum_fusion.8), channel_id=1, source_target_pairs={{0,2},{2,0},{4,6},{6,4},{8,10},{10,8},{12,14},{14,12},{16,18},{18,... | collective-permute-start | bytes 884744 | tf_op jit(solution)/shard_map/ppermute | solution.py:194
  257.7 8.5 %collective-permute-start.49 = (bf16[1,48,1536]{2,1,0:T(8,128)(2,1)S(1)}, bf16[1,48,1536]{2,1,0:T(8,128)(2,1)S(1)}, u32[]{:S(2)}, u32[]{:S(2)}) collective-permute-start(bf16[1,48,1536]{2,1,0:T(8,128)(2,1)S(1)} %collective-permute-done.44), channel_id=1, source_target_pairs={{0,8},{2,10},{4,12},{6,14},{8,16},{10,18},{12,20},{14,22},{16,24},... | collective-permute-start | bytes 442376 | tf_op jit(solution)/shard_map/ppermute | solution.py:194
  258.8 7.3 %collective-permute-start.48 = (bf16[1,48,1536]{2,1,0:T(8,128)(2,1)S(1)}, bf16[1,48,1536]{2,1,0:T(8,128)(2,1)S(1)}, u32[]{:S(2)}, u32[]{:S(2)}) collective-permute-start(bf16[1,48,1536]{2,1,0:T(8,128)(2,1)S(1)} %collective-permute-done.43), channel_id=1, source_target_pairs={{0,8},{2,10},{4,12},{6,14},{8,16},{10,18},{12,20},{14,22},{16,24},... | collective-permute-start | bytes 442376 | tf_op jit(solution)/shard_map/ppermute | solution.py:194
  266.2 15.0 %collective-permute-start.55 = (bf16[8,48,768]{2,1,0:T(8,128)(2,1)S(1)}, bf16[8,48,768]{2,1,0:T(8,128)(2,1)S(1)}, u32[]{:S(2)}, u32[]{:S(2)}) collective-permute-start(bf16[8,48,768]{2,1,0:T(8,128)(2,1)S(1)} %constant_dynamic-update-slice_fusion.25.refs_2_), channel_id=1, source_target_pairs={{0,2},{2,0},{4,6},{6,4},{8,10},{10,8},{12,14},{14,12},{16,18},{18,... | collective-permute-start | bytes 1769480 | tf_op jit(solution)/shard_map/ppermute | solution.py:194
  267.7 13.6 %collective-permute-start.53 = (bf16[4,48,1536]{2,1,0:T(8,128)(2,1)S(1)}, bf16[4,48,1536]{2,1,0:T(8,128)(2,1)S(1)}, u32[]{:S(2)}, u32[]{:S(2)}) collective-permute-start(bf16[4,48,1536]{2,1,0:T(8,128)(2,1)S(1)} %pad_maximum_fusion.4), channel_id=1, source_target_pairs={{0,4},{2,6},{4,0},{6,2},{8,12},{10,14},{12,8},{14,10},{16,20},{18,... | collective-permute-start | bytes 1769480 | tf_op jit(solution)/shard_map/ppermute | solution.py:194
  268.6 22.9 %collective-permute-start.52 = (bf16[4,48,1536]{2,1,0:T(8,128)(2,1)S(1)}, bf16[4,48,1536]{2,1,0:T(8,128)(2,1)S(1)}, u32[]{:S(2)}, u32[]{:S(2)}) collective-permute-start(bf16[4,48,1536]{2,1,0:T(8,128)(2,1)S(1)} %pad_maximum_fusion.3), channel_id=1, source_target_pairs={{0,2},{2,0},{4,6},{6,4},{8,10},{10,8},{12,14},{14,12},{16,18},{18,... | collective-permute-start | bytes 1769480 | tf_op jit(solution)/shard_map/ppermute | solution.py:194
  269.3 22.2 %collective-permute-start.54 = (bf16[8,48,768]{2,1,0:T(8,128)(2,1)S(1)}, bf16[8,48,768]{2,1,0:T(8,128)(2,1)S(1)}, u32[]{:S(2)}, u32[]{:S(2)}) collective-permute-start(bf16[8,48,768]{2,1,0:T(8,128)(2,1)S(1)} %constant_dynamic-update-slice_fusion.20.refs_0_), channel_id=1, source_target_pairs={{0,4},{2,6},{4,0},{6,2},{8,12},{10,14},{12,8},{14,10},{16,20},{18,... | collective-permute-start | bytes 1769480 | tf_op jit(solution)/shard_map/ppermute | solution.py:194
  292.4 20.6 %collective-permute-start.57 = (bf16[8,48,1536]{2,1,0:T(8,128)(2,1)S(1)}, bf16[8,48,1536]{2,1,0:T(8,128)(2,1)}, u32[]{:S(2)}, u32[]{:S(2)}) collective-permute-start(bf16[8,48,1536]{2,1,0:T(8,128)(2,1)S(1)} %constant_dynamic-update-slice_fusion.35.refs_0_), channel_id=1, source_target_pairs={{0,2},{2,0},{4,6},{6,4},{8,10},{10,8},{12,14},{14,12},{16,18},{18,... | collective-permute-start | bytes 3538952 | tf_op jit(solution)/shard_map/ppermute | solution.py:194
  294.6 18.4 %collective-permute-start.56 = (bf16[8,48,1536]{2,1,0:T(8,128)(2,1)}, bf16[8,48,1536]{2,1,0:T(8,128)(2,1)}, u32[]{:S(2)}, u32[]{:S(2)}) collective-permute-start(bf16[8,48,1536]{2,1,0:T(8,128)(2,1)} %constant_dynamic-update-slice_fusion.30.refs_0_), channel_id=1, source_target_pairs={{0,4},{2,6},{4,0},{6,2},{8,12},{10,14},{12,8},{14,10},{16,20},{18,... | collective-permute-start | bytes 3538952 | tf_op jit(solution)/shard_map/ppermute | solution.py:194
  326.9 4.9 %collective-permute-start.58 = (f32[768,768]{1,0:T(8,128)}, f32[768,768]{1,0:T(8,128)}, u32[]{:S(2)}, u32[]{:S(2)}) collective-permute-start(f32[768,768]{1,0:T(8,128)} %get-tuple-element.284), channel_id=1, source_target_pairs={{0,1},{1,0},{2,3},{3,2},{4,5},{5,4},{6,7},{7,6},{8,9},{9,8},{10,11... | collective-permute-start | bytes 7077896 | tf_op jit(solution)/shard_map/ppermute | solution.py:254
  364.2 2.6 collective-permute-start.61
  365.1 6.7 %collective-permute-start.59 = (f32[48,768]{1,0:T(8,128)S(1)}, f32[48,768]{1,0:T(8,128)S(1)}, u32[]{:S(2)}, u32[]{:S(2)}) collective-permute-start(f32[48,768]{1,0:T(8,128)S(1)} %get-tuple-element.297), channel_id=1, source_target_pairs={{0,2},{1,3},{2,0},{3,1},{4,6},{5,7},{6,4},{7,5},{8,10},{9,11},{10,... | collective-permute-start | bytes 442376 | tf_op jit(solution)/shard_map/ppermute | solution.py:809
  366.5 7.3 %collective-permute-start.60 = (f32[48,768]{1,0:T(8,128)S(1)}, f32[48,768]{1,0:T(8,128)S(1)}, u32[]{:S(2)}, u32[]{:S(2)}) collective-permute-start(f32[48,768]{1,0:T(8,128)S(1)} %get-tuple-element.297), channel_id=1, source_target_pairs={{0,3},{1,2},{2,1},{3,0},{4,7},{5,6},{6,5},{7,4},{8,11},{9,10},{10,... | collective-permute-start | bytes 442376 | tf_op jit(solution)/shard_map/ppermute | solution.py:809
  (44 other events, 454.7 us)
